TPU v7x, 128 devices: a whole 4x4x4 slice. The times are simulated.
128 devices in a mesh: seq: 8 (over x, z_hi), head: 16 (over y, z_lo, core).
Axes of the slice: x: 4, y: 4, z: 4 (z_hi: 2, z_lo: 2; z = z_hi * 2 + z_lo), core: 2. Of those that a mesh axis runs over, the one named last changes fastest.
Arguments:
- queries: bfloat16 [8192, 8192], P('seq', 'head'), may hold values from -8 to 8
- keys: bfloat16 [8192, 1024], P('seq'), may hold values from -8 to 8
- values: bfloat16 [8192, 1024], P('seq'), may hold values from -24 to 24
- w_out: bfloat16 [8192, 6144], P('head'), may hold values from -0.0625 to 0.0625
Outputs:
- mixed: bfloat16 [8192, 6144], P(('seq', 'head'))
All inputs are finite; a program needn't handle non-finite values.
Results may differ from a plain program's by a relative error of at most 0.023.
Values may be sent and summed in bfloat16 or wider, within the bound.
No kernel may reach another device: no remote copies, remote signals or barrier semaphores. Data moves between devices by JAX's collectives and lax.ppermute only.
A program may use at most 128 MiB of HBM per device.

v0:
```python
import functools

import jax
import jax.numpy as jnp
from jax import lax
from jax.experimental import pallas as pl
from jax.experimental.pallas import tpu as pltpu
from jax.sharding import PartitionSpec as P

KV_HEADS = 8
DH = 128
LOG2E = 1.4426950408889634
NEG = -1e30
LIMIT = 60.0
BF = jnp.bfloat16
F32 = jnp.float32
PARAMS = pltpu.CompilerParams(vmem_limit_bytes=56 << 20)
FETCH = ((7, 3), (6, 2), (5, 1), (4, None))
SLOTS = [d for pair in FETCH for d in pair if d is not None]
TABLE = 6


def after(x, *deps):
    return lax.optimization_barrier((x, *deps))[0]


def prep_kernel(info, k_ref, v_ref, kv_ref):
    rows = k_ref.shape[0]
    kv_ref[0:rows, :] = k_ref[...]
    for t in range(rows // DH):
        kv_ref[rows + t * DH : rows + (t + 1) * DH, :] = v_ref[t * DH : (t + 1) * DH, :].T


def prep(info, keys, values):
    rows = keys.shape[0]
    col = pl.BlockSpec((rows, DH), lambda i, info: (0, info[1]))
    return pl.pallas_call(
        prep_kernel,
        grid_spec=pltpu.PrefetchScalarGridSpec(
            num_scalar_prefetch=1,
            grid=(1,),
            in_specs=[col, col],
            out_specs=pl.BlockSpec((2 * rows, DH), lambda i, info: (0, 0)),
        ),
        out_shape=jax.ShapeDtypeStruct((2 * rows, DH), BF),
        name="prep",
        compiler_params=PARAMS,
    )(info, keys, values)


def keys_of(kv):
    k = kv[0 : kv.shape[0] // 2, :]
    return jnp.concatenate([k, k], axis=1)


def values_of(kv):
    rows = kv.shape[0] // 2
    tiles = [kv[rows + t * DH : rows + (t + 1) * DH, :] for t in range(rows // DH)]
    return jnp.concatenate([jnp.concatenate(tiles, axis=1), jnp.ones((16, rows), BF)], axis=0)


def load_queries(q, h, qt_ref):
    qb = q.shape[0]
    scaled = q.astype(F32) * (DH**-0.5 * LOG2E)
    high = scaled.astype(BF)
    low = (scaled - high.astype(F32)).astype(BF)
    qt_ref[0:DH, h * qb : (h + 1) * qb] = high.T
    qt_ref[DH : 2 * DH, h * qb : (h + 1) * qb] = low.T


def exact_block(kv, behind, second, groups, qt_ref, acc, m_ref):
    rows = kv.shape[0] // 2
    heads = KV_HEADS // 2
    qb = qt_ref.shape[1] // heads
    sub = qb // groups
    kk, vt = keys_of(kv), values_of(kv)
    j = lax.broadcasted_iota(jnp.int32, (rows, qb), 1)
    pos = behind * rows + j // sub * (rows // groups) + second * sub + j % sub
    allowed = lax.broadcasted_iota(jnp.int32, (rows, qb), 0) <= pos
    for h in range(heads):
        c = slice(h * qb, (h + 1) * qb)
        s = jnp.where(allowed, jnp.dot(kk, qt_ref[:, c], preferred_element_type=F32), NEG)
        m = m_ref[0:1, c]
        top = jnp.maximum(m, jnp.max(s, axis=0, keepdims=True))
        acc[:, c] = acc[:, c] * jnp.exp2(m - top) + jnp.dot(
            vt, jnp.exp2(s - top).astype(BF), preferred_element_type=F32
        )
        m_ref[:, c] = jnp.broadcast_to(top, (8, qb))


def own_kernel(groups, q_ref, kv_ref, qt_ref, acc_ref, m_ref):
    _, _, sub, width = q_ref.shape
    for h in range(width // DH):
        load_queries(q_ref[:, 0, :, h * DH : (h + 1) * DH].reshape(groups * sub, DH), h, qt_ref)
    acc_ref[...] = jnp.zeros_like(acc_ref)
    m_ref[...] = jnp.full_like(m_ref, NEG)
    exact_block(kv_ref, 0, 0, groups, qt_ref, acc_ref, m_ref)


def own(q4, kv):
    groups, _, sub, width = q4.shape
    cols = groups * sub * width // DH
    return pl.pallas_call(
        functools.partial(own_kernel, groups),
        grid=(1,),
        in_specs=[
            pl.BlockSpec((groups, 1, sub, width), lambda i: (0, 0, 0, 0)),
            pl.BlockSpec(kv.shape, lambda i: (0, 0)),
        ],
        out_specs=[
            pl.BlockSpec((2 * DH, cols), lambda i: (0, 0)),
            pl.BlockSpec((DH + 16, cols), lambda i: (0, 0)),
            pl.BlockSpec((8, cols), lambda i: (0, 0)),
        ],
        out_shape=[
            jax.ShapeDtypeStruct((2 * DH, cols), BF),
            jax.ShapeDtypeStruct((DH + 16, cols), F32),
            jax.ShapeDtypeStruct((8, cols), F32),
        ],
        name="own",
        cost_estimate=pl.CostEstimate(
            flops=2 * cols * kv.shape[0] * 2 * DH, bytes_accessed=8 << 20, transcendentals=0
        ),
        compiler_params=PARAMS,
    )(q4, kv)


def attend_kernel(foreign, groups, n_y, n_seq, info, own_ref, *refs):
    ops = n_seq // 2
    inputs = 1 if foreign else 3
    mine, other = refs[inputs : inputs + ops], refs[inputs + ops : inputs + 2 * ops]
    o_ref, peer_ref, q_buf, kv_buf, qt_ref, acc_ref, m_ref, mx_ref, count, sems = refs[inputs + 2 * ops :]
    place, core, partner = info[0], info[2], info[5]
    rows = own_ref.shape[0] // 2
    cols = qt_ref.shape[1]
    heads = KV_HEADS // 2
    qb = cols // heads
    sub = qb // groups
    half = cols // 4
    limit = partner if foreign else place
    n = len(SLOTS)
    if foreign:
        state = [pltpu.make_async_copy(refs[0], q_buf, sems.at[n + 1])]
    else:
        state = [
            pltpu.make_async_copy(refs[0], qt_ref, sems.at[n + 1]),
            pltpu.make_async_copy(refs[1], acc_ref.at[0], sems.at[n + 2]),
            pltpu.make_async_copy(refs[2], m_ref, sems.at[n + 3]),
        ]

    def behind(i):
        return limit - lax.bitwise_xor(place, info[TABLE + i])

    def start(src, slot):
        pltpu.make_async_copy(src, kv_buf.at[slot], sems.at[slot]).start()

    def wait(slot):
        pltpu.make_async_copy(own_ref, kv_buf.at[slot], sems.at[slot]).wait()

    for load in state:
        load.start()
    if foreign:

        @pl.when(place < limit)
        def _():
            start(own_ref, 0)

    for i in range(n):

        @pl.when(jnp.logical_and(behind(i) >= 0, core == i % 2))
        def _():
            start(mine[i // 2], i + 1)

        @pl.when(jnp.logical_and(behind(i) >= 0, core != i % 2))
        def _():
            start(other[i // 2], i + 1)

    for load in state:
        load.wait()
    count[0] = 0
    if foreign:
        for h in range(heads):
            load_queries(q_buf[:, :, h * DH : (h + 1) * DH].reshape(qb, DH), h, qt_ref)
        acc_ref[0] = jnp.zeros(acc_ref.shape[1:], F32)
        m_ref[...] = jnp.full_like(m_ref, NEG)

        def exact(slot, _):
            back = limit - jnp.where(slot == 0, place, partner)

            @pl.when(back >= 0)
            def _():
                wait(slot)
                exact_block(kv_buf.at[slot], back, 1, groups, qt_ref, acc_ref.at[0], m_ref)

            return 0

        lax.fori_loop(0, 2, exact, 0)

    def scores(kk, c0):
        return jnp.dot(kk, qt_ref[:, c0 : c0 + half], preferred_element_type=F32)

    def add_block(i, _):
        @pl.when(behind(i) > 0)
        def _():
            slot = i + 1
            wait(slot)
            old = count[0] % 2
            new = 1 - old
            count[0] = count[0] + 1
            kk, vt = keys_of(kv_buf.at[slot]), values_of(kv_buf.at[slot])
            for c0 in range(0, cols, half):
                s = scores(kk, c0)
                mx_ref[:, c0 : c0 + half] = jnp.max(s.reshape(rows // 8, 8, half), axis=0)
                p = jnp.exp2(s - m_ref[0:1, c0 : c0 + half]).astype(BF)
                acc_ref[new, :, c0 : c0 + half] = acc_ref[old, :, c0 : c0 + half] + jnp.dot(
                    vt, p, preferred_element_type=F32
                )
            over = jnp.max(mx_ref[...] - m_ref[...])

            @pl.when(over > LIMIT)
            def _():
                for c0 in range(0, cols, half):
                    m = m_ref[0:1, c0 : c0 + half]
                    top = jnp.maximum(m, jnp.max(mx_ref[:, c0 : c0 + half], axis=0, keepdims=True))
                    p = jnp.exp2(scores(kk, c0) - top).astype(BF)
                    acc_ref[new, :, c0 : c0 + half] = acc_ref[old, :, c0 : c0 + half] * jnp.exp2(
                        m - top
                    ) + jnp.dot(vt, p, preferred_element_type=F32)
                    m_ref[:, c0 : c0 + half] = jnp.broadcast_to(top, (8, half))

        return 0

    lax.fori_loop(0, n, add_block, 0)
    last = count[0] % 2
    for h in range(heads):
        o = acc_ref[last, :, h * qb : (h + 1) * qb]
        o = (o[0:DH] * (1.0 / o[DH : DH + 1])).astype(BF).T
        for g in range(groups):
            ry = (g // 4 + n_y - info[3]) % n_y
            rz = (g // 2 % 2) ^ info[4]
            by_y = ((ry * 2 + rz) * 2 + g % 2) * sub
            by_z = (((ry // 2 * 2 + rz) * 2 + ry % 2) * 2 + g % 2) * sub
            piece = o[g * sub : (g + 1) * sub, :]
            here = pl.multiple_of(jnp.where(core == 0, by_y, by_z), sub)
            there = pl.multiple_of(jnp.where(core == 0, by_z, by_y), sub)
            o_ref[pl.ds(here, sub), h * DH : (h + 1) * DH] = piece
            peer_ref[pl.ds(there, sub), h * DH : (h + 1) * DH] = piece


def attend(info, kv, state, q_shape, mine, other, n_y, n_seq):
    foreign = len(state) == 1
    groups, sub, width = q_shape
    qb = groups * sub
    cols = qb * width // DH
    any_space = pl.BlockSpec(memory_space=pl.ANY)
    out = pl.BlockSpec((qb, width), lambda i, info: (0, 0))
    return pl.pallas_call(
        functools.partial(attend_kernel, foreign, groups, n_y, n_seq),
        grid_spec=pltpu.PrefetchScalarGridSpec(
            num_scalar_prefetch=1,
            grid=(1,),
            in_specs=[any_space] * (1 + len(state) + 2 * len(mine)),
            out_specs=[out, out],
            scratch_shapes=[
                pltpu.VMEM(q_shape, BF),
                pltpu.VMEM((len(SLOTS) + 1, *kv.shape), BF),
                pltpu.VMEM((2 * DH, cols), BF),
                pltpu.VMEM((2, DH + 16, cols), F32),
                pltpu.VMEM((8, cols), F32),
                pltpu.VMEM((8, cols), F32),
                pltpu.SMEM((1,), jnp.int32),
                pltpu.SemaphoreType.DMA((len(SLOTS) + 4,)),
            ],
        ),
        out_shape=[jax.ShapeDtypeStruct((qb, width), BF)] * 2,
        name="attend_foreign" if foreign else "attend_own",
        cost_estimate=pl.CostEstimate(
            flops=2 * cols * kv.shape[0] * 4 * DH, bytes_accessed=4 << 20, transcendentals=0
        ),
        compiler_params=PARAMS,
    )(info, kv, *state, *mine, *other)


def project(info, mine, other, w, w_other, parts, tile):
    rows, width = mine.shape
    n = w.shape[1] // 2
    steps = n // tile

    def body(info, a, b, wa, wb, *outs):
        s = jnp.dot(a[...], wa[...], preferred_element_type=F32) + jnp.dot(
            b[...], wb[...], preferred_element_type=F32
        )
        part = s.shape[0] // len(outs)
        for i, o in enumerate(outs):
            o[...] = s[i * part : (i + 1) * part].astype(BF)

    whole = pl.BlockSpec((rows, width), lambda i, info: (0, 0))
    weights = pl.BlockSpec((width, tile), lambda i, info: (0, info[2] * steps + i))
    return pl.pallas_call(
        body,
        grid_spec=pltpu.PrefetchScalarGridSpec(
            num_scalar_prefetch=1,
            grid=(steps,),
            in_specs=[whole, whole, weights, weights],
            out_specs=[pl.BlockSpec((rows // parts, tile), lambda i, info: (0, i))] * parts,
        ),
        out_shape=[jax.ShapeDtypeStruct((rows // parts, n), BF)] * parts,
        name="project",
        cost_estimate=pl.CostEstimate(
            flops=4 * rows * width * n, bytes_accessed=4 * width * n + 4 * rows * n, transcendentals=0
        ),
        compiler_params=PARAMS,
    )(info, mine, other, w, w_other)


def sum_one(info, parts, got, tile):
    def body(info, p0, p2, g0, g1, g2, a0, a1, b0, b1):
        first = p0[...].astype(F32) + g0[...].astype(F32)
        middle = g1[...].astype(F32)
        first = first + jnp.where(info[2] == 0, middle + g2[...].astype(F32), 0.0)
        second = p2[...].astype(F32) + middle
        n = a0.shape[0]
        a0[...] = first[:n].astype(BF)
        a1[...] = first[n:].astype(BF)
        b0[...] = second[:n].astype(BF)
        b1[...] = second[n:].astype(BF)

    rows, cols = parts[0].shape
    whole = pl.BlockSpec((rows, tile), lambda i, info: (0, i))
    half = pl.BlockSpec((rows // 2, tile), lambda i, info: (0, i))
    return pl.pallas_call(
        body,
        grid_spec=pltpu.PrefetchScalarGridSpec(
            num_scalar_prefetch=1, grid=(cols // tile,), in_specs=[whole] * 5, out_specs=[half] * 4
        ),
        out_shape=[jax.ShapeDtypeStruct((rows // 2, cols), BF)] * 4,
        name="sum_one",
        compiler_params=PARAMS,
    )(info, parts[0], parts[2], *got)


def add(*terms):
    total = terms[0].astype(F32)
    for t in terms[1:]:
        total = total + t.astype(F32)
    return total.astype(BF)


def local(queries, keys, values, w_out):
    n_seq, n_head = lax.axis_size("seq"), lax.axis_size("head")
    rows, width = queries.shape
    cols = w_out.shape[1]
    place = lax.axis_index("seq")
    head = lax.axis_index("head")
    core, y, z = head % 2, head // 4, head // 2 % 2
    n_y = n_head // 4
    partner = n_seq - 1 - place
    info = jnp.stack([place, head * KV_HEADS // n_head, core, y, z, partner, *SLOTS]).astype(jnp.int32)

    def over_all(x, f):
        pairs = []
        for s in range(n_seq):
            for h in range(n_head):
                to = f(s, h // 4, h // 2 % 2, h % 2)
                if to is not None:
                    s2, y2, z2, c2 = to
                    pairs.append((s * n_head + h, s2 * n_head + (y2 % n_y) * 4 + z2 * 2 + c2))
        return lax.ppermute(x, ("seq", "head"), pairs)

    def swap_core(x):
        return over_all(x, lambda s, y, z, c: (s, y, z, 1 - c))

    def fetch(x, pair):
        def to(s, y, z, c):
            if pair[c] is None:
                return None
            t = s ^ pair[c]
            return (t, y, z, c) if s <= max(t, n_seq - 1 - t) else None

        return over_all(x, to)

    sub = rows // n_head // 2
    q4 = queries.reshape(n_head, 2, sub, width)
    w_other = swap_core(w_out)
    kv = prep(info, keys, values)
    mine = [fetch(kv, pair) for pair in FETCH]
    state = own(q4, kv)
    other = [swap_core(after(x, state[2])) for x in mine]
    q_far = over_all(after(q4[:, 1], state[2], *mine), lambda s, y, z, c: (n_seq - 1 - s, y, z, c))

    def stage_one(parts):
        return [
            over_all(parts[1], lambda s, y, z, c: (s, y, 1 - z, c) if c else (s, y + 1, z, c)),
            over_all(parts[3], lambda s, y, z, c: (s, y, 1 - z, c) if c else (s, y - 1, z, c)),
            over_all(parts[2], lambda s, y, z, c: None if c else (s, y + 2, z, c)),
        ]

    def stage_two(total):
        return [
            over_all(total[1], lambda s, y, z, c: (s, y + 1, z, c) if c else (s, y, 1 - z, c)),
            over_all(total[3], lambda s, y, z, c: (s, y - 1, z, c) if c else None),
            over_all(total[2], lambda s, y, z, c: (s, y + 2, z, c) if c else None),
        ]

    half = (n_head, sub, width)
    near, near_peer = attend(info, kv, state, half, mine, other, n_y, n_seq)
    near_far = swap_core(near_peer)
    parts_n = project(info, near, near_far, w_out, w_other, n_y, cols // 4)
    got_n = stage_one(parts_n)
    far, far_peer = attend(after(info, parts_n[0]), kv, [q_far], half, mine, other, n_y, n_seq)
    far_far = swap_core(far_peer)
    total_n = sum_one(info, parts_n, got_n, cols // 4)
    got2_n = stage_two(total_n)
    parts_f = project(after(info, *total_n), far, far_far, w_out, w_other, n_y, cols // 4)
    done_n = add(total_n[0], *got2_n).reshape(2, sub, cols // 2)
    parts_f = [after(p, done_n) for p in parts_f]
    got_f = stage_one(parts_f)

    def by_core(x, same):
        return jnp.where((core == 0) == same, x[0], x[1])

    own_other = swap_core(by_core(done_n, False))
    total_f = sum_one(info, parts_f, got_f, cols // 4)
    got2_f = stage_two(total_f)
    done_f = add(total_f[0], *got2_f).reshape(2, sub, cols // 2)
    home = over_all(by_core(done_f, True), lambda s, y, z, c: (n_seq - 1 - s, y, z, c))
    home_other = over_all(by_core(done_f, False), lambda s, y, z, c: (n_seq - 1 - s, y, z, 1 - c))
    here = jnp.concatenate([by_core(done_n, True), home], axis=0)
    there = jnp.concatenate([own_other, home_other], axis=0)
    left = jnp.where(core == 0, here, there)
    right = jnp.where(core == 0, there, here)
    return jnp.concatenate([left, right], axis=1)


def solution(mesh):
    placed = (P("seq", "head"), P("seq", None), P("seq", None), P("head", None))
    return jax.shard_map(
        local, mesh=mesh, in_specs=placed, out_specs=P(("seq", "head"), None), check_vma=False
    )
```

profile of v0, /device:TPU:1, one launch (start us, length us, event | category | flops | bytes accessed | tf_op | source)
XLA Modules:
  0.0 178.4 jit_solution(11564009622987975069)
XLA Ops:
  0.0 1.4 collective-permute-start.9
  2.1 2.7 %prep.1.kv_ref.own_ref = bf16[2048,128]{1,0:T(8,128)(2,1)} custom-call(s32[13]{0:T(128)} %stack.27.info, bf16[1024,1024]{1,0:T(8,128)(2,1)} %k_ref.1, bf16[1024,1024]{1,0:T(8,128)(2,1)} %v_ref.1), custom_call_target="tpu_custom_call" | custom-call | tf_op jit(solution)/shard_map/prep/pallas_call | solution.py:37
  4.7 6.5 %collective-permute-start = (bf16[2048,128]{1,0:T(8,128)(2,1)}, bf16[2048,128]{1,0:T(8,128)(2,1)S(1)}, u32[]{:S(2)}, u32[]{:S(2)}) collective-permute-start(bf16[2048,128]{1,0:T(8,128)(2,1)} %prep.1.kv_ref.own_ref), channel_id=1, source_target_pairs={{0,112},{1,49},{2,114},{3,51},{4,116},{5,53},{6,118},{7,55},{8,120... | collective-permute-start | bytes 1572872 | tf_op jit(solution)/shard_map/ppermute | solution.py:368
  11.2 2.2 %collective-permute-start.1 = (bf16[2048,128]{1,0:T(8,128)(2,1)}, bf16[2048,128]{1,0:T(8,128)(2,1)S(1)}, u32[]{:S(2)}, u32[]{:S(2)}) collective-permute-start(bf16[2048,128]{1,0:T(8,128)(2,1)} %prep.1.kv_ref.own_ref), channel_id=1, source_target_pairs={{0,96},{1,33},{2,98},{3,35},{4,100},{5,37},{6,102},{7,39},{8,104},... | collective-permute-start | bytes 1572872 | tf_op jit(solution)/shard_map/ppermute | solution.py:368
  13.4 1.9 %collective-permute-start.2 = (bf16[2048,128]{1,0:T(8,128)(2,1)}, bf16[2048,128]{1,0:T(8,128)(2,1)S(1)}, u32[]{:S(2)}, u32[]{:S(2)}) collective-permute-start(bf16[2048,128]{1,0:T(8,128)(2,1)} %prep.1.kv_ref.own_ref), channel_id=1, source_target_pairs={{0,80},{1,17},{2,82},{3,19},{4,84},{5,21},{6,86},{7,23},{8,88},{9,... | collective-permute-start | bytes 1572872 | tf_op jit(solution)/shard_map/ppermute | solution.py:368
  15.4 0.7 collective-permute-start.3
  16.1 6.3 %own.1 = (bf16[256,2048]{1,0:T(8,128)(2,1)}, f32[144,2048]{1,0:T(8,128)}, f32[8,2048]{1,0:T(8,128)}) custom-call(bf16[16,2,32,512]{3,2,1,0:T(8,128)(2,1)} %bitcast.12, bf16[2048,128]{1,0:T(8,128)(2,1)} %prep.1.kv_ref.own_ref), custom_call_target="tpu_custom_call" | custom-call | flops 2147483648 | bytes 8388608 | tf_op jit(solution)/shard_map/own/pallas_call | solution.py:103
  22.4 1.3 collective-permute-done.refs_3_.refs_1_
  23.7 4.8 %collective-permute-start.4 = (bf16[2048,128]{1,0:T(8,128)(2,1)S(1)}, bf16[2048,128]{1,0:T(8,128)(2,1)S(1)}, u32[]{:S(2)}, u32[]{:S(2)}) collective-permute-start(bf16[2048,128]{1,0:T(8,128)(2,1)S(1)} %collective-permute-done.refs_3_.refs_1_), channel_id=1, source_target_pairs={{0,1},{1,0},{2,3},{3,2},{4,5},{5,4},{6,7},{7,6},{8,9},{9,8},{10,11... | collective-permute-start | bytes 1572872 | tf_op jit(solution)/shard_map/ppermute | solution.py:368
  28.5 5.4 %collective-permute-done.1.refs_4_.refs_2_ = bf16[2048,128]{1,0:T(8,128)(2,1)S(1)} collective-permute-done((bf16[2048,128]{1,0:T(8,128)(2,1)}, bf16[2048,128]{1,0:T(8,128)(2,1)S(1)}, u32[]{:S(2)}, u32[]{:S(2)}) %collective-permute-start.1) | collective-permute-done | bytes 524320 | tf_op jit(solution)/shard_map/ppermute | solution.py:368
  34.0 7.0 %collective-permute-start.5 = (bf16[2048,128]{1,0:T(8,128)(2,1)S(1)}, bf16[2048,128]{1,0:T(8,128)(2,1)S(1)}, u32[]{:S(2)}, u32[]{:S(2)}) collective-permute-start(bf16[2048,128]{1,0:T(8,128)(2,1)S(1)} %collective-permute-done.1.refs_4_.refs_2_), channel_id=1, source_target_pairs={{0,1},{1,0},{2,3},{3,2},{4,5},{5,4},{6,7},{7,6},{8,9},{9,8},{10,11... | collective-permute-start | bytes 1572872 | tf_op jit(solution)/shard_map/ppermute | solution.py:368
  41.5 1.0 collective-permute-done.5.refs_8_.refs_6_
  42.5 0.7 collective-permute-done.6.refs_9_.refs_7_
  43.3 0.7 collective-permute-done.7.refs_10_.refs_8_
  44.1 0.7 copy-done.17
  44.9 3.8 %attend_own.1 = (bf16[512,512]{1,0:T(8,128)(2,1)}, bf16[512,512]{1,0:T(8,128)(2,1)}) custom-call(s32[13]{0:T(128)} %stack.27.info, bf16[2048,128]{1,0:T(8,128)(2,1)} %prep.1.kv_ref.own_ref, bf16[256,2048]{1,0:T(8,128)(2,1)} %get-tuple-element.39.refs_0_, f32[144,2048]{1,0:T(8,128)} %get-tuple-element.40.refs_1_, f32[8,2048]{1,0:T(8,128)} %get-tuple-element.41.refs_2_, ...), custom_call_target="tpu_custom_call" | custom-call | flops 4294967296 | bytes 4194304 | tf_op jit(solution)/shard_map/attend_own/pallas_call | solution.py:257
  49.2 14.8 %collective-permute-start.16 = (bf16[16,32,512]{2,1,0:T(8,128)(2,1)S(1)}, bf16[16,32,512]{2,1,0:T(8,128)(2,1)S(1)}, u32[]{:S(2)}, u32[]{:S(2)}) collective-permute-start(bf16[16,32,512]{2,1,0:T(8,128)(2,1)S(1)} %slice_bitcast_fusion), channel_id=1, source_target_pairs={{0,112},{1,113},{2,114},{3,115},{4,116},{5,117},{6,118},{7,119},{8... | collective-permute-start | bytes 1572872 | tf_op jit(solution)/shard_map/ppermute | solution.py:368
  64.0 0.8 copy-done.7
  64.8 7.5 %project.2 = (bf16[128,3072]{1,0:T(8,128)(2,1)}, bf16[128,3072]{1,0:T(8,128)(2,1)}, bf16[128,3072]{1,0:T(8,128)(2,1)}, bf16[128,3072]{1,0:T(8,128)(2,1)}) custom-call(s32[13]{0:T(128)} %stack.27.info, bf16[512,512]{1,0:T(8,128)(2,1)} %get-tuple-element.46.a, bf16[512,512]{1,0:T(8,128)(2,1)} %copy-done.7, bf16[512,6144]{1,0:T(8,128)(2,1)} %wa.3, ...), custom_call_target="tpu_custom_call" | custom-call | flops 3221225472 | bytes 12582912 | tf_op jit(solution)/shard_map/project/pallas_call | solution.py:299
  72.3 0.8 collective-permute-start.10
  73.1 0.8 collective-permute-start.11
  73.9 0.7 collective-permute-start.12
  74.6 1.6 collective-permute-done.16.refs_0_
  76.1 0.8 copy-done.18
  76.9 23.6 %attend_foreign.1 = (bf16[512,512]{1,0:T(8,128)(2,1)}, bf16[512,512]{1,0:T(8,128)(2,1)}) custom-call(s32[13]{0:T(128)} %stack.27.info, bf16[2048,128]{1,0:T(8,128)(2,1)} %prep.1.kv_ref.own_ref, bf16[16,32,512]{2,1,0:T(8,128)(2,1)} %copy-done.18, bf16[2048,128]{1,0:T(8,128)(2,1)} %copy-done.10, bf16[2048,128]{1,0:T(8,128)(2,1)} %copy-done.11, ...), custom_call_target="tpu_custom_call" | custom-call | flops 4294967296 | bytes 4194304 | tf_op jit(solution)/shard_map/attend_foreign/pallas_call | solution.py:257
  100.5 3.9 %collective-permute-start.17 = (bf16[512,512]{1,0:T(8,128)(2,1)}, bf16[512,512]{1,0:T(8,128)(2,1)S(1)}, u32[]{:S(2)}, u32[]{:S(2)}) collective-permute-start(bf16[512,512]{1,0:T(8,128)(2,1)} %get-tuple-element.60), channel_id=1, source_target_pairs={{0,1},{1,0},{2,3},{3,2},{4,5},{5,4},{6,7},{7,6},{8,9},{9,8},{10,11... | collective-permute-start | bytes 1572872 | tf_op jit(solution)/shard_map/ppermute | solution.py:368
  104.5 0.9 copy-done
  105.6 0.9 copy-done.2
  106.5 3.8 %sum_one.2 = (bf16[64,3072]{1,0:T(8,128)(2,1)}, bf16[64,3072]{1,0:T(8,128)(2,1)}, bf16[64,3072]{1,0:T(8,128)(2,1)}, bf16[64,3072]{1,0:T(8,128)(2,1)}) custom-call(s32[13]{0:T(128)} %stack.27.info, bf16[128,3072]{1,0:T(8,128)(2,1)} %get-tuple-element.48.p0, bf16[128,3072]{1,0:T(8,128)(2,1)} %get-tuple-element.49.p2, bf16[128,3072]{1,0:T(8,128)(2,1)} %copy-done, ...), custom_call_target="tpu_custom_call" | custom-call | tf_op jit(solution)/shard_map/sum_one/pallas_call | solution.py:331
  110.7 4.2 %collective-permute-start.14 = (bf16[64,3072]{1,0:T(8,128)(2,1)}, bf16[64,3072]{1,0:T(8,128)(2,1)S(1)}, u32[]{:S(2)}, u32[]{:S(2)}) collective-permute-start(bf16[64,3072]{1,0:T(8,128)(2,1)} %get-tuple-element.54), channel_id=1, source_target_pairs={{1,13},{3,15},{5,1},{7,3},{9,5},{11,7},{13,9},{15,11},{17,29},{19,... | collective-permute-start | bytes 1179656 | tf_op jit(solution)/shard_map/ppermute | solution.py:368
  114.9 1.9 %collective-permute-start.15 = (bf16[64,3072]{1,0:T(8,128)(2,1)}, bf16[64,3072]{1,0:T(8,128)(2,1)S(1)}, u32[]{:S(2)}, u32[]{:S(2)}) collective-permute-start(bf16[64,3072]{1,0:T(8,128)(2,1)} %get-tuple-element.55), channel_id=1, source_target_pairs={{1,9},{3,11},{5,13},{7,15},{9,1},{11,3},{13,5},{15,7},{17,25},{19,... | collective-permute-start | bytes 1179656 | tf_op jit(solution)/shard_map/ppermute | solution.py:368
  116.9 0.8 copy-done.6
  117.7 7.7 %project.3 = (bf16[128,3072]{1,0:T(8,128)(2,1)}, bf16[128,3072]{1,0:T(8,128)(2,1)}, bf16[128,3072]{1,0:T(8,128)(2,1)}, bf16[128,3072]{1,0:T(8,128)(2,1)}) custom-call(s32[13]{0:T(128)} %stack.27.info, bf16[512,512]{1,0:T(8,128)(2,1)} %get-tuple-element.59.a, bf16[512,512]{1,0:T(8,128)(2,1)} %copy-done.6, bf16[512,6144]{1,0:T(8,128)(2,1)} %wa.3, ...), custom_call_target="tpu_custom_call" | custom-call | flops 3221225472 | bytes 12582912 | tf_op jit(solution)/shard_map/project/pallas_call | solution.py:299
  125.7 0.7 collective-permute-start.19
  126.4 0.8 collective-permute-start.18
  127.2 0.7 collective-permute-start.20
  127.9 9.2 %collective-permute-done.19.g1 = bf16[128,3072]{1,0:T(8,128)(2,1)S(1)} collective-permute-done((bf16[128,3072]{1,0:T(8,128)(2,1)}, bf16[128,3072]{1,0:T(8,128)(2,1)S(1)}, u32[]{:S(2)}, u32[]{:S(2)}) %collective-permute-start.19) | collective-permute-done | bytes 786464 | tf_op jit(solution)/shard_map/ppermute | solution.py:368
  137.1 8.1 %collective-permute-done.18.g0 = bf16[128,3072]{1,0:T(8,128)(2,1)S(1)} collective-permute-done((bf16[128,3072]{1,0:T(8,128)(2,1)}, bf16[128,3072]{1,0:T(8,128)(2,1)S(1)}, u32[]{:S(2)}, u32[]{:S(2)}) %collective-permute-start.18) | collective-permute-done | bytes 786464 | tf_op jit(solution)/shard_map/ppermute | solution.py:368
  145.2 0.9 copy-done.4
  146.1 0.9 copy-done.5
  147.0 3.8 %sum_one.3 = (bf16[64,3072]{1,0:T(8,128)(2,1)}, bf16[64,3072]{1,0:T(8,128)(2,1)}, bf16[64,3072]{1,0:T(8,128)(2,1)}, bf16[64,3072]{1,0:T(8,128)(2,1)}) custom-call(s32[13]{0:T(128)} %stack.27.info, bf16[128,3072]{1,0:T(8,128)(2,1)} %get-tuple-element.62.p0, bf16[128,3072]{1,0:T(8,128)(2,1)} %get-tuple-element.64.p2, bf16[128,3072]{1,0:T(8,128)(2,1)} %copy-done.4, ...), custom_call_target="tpu_custom_call" | custom-call | tf_op jit(solution)/shard_map/sum_one/pallas_call | solution.py:331
  151.3 4.0 %collective-permute-start.22 = (bf16[64,3072]{1,0:T(8,128)(2,1)}, bf16[64,3072]{1,0:T(8,128)(2,1)S(1)}, u32[]{:S(2)}, u32[]{:S(2)}) collective-permute-start(bf16[64,3072]{1,0:T(8,128)(2,1)} %get-tuple-element.71), channel_id=1, source_target_pairs={{1,13},{3,15},{5,1},{7,3},{9,5},{11,7},{13,9},{15,11},{17,29},{19,... | collective-permute-start | bytes 1179656 | tf_op jit(solution)/shard_map/ppermute | solution.py:368
  155.4 3.6 %collective-permute-start.23 = (bf16[64,3072]{1,0:T(8,128)(2,1)}, bf16[64,3072]{1,0:T(8,128)(2,1)S(1)}, u32[]{:S(2)}, u32[]{:S(2)}) collective-permute-start(bf16[64,3072]{1,0:T(8,128)(2,1)} %get-tuple-element.72), channel_id=1, source_target_pairs={{1,9},{3,11},{5,13},{7,15},{9,1},{11,3},{13,5},{15,7},{17,25},{19,... | collective-permute-start | bytes 1179656 | tf_op jit(solution)/shard_map/ppermute | solution.py:368
  159.2 5.5 %collective-permute-done.22 = bf16[64,3072]{1,0:T(8,128)(2,1)S(1)} collective-permute-done((bf16[64,3072]{1,0:T(8,128)(2,1)}, bf16[64,3072]{1,0:T(8,128)(2,1)S(1)}, u32[]{:S(2)}, u32[]{:S(2)}) %collective-permute-start.22) | collective-permute-done | bytes 393248 | tf_op jit(solution)/shard_map/ppermute | solution.py:368
  164.6 1.0 collective-permute-done.23
  165.6 1.2 add_convert_fusion
  167.5 9.8 %collective-permute-done.26 = bf16[32,3072]{1,0:T(8,128)(2,1)S(1)} collective-permute-done((bf16[32,3072]{1,0:T(8,128)(2,1)S(1)}, bf16[32,3072]{1,0:T(8,128)(2,1)S(1)}, u32[]{:S(2)}, u32[]{:S(2)}) %collective-permute-start.26) | collective-permute-done | bytes 196640 | tf_op jit(solution)/shard_map/ppermute | solution.py:368
  177.5 0.9 pad_maximum_fusion
  (62 shorter events, 4.1 us)
Async XLA Ops:
  0.0 64.0 %collective-permute-start.9 = (bf16[512,6144]{1,0:T(8,128)(2,1)}, bf16[512,6144]{1,0:T(8,128)(2,1)}, u32[]{:S(2)}, u32[]{:S(2)}) collective-permute-start(bf16[512,6144]{1,0:T(8,128)(2,1)} %wa.3), channel_id=1, source_target_pairs={{0,1},{1,0},{2,3},{3,2},{4,5},{5,4},{6,7},{7,6},{8,9},{9,8},{10,11... | collective-permute-start | bytes 18874376 | tf_op jit(solution)/shard_map/ppermute | solution.py:368
  4.7 19.0 %collective-permute-start = (bf16[2048,128]{1,0:T(8,128)(2,1)}, bf16[2048,128]{1,0:T(8,128)(2,1)S(1)}, u32[]{:S(2)}, u32[]{:S(2)}) collective-permute-start(bf16[2048,128]{1,0:T(8,128)(2,1)} %prep.1.kv_ref.own_ref), channel_id=1, source_target_pairs={{0,112},{1,49},{2,114},{3,51},{4,116},{5,53},{6,118},{7,55},{8,120... | collective-permute-start | bytes 1572872 | tf_op jit(solution)/shard_map/ppermute | solution.py:368
  11.2 22.7 %collective-permute-start.1 = (bf16[2048,128]{1,0:T(8,128)(2,1)}, bf16[2048,128]{1,0:T(8,128)(2,1)S(1)}, u32[]{:S(2)}, u32[]{:S(2)}) collective-permute-start(bf16[2048,128]{1,0:T(8,128)(2,1)} %prep.1.kv_ref.own_ref), channel_id=1, source_target_pairs={{0,96},{1,33},{2,98},{3,35},{4,100},{5,37},{6,102},{7,39},{8,104},... | collective-permute-start | bytes 1572872 | tf_op jit(solution)/shard_map/ppermute | solution.py:368
  13.4 27.6 %collective-permute-start.2 = (bf16[2048,128]{1,0:T(8,128)(2,1)}, bf16[2048,128]{1,0:T(8,128)(2,1)S(1)}, u32[]{:S(2)}, u32[]{:S(2)}) collective-permute-start(bf16[2048,128]{1,0:T(8,128)(2,1)} %prep.1.kv_ref.own_ref), channel_id=1, source_target_pairs={{0,80},{1,17},{2,82},{3,19},{4,84},{5,21},{6,86},{7,23},{8,88},{9,... | collective-permute-start | bytes 1572872 | tf_op jit(solution)/shard_map/ppermute | solution.py:368
  15.4 25.7 %collective-permute-start.3 = (bf16[2048,128]{1,0:T(8,128)(2,1)}, bf16[2048,128]{1,0:T(8,128)(2,1)S(1)}, u32[]{:S(2)}, u32[]{:S(2)}) collective-permute-start(bf16[2048,128]{1,0:T(8,128)(2,1)} %prep.1.kv_ref.own_ref), channel_id=1, source_target_pairs={{0,64},{2,66},{4,68},{6,70},{8,72},{10,74},{12,76},{14,78},{16,80}... | collective-permute-start | bytes 1572872 | tf_op jit(solution)/shard_map/ppermute | solution.py:368
  23.7 20.3 %copy-start.10 = (bf16[2048,128]{1,0:T(8,128)(2,1)}, bf16[2048,128]{1,0:T(8,128)(2,1)S(1)}, u32[]{:S(2)}) copy-start(bf16[2048,128]{1,0:T(8,128)(2,1)S(1)} %collective-permute-done.refs_3_.refs_1_) | copy-start | bytes 1572868
  23.7 17.8 %collective-permute-start.4 = (bf16[2048,128]{1,0:T(8,128)(2,1)S(1)}, bf16[2048,128]{1,0:T(8,128)(2,1)S(1)}, u32[]{:S(2)}, u32[]{:S(2)}) collective-permute-start(bf16[2048,128]{1,0:T(8,128)(2,1)S(1)} %collective-permute-done.refs_3_.refs_1_), channel_id=1, source_target_pairs={{0,1},{1,0},{2,3},{3,2},{4,5},{5,4},{6,7},{7,6},{8,9},{9,8},{10,11... | collective-permute-start | bytes 1572872 | tf_op jit(solution)/shard_map/ppermute | solution.py:368
  34.0 10.1 %copy-start.11 = (bf16[2048,128]{1,0:T(8,128)(2,1)}, bf16[2048,128]{1,0:T(8,128)(2,1)S(1)}, u32[]{:S(2)}) copy-start(bf16[2048,128]{1,0:T(8,128)(2,1)S(1)} %collective-permute-done.1.refs_4_.refs_2_) | copy-start | bytes 1572868
  34.0 8.6 %collective-permute-start.5 = (bf16[2048,128]{1,0:T(8,128)(2,1)S(1)}, bf16[2048,128]{1,0:T(8,128)(2,1)S(1)}, u32[]{:S(2)}, u32[]{:S(2)}) collective-permute-start(bf16[2048,128]{1,0:T(8,128)(2,1)S(1)} %collective-permute-done.1.refs_4_.refs_2_), channel_id=1, source_target_pairs={{0,1},{1,0},{2,3},{3,2},{4,5},{5,4},{6,7},{7,6},{8,9},{9,8},{10,11... | collective-permute-start | bytes 1572872 | tf_op jit(solution)/shard_map/ppermute | solution.py:368
  41.0 3.0 %copy-start.12 = (bf16[2048,128]{1,0:T(8,128)(2,1)}, bf16[2048,128]{1,0:T(8,128)(2,1)S(1)}, u32[]{:S(2)}) copy-start(bf16[2048,128]{1,0:T(8,128)(2,1)S(1)} %collective-permute-done.2.refs_5_.refs_3_) | copy-start | bytes 1572868
  41.0 2.3 %collective-permute-start.6 = (bf16[2048,128]{1,0:T(8,128)(2,1)S(1)}, bf16[2048,128]{1,0:T(8,128)(2,1)S(1)}, u32[]{:S(2)}, u32[]{:S(2)}) collective-permute-start(bf16[2048,128]{1,0:T(8,128)(2,1)S(1)} %collective-permute-done.2.refs_5_.refs_3_), channel_id=1, source_target_pairs={{0,1},{1,0},{2,3},{3,2},{4,5},{5,4},{6,7},{7,6},{8,9},{9,8},{10,11... | collective-permute-start | bytes 1572872 | tf_op jit(solution)/shard_map/ppermute | solution.py:368
  41.1 3.0 %copy-start.13 = (bf16[2048,128]{1,0:T(8,128)(2,1)}, bf16[2048,128]{1,0:T(8,128)(2,1)S(1)}, u32[]{:S(2)}) copy-start(bf16[2048,128]{1,0:T(8,128)(2,1)S(1)} %collective-permute-done.3.refs_6_.refs_4_) | copy-start | bytes 1572868
  41.1 2.9 %collective-permute-start.7 = (bf16[2048,128]{1,0:T(8,128)(2,1)S(1)}, bf16[2048,128]{1,0:T(8,128)(2,1)S(1)}, u32[]{:S(2)}, u32[]{:S(2)}) collective-permute-start(bf16[2048,128]{1,0:T(8,128)(2,1)S(1)} %collective-permute-done.3.refs_6_.refs_4_), channel_id=1, source_target_pairs={{0,1},{1,0},{2,3},{3,2},{4,5},{5,4},{6,7},{7,6},{8,9},{9,8},{10,11... | collective-permute-start | bytes 1572872 | tf_op jit(solution)/shard_map/ppermute | solution.py:368
  41.5 2.5 %copy-start.14 = (bf16[2048,128]{1,0:T(8,128)(2,1)}, bf16[2048,128]{1,0:T(8,128)(2,1)S(1)}, u32[]{:S(2)}) copy-start(bf16[2048,128]{1,0:T(8,128)(2,1)S(1)} %collective-permute-done.4.refs_7_.refs_5_) | copy-start | bytes 1572868
  42.5 1.5 copy-start.15
  43.3 0.8 copy-start.16
  44.0 0.8 copy-start.17
  44.9 4.3 %copy-start.9 = (bf16[1024,512]{1,0:T(8,128)(2,1)S(1)}, bf16[1024,512]{1,0:T(8,128)(2,1)}, u32[]{:S(2)}) copy-start(bf16[1024,512]{1,0:T(8,128)(2,1)} %param.4) | copy-start | bytes 3145732
  48.7 15.3 %collective-permute-start.8 = (bf16[512,512]{1,0:T(8,128)(2,1)}, bf16[512,512]{1,0:T(8,128)(2,1)S(1)}, u32[]{:S(2)}, u32[]{:S(2)}) collective-permute-start(bf16[512,512]{1,0:T(8,128)(2,1)} %get-tuple-element.47), channel_id=1, source_target_pairs={{0,1},{1,0},{2,3},{3,2},{4,5},{5,4},{6,7},{7,6},{8,9},{9,8},{10,11... | collective-permute-start | bytes 1572872 | tf_op jit(solution)/shard_map/ppermute | solution.py:368
  49.2 26.9 %collective-permute-start.16 = (bf16[16,32,512]{2,1,0:T(8,128)(2,1)S(1)}, bf16[16,32,512]{2,1,0:T(8,128)(2,1)S(1)}, u32[]{:S(2)}, u32[]{:S(2)}) collective-permute-start(bf16[16,32,512]{2,1,0:T(8,128)(2,1)S(1)} %slice_bitcast_fusion), channel_id=1, source_target_pairs={{0,112},{1,113},{2,114},{3,115},{4,116},{5,117},{6,118},{7,119},{8... | collective-permute-start | bytes 1572872 | tf_op jit(solution)/shard_map/ppermute | solution.py:368
  64.0 0.8 copy-start.7
  72.3 32.1 %collective-permute-start.10 = (bf16[128,3072]{1,0:T(8,128)(2,1)}, bf16[128,3072]{1,0:T(8,128)(2,1)S(1)}, u32[]{:S(2)}, u32[]{:S(2)}) collective-permute-start(bf16[128,3072]{1,0:T(8,128)(2,1)} %get-tuple-element.50), channel_id=1, source_target_pairs={{0,4},{1,3},{2,6},{3,1},{4,8},{5,7},{6,10},{7,5},{8,12},{9,11},{10... | collective-permute-start | bytes 2359304 | tf_op jit(solution)/shard_map/ppermute | solution.py:368
  73.1 31.4 %collective-permute-start.11 = (bf16[128,3072]{1,0:T(8,128)(2,1)}, bf16[128,3072]{1,0:T(8,128)(2,1)S(1)}, u32[]{:S(2)}, u32[]{:S(2)}) collective-permute-start(bf16[128,3072]{1,0:T(8,128)(2,1)} %get-tuple-element.51), channel_id=1, source_target_pairs={{0,12},{1,3},{2,14},{3,1},{4,0},{5,7},{6,2},{7,5},{8,4},{9,11},{10... | collective-permute-start | bytes 2359304 | tf_op jit(solution)/shard_map/ppermute | solution.py:368
  73.9 30.6 %collective-permute-start.12 = (bf16[128,3072]{1,0:T(8,128)(2,1)}, bf16[128,3072]{1,0:T(8,128)(2,1)S(1)}, u32[]{:S(2)}, u32[]{:S(2)}) collective-permute-start(bf16[128,3072]{1,0:T(8,128)(2,1)} %get-tuple-element.49.p2), channel_id=1, source_target_pairs={{0,8},{2,10},{4,12},{6,14},{8,0},{10,2},{12,4},{14,6},{16,24},{18,... | collective-permute-start | bytes 2359304 | tf_op jit(solution)/shard_map/ppermute | solution.py:368
  76.1 0.8 copy-start.18
  100.5 16.3 %collective-permute-start.17 = (bf16[512,512]{1,0:T(8,128)(2,1)}, bf16[512,512]{1,0:T(8,128)(2,1)S(1)}, u32[]{:S(2)}, u32[]{:S(2)}) collective-permute-start(bf16[512,512]{1,0:T(8,128)(2,1)} %get-tuple-element.60), channel_id=1, source_target_pairs={{0,1},{1,0},{2,3},{3,2},{4,5},{5,4},{6,7},{7,6},{8,9},{9,8},{10,11... | collective-permute-start | bytes 1572872 | tf_op jit(solution)/shard_map/ppermute | solution.py:368
  104.5 0.9 copy-start
  104.5 1.1 copy-start.1
  105.6 0.9 copy-start.2
  110.3 15.1 %collective-permute-start.13 = (bf16[64,3072]{1,0:T(8,128)(2,1)}, bf16[64,3072]{1,0:T(8,128)(2,1)S(1)}, u32[]{:S(2)}, u32[]{:S(2)}) collective-permute-start(bf16[64,3072]{1,0:T(8,128)(2,1)} %get-tuple-element.53), channel_id=1, source_target_pairs={{0,2},{1,5},{2,0},{3,7},{4,6},{5,9},{6,4},{7,11},{8,10},{9,13},{10... | collective-permute-start | bytes 1179656 | tf_op jit(solution)/shard_map/ppermute | solution.py:368
  110.7 14.7 %collective-permute-start.14 = (bf16[64,3072]{1,0:T(8,128)(2,1)}, bf16[64,3072]{1,0:T(8,128)(2,1)S(1)}, u32[]{:S(2)}, u32[]{:S(2)}) collective-permute-start(bf16[64,3072]{1,0:T(8,128)(2,1)} %get-tuple-element.54), channel_id=1, source_target_pairs={{1,13},{3,15},{5,1},{7,3},{9,5},{11,7},{13,9},{15,11},{17,29},{19,... | collective-permute-start | bytes 1179656 | tf_op jit(solution)/shard_map/ppermute | solution.py:368
  114.9 10.5 %collective-permute-start.15 = (bf16[64,3072]{1,0:T(8,128)(2,1)}, bf16[64,3072]{1,0:T(8,128)(2,1)S(1)}, u32[]{:S(2)}, u32[]{:S(2)}) collective-permute-start(bf16[64,3072]{1,0:T(8,128)(2,1)} %get-tuple-element.55), channel_id=1, source_target_pairs={{1,9},{3,11},{5,13},{7,15},{9,1},{11,3},{13,5},{15,7},{17,25},{19,... | collective-permute-start | bytes 1179656 | tf_op jit(solution)/shard_map/ppermute | solution.py:368
  116.9 0.8 copy-start.6
  117.7 7.7 %copy-start.8 = (bf16[64,3072]{1,0:T(8,128)(2,1)S(1)}, bf16[64,3072]{1,0:T(8,128)(2,1)}, u32[]{:S(2)}) copy-start(bf16[64,3072]{1,0:T(8,128)(2,1)} %get-tuple-element.52) | copy-start | bytes 1179652
  125.7 11.4 %collective-permute-start.19 = (bf16[128,3072]{1,0:T(8,128)(2,1)}, bf16[128,3072]{1,0:T(8,128)(2,1)S(1)}, u32[]{:S(2)}, u32[]{:S(2)}) collective-permute-start(bf16[128,3072]{1,0:T(8,128)(2,1)} %get-tuple-element.68), channel_id=1, source_target_pairs={{0,12},{1,3},{2,14},{3,1},{4,0},{5,7},{6,2},{7,5},{8,4},{9,11},{10... | collective-permute-start | bytes 2359304 | tf_op jit(solution)/shard_map/ppermute | solution.py:368
  126.4 18.9 %collective-permute-start.18 = (bf16[128,3072]{1,0:T(8,128)(2,1)}, bf16[128,3072]{1,0:T(8,128)(2,1)S(1)}, u32[]{:S(2)}, u32[]{:S(2)}) collective-permute-start(bf16[128,3072]{1,0:T(8,128)(2,1)} %get-tuple-element.66), channel_id=1, source_target_pairs={{0,4},{1,3},{2,6},{3,1},{4,8},{5,7},{6,10},{7,5},{8,12},{9,11},{10... | collective-permute-start | bytes 2359304 | tf_op jit(solution)/shard_map/ppermute | solution.py:368
  127.2 18.0 %collective-permute-start.20 = (bf16[128,3072]{1,0:T(8,128)(2,1)}, bf16[128,3072]{1,0:T(8,128)(2,1)S(1)}, u32[]{:S(2)}, u32[]{:S(2)}) collective-permute-start(bf16[128,3072]{1,0:T(8,128)(2,1)} %get-tuple-element.64.p2), channel_id=1, source_target_pairs={{0,8},{2,10},{4,12},{6,14},{8,0},{10,2},{12,4},{14,6},{16,24},{18,... | collective-permute-start | bytes 2359304 | tf_op jit(solution)/shard_map/ppermute | solution.py:368
  137.1 8.1 %copy-start.3 = (bf16[128,3072]{1,0:T(8,128)(2,1)}, bf16[128,3072]{1,0:T(8,128)(2,1)S(1)}, u32[]{:S(2)}) copy-start(bf16[128,3072]{1,0:T(8,128)(2,1)S(1)} %collective-permute-done.19.g1) | copy-start | bytes 2359300
  145.2 0.9 copy-start.4
  146.1 0.9 copy-start.5
  150.8 8.4 %collective-permute-start.21 = (bf16[64,3072]{1,0:T(8,128)(2,1)}, bf16[64,3072]{1,0:T(8,128)(2,1)S(1)}, u32[]{:S(2)}, u32[]{:S(2)}) collective-permute-start(bf16[64,3072]{1,0:T(8,128)(2,1)} %get-tuple-element.70), channel_id=1, source_target_pairs={{0,2},{1,5},{2,0},{3,7},{4,6},{5,9},{6,4},{7,11},{8,10},{9,13},{10... | collective-permute-start | bytes 1179656 | tf_op jit(solution)/shard_map/ppermute | solution.py:368
  151.3 13.3 %collective-permute-start.22 = (bf16[64,3072]{1,0:T(8,128)(2,1)}, bf16[64,3072]{1,0:T(8,128)(2,1)S(1)}, u32[]{:S(2)}, u32[]{:S(2)}) collective-permute-start(bf16[64,3072]{1,0:T(8,128)(2,1)} %get-tuple-element.71), channel_id=1, source_target_pairs={{1,13},{3,15},{5,1},{7,3},{9,5},{11,7},{13,9},{15,11},{17,29},{19,... | collective-permute-start | bytes 1179656 | tf_op jit(solution)/shard_map/ppermute | solution.py:368
  155.4 10.2 %collective-permute-start.23 = (bf16[64,3072]{1,0:T(8,128)(2,1)}, bf16[64,3072]{1,0:T(8,128)(2,1)S(1)}, u32[]{:S(2)}, u32[]{:S(2)}) collective-permute-start(bf16[64,3072]{1,0:T(8,128)(2,1)} %get-tuple-element.72), channel_id=1, source_target_pairs={{1,9},{3,11},{5,13},{7,15},{9,1},{11,3},{13,5},{15,7},{17,25},{19,... | collective-permute-start | bytes 1179656 | tf_op jit(solution)/shard_map/ppermute | solution.py:368
  159.1 7.9 %collective-permute-start.25 = (bf16[32,3072]{1,0:T(8,128)(2,1)S(1)}, bf16[32,3072]{1,0:T(8,128)(2,1)S(1)}, u32[]{:S(2)}, u32[]{:S(2)}) collective-permute-start(bf16[32,3072]{1,0:T(8,128)(2,1)S(1)} %get-tuple-element.76), channel_id=1, source_target_pairs={{0,1},{1,0},{2,3},{3,2},{4,5},{5,4},{6,7},{7,6},{8,9},{9,8},{10,11... | collective-permute-start | bytes 589832 | tf_op jit(solution)/shard_map/ppermute | solution.py:368
  166.8 10.4 %collective-permute-start.26 = (bf16[32,3072]{1,0:T(8,128)(2,1)S(1)}, bf16[32,3072]{1,0:T(8,128)(2,1)S(1)}, u32[]{:S(2)}, u32[]{:S(2)}) collective-permute-start(bf16[32,3072]{1,0:T(8,128)(2,1)S(1)} %get-tuple-element.78), channel_id=1, source_target_pairs={{0,113},{1,112},{2,115},{3,114},{4,117},{5,116},{6,119},{7,118},{8... | collective-permute-start | bytes 589832 | tf_op jit(solution)/shard_map/ppermute | solution.py:368
  167.0 10.3 %collective-permute-start.24 = (bf16[32,3072]{1,0:T(8,128)(2,1)S(1)}, bf16[32,3072]{1,0:T(8,128)(2,1)S(1)}, u32[]{:S(2)}, u32[]{:S(2)}) collective-permute-start(bf16[32,3072]{1,0:T(8,128)(2,1)S(1)} %get-tuple-element.77), channel_id=1, source_target_pairs={{0,112},{1,113},{2,114},{3,115},{4,116},{5,117},{6,118},{7,119},{8... | collective-permute-start | bytes 589832 | tf_op jit(solution)/shard_map/ppermute | solution.py:368
where the time goes:
time: 180 us; the launch traced here: 178 us
  starting transfers between devices  64.1 us (36%)
  Pallas kernels  59.3 us (33%)
  waiting for transfers between devices  44.5 us (25%)
  local copies, waits for them, and re-layouts  7.75 us (4%)
  other arithmetic  2.53 us (1%)
    ppermute x27, starting transfers between devices, over_all(): return lax.ppermute(x, ('seq', 'head'), pairs)  64.1 us
    ppermute x27, waiting for transfers between devices, over_all(): return lax.ppermute(x, ('seq', 'head'), pairs)  44.5 us
    pallas_call x2, Pallas kernels, attend(): pl.pallas_call(functools.partial(attend_kernel, foreign, groups, n_y, n_s...  27.4 us
    pallas_call x2, Pallas kernels, project(): pl.pallas_call(body, grid_spec=pltpu.PrefetchScalarGridSpec(num_scalar_pr...  15.2 us
    pallas_call x2, Pallas kernels, sum_one(): pl.pallas_call(body, grid_spec=pltpu.PrefetchScalarGridSpec(num_scalar_pr...  7.61 us
    unnamed x39, local copies, waits for them, and re-layouts  7.06 us
    pallas_call x1, Pallas kernels, own(): pl.pallas_call(functools.partial(own_kernel, groups), grid=(1,), in_specs...  6.33 us
  transfers between devices with their start and end apart: 27, of which 11 were waited for; matrix products, arithmetic and copies ran while one was open for 1% of the time, Pallas kernels for 31%

commit v1 on v0

--- a/solution.py
+++ b/solution.py
@@ -14,7 +14,7 @@
 LIMIT = 60.0
 BF = jnp.bfloat16
 F32 = jnp.float32
-PARAMS = pltpu.CompilerParams(vmem_limit_bytes=56 << 20)
+PARAMS = pltpu.CompilerParams(vmem_limit_bytes=62 << 20)
 FETCH = ((7, 3), (6, 2), (5, 1), (4, None))
 SLOTS = [d for pair in FETCH for d in pair if d is not None]
 TABLE = 6
@@ -313,32 +313,6 @@
     )(info, mine, other, w, w_other)
 
 
-def sum_one(info, parts, got, tile):
-    def body(info, p0, p2, g0, g1, g2, a0, a1, b0, b1):
-        first = p0[...].astype(F32) + g0[...].astype(F32)
-        middle = g1[...].astype(F32)
-        first = first + jnp.where(info[2] == 0, middle + g2[...].astype(F32), 0.0)
-        second = p2[...].astype(F32) + middle
-        n = a0.shape[0]
-        a0[...] = first[:n].astype(BF)
-        a1[...] = first[n:].astype(BF)
-        b0[...] = second[:n].astype(BF)
-        b1[...] = second[n:].astype(BF)
-
-    rows, cols = parts[0].shape
-    whole = pl.BlockSpec((rows, tile), lambda i, info: (0, i))
-    half = pl.BlockSpec((rows // 2, tile), lambda i, info: (0, i))
-    return pl.pallas_call(
-        body,
-        grid_spec=pltpu.PrefetchScalarGridSpec(
-            num_scalar_prefetch=1, grid=(cols // tile,), in_specs=[whole] * 5, out_specs=[half] * 4
-        ),
-        out_shape=[jax.ShapeDtypeStruct((rows // 2, cols), BF)] * 4,
-        name="sum_one",
-        compiler_params=PARAMS,
-    )(info, parts[0], parts[2], *got)
-
-
 def add(*terms):
     total = terms[0].astype(F32)
     for t in terms[1:]:
@@ -384,9 +358,9 @@
     w_other = swap_core(w_out)
     kv = prep(info, keys, values)
     mine = [fetch(kv, pair) for pair in FETCH]
+    q_far = over_all(q4[:, 1], lambda s, y, z, c: (n_seq - 1 - s, y, z, c))
     state = own(q4, kv)
-    other = [swap_core(after(x, state[2])) for x in mine]
-    q_far = over_all(after(q4[:, 1], state[2], *mine), lambda s, y, z, c: (n_seq - 1 - s, y, z, c))
+    other = [swap_core(after(x, state[2], q_far)) for x in mine]
 
     def stage_one(parts):
         return [
@@ -394,6 +368,14 @@
             over_all(parts[3], lambda s, y, z, c: (s, y, 1 - z, c) if c else (s, y - 1, z, c)),
             over_all(parts[2], lambda s, y, z, c: None if c else (s, y + 2, z, c)),
         ]
+
+    def sum_one(parts, got):
+        first = parts[0].astype(F32) + got[0].astype(F32)
+        extra = got[1].astype(F32) + got[2].astype(F32)
+        a = (first + jnp.where(core == 0, extra, 0.0)).astype(BF)
+        b = add(parts[2], got[1])
+        n = a.shape[0] // 2
+        return a[:n], a[n:], b[:n], b[n:]
 
     def stage_two(total):
         return [
@@ -409,18 +391,18 @@
     got_n = stage_one(parts_n)
     far, far_peer = attend(after(info, parts_n[0]), kv, [q_far], half, mine, other, n_y, n_seq)
     far_far = swap_core(far_peer)
-    total_n = sum_one(info, parts_n, got_n, cols // 4)
+    total_n = sum_one([after(p, far) for p in parts_n], got_n)
     got2_n = stage_two(total_n)
     parts_f = project(after(info, *total_n), far, far_far, w_out, w_other, n_y, cols // 4)
     done_n = add(total_n[0], *got2_n).reshape(2, sub, cols // 2)
-    parts_f = [after(p, done_n) for p in parts_f]
-    got_f = stage_one(parts_f)
 
     def by_core(x, same):
         return jnp.where((core == 0) == same, x[0], x[1])
 
     own_other = swap_core(by_core(done_n, False))
-    total_f = sum_one(info, parts_f, got_f, cols // 4)
+    parts_f = [after(p, own_other) for p in parts_f]
+    got_f = stage_one(parts_f)
+    total_f = sum_one(parts_f, got_f)
     got2_f = stage_two(total_f)
     done_f = add(total_f[0], *got2_f).reshape(2, sub, cols // 2)
     home = over_all(by_core(done_f, True), lambda s, y, z, c: (n_seq - 1 - s, y, z, c))

time: 180 us -> 188 us (1.044)
  waiting for transfers between devices: 44.5 us -> 58.6 us
  Pallas kernels: 59.3 us -> 51.7 us
  other arithmetic: 2.53 us -> 6.89 us
  local copies, waits for them, and re-layouts: 7.75 us -> 4.86 us
    ppermute x27, waiting for transfers between devices: 44.5 us -> 58.6 us  [over_all(): return lax.ppermute(x, ('seq', 'head'), pairs)]
    pallas_call x2 -> x0, Pallas kernels: 7.61 us -> none  [sum_one(): pl.pallas_call(body, grid_spec=pltpu.PrefetchScalarGridSpec(num_scalar_pr...]
    convert_element_type x0 -> x2, other arithmetic: none -> 4.36 us  [sum_one(): a = (first + jnp.where(core == 0, extra, 0.0)).astype(BF)]
    unnamed x39 -> x23, local copies, waits for them, and re-layouts: 7.06 us -> 4.06 us
  transfers between devices with their start and end apart: 27 -> 27, of which waited for: 11 -> 15; matrix products, arithmetic and copies ran while one was open for 1% -> 1% of each run, Pallas kernels for 31% -> 24%
where the time goes in v1:
time: 188 us; the launch traced here: 186 us
  starting transfers between devices  63.2 us (34%)
  waiting for transfers between devices  58.6 us (31%)
  Pallas kernels  51.7 us (28%)
  other arithmetic  6.89 us (4%)
  local copies, waits for them, and re-layouts  4.86 us (3%)
    ppermute x27, starting transfers between devices, over_all(): return lax.ppermute(x, ('seq', 'head'), pairs)  63.2 us
    ppermute x27, waiting for transfers between devices, over_all(): return lax.ppermute(x, ('seq', 'head'), pairs)  58.6 us
    pallas_call x2, Pallas kernels, attend(): pl.pallas_call(functools.partial(attend_kernel, foreign, groups, n_y, n_s...  27.4 us
    pallas_call x2, Pallas kernels, project(): pl.pallas_call(body, grid_spec=pltpu.PrefetchScalarGridSpec(num_scalar_pr...  15.2 us
    pallas_call x1, Pallas kernels, own(): pl.pallas_call(functools.partial(own_kernel, groups), grid=(1,), in_specs...  6.3 us
    convert_element_type x2, other arithmetic, sum_one(): a = (first + jnp.where(core == 0, extra, 0.0)).astype(BF)  4.36 us
    unnamed x23, local copies, waits for them, and re-layouts  4.06 us
  transfers between devices with their start and end apart: 27, of which 15 were waited for; matrix products, arithmetic and copies ran while one was open for 1% of the time, Pallas kernels for 24%

profile of v1, /device:TPU:1, one launch (start us, length us, event | category | flops | bytes accessed | tf_op | source)
XLA Modules:
  0.0 185.5 jit_solution(6961656573370585002)
XLA Ops:
  0.0 1.4 collective-permute-start.10
  2.0 2.8 %prep.1.kv_ref.own_ref = bf16[2048,128]{1,0:T(8,128)(2,1)} custom-call(s32[13]{0:T(128)} %stack.27.info, bf16[1024,1024]{1,0:T(8,128)(2,1)} %k_ref.1, bf16[1024,1024]{1,0:T(8,128)(2,1)} %v_ref.1), custom_call_target="tpu_custom_call" | custom-call | tf_op jit(solution)/shard_map/prep/pallas_call | solution.py:37
  4.8 6.5 %collective-permute-start = (bf16[2048,128]{1,0:T(8,128)(2,1)}, bf16[2048,128]{1,0:T(8,128)(2,1)}, u32[]{:S(2)}, u32[]{:S(2)}) collective-permute-start(bf16[2048,128]{1,0:T(8,128)(2,1)} %prep.1.kv_ref.own_ref), channel_id=1, source_target_pairs={{0,112},{1,49},{2,114},{3,51},{4,116},{5,53},{6,118},{7,55},{8,120... | collective-permute-start | bytes 1572872 | tf_op jit(solution)/shard_map/ppermute | solution.py:342
  12.1 3.2 %collective-permute-start.1 = (bf16[2048,128]{1,0:T(8,128)(2,1)}, bf16[2048,128]{1,0:T(8,128)(2,1)S(1)}, u32[]{:S(2)}, u32[]{:S(2)}) collective-permute-start(bf16[2048,128]{1,0:T(8,128)(2,1)} %prep.1.kv_ref.own_ref), channel_id=1, source_target_pairs={{0,96},{1,33},{2,98},{3,35},{4,100},{5,37},{6,102},{7,39},{8,104},... | collective-permute-start | bytes 1572872 | tf_op jit(solution)/shard_map/ppermute | solution.py:342
  15.3 5.5 %collective-permute-start.2 = (bf16[2048,128]{1,0:T(8,128)(2,1)}, bf16[2048,128]{1,0:T(8,128)(2,1)}, u32[]{:S(2)}, u32[]{:S(2)}) collective-permute-start(bf16[2048,128]{1,0:T(8,128)(2,1)} %prep.1.kv_ref.own_ref), channel_id=1, source_target_pairs={{0,80},{1,17},{2,82},{3,19},{4,84},{5,21},{6,86},{7,23},{8,88},{9,... | collective-permute-start | bytes 1572872 | tf_op jit(solution)/shard_map/ppermute | solution.py:342
  20.8 3.4 %collective-permute-done.refs_3_.refs_1_ = bf16[2048,128]{1,0:T(8,128)(2,1)} collective-permute-done((bf16[2048,128]{1,0:T(8,128)(2,1)}, bf16[2048,128]{1,0:T(8,128)(2,1)}, u32[]{:S(2)}, u32[]{:S(2)}) %collective-permute-start) | collective-permute-done | bytes 524320 | tf_op jit(solution)/shard_map/ppermute | solution.py:342
  24.2 1.5 collective-permute-start.3
  25.6 6.3 %own.1 = (bf16[256,2048]{1,0:T(8,128)(2,1)}, f32[144,2048]{1,0:T(8,128)}, f32[8,2048]{1,0:T(8,128)}) custom-call(bf16[16,2,32,512]{3,2,1,0:T(8,128)(2,1)} %bitcast.11, bf16[2048,128]{1,0:T(8,128)(2,1)} %prep.1.kv_ref.own_ref), custom_call_target="tpu_custom_call" | custom-call | flops 2147483648 | bytes 8388608 | tf_op jit(solution)/shard_map/own/pallas_call | solution.py:103
  31.9 6.2 %collective-permute-done.4.refs_0_ = bf16[16,32,512]{2,1,0:T(8,128)(2,1)S(1)} collective-permute-done((bf16[16,32,512]{2,1,0:T(8,128)(2,1)S(1)}, bf16[16,32,512]{2,1,0:T(8,128)(2,1)S(1)}, u32[]{:S(2)}, u32[]{:S(2)}) %collective-permute-start.4) | collective-permute-done | bytes 524320 | tf_op jit(solution)/shard_map/ppermute | solution.py:342
  38.2 5.1 %collective-permute-start.5 = (bf16[2048,128]{1,0:T(8,128)(2,1)}, bf16[2048,128]{1,0:T(8,128)(2,1)S(1)}, u32[]{:S(2)}, u32[]{:S(2)}) collective-permute-start(bf16[2048,128]{1,0:T(8,128)(2,1)} %collective-permute-done.refs_3_.refs_1_), channel_id=1, source_target_pairs={{0,1},{1,0},{2,3},{3,2},{4,5},{5,4},{6,7},{7,6},{8,9},{9,8},{10,11... | collective-permute-start | bytes 1572872 | tf_op jit(solution)/shard_map/ppermute | solution.py:342
  43.3 9.5 %collective-permute-start.6 = (bf16[2048,128]{1,0:T(8,128)(2,1)S(1)}, bf16[2048,128]{1,0:T(8,128)(2,1)S(1)}, u32[]{:S(2)}, u32[]{:S(2)}) collective-permute-start(bf16[2048,128]{1,0:T(8,128)(2,1)S(1)} %collective-permute-done.1.refs_4_.refs_2_), channel_id=1, source_target_pairs={{0,1},{1,0},{2,3},{3,2},{4,5},{5,4},{6,7},{7,6},{8,9},{9,8},{10,11... | collective-permute-start | bytes 1572872 | tf_op jit(solution)/shard_map/ppermute | solution.py:342
  53.2 1.0 collective-permute-done.6.refs_8_.refs_6_
  54.3 0.8 copy-done.8
  55.2 0.8 copy-done.9
  56.1 0.8 copy-done.10
  56.9 3.7 %attend_own.1 = (bf16[512,512]{1,0:T(8,128)(2,1)}, bf16[512,512]{1,0:T(8,128)(2,1)}) custom-call(s32[13]{0:T(128)} %stack.27.info, bf16[2048,128]{1,0:T(8,128)(2,1)} %prep.1.kv_ref.own_ref, bf16[256,2048]{1,0:T(8,128)(2,1)} %get-tuple-element.32.refs_0_, f32[144,2048]{1,0:T(8,128)} %get-tuple-element.33.refs_1_, f32[8,2048]{1,0:T(8,128)} %get-tuple-element.34.refs_2_, ...), custom_call_target="tpu_custom_call" | custom-call | flops 4294967296 | bytes 4194304 | tf_op jit(solution)/shard_map/attend_own/pallas_call | solution.py:257
  61.1 1.7 collective-permute-done.9.b
  62.8 0.8 copy-done.3
  63.6 7.6 %project.2 = (bf16[128,3072]{1,0:T(8,128)(2,1)}, bf16[128,3072]{1,0:T(8,128)(2,1)}, bf16[128,3072]{1,0:T(8,128)(2,1)}, bf16[128,3072]{1,0:T(8,128)(2,1)}) custom-call(s32[13]{0:T(128)} %stack.27.info, bf16[512,512]{1,0:T(8,128)(2,1)} %get-tuple-element.39.a, bf16[512,512]{1,0:T(8,128)(2,1)} %copy-done.3, bf16[512,6144]{1,0:T(8,128)(2,1)} %wa.3, ...), custom_call_target="tpu_custom_call" | custom-call | flops 3221225472 | bytes 12582912 | tf_op jit(solution)/shard_map/project/pallas_call | solution.py:299
  71.2 0.7 collective-permute-start.11
  72.7 1.6 collective-permute-start.13
  74.3 23.7 %attend_foreign.1 = (bf16[512,512]{1,0:T(8,128)(2,1)}, bf16[512,512]{1,0:T(8,128)(2,1)}) custom-call(s32[13]{0:T(128)} %stack.27.info, bf16[2048,128]{1,0:T(8,128)(2,1)} %prep.1.kv_ref.own_ref, bf16[16,32,512]{2,1,0:T(8,128)(2,1)} %copy-done.5, bf16[2048,128]{1,0:T(8,128)(2,1)} %collective-permute-done.refs_3_.refs_1_, bf16[2048,128]{1,0:T(8,128)(2,1)} %copy-done.6, ...), custom_call_target="tpu_custom_call" | custom-call | flops 4294967296 | bytes 4194304 | tf_op jit(solution)/shard_map/attend_foreign/pallas_call | solution.py:257
  98.0 2.3 %fusion.2 = (bf16[128,3072]{1,0:T(8,128)(2,1)S(1)}, bf16[128,3072]{1,0:T(8,128)(2,1)S(1)}) fusion(bf16[128,3072]{1,0:T(8,128)(2,1)} %collective-permute-done.12, bf16[128,3072]{1,0:T(8,128)(2,1)} %collective-permute-done.13, bf16[128,3072]{1,0:T(8,128)(2,1)} %collective-permute-done.11, bf16[128,3072]{1,0:T(8,128)(2,1)S(1)} %copy-done, pred[]{:T(512)S(6)} %eq.7, ...), kind=kLoop, calls=%fused_computation.6 | loop fusion | flops 4718592 | bytes 5505025 | tf_op jit(solution)/shard_map/convert_element_type | solution.py:375
  100.4 4.7 %collective-permute-start.15 = (bf16[64,3072]{1,0:T(8,128)(2,1)S(1)}, bf16[64,3072]{1,0:T(8,128)(2,1)S(1)}, u32[]{:S(2)}, u32[]{:S(2)}) collective-permute-start(bf16[64,3072]{1,0:T(8,128)(2,1)S(1)} %get-tuple-element.67), channel_id=1, source_target_pairs={{1,13},{3,15},{5,1},{7,3},{9,5},{11,7},{13,9},{15,11},{17,29},{19,... | collective-permute-start | bytes 1179656 | tf_op jit(solution)/shard_map/ppermute | solution.py:342
  105.1 2.3 %collective-permute-start.16 = (bf16[64,3072]{1,0:T(8,128)(2,1)S(1)}, bf16[64,3072]{1,0:T(8,128)(2,1)S(1)}, u32[]{:S(2)}, u32[]{:S(2)}) collective-permute-start(bf16[64,3072]{1,0:T(8,128)(2,1)S(1)} %get-tuple-element.68), channel_id=1, source_target_pairs={{1,9},{3,11},{5,13},{7,15},{9,1},{11,3},{13,5},{15,7},{17,25},{19,... | collective-permute-start | bytes 1179656 | tf_op jit(solution)/shard_map/ppermute | solution.py:342
  107.4 0.8 collective-permute-start.14
  108.1 5.9 %collective-permute-done.15 = bf16[64,3072]{1,0:T(8,128)(2,1)S(1)} collective-permute-done((bf16[64,3072]{1,0:T(8,128)(2,1)S(1)}, bf16[64,3072]{1,0:T(8,128)(2,1)S(1)}, u32[]{:S(2)}, u32[]{:S(2)}) %collective-permute-start.15) | collective-permute-done | bytes 393248 | tf_op jit(solution)/shard_map/ppermute | solution.py:342
  114.0 1.2 collective-permute-done.16
  115.2 4.2 %collective-permute-done.14 = bf16[64,3072]{1,0:T(8,128)(2,1)} collective-permute-done((bf16[64,3072]{1,0:T(8,128)(2,1)S(1)}, bf16[64,3072]{1,0:T(8,128)(2,1)}, u32[]{:S(2)}, u32[]{:S(2)}) %collective-permute-start.14) | collective-permute-done | bytes 393248 | tf_op jit(solution)/shard_map/ppermute | solution.py:342
  119.4 1.2 add_convert_fusion.1
  120.8 0.8 copy-done.2
  121.6 7.6 %project.3 = (bf16[128,3072]{1,0:T(8,128)(2,1)}, bf16[128,3072]{1,0:T(8,128)(2,1)}, bf16[128,3072]{1,0:T(8,128)(2,1)}, bf16[128,3072]{1,0:T(8,128)(2,1)}) custom-call(s32[13]{0:T(128)} %stack.27.info, bf16[512,512]{1,0:T(8,128)(2,1)} %get-tuple-element.43.a, bf16[512,512]{1,0:T(8,128)(2,1)} %copy-done.2, bf16[512,6144]{1,0:T(8,128)(2,1)} %wa.3, ...), custom_call_target="tpu_custom_call" | custom-call | flops 3221225472 | bytes 12582912 | tf_op jit(solution)/shard_map/project/pallas_call | solution.py:299
  129.2 1.0 collective-permute-start.19
  130.9 0.8 collective-permute-start.20
  131.7 9.1 %collective-permute-done.19 = bf16[128,3072]{1,0:T(8,128)(2,1)S(1)} collective-permute-done((bf16[128,3072]{1,0:T(8,128)(2,1)}, bf16[128,3072]{1,0:T(8,128)(2,1)S(1)}, u32[]{:S(2)}, u32[]{:S(2)}) %collective-permute-start.19) | collective-permute-done | bytes 786464 | tf_op jit(solution)/shard_map/ppermute | solution.py:342
  140.8 8.4 %collective-permute-done.20 = bf16[128,3072]{1,0:T(8,128)(2,1)S(1)} collective-permute-done((bf16[128,3072]{1,0:T(8,128)(2,1)}, bf16[128,3072]{1,0:T(8,128)(2,1)S(1)}, u32[]{:S(2)}, u32[]{:S(2)}) %collective-permute-start.20) | collective-permute-done | bytes 786464 | tf_op jit(solution)/shard_map/ppermute | solution.py:342
  149.2 2.1 %fusion.6 = (bf16[128,3072]{1,0:T(8,128)(2,1)S(1)}, bf16[128,3072]{1,0:T(8,128)(2,1)S(1)}) fusion(bf16[128,3072]{1,0:T(8,128)(2,1)S(1)} %collective-permute-done.20, bf16[128,3072]{1,0:T(8,128)(2,1)S(1)} %collective-permute-done.21, bf16[128,3072]{1,0:T(8,128)(2,1)S(1)} %collective-permute-done.19, bf16[128,3072]{1,0:T(8,128)(2,1)} %get-tuple-element.52, ...), kind=kLoop, calls=%fused_computation.10 | loop fusion | flops 4718592 | bytes 5505025 | tf_op jit(solution)/shard_map/convert_element_type | solution.py:375
  151.4 2.2 %collective-permute-start.23 = (bf16[64,3072]{1,0:T(8,128)(2,1)S(1)}, bf16[64,3072]{1,0:T(8,128)(2,1)S(1)}, u32[]{:S(2)}, u32[]{:S(2)}) collective-permute-start(bf16[64,3072]{1,0:T(8,128)(2,1)S(1)} %get-tuple-element.63), channel_id=1, source_target_pairs={{1,13},{3,15},{5,1},{7,3},{9,5},{11,7},{13,9},{15,11},{17,29},{19,... | collective-permute-start | bytes 1179656 | tf_op jit(solution)/shard_map/ppermute | solution.py:342
  153.6 2.3 %collective-permute-start.24 = (bf16[64,3072]{1,0:T(8,128)(2,1)S(1)}, bf16[64,3072]{1,0:T(8,128)(2,1)S(1)}, u32[]{:S(2)}, u32[]{:S(2)}) collective-permute-start(bf16[64,3072]{1,0:T(8,128)(2,1)S(1)} %get-tuple-element.64), channel_id=1, source_target_pairs={{1,9},{3,11},{5,13},{7,15},{9,1},{11,3},{13,5},{15,7},{17,25},{19,... | collective-permute-start | bytes 1179656 | tf_op jit(solution)/shard_map/ppermute | solution.py:342
  155.9 0.9 collective-permute-start.22
  156.8 3.1 %collective-permute-done.23 = bf16[64,3072]{1,0:T(8,128)(2,1)S(1)} collective-permute-done((bf16[64,3072]{1,0:T(8,128)(2,1)S(1)}, bf16[64,3072]{1,0:T(8,128)(2,1)S(1)}, u32[]{:S(2)}, u32[]{:S(2)}) %collective-permute-start.23) | collective-permute-done | bytes 393248 | tf_op jit(solution)/shard_map/ppermute | solution.py:342
  159.9 3.9 %collective-permute-done.24 = bf16[64,3072]{1,0:T(8,128)(2,1)S(1)} collective-permute-done((bf16[64,3072]{1,0:T(8,128)(2,1)S(1)}, bf16[64,3072]{1,0:T(8,128)(2,1)S(1)}, u32[]{:S(2)}, u32[]{:S(2)}) %collective-permute-start.24) | collective-permute-done | bytes 393248 | tf_op jit(solution)/shard_map/ppermute | solution.py:342
  163.8 4.1 %collective-permute-done.22 = bf16[64,3072]{1,0:T(8,128)(2,1)S(1)} collective-permute-done((bf16[64,3072]{1,0:T(8,128)(2,1)S(1)}, bf16[64,3072]{1,0:T(8,128)(2,1)S(1)}, u32[]{:S(2)}, u32[]{:S(2)}) %collective-permute-start.22) | collective-permute-done | bytes 393248 | tf_op jit(solution)/shard_map/ppermute | solution.py:342
  168.1 8.1 %collective-permute-start.26 = (bf16[32,3072]{1,0:T(8,128)(2,1)S(1)}, bf16[32,3072]{1,0:T(8,128)(2,1)S(1)}, u32[]{:S(2)}, u32[]{:S(2)}) collective-permute-start(bf16[32,3072]{1,0:T(8,128)(2,1)S(1)} %get-tuple-element.72), channel_id=1, source_target_pairs={{0,113},{1,112},{2,115},{3,114},{4,117},{5,116},{6,119},{7,118},{8... | collective-permute-start | bytes 589832 | tf_op jit(solution)/shard_map/ppermute | solution.py:342
  176.2 2.1 %collective-permute-start.25 = (bf16[32,3072]{1,0:T(8,128)(2,1)S(1)}, bf16[32,3072]{1,0:T(8,128)(2,1)S(1)}, u32[]{:S(2)}, u32[]{:S(2)}) collective-permute-start(bf16[32,3072]{1,0:T(8,128)(2,1)S(1)} %get-tuple-element.71), channel_id=1, source_target_pairs={{0,112},{1,113},{2,114},{3,115},{4,116},{5,117},{6,118},{7,119},{8... | collective-permute-start | bytes 589832 | tf_op jit(solution)/shard_map/ppermute | solution.py:342
  178.3 1.9 %collective-permute-done.26 = bf16[32,3072]{1,0:T(8,128)(2,1)S(1)} collective-permute-done((bf16[32,3072]{1,0:T(8,128)(2,1)S(1)}, bf16[32,3072]{1,0:T(8,128)(2,1)S(1)}, u32[]{:S(2)}, u32[]{:S(2)}) %collective-permute-start.26) | collective-permute-done | bytes 196640 | tf_op jit(solution)/shard_map/ppermute | solution.py:342
  180.2 4.2 %collective-permute-done.25 = bf16[32,3072]{1,0:T(8,128)(2,1)S(1)} collective-permute-done((bf16[32,3072]{1,0:T(8,128)(2,1)S(1)}, bf16[32,3072]{1,0:T(8,128)(2,1)S(1)}, u32[]{:S(2)}, u32[]{:S(2)}) %collective-permute-start.25) | collective-permute-done | bytes 196640 | tf_op jit(solution)/shard_map/ppermute | solution.py:342
  184.6 0.9 pad_maximum_fusion
  (50 shorter events, 4.6 us)
Async XLA Ops:
  0.0 62.8 %collective-permute-start.10 = (bf16[512,6144]{1,0:T(8,128)(2,1)}, bf16[512,6144]{1,0:T(8,128)(2,1)}, u32[]{:S(2)}, u32[]{:S(2)}) collective-permute-start(bf16[512,6144]{1,0:T(8,128)(2,1)} %wa.3), channel_id=1, source_target_pairs={{0,1},{1,0},{2,3},{3,2},{4,5},{5,4},{6,7},{7,6},{8,9},{9,8},{10,11... | collective-permute-start | bytes 18874376 | tf_op jit(solution)/shard_map/ppermute | solution.py:342
  2.0 9.3 %copy-start.4 = (bf16[1024,512]{1,0:T(8,128)(2,1)S(1)}, bf16[1024,512]{1,0:T(8,128)(2,1)}, u32[]{:S(2)}) copy-start(bf16[1024,512]{1,0:T(8,128)(2,1)} %param.4) | copy-start | bytes 3145732
  4.8 19.4 %collective-permute-start = (bf16[2048,128]{1,0:T(8,128)(2,1)}, bf16[2048,128]{1,0:T(8,128)(2,1)}, u32[]{:S(2)}, u32[]{:S(2)}) collective-permute-start(bf16[2048,128]{1,0:T(8,128)(2,1)} %prep.1.kv_ref.own_ref), channel_id=1, source_target_pairs={{0,112},{1,49},{2,114},{3,51},{4,116},{5,53},{6,118},{7,55},{8,120... | collective-permute-start | bytes 1572872 | tf_op jit(solution)/shard_map/ppermute | solution.py:342
  11.3 26.9 %collective-permute-start.4 = (bf16[16,32,512]{2,1,0:T(8,128)(2,1)S(1)}, bf16[16,32,512]{2,1,0:T(8,128)(2,1)S(1)}, u32[]{:S(2)}, u32[]{:S(2)}) collective-permute-start(bf16[16,32,512]{2,1,0:T(8,128)(2,1)S(1)} %slice_bitcast_fusion), channel_id=1, source_target_pairs={{0,112},{1,113},{2,114},{3,115},{4,116},{5,117},{6,118},{7,119},{8... | collective-permute-start | bytes 1572872 | tf_op jit(solution)/shard_map/ppermute | solution.py:342
  12.1 31.2 %collective-permute-start.1 = (bf16[2048,128]{1,0:T(8,128)(2,1)}, bf16[2048,128]{1,0:T(8,128)(2,1)S(1)}, u32[]{:S(2)}, u32[]{:S(2)}) collective-permute-start(bf16[2048,128]{1,0:T(8,128)(2,1)} %prep.1.kv_ref.own_ref), channel_id=1, source_target_pairs={{0,96},{1,33},{2,98},{3,35},{4,100},{5,37},{6,102},{7,39},{8,104},... | collective-permute-start | bytes 1572872 | tf_op jit(solution)/shard_map/ppermute | solution.py:342
  15.3 37.4 %collective-permute-start.2 = (bf16[2048,128]{1,0:T(8,128)(2,1)}, bf16[2048,128]{1,0:T(8,128)(2,1)}, u32[]{:S(2)}, u32[]{:S(2)}) collective-permute-start(bf16[2048,128]{1,0:T(8,128)(2,1)} %prep.1.kv_ref.own_ref), channel_id=1, source_target_pairs={{0,80},{1,17},{2,82},{3,19},{4,84},{5,21},{6,86},{7,23},{8,88},{9,... | collective-permute-start | bytes 1572872 | tf_op jit(solution)/shard_map/ppermute | solution.py:342
  24.2 28.6 %collective-permute-start.3 = (bf16[2048,128]{1,0:T(8,128)(2,1)}, bf16[2048,128]{1,0:T(8,128)(2,1)}, u32[]{:S(2)}, u32[]{:S(2)}) collective-permute-start(bf16[2048,128]{1,0:T(8,128)(2,1)} %prep.1.kv_ref.own_ref), channel_id=1, source_target_pairs={{0,64},{2,66},{4,68},{6,70},{8,72},{10,74},{12,76},{14,78},{16,80}... | collective-permute-start | bytes 1572872 | tf_op jit(solution)/shard_map/ppermute | solution.py:342
  38.2 22.4 %copy-start.5 = (bf16[16,32,512]{2,1,0:T(8,128)(2,1)}, bf16[16,32,512]{2,1,0:T(8,128)(2,1)S(1)}, u32[]{:S(2)}) copy-start(bf16[16,32,512]{2,1,0:T(8,128)(2,1)S(1)} %collective-permute-done.4.refs_0_) | copy-start | bytes 1572868
  38.2 15.1 %collective-permute-start.5 = (bf16[2048,128]{1,0:T(8,128)(2,1)}, bf16[2048,128]{1,0:T(8,128)(2,1)S(1)}, u32[]{:S(2)}, u32[]{:S(2)}) collective-permute-start(bf16[2048,128]{1,0:T(8,128)(2,1)} %collective-permute-done.refs_3_.refs_1_), channel_id=1, source_target_pairs={{0,1},{1,0},{2,3},{3,2},{4,5},{5,4},{6,7},{7,6},{8,9},{9,8},{10,11... | collective-permute-start | bytes 1572872 | tf_op jit(solution)/shard_map/ppermute | solution.py:342
  43.3 13.6 %copy-start.6 = (bf16[2048,128]{1,0:T(8,128)(2,1)}, bf16[2048,128]{1,0:T(8,128)(2,1)S(1)}, u32[]{:S(2)}) copy-start(bf16[2048,128]{1,0:T(8,128)(2,1)S(1)} %collective-permute-done.1.refs_4_.refs_2_) | copy-start | bytes 1572868
  43.3 11.0 %collective-permute-start.6 = (bf16[2048,128]{1,0:T(8,128)(2,1)S(1)}, bf16[2048,128]{1,0:T(8,128)(2,1)S(1)}, u32[]{:S(2)}, u32[]{:S(2)}) collective-permute-start(bf16[2048,128]{1,0:T(8,128)(2,1)S(1)} %collective-permute-done.1.refs_4_.refs_2_), channel_id=1, source_target_pairs={{0,1},{1,0},{2,3},{3,2},{4,5},{5,4},{6,7},{7,6},{8,9},{9,8},{10,11... | collective-permute-start | bytes 1572872 | tf_op jit(solution)/shard_map/ppermute | solution.py:342
  52.7 2.5 %collective-permute-start.7 = (bf16[2048,128]{1,0:T(8,128)(2,1)}, bf16[2048,128]{1,0:T(8,128)(2,1)S(1)}, u32[]{:S(2)}, u32[]{:S(2)}) collective-permute-start(bf16[2048,128]{1,0:T(8,128)(2,1)} %collective-permute-done.2.refs_5_.refs_3_), channel_id=1, source_target_pairs={{0,1},{1,0},{2,3},{3,2},{4,5},{5,4},{6,7},{7,6},{8,9},{9,8},{10,11... | collective-permute-start | bytes 1572872 | tf_op jit(solution)/shard_map/ppermute | solution.py:342
  52.8 3.2 %collective-permute-start.8 = (bf16[2048,128]{1,0:T(8,128)(2,1)}, bf16[2048,128]{1,0:T(8,128)(2,1)S(1)}, u32[]{:S(2)}, u32[]{:S(2)}) collective-permute-start(bf16[2048,128]{1,0:T(8,128)(2,1)} %collective-permute-done.3.refs_6_.refs_4_), channel_id=1, source_target_pairs={{0,1},{1,0},{2,3},{3,2},{4,5},{5,4},{6,7},{7,6},{8,9},{9,8},{10,11... | collective-permute-start | bytes 1572872 | tf_op jit(solution)/shard_map/ppermute | solution.py:342
  53.2 3.6 %copy-start.7 = (bf16[2048,128]{1,0:T(8,128)(2,1)}, bf16[2048,128]{1,0:T(8,128)(2,1)S(1)}, u32[]{:S(2)}) copy-start(bf16[2048,128]{1,0:T(8,128)(2,1)S(1)} %collective-permute-done.5.refs_7_.refs_5_) | copy-start | bytes 1572868
  54.3 0.8 copy-start.8
  55.2 0.8 copy-start.9
  56.1 0.8 copy-start.10
  60.6 2.2 %collective-permute-start.9 = (bf16[512,512]{1,0:T(8,128)(2,1)}, bf16[512,512]{1,0:T(8,128)(2,1)S(1)}, u32[]{:S(2)}, u32[]{:S(2)}) collective-permute-start(bf16[512,512]{1,0:T(8,128)(2,1)} %get-tuple-element.40), channel_id=1, source_target_pairs={{0,1},{1,0},{2,3},{3,2},{4,5},{5,4},{6,7},{7,6},{8,9},{9,8},{10,11... | collective-permute-start | bytes 1572872 | tf_op jit(solution)/shard_map/ppermute | solution.py:342
  62.8 0.8 copy-start.3
  71.2 26.8 %collective-permute-start.11 = (bf16[128,3072]{1,0:T(8,128)(2,1)}, bf16[128,3072]{1,0:T(8,128)(2,1)}, u32[]{:S(2)}, u32[]{:S(2)}) collective-permute-start(bf16[128,3072]{1,0:T(8,128)(2,1)} %get-tuple-element.45), channel_id=1, source_target_pairs={{0,4},{1,3},{2,6},{3,1},{4,8},{5,7},{6,10},{7,5},{8,12},{9,11},{10... | collective-permute-start | bytes 2359304 | tf_op jit(solution)/shard_map/ppermute | solution.py:342
  72.0 26.0 %collective-permute-start.12 = (bf16[128,3072]{1,0:T(8,128)(2,1)}, bf16[128,3072]{1,0:T(8,128)(2,1)}, u32[]{:S(2)}, u32[]{:S(2)}) collective-permute-start(bf16[128,3072]{1,0:T(8,128)(2,1)} %get-tuple-element.46), channel_id=1, source_target_pairs={{0,12},{1,3},{2,14},{3,1},{4,0},{5,7},{6,2},{7,5},{8,4},{9,11},{10... | collective-permute-start | bytes 2359304 | tf_op jit(solution)/shard_map/ppermute | solution.py:342
  72.7 25.3 %collective-permute-start.13 = (bf16[128,3072]{1,0:T(8,128)(2,1)}, bf16[128,3072]{1,0:T(8,128)(2,1)}, u32[]{:S(2)}, u32[]{:S(2)}) collective-permute-start(bf16[128,3072]{1,0:T(8,128)(2,1)} %get-tuple-element.48), channel_id=1, source_target_pairs={{0,8},{2,10},{4,12},{6,14},{8,0},{10,2},{12,4},{14,6},{16,24},{18,... | collective-permute-start | bytes 2359304 | tf_op jit(solution)/shard_map/ppermute | solution.py:342
  74.2 23.8 %copy-start = (bf16[128,3072]{1,0:T(8,128)(2,1)S(1)}, bf16[128,3072]{1,0:T(8,128)(2,1)}, u32[]{:S(2)}) copy-start(bf16[128,3072]{1,0:T(8,128)(2,1)} %get-tuple-element.44) | copy-start | bytes 2359300
  74.3 23.8 %copy-start.1 = (bf16[128,3072]{1,0:T(8,128)(2,1)S(1)}, bf16[128,3072]{1,0:T(8,128)(2,1)}, u32[]{:S(2)}) copy-start(bf16[128,3072]{1,0:T(8,128)(2,1)} %get-tuple-element.48) | copy-start | bytes 2359300
  100.4 13.6 %collective-permute-start.15 = (bf16[64,3072]{1,0:T(8,128)(2,1)S(1)}, bf16[64,3072]{1,0:T(8,128)(2,1)S(1)}, u32[]{:S(2)}, u32[]{:S(2)}) collective-permute-start(bf16[64,3072]{1,0:T(8,128)(2,1)S(1)} %get-tuple-element.67), channel_id=1, source_target_pairs={{1,13},{3,15},{5,1},{7,3},{9,5},{11,7},{13,9},{15,11},{17,29},{19,... | collective-permute-start | bytes 1179656 | tf_op jit(solution)/shard_map/ppermute | solution.py:342
  105.1 10.1 %collective-permute-start.16 = (bf16[64,3072]{1,0:T(8,128)(2,1)S(1)}, bf16[64,3072]{1,0:T(8,128)(2,1)S(1)}, u32[]{:S(2)}, u32[]{:S(2)}) collective-permute-start(bf16[64,3072]{1,0:T(8,128)(2,1)S(1)} %get-tuple-element.68), channel_id=1, source_target_pairs={{1,9},{3,11},{5,13},{7,15},{9,1},{11,3},{13,5},{15,7},{17,25},{19,... | collective-permute-start | bytes 1179656 | tf_op jit(solution)/shard_map/ppermute | solution.py:342
  107.4 12.1 %collective-permute-start.14 = (bf16[64,3072]{1,0:T(8,128)(2,1)S(1)}, bf16[64,3072]{1,0:T(8,128)(2,1)}, u32[]{:S(2)}, u32[]{:S(2)}) collective-permute-start(bf16[64,3072]{1,0:T(8,128)(2,1)S(1)} %slice.62), channel_id=1, source_target_pairs={{0,2},{1,5},{2,0},{3,7},{4,6},{5,9},{6,4},{7,11},{8,10},{9,13},{10... | collective-permute-start | bytes 1179656 | tf_op jit(solution)/shard_map/ppermute | solution.py:342
  108.1 12.7 %collective-permute-start.17 = (bf16[512,512]{1,0:T(8,128)(2,1)}, bf16[512,512]{1,0:T(8,128)(2,1)S(1)}, u32[]{:S(2)}, u32[]{:S(2)}) collective-permute-start(bf16[512,512]{1,0:T(8,128)(2,1)} %get-tuple-element.50), channel_id=1, source_target_pairs={{0,1},{1,0},{2,3},{3,2},{4,5},{5,4},{6,7},{7,6},{8,9},{9,8},{10,11... | collective-permute-start | bytes 1572872 | tf_op jit(solution)/shard_map/ppermute | solution.py:342
  120.7 8.5 %collective-permute-start.18 = (bf16[32,3072]{1,0:T(8,128)(2,1)S(1)}, bf16[32,3072]{1,0:T(8,128)(2,1)S(1)}, u32[]{:S(2)}, u32[]{:S(2)}) collective-permute-start(bf16[32,3072]{1,0:T(8,128)(2,1)S(1)} %get-tuple-element.70), channel_id=1, source_target_pairs={{0,1},{1,0},{2,3},{3,2},{4,5},{5,4},{6,7},{7,6},{8,9},{9,8},{10,11... | collective-permute-start | bytes 589832 | tf_op jit(solution)/shard_map/ppermute | solution.py:342
  120.8 0.8 copy-start.2
  129.2 11.6 %collective-permute-start.19 = (bf16[128,3072]{1,0:T(8,128)(2,1)}, bf16[128,3072]{1,0:T(8,128)(2,1)S(1)}, u32[]{:S(2)}, u32[]{:S(2)}) collective-permute-start(bf16[128,3072]{1,0:T(8,128)(2,1)} %get-tuple-element.54), channel_id=1, source_target_pairs={{0,4},{1,3},{2,6},{3,1},{4,8},{5,7},{6,10},{7,5},{8,12},{9,11},{10... | collective-permute-start | bytes 2359304 | tf_op jit(solution)/shard_map/ppermute | solution.py:342
  130.2 10.6 %collective-permute-start.21 = (bf16[128,3072]{1,0:T(8,128)(2,1)}, bf16[128,3072]{1,0:T(8,128)(2,1)S(1)}, u32[]{:S(2)}, u32[]{:S(2)}) collective-permute-start(bf16[128,3072]{1,0:T(8,128)(2,1)} %get-tuple-element.58), channel_id=1, source_target_pairs={{0,8},{2,10},{4,12},{6,14},{8,0},{10,2},{12,4},{14,6},{16,24},{18,... | collective-permute-start | bytes 2359304 | tf_op jit(solution)/shard_map/ppermute | solution.py:342
  130.9 18.3 %collective-permute-start.20 = (bf16[128,3072]{1,0:T(8,128)(2,1)}, bf16[128,3072]{1,0:T(8,128)(2,1)S(1)}, u32[]{:S(2)}, u32[]{:S(2)}) collective-permute-start(bf16[128,3072]{1,0:T(8,128)(2,1)} %get-tuple-element.56), channel_id=1, source_target_pairs={{0,12},{1,3},{2,14},{3,1},{4,0},{5,7},{6,2},{7,5},{8,4},{9,11},{10... | collective-permute-start | bytes 2359304 | tf_op jit(solution)/shard_map/ppermute | solution.py:342
  151.4 8.5 %collective-permute-start.23 = (bf16[64,3072]{1,0:T(8,128)(2,1)S(1)}, bf16[64,3072]{1,0:T(8,128)(2,1)S(1)}, u32[]{:S(2)}, u32[]{:S(2)}) collective-permute-start(bf16[64,3072]{1,0:T(8,128)(2,1)S(1)} %get-tuple-element.63), channel_id=1, source_target_pairs={{1,13},{3,15},{5,1},{7,3},{9,5},{11,7},{13,9},{15,11},{17,29},{19,... | collective-permute-start | bytes 1179656 | tf_op jit(solution)/shard_map/ppermute | solution.py:342
  153.6 10.1 %collective-permute-start.24 = (bf16[64,3072]{1,0:T(8,128)(2,1)S(1)}, bf16[64,3072]{1,0:T(8,128)(2,1)S(1)}, u32[]{:S(2)}, u32[]{:S(2)}) collective-permute-start(bf16[64,3072]{1,0:T(8,128)(2,1)S(1)} %get-tuple-element.64), channel_id=1, source_target_pairs={{1,9},{3,11},{5,13},{7,15},{9,1},{11,3},{13,5},{15,7},{17,25},{19,... | collective-permute-start | bytes 1179656 | tf_op jit(solution)/shard_map/ppermute | solution.py:342
  155.9 11.9 %collective-permute-start.22 = (bf16[64,3072]{1,0:T(8,128)(2,1)S(1)}, bf16[64,3072]{1,0:T(8,128)(2,1)S(1)}, u32[]{:S(2)}, u32[]{:S(2)}) collective-permute-start(bf16[64,3072]{1,0:T(8,128)(2,1)S(1)} %slice.68), channel_id=1, source_target_pairs={{0,2},{1,5},{2,0},{3,7},{4,6},{5,9},{6,4},{7,11},{8,10},{9,13},{10... | collective-permute-start | bytes 1179656 | tf_op jit(solution)/shard_map/ppermute | solution.py:342
  168.1 12.1 %collective-permute-start.26 = (bf16[32,3072]{1,0:T(8,128)(2,1)S(1)}, bf16[32,3072]{1,0:T(8,128)(2,1)S(1)}, u32[]{:S(2)}, u32[]{:S(2)}) collective-permute-start(bf16[32,3072]{1,0:T(8,128)(2,1)S(1)} %get-tuple-element.72), channel_id=1, source_target_pairs={{0,113},{1,112},{2,115},{3,114},{4,117},{5,116},{6,119},{7,118},{8... | collective-permute-start | bytes 589832 | tf_op jit(solution)/shard_map/ppermute | solution.py:342
  176.2 8.2 %collective-permute-start.25 = (bf16[32,3072]{1,0:T(8,128)(2,1)S(1)}, bf16[32,3072]{1,0:T(8,128)(2,1)S(1)}, u32[]{:S(2)}, u32[]{:S(2)}) collective-permute-start(bf16[32,3072]{1,0:T(8,128)(2,1)S(1)} %get-tuple-element.71), channel_id=1, source_target_pairs={{0,112},{1,113},{2,114},{3,115},{4,116},{5,117},{6,118},{7,119},{8... | collective-permute-start | bytes 589832 | tf_op jit(solution)/shard_map/ppermute | solution.py:342

commit v2 on v1

--- a/solution.py
+++ b/solution.py
@@ -252,7 +252,7 @@
     groups, sub, width = q_shape
     qb = groups * sub
     cols = qb * width // DH
-    any_space = pl.BlockSpec(memory_space=pl.ANY)
+    any_space = pl.BlockSpec(memory_space=pltpu.HBM)
     out = pl.BlockSpec((qb, width), lambda i, info: (0, 0))
     return pl.pallas_call(
         functools.partial(attend_kernel, foreign, groups, n_y, n_seq),
@@ -358,9 +358,9 @@
     w_other = swap_core(w_out)
     kv = prep(info, keys, values)
     mine = [fetch(kv, pair) for pair in FETCH]
-    q_far = over_all(q4[:, 1], lambda s, y, z, c: (n_seq - 1 - s, y, z, c))
     state = own(q4, kv)
-    other = [swap_core(after(x, state[2], q_far)) for x in mine]
+    other = [swap_core(after(x, state[2])) for x in mine]
+    q_far = over_all(after(q4[:, 1], state[2], *mine), lambda s, y, z, c: (n_seq - 1 - s, y, z, c))
 
     def stage_one(parts):
         return [
@@ -386,7 +386,7 @@
 
     half = (n_head, sub, width)
     near, near_peer = attend(info, kv, state, half, mine, other, n_y, n_seq)
-    near_far = swap_core(near_peer)
+    near_far = swap_core(after(near_peer, q_far))
     parts_n = project(info, near, near_far, w_out, w_other, n_y, cols // 4)
     got_n = stage_one(parts_n)
     far, far_peer = attend(after(info, parts_n[0]), kv, [q_far], half, mine, other, n_y, n_seq)

time: 188 us -> 181 us (0.963)
  starting transfers between devices: 63.2 us -> 50.3 us
  waiting for transfers between devices: 58.6 us -> 64 us
    ppermute x27, starting transfers between devices: 63.2 us -> 50.3 us  [over_all(): return lax.ppermute(x, ('seq', 'head'), pairs)]
    ppermute x27, waiting for transfers between devices: 58.6 us -> 64 us  [over_all(): return lax.ppermute(x, ('seq', 'head'), pairs)]
    unnamed x23 -> x21, local copies, waits for them, and re-layouts: 4.06 us -> 4.86 us
  transfers between devices with their start and end apart: 27 -> 27, of which waited for: 15 -> 13; matrix products, arithmetic and copies ran while one was open for 1% -> 1% of each run, Pallas kernels for 24% -> 25%
where the time goes in v2:
time: 181 us; the launch traced here: 179 us
  waiting for transfers between devices  64 us (35%)
  Pallas kernels  51.6 us (29%)
  starting transfers between devices  50.3 us (28%)
  other arithmetic  6.89 us (4%)
  local copies, waits for them, and re-layouts  5.74 us (3%)
    ppermute x27, waiting for transfers between devices, over_all(): return lax.ppermute(x, ('seq', 'head'), pairs)  64 us
    ppermute x27, starting transfers between devices, over_all(): return lax.ppermute(x, ('seq', 'head'), pairs)  50.3 us
    pallas_call x2, Pallas kernels, attend(): pl.pallas_call(functools.partial(attend_kernel, foreign, groups, n_y, n_s...  27.4 us
    pallas_call x2, Pallas kernels, project(): pl.pallas_call(body, grid_spec=pltpu.PrefetchScalarGridSpec(num_scalar_pr...  15.2 us
    pallas_call x1, Pallas kernels, own(): pl.pallas_call(functools.partial(own_kernel, groups), grid=(1,), in_specs...  6.39 us
    unnamed x21, local copies, waits for them, and re-layouts  4.86 us
    convert_element_type x2, other arithmetic, sum_one(): a = (first + jnp.where(core == 0, extra, 0.0)).astype(BF)  4.36 us
  transfers between devices with their start and end apart: 27, of which 13 were waited for; matrix products, arithmetic and copies ran while one was open for 1% of the time, Pallas kernels for 25%

profile of v2, /device:TPU:1, one launch (start us, length us, event | category | flops | bytes accessed | tf_op | source)
XLA Modules:
  0.0 178.8 jit_solution(11164383172535401601)
XLA Ops:
  0.0 1.4 collective-permute-start.10
  2.1 2.6 %prep.1.kv_ref.own_ref = bf16[2048,128]{1,0:T(8,128)(2,1)} custom-call(s32[13]{0:T(128)} %stack.27.info, bf16[1024,1024]{1,0:T(8,128)(2,1)} %k_ref.1, bf16[1024,1024]{1,0:T(8,128)(2,1)} %v_ref.1), custom_call_target="tpu_custom_call" | custom-call | tf_op jit(solution)/shard_map/prep/pallas_call | solution.py:37
  4.7 6.5 %collective-permute-start = (bf16[2048,128]{1,0:T(8,128)(2,1)}, bf16[2048,128]{1,0:T(8,128)(2,1)}, u32[]{:S(2)}, u32[]{:S(2)}) collective-permute-start(bf16[2048,128]{1,0:T(8,128)(2,1)} %prep.1.kv_ref.own_ref), channel_id=1, source_target_pairs={{0,112},{1,49},{2,114},{3,51},{4,116},{5,53},{6,118},{7,55},{8,120... | collective-permute-start | bytes 1572872 | tf_op jit(solution)/shard_map/ppermute | solution.py:342
  11.2 2.2 %collective-permute-start.1 = (bf16[2048,128]{1,0:T(8,128)(2,1)}, bf16[2048,128]{1,0:T(8,128)(2,1)}, u32[]{:S(2)}, u32[]{:S(2)}) collective-permute-start(bf16[2048,128]{1,0:T(8,128)(2,1)} %prep.1.kv_ref.own_ref), channel_id=1, source_target_pairs={{0,96},{1,33},{2,98},{3,35},{4,100},{5,37},{6,102},{7,39},{8,104},... | collective-permute-start | bytes 1572872 | tf_op jit(solution)/shard_map/ppermute | solution.py:342
  13.4 1.9 %collective-permute-start.2 = (bf16[2048,128]{1,0:T(8,128)(2,1)}, bf16[2048,128]{1,0:T(8,128)(2,1)}, u32[]{:S(2)}, u32[]{:S(2)}) collective-permute-start(bf16[2048,128]{1,0:T(8,128)(2,1)} %prep.1.kv_ref.own_ref), channel_id=1, source_target_pairs={{0,80},{1,17},{2,82},{3,19},{4,84},{5,21},{6,86},{7,23},{8,88},{9,... | collective-permute-start | bytes 1572872 | tf_op jit(solution)/shard_map/ppermute | solution.py:342
  15.4 1.5 collective-permute-start.3
  16.8 6.4 %own.1 = (bf16[256,2048]{1,0:T(8,128)(2,1)}, f32[144,2048]{1,0:T(8,128)}, f32[8,2048]{1,0:T(8,128)}) custom-call(bf16[16,2,32,512]{3,2,1,0:T(8,128)(2,1)} %bitcast.11, bf16[2048,128]{1,0:T(8,128)(2,1)} %prep.1.kv_ref.own_ref), custom_call_target="tpu_custom_call" | custom-call | flops 2147483648 | bytes 8388608 | tf_op jit(solution)/shard_map/own/pallas_call | solution.py:103
  23.8 5.5 %collective-permute-start.4 = (bf16[2048,128]{1,0:T(8,128)(2,1)}, bf16[2048,128]{1,0:T(8,128)(2,1)S(1)}, u32[]{:S(2)}, u32[]{:S(2)}) collective-permute-start(bf16[2048,128]{1,0:T(8,128)(2,1)} %collective-permute-done.refs_3_.refs_1_), channel_id=1, source_target_pairs={{0,1},{1,0},{2,3},{3,2},{4,5},{5,4},{6,7},{7,6},{8,9},{9,8},{10,11... | collective-permute-start | bytes 1572872 | tf_op jit(solution)/shard_map/ppermute | solution.py:342
  29.3 4.8 %collective-permute-done.1.refs_4_.refs_2_ = bf16[2048,128]{1,0:T(8,128)(2,1)} collective-permute-done((bf16[2048,128]{1,0:T(8,128)(2,1)}, bf16[2048,128]{1,0:T(8,128)(2,1)}, u32[]{:S(2)}, u32[]{:S(2)}) %collective-permute-start.1) | collective-permute-done | bytes 524320 | tf_op jit(solution)/shard_map/ppermute | solution.py:342
  34.1 6.5 %collective-permute-start.5 = (bf16[2048,128]{1,0:T(8,128)(2,1)}, bf16[2048,128]{1,0:T(8,128)(2,1)S(1)}, u32[]{:S(2)}, u32[]{:S(2)}) collective-permute-start(bf16[2048,128]{1,0:T(8,128)(2,1)} %collective-permute-done.1.refs_4_.refs_2_), channel_id=1, source_target_pairs={{0,1},{1,0},{2,3},{3,2},{4,5},{5,4},{6,7},{7,6},{8,9},{9,8},{10,11... | collective-permute-start | bytes 1572872 | tf_op jit(solution)/shard_map/ppermute | solution.py:342
  40.6 0.7 collective-permute-start.7
  41.4 1.3 collective-permute-start.8
  42.7 0.8 copy-done.6
  43.5 0.8 copy-done.7
  44.4 0.8 copy-done.8
  45.2 3.7 %attend_own.1 = (bf16[512,512]{1,0:T(8,128)(2,1)}, bf16[512,512]{1,0:T(8,128)(2,1)}) custom-call(s32[13]{0:T(128)} %stack.27.info, bf16[2048,128]{1,0:T(8,128)(2,1)} %prep.1.kv_ref.own_ref, bf16[256,2048]{1,0:T(8,128)(2,1)} %get-tuple-element.34.refs_0_, f32[144,2048]{1,0:T(8,128)} %get-tuple-element.35.refs_1_, f32[8,2048]{1,0:T(8,128)} %get-tuple-element.36.refs_2_, ...), custom_call_target="tpu_custom_call" | custom-call | flops 4294967296 | bytes 4194304 | tf_op jit(solution)/shard_map/attend_own/pallas_call | solution.py:257
  48.9 9.8 %collective-permute-done.8.refs_0_ = bf16[16,32,512]{2,1,0:T(8,128)(2,1)S(1)} collective-permute-done((bf16[16,32,512]{2,1,0:T(8,128)(2,1)S(1)}, bf16[16,32,512]{2,1,0:T(8,128)(2,1)S(1)}, u32[]{:S(2)}, u32[]{:S(2)}) %collective-permute-start.8) | collective-permute-done | bytes 524320 | tf_op jit(solution)/shard_map/ppermute | solution.py:342
  58.7 0.8 copy-done.9
  59.5 0.8 collective-permute-start.9
  60.3 1.7 collective-permute-done.9.b
  62.0 0.8 copy-done.3
  62.8 7.6 %project.2 = (bf16[128,3072]{1,0:T(8,128)(2,1)}, bf16[128,3072]{1,0:T(8,128)(2,1)}, bf16[128,3072]{1,0:T(8,128)(2,1)}, bf16[128,3072]{1,0:T(8,128)(2,1)}) custom-call(s32[13]{0:T(128)} %stack.27.info, bf16[512,512]{1,0:T(8,128)(2,1)} %get-tuple-element.41.a, bf16[512,512]{1,0:T(8,128)(2,1)} %copy-done.3, bf16[512,6144]{1,0:T(8,128)(2,1)} %wa.3, ...), custom_call_target="tpu_custom_call" | custom-call | flops 3221225472 | bytes 12582912 | tf_op jit(solution)/shard_map/project/pallas_call | solution.py:299
  70.4 1.0 collective-permute-start.11
  71.9 1.6 collective-permute-start.13
  73.5 23.7 %attend_foreign.1 = (bf16[512,512]{1,0:T(8,128)(2,1)}, bf16[512,512]{1,0:T(8,128)(2,1)}) custom-call(s32[13]{0:T(128)} %stack.27.info, bf16[2048,128]{1,0:T(8,128)(2,1)} %prep.1.kv_ref.own_ref, bf16[16,32,512]{2,1,0:T(8,128)(2,1)} %copy-done.9, bf16[2048,128]{1,0:T(8,128)(2,1)} %collective-permute-done.refs_3_.refs_1_, ...), custom_call_target="tpu_custom_call" | custom-call | flops 4294967296 | bytes 4194304 | tf_op jit(solution)/shard_map/attend_foreign/pallas_call | solution.py:257
  97.3 2.3 %fusion.2 = (bf16[128,3072]{1,0:T(8,128)(2,1)S(1)}, bf16[128,3072]{1,0:T(8,128)(2,1)S(1)}) fusion(bf16[128,3072]{1,0:T(8,128)(2,1)} %collective-permute-done.12, bf16[128,3072]{1,0:T(8,128)(2,1)} %collective-permute-done.13, bf16[128,3072]{1,0:T(8,128)(2,1)} %collective-permute-done.11, bf16[128,3072]{1,0:T(8,128)(2,1)S(1)} %copy-done, pred[]{:T(512)S(6)} %eq.7, ...), kind=kLoop, calls=%fused_computation.6 | loop fusion | flops 4718592 | bytes 5505025 | tf_op jit(solution)/shard_map/convert_element_type | solution.py:375
  99.7 4.6 %collective-permute-start.15 = (bf16[64,3072]{1,0:T(8,128)(2,1)S(1)}, bf16[64,3072]{1,0:T(8,128)(2,1)S(1)}, u32[]{:S(2)}, u32[]{:S(2)}) collective-permute-start(bf16[64,3072]{1,0:T(8,128)(2,1)S(1)} %get-tuple-element.71), channel_id=1, source_target_pairs={{1,13},{3,15},{5,1},{7,3},{9,5},{11,7},{13,9},{15,11},{17,29},{19,... | collective-permute-start | bytes 1179656 | tf_op jit(solution)/shard_map/ppermute | solution.py:342
  104.3 2.2 %collective-permute-start.16 = (bf16[64,3072]{1,0:T(8,128)(2,1)S(1)}, bf16[64,3072]{1,0:T(8,128)(2,1)S(1)}, u32[]{:S(2)}, u32[]{:S(2)}) collective-permute-start(bf16[64,3072]{1,0:T(8,128)(2,1)S(1)} %get-tuple-element.72), channel_id=1, source_target_pairs={{1,9},{3,11},{5,13},{7,15},{9,1},{11,3},{13,5},{15,7},{17,25},{19,... | collective-permute-start | bytes 1179656 | tf_op jit(solution)/shard_map/ppermute | solution.py:342
  106.6 0.8 collective-permute-start.14
  107.3 5.9 %collective-permute-done.15 = bf16[64,3072]{1,0:T(8,128)(2,1)S(1)} collective-permute-done((bf16[64,3072]{1,0:T(8,128)(2,1)S(1)}, bf16[64,3072]{1,0:T(8,128)(2,1)S(1)}, u32[]{:S(2)}, u32[]{:S(2)}) %collective-permute-start.15) | collective-permute-done | bytes 393248 | tf_op jit(solution)/shard_map/ppermute | solution.py:342
  113.2 1.2 collective-permute-done.16
  114.4 4.2 %collective-permute-done.14 = bf16[64,3072]{1,0:T(8,128)(2,1)} collective-permute-done((bf16[64,3072]{1,0:T(8,128)(2,1)S(1)}, bf16[64,3072]{1,0:T(8,128)(2,1)}, u32[]{:S(2)}, u32[]{:S(2)}) %collective-permute-start.14) | collective-permute-done | bytes 393248 | tf_op jit(solution)/shard_map/ppermute | solution.py:342
  118.6 1.2 add_convert_fusion.1
  120.0 0.8 copy-done.2
  120.8 7.6 %project.3 = (bf16[128,3072]{1,0:T(8,128)(2,1)}, bf16[128,3072]{1,0:T(8,128)(2,1)}, bf16[128,3072]{1,0:T(8,128)(2,1)}, bf16[128,3072]{1,0:T(8,128)(2,1)}) custom-call(s32[13]{0:T(128)} %stack.27.info, bf16[512,512]{1,0:T(8,128)(2,1)} %get-tuple-element.47.a, bf16[512,512]{1,0:T(8,128)(2,1)} %copy-done.2, bf16[512,6144]{1,0:T(8,128)(2,1)} %wa.3, ...), custom_call_target="tpu_custom_call" | custom-call | flops 3221225472 | bytes 12582912 | tf_op jit(solution)/shard_map/project/pallas_call | solution.py:299
  128.4 1.2 collective-permute-start.19
  130.9 9.1 %collective-permute-done.19 = bf16[128,3072]{1,0:T(8,128)(2,1)S(1)} collective-permute-done((bf16[128,3072]{1,0:T(8,128)(2,1)}, bf16[128,3072]{1,0:T(8,128)(2,1)S(1)}, u32[]{:S(2)}, u32[]{:S(2)}) %collective-permute-start.19) | collective-permute-done | bytes 786464 | tf_op jit(solution)/shard_map/ppermute | solution.py:342
  140.0 8.4 %collective-permute-done.20 = bf16[128,3072]{1,0:T(8,128)(2,1)S(1)} collective-permute-done((bf16[128,3072]{1,0:T(8,128)(2,1)}, bf16[128,3072]{1,0:T(8,128)(2,1)S(1)}, u32[]{:S(2)}, u32[]{:S(2)}) %collective-permute-start.20) | collective-permute-done | bytes 786464 | tf_op jit(solution)/shard_map/ppermute | solution.py:342
  148.4 2.1 %fusion.6 = (bf16[128,3072]{1,0:T(8,128)(2,1)S(1)}, bf16[128,3072]{1,0:T(8,128)(2,1)S(1)}) fusion(bf16[128,3072]{1,0:T(8,128)(2,1)S(1)} %collective-permute-done.20, bf16[128,3072]{1,0:T(8,128)(2,1)S(1)} %collective-permute-done.21, bf16[128,3072]{1,0:T(8,128)(2,1)S(1)} %collective-permute-done.19, bf16[128,3072]{1,0:T(8,128)(2,1)} %get-tuple-element.56, ...), kind=kLoop, calls=%fused_computation.10 | loop fusion | flops 4718592 | bytes 5505025 | tf_op jit(solution)/shard_map/convert_element_type | solution.py:375
  150.6 2.2 %collective-permute-start.23 = (bf16[64,3072]{1,0:T(8,128)(2,1)S(1)}, bf16[64,3072]{1,0:T(8,128)(2,1)S(1)}, u32[]{:S(2)}, u32[]{:S(2)}) collective-permute-start(bf16[64,3072]{1,0:T(8,128)(2,1)S(1)} %get-tuple-element.67), channel_id=1, source_target_pairs={{1,13},{3,15},{5,1},{7,3},{9,5},{11,7},{13,9},{15,11},{17,29},{19,... | collective-permute-start | bytes 1179656 | tf_op jit(solution)/shard_map/ppermute | solution.py:342
  152.8 2.2 %collective-permute-start.24 = (bf16[64,3072]{1,0:T(8,128)(2,1)S(1)}, bf16[64,3072]{1,0:T(8,128)(2,1)S(1)}, u32[]{:S(2)}, u32[]{:S(2)}) collective-permute-start(bf16[64,3072]{1,0:T(8,128)(2,1)S(1)} %get-tuple-element.68), channel_id=1, source_target_pairs={{1,9},{3,11},{5,13},{7,15},{9,1},{11,3},{13,5},{15,7},{17,25},{19,... | collective-permute-start | bytes 1179656 | tf_op jit(solution)/shard_map/ppermute | solution.py:342
  155.1 0.9 collective-permute-start.22
  156.0 3.1 %collective-permute-done.23 = bf16[64,3072]{1,0:T(8,128)(2,1)S(1)} collective-permute-done((bf16[64,3072]{1,0:T(8,128)(2,1)S(1)}, bf16[64,3072]{1,0:T(8,128)(2,1)S(1)}, u32[]{:S(2)}, u32[]{:S(2)}) %collective-permute-start.23) | collective-permute-done | bytes 393248 | tf_op jit(solution)/shard_map/ppermute | solution.py:342
  159.1 3.9 %collective-permute-done.24 = bf16[64,3072]{1,0:T(8,128)(2,1)S(1)} collective-permute-done((bf16[64,3072]{1,0:T(8,128)(2,1)S(1)}, bf16[64,3072]{1,0:T(8,128)(2,1)S(1)}, u32[]{:S(2)}, u32[]{:S(2)}) %collective-permute-start.24) | collective-permute-done | bytes 393248 | tf_op jit(solution)/shard_map/ppermute | solution.py:342
  162.9 4.1 %collective-permute-done.22 = bf16[64,3072]{1,0:T(8,128)(2,1)S(1)} collective-permute-done((bf16[64,3072]{1,0:T(8,128)(2,1)S(1)}, bf16[64,3072]{1,0:T(8,128)(2,1)S(1)}, u32[]{:S(2)}, u32[]{:S(2)}) %collective-permute-start.22) | collective-permute-done | bytes 393248 | tf_op jit(solution)/shard_map/ppermute | solution.py:342
  167.4 3.1 %collective-permute-start.25 = (bf16[32,3072]{1,0:T(8,128)(2,1)S(1)}, bf16[32,3072]{1,0:T(8,128)(2,1)S(1)}, u32[]{:S(2)}, u32[]{:S(2)}) collective-permute-start(bf16[32,3072]{1,0:T(8,128)(2,1)S(1)} %get-tuple-element.75), channel_id=1, source_target_pairs={{0,112},{1,113},{2,114},{3,115},{4,116},{5,117},{6,118},{7,119},{8... | collective-permute-start | bytes 589832 | tf_op jit(solution)/shard_map/ppermute | solution.py:342
  170.6 7.2 %collective-permute-done.26 = bf16[32,3072]{1,0:T(8,128)(2,1)S(1)} collective-permute-done((bf16[32,3072]{1,0:T(8,128)(2,1)S(1)}, bf16[32,3072]{1,0:T(8,128)(2,1)S(1)}, u32[]{:S(2)}, u32[]{:S(2)}) %collective-permute-start.26) | collective-permute-done | bytes 196640 | tf_op jit(solution)/shard_map/ppermute | solution.py:342
  177.9 0.9 pad_maximum_fusion
  (48 shorter events, 4.0 us)
Async XLA Ops:
  0.0 62.0 %collective-permute-start.10 = (bf16[512,6144]{1,0:T(8,128)(2,1)}, bf16[512,6144]{1,0:T(8,128)(2,1)}, u32[]{:S(2)}, u32[]{:S(2)}) collective-permute-start(bf16[512,6144]{1,0:T(8,128)(2,1)} %wa.3), channel_id=1, source_target_pairs={{0,1},{1,0},{2,3},{3,2},{4,5},{5,4},{6,7},{7,6},{8,9},{9,8},{10,11... | collective-permute-start | bytes 18874376 | tf_op jit(solution)/shard_map/ppermute | solution.py:342
  4.7 19.1 %collective-permute-start = (bf16[2048,128]{1,0:T(8,128)(2,1)}, bf16[2048,128]{1,0:T(8,128)(2,1)}, u32[]{:S(2)}, u32[]{:S(2)}) collective-permute-start(bf16[2048,128]{1,0:T(8,128)(2,1)} %prep.1.kv_ref.own_ref), channel_id=1, source_target_pairs={{0,112},{1,49},{2,114},{3,51},{4,116},{5,53},{6,118},{7,55},{8,120... | collective-permute-start | bytes 1572872 | tf_op jit(solution)/shard_map/ppermute | solution.py:342
  11.2 22.8 %collective-permute-start.1 = (bf16[2048,128]{1,0:T(8,128)(2,1)}, bf16[2048,128]{1,0:T(8,128)(2,1)}, u32[]{:S(2)}, u32[]{:S(2)}) collective-permute-start(bf16[2048,128]{1,0:T(8,128)(2,1)} %prep.1.kv_ref.own_ref), channel_id=1, source_target_pairs={{0,96},{1,33},{2,98},{3,35},{4,100},{5,37},{6,102},{7,39},{8,104},... | collective-permute-start | bytes 1572872 | tf_op jit(solution)/shard_map/ppermute | solution.py:342
  13.4 27.2 %collective-permute-start.2 = (bf16[2048,128]{1,0:T(8,128)(2,1)}, bf16[2048,128]{1,0:T(8,128)(2,1)}, u32[]{:S(2)}, u32[]{:S(2)}) collective-permute-start(bf16[2048,128]{1,0:T(8,128)(2,1)} %prep.1.kv_ref.own_ref), channel_id=1, source_target_pairs={{0,80},{1,17},{2,82},{3,19},{4,84},{5,21},{6,86},{7,23},{8,88},{9,... | collective-permute-start | bytes 1572872 | tf_op jit(solution)/shard_map/ppermute | solution.py:342
  15.4 25.3 %collective-permute-start.3 = (bf16[2048,128]{1,0:T(8,128)(2,1)}, bf16[2048,128]{1,0:T(8,128)(2,1)}, u32[]{:S(2)}, u32[]{:S(2)}) collective-permute-start(bf16[2048,128]{1,0:T(8,128)(2,1)} %prep.1.kv_ref.own_ref), channel_id=1, source_target_pairs={{0,64},{2,66},{4,68},{6,70},{8,72},{10,74},{12,76},{14,78},{16,80}... | collective-permute-start | bytes 1572872 | tf_op jit(solution)/shard_map/ppermute | solution.py:342
  16.8 24.5 %copy-start.4 = (bf16[1024,512]{1,0:T(8,128)(2,1)S(1)}, bf16[1024,512]{1,0:T(8,128)(2,1)}, u32[]{:S(2)}) copy-start(bf16[1024,512]{1,0:T(8,128)(2,1)} %param.4) | copy-start | bytes 3145732
  23.8 17.6 %collective-permute-start.4 = (bf16[2048,128]{1,0:T(8,128)(2,1)}, bf16[2048,128]{1,0:T(8,128)(2,1)S(1)}, u32[]{:S(2)}, u32[]{:S(2)}) collective-permute-start(bf16[2048,128]{1,0:T(8,128)(2,1)} %collective-permute-done.refs_3_.refs_1_), channel_id=1, source_target_pairs={{0,1},{1,0},{2,3},{3,2},{4,5},{5,4},{6,7},{7,6},{8,9},{9,8},{10,11... | collective-permute-start | bytes 1572872 | tf_op jit(solution)/shard_map/ppermute | solution.py:342
  34.1 8.7 %collective-permute-start.5 = (bf16[2048,128]{1,0:T(8,128)(2,1)}, bf16[2048,128]{1,0:T(8,128)(2,1)S(1)}, u32[]{:S(2)}, u32[]{:S(2)}) collective-permute-start(bf16[2048,128]{1,0:T(8,128)(2,1)} %collective-permute-done.1.refs_4_.refs_2_), channel_id=1, source_target_pairs={{0,1},{1,0},{2,3},{3,2},{4,5},{5,4},{6,7},{7,6},{8,9},{9,8},{10,11... | collective-permute-start | bytes 1572872 | tf_op jit(solution)/shard_map/ppermute | solution.py:342
  40.6 2.9 %collective-permute-start.6 = (bf16[2048,128]{1,0:T(8,128)(2,1)}, bf16[2048,128]{1,0:T(8,128)(2,1)S(1)}, u32[]{:S(2)}, u32[]{:S(2)}) collective-permute-start(bf16[2048,128]{1,0:T(8,128)(2,1)} %collective-permute-done.2.refs_5_.refs_3_), channel_id=1, source_target_pairs={{0,1},{1,0},{2,3},{3,2},{4,5},{5,4},{6,7},{7,6},{8,9},{9,8},{10,11... | collective-permute-start | bytes 1572872 | tf_op jit(solution)/shard_map/ppermute | solution.py:342
  40.6 3.7 %collective-permute-start.7 = (bf16[2048,128]{1,0:T(8,128)(2,1)}, bf16[2048,128]{1,0:T(8,128)(2,1)S(1)}, u32[]{:S(2)}, u32[]{:S(2)}) collective-permute-start(bf16[2048,128]{1,0:T(8,128)(2,1)} %collective-permute-done.3.refs_6_.refs_4_), channel_id=1, source_target_pairs={{0,1},{1,0},{2,3},{3,2},{4,5},{5,4},{6,7},{7,6},{8,9},{9,8},{10,11... | collective-permute-start | bytes 1572872 | tf_op jit(solution)/shard_map/ppermute | solution.py:342
  41.4 1.3 copy-start.5
  41.4 17.2 %collective-permute-start.8 = (bf16[16,32,512]{2,1,0:T(8,128)(2,1)S(1)}, bf16[16,32,512]{2,1,0:T(8,128)(2,1)S(1)}, u32[]{:S(2)}, u32[]{:S(2)}) collective-permute-start(bf16[16,32,512]{2,1,0:T(8,128)(2,1)S(1)} %slice_bitcast_fusion), channel_id=1, source_target_pairs={{0,112},{1,113},{2,114},{3,115},{4,116},{5,117},{6,118},{7,119},{8... | collective-permute-start | bytes 1572872 | tf_op jit(solution)/shard_map/ppermute | solution.py:342
  42.7 0.8 copy-start.6
  43.5 0.8 copy-start.7
  44.4 0.8 copy-start.8
  58.7 0.8 copy-start.9
  59.5 2.5 %collective-permute-start.9 = (bf16[512,512]{1,0:T(8,128)(2,1)}, bf16[512,512]{1,0:T(8,128)(2,1)S(1)}, u32[]{:S(2)}, u32[]{:S(2)}) collective-permute-start(bf16[512,512]{1,0:T(8,128)(2,1)} %get-tuple-element.44), channel_id=1, source_target_pairs={{0,1},{1,0},{2,3},{3,2},{4,5},{5,4},{6,7},{7,6},{8,9},{9,8},{10,11... | collective-permute-start | bytes 1572872 | tf_op jit(solution)/shard_map/ppermute | solution.py:342
  62.0 0.8 copy-start.3
  70.4 26.8 %collective-permute-start.11 = (bf16[128,3072]{1,0:T(8,128)(2,1)}, bf16[128,3072]{1,0:T(8,128)(2,1)}, u32[]{:S(2)}, u32[]{:S(2)}) collective-permute-start(bf16[128,3072]{1,0:T(8,128)(2,1)} %get-tuple-element.49), channel_id=1, source_target_pairs={{0,4},{1,3},{2,6},{3,1},{4,8},{5,7},{6,10},{7,5},{8,12},{9,11},{10... | collective-permute-start | bytes 2359304 | tf_op jit(solution)/shard_map/ppermute | solution.py:342
  71.4 25.9 %collective-permute-start.12 = (bf16[128,3072]{1,0:T(8,128)(2,1)}, bf16[128,3072]{1,0:T(8,128)(2,1)}, u32[]{:S(2)}, u32[]{:S(2)}) collective-permute-start(bf16[128,3072]{1,0:T(8,128)(2,1)} %get-tuple-element.50), channel_id=1, source_target_pairs={{0,12},{1,3},{2,14},{3,1},{4,0},{5,7},{6,2},{7,5},{8,4},{9,11},{10... | collective-permute-start | bytes 2359304 | tf_op jit(solution)/shard_map/ppermute | solution.py:342
  71.9 25.3 %collective-permute-start.13 = (bf16[128,3072]{1,0:T(8,128)(2,1)}, bf16[128,3072]{1,0:T(8,128)(2,1)}, u32[]{:S(2)}, u32[]{:S(2)}) collective-permute-start(bf16[128,3072]{1,0:T(8,128)(2,1)} %get-tuple-element.52), channel_id=1, source_target_pairs={{0,8},{2,10},{4,12},{6,14},{8,0},{10,2},{12,4},{14,6},{16,24},{18,... | collective-permute-start | bytes 2359304 | tf_op jit(solution)/shard_map/ppermute | solution.py:342
  73.5 23.8 %copy-start = (bf16[128,3072]{1,0:T(8,128)(2,1)S(1)}, bf16[128,3072]{1,0:T(8,128)(2,1)}, u32[]{:S(2)}) copy-start(bf16[128,3072]{1,0:T(8,128)(2,1)} %get-tuple-element.48) | copy-start | bytes 2359300
  73.5 23.8 %copy-start.1 = (bf16[128,3072]{1,0:T(8,128)(2,1)S(1)}, bf16[128,3072]{1,0:T(8,128)(2,1)}, u32[]{:S(2)}) copy-start(bf16[128,3072]{1,0:T(8,128)(2,1)} %get-tuple-element.52) | copy-start | bytes 2359300
  99.7 13.6 %collective-permute-start.15 = (bf16[64,3072]{1,0:T(8,128)(2,1)S(1)}, bf16[64,3072]{1,0:T(8,128)(2,1)S(1)}, u32[]{:S(2)}, u32[]{:S(2)}) collective-permute-start(bf16[64,3072]{1,0:T(8,128)(2,1)S(1)} %get-tuple-element.71), channel_id=1, source_target_pairs={{1,13},{3,15},{5,1},{7,3},{9,5},{11,7},{13,9},{15,11},{17,29},{19,... | collective-permute-start | bytes 1179656 | tf_op jit(solution)/shard_map/ppermute | solution.py:342
  104.3 10.1 %collective-permute-start.16 = (bf16[64,3072]{1,0:T(8,128)(2,1)S(1)}, bf16[64,3072]{1,0:T(8,128)(2,1)S(1)}, u32[]{:S(2)}, u32[]{:S(2)}) collective-permute-start(bf16[64,3072]{1,0:T(8,128)(2,1)S(1)} %get-tuple-element.72), channel_id=1, source_target_pairs={{1,9},{3,11},{5,13},{7,15},{9,1},{11,3},{13,5},{15,7},{17,25},{19,... | collective-permute-start | bytes 1179656 | tf_op jit(solution)/shard_map/ppermute | solution.py:342
  106.6 12.1 %collective-permute-start.14 = (bf16[64,3072]{1,0:T(8,128)(2,1)S(1)}, bf16[64,3072]{1,0:T(8,128)(2,1)}, u32[]{:S(2)}, u32[]{:S(2)}) collective-permute-start(bf16[64,3072]{1,0:T(8,128)(2,1)S(1)} %slice.62), channel_id=1, source_target_pairs={{0,2},{1,5},{2,0},{3,7},{4,6},{5,9},{6,4},{7,11},{8,10},{9,13},{10... | collective-permute-start | bytes 1179656 | tf_op jit(solution)/shard_map/ppermute | solution.py:342
  107.3 12.7 %collective-permute-start.17 = (bf16[512,512]{1,0:T(8,128)(2,1)}, bf16[512,512]{1,0:T(8,128)(2,1)S(1)}, u32[]{:S(2)}, u32[]{:S(2)}) collective-permute-start(bf16[512,512]{1,0:T(8,128)(2,1)} %get-tuple-element.54), channel_id=1, source_target_pairs={{0,1},{1,0},{2,3},{3,2},{4,5},{5,4},{6,7},{7,6},{8,9},{9,8},{10,11... | collective-permute-start | bytes 1572872 | tf_op jit(solution)/shard_map/ppermute | solution.py:342
  119.9 8.5 %collective-permute-start.18 = (bf16[32,3072]{1,0:T(8,128)(2,1)S(1)}, bf16[32,3072]{1,0:T(8,128)(2,1)S(1)}, u32[]{:S(2)}, u32[]{:S(2)}) collective-permute-start(bf16[32,3072]{1,0:T(8,128)(2,1)S(1)} %get-tuple-element.74), channel_id=1, source_target_pairs={{0,1},{1,0},{2,3},{3,2},{4,5},{5,4},{6,7},{7,6},{8,9},{9,8},{10,11... | collective-permute-start | bytes 589832 | tf_op jit(solution)/shard_map/ppermute | solution.py:342
  120.0 0.8 copy-start.2
  128.4 11.6 %collective-permute-start.19 = (bf16[128,3072]{1,0:T(8,128)(2,1)}, bf16[128,3072]{1,0:T(8,128)(2,1)S(1)}, u32[]{:S(2)}, u32[]{:S(2)}) collective-permute-start(bf16[128,3072]{1,0:T(8,128)(2,1)} %get-tuple-element.58), channel_id=1, source_target_pairs={{0,4},{1,3},{2,6},{3,1},{4,8},{5,7},{6,10},{7,5},{8,12},{9,11},{10... | collective-permute-start | bytes 2359304 | tf_op jit(solution)/shard_map/ppermute | solution.py:342
  129.6 10.4 %collective-permute-start.21 = (bf16[128,3072]{1,0:T(8,128)(2,1)}, bf16[128,3072]{1,0:T(8,128)(2,1)S(1)}, u32[]{:S(2)}, u32[]{:S(2)}) collective-permute-start(bf16[128,3072]{1,0:T(8,128)(2,1)} %get-tuple-element.62), channel_id=1, source_target_pairs={{0,8},{2,10},{4,12},{6,14},{8,0},{10,2},{12,4},{14,6},{16,24},{18,... | collective-permute-start | bytes 2359304 | tf_op jit(solution)/shard_map/ppermute | solution.py:342
  130.3 18.1 %collective-permute-start.20 = (bf16[128,3072]{1,0:T(8,128)(2,1)}, bf16[128,3072]{1,0:T(8,128)(2,1)S(1)}, u32[]{:S(2)}, u32[]{:S(2)}) collective-permute-start(bf16[128,3072]{1,0:T(8,128)(2,1)} %get-tuple-element.60), channel_id=1, source_target_pairs={{0,12},{1,3},{2,14},{3,1},{4,0},{5,7},{6,2},{7,5},{8,4},{9,11},{10... | collective-permute-start | bytes 2359304 | tf_op jit(solution)/shard_map/ppermute | solution.py:342
  150.6 8.5 %collective-permute-start.23 = (bf16[64,3072]{1,0:T(8,128)(2,1)S(1)}, bf16[64,3072]{1,0:T(8,128)(2,1)S(1)}, u32[]{:S(2)}, u32[]{:S(2)}) collective-permute-start(bf16[64,3072]{1,0:T(8,128)(2,1)S(1)} %get-tuple-element.67), channel_id=1, source_target_pairs={{1,13},{3,15},{5,1},{7,3},{9,5},{11,7},{13,9},{15,11},{17,29},{19,... | collective-permute-start | bytes 1179656 | tf_op jit(solution)/shard_map/ppermute | solution.py:342
  152.8 10.1 %collective-permute-start.24 = (bf16[64,3072]{1,0:T(8,128)(2,1)S(1)}, bf16[64,3072]{1,0:T(8,128)(2,1)S(1)}, u32[]{:S(2)}, u32[]{:S(2)}) collective-permute-start(bf16[64,3072]{1,0:T(8,128)(2,1)S(1)} %get-tuple-element.68), channel_id=1, source_target_pairs={{1,9},{3,11},{5,13},{7,15},{9,1},{11,3},{13,5},{15,7},{17,25},{19,... | collective-permute-start | bytes 1179656 | tf_op jit(solution)/shard_map/ppermute | solution.py:342
  155.1 12.0 %collective-permute-start.22 = (bf16[64,3072]{1,0:T(8,128)(2,1)S(1)}, bf16[64,3072]{1,0:T(8,128)(2,1)S(1)}, u32[]{:S(2)}, u32[]{:S(2)}) collective-permute-start(bf16[64,3072]{1,0:T(8,128)(2,1)S(1)} %slice.68), channel_id=1, source_target_pairs={{0,2},{1,5},{2,0},{3,7},{4,6},{5,9},{6,4},{7,11},{8,10},{9,13},{10... | collective-permute-start | bytes 1179656 | tf_op jit(solution)/shard_map/ppermute | solution.py:342
  167.3 10.4 %collective-permute-start.26 = (bf16[32,3072]{1,0:T(8,128)(2,1)S(1)}, bf16[32,3072]{1,0:T(8,128)(2,1)S(1)}, u32[]{:S(2)}, u32[]{:S(2)}) collective-permute-start(bf16[32,3072]{1,0:T(8,128)(2,1)S(1)} %get-tuple-element.76), channel_id=1, source_target_pairs={{0,113},{1,112},{2,115},{3,114},{4,117},{5,116},{6,119},{7,118},{8... | collective-permute-start | bytes 589832 | tf_op jit(solution)/shard_map/ppermute | solution.py:342
  167.4 10.3 %collective-permute-start.25 = (bf16[32,3072]{1,0:T(8,128)(2,1)S(1)}, bf16[32,3072]{1,0:T(8,128)(2,1)S(1)}, u32[]{:S(2)}, u32[]{:S(2)}) collective-permute-start(bf16[32,3072]{1,0:T(8,128)(2,1)S(1)} %get-tuple-element.75), channel_id=1, source_target_pairs={{0,112},{1,113},{2,114},{3,115},{4,116},{5,117},{6,118},{7,119},{8... | collective-permute-start | bytes 589832 | tf_op jit(solution)/shard_map/ppermute | solution.py:342

commit v3 on v2

--- a/solution.py
+++ b/solution.py
@@ -14,7 +14,7 @@
 LIMIT = 60.0
 BF = jnp.bfloat16
 F32 = jnp.float32
-PARAMS = pltpu.CompilerParams(vmem_limit_bytes=62 << 20)
+PARAMS = pltpu.CompilerParams(vmem_limit_bytes=64 << 20)
 FETCH = ((7, 3), (6, 2), (5, 1), (4, None))
 SLOTS = [d for pair in FETCH for d in pair if d is not None]
 TABLE = 6
@@ -184,25 +184,17 @@
         acc_ref[0] = jnp.zeros(acc_ref.shape[1:], F32)
         m_ref[...] = jnp.full_like(m_ref, NEG)
 
-        def exact(slot, _):
-            back = limit - jnp.where(slot == 0, place, partner)
-
-            @pl.when(back >= 0)
-            def _():
-                wait(slot)
-                exact_block(kv_buf.at[slot], back, 1, groups, qt_ref, acc_ref.at[0], m_ref)
-
-            return 0
-
-        lax.fori_loop(0, 2, exact, 0)
+        wait(1)
+        exact_block(kv_buf.at[1], 0, 1, groups, qt_ref, acc_ref.at[0], m_ref)
 
     def scores(kk, c0):
         return jnp.dot(kk, qt_ref[:, c0 : c0 + half], preferred_element_type=F32)
 
-    def add_block(i, _):
-        @pl.when(behind(i) > 0)
+    def add_block(slot, _):
+        i = jnp.maximum(slot - 1, 0)
+
+        @pl.when(jnp.where(slot == 0, limit - place, behind(i)) > 0)
         def _():
-            slot = i + 1
             wait(slot)
             old = count[0] % 2
             new = 1 - old
@@ -230,7 +222,7 @@
 
         return 0
 
-    lax.fori_loop(0, n, add_block, 0)
+    lax.fori_loop(0, n + 1, add_block, 0)
     last = count[0] % 2
     for h in range(heads):
         o = acc_ref[last, :, h * qb : (h + 1) * qb]
@@ -386,8 +378,8 @@
 
     half = (n_head, sub, width)
     near, near_peer = attend(info, kv, state, half, mine, other, n_y, n_seq)
-    near_far = swap_core(after(near_peer, q_far))
-    parts_n = project(info, near, near_far, w_out, w_other, n_y, cols // 4)
+    near_far = swap_core(near_peer)
+    parts_n = project(after(info, q_far), near, near_far, w_out, w_other, n_y, cols // 4)
     got_n = stage_one(parts_n)
     far, far_peer = attend(after(info, parts_n[0]), kv, [q_far], half, mine, other, n_y, n_seq)
     far_far = swap_core(far_peer)
@@ -399,10 +391,10 @@
     def by_core(x, same):
         return jnp.where((core == 0) == same, x[0], x[1])
 
+    parts_f = [after(p, done_n) for p in parts_f]
+    got_f = stage_one(parts_f)
     own_other = swap_core(by_core(done_n, False))
-    parts_f = [after(p, own_other) for p in parts_f]
-    got_f = stage_one(parts_f)
-    total_f = sum_one(parts_f, got_f)
+    total_f = sum_one([after(p, own_other) for p in parts_f], got_f)
     got2_f = stage_two(total_f)
     done_f = add(total_f[0], *got2_f).reshape(2, sub, cols // 2)
     home = over_all(by_core(done_f, True), lambda s, y, z, c: (n_seq - 1 - s, y, z, c))

time: 181 us -> 173 us (0.956)
  waiting for transfers between devices: 64 us -> 58.2 us
  Pallas kernels: 51.6 us -> 49.6 us
    ppermute x27, waiting for transfers between devices: 64 us -> 58.2 us  [over_all(): return lax.ppermute(x, ('seq', 'head'), pairs)]
    unnamed x21 -> x7, local copies, waits for them, and re-layouts: 4.86 us -> 0.03 us
    pallas_call x2, Pallas kernels: 27.4 us -> 25.5 us  [attend(): pl.pallas_call(functools.partial(attend_kernel, foreign, groups, n_y, n_s...]
    squeeze x1, local copies, waits for them, and re-layouts: 0.04 us -> 1.9 us  [local(): q4[:, 1]]
  transfers between devices with their start and end apart: 27 -> 27, of which waited for: 13 -> 11; matrix products, arithmetic and copies ran while one was open for 1% -> 4% of each run, Pallas kernels for 25% -> 25%
where the time goes in v3:
time: 173 us; the launch traced here: 171 us
  waiting for transfers between devices  58.2 us (34%)
  starting transfers between devices  51.8 us (30%)
  Pallas kernels  49.6 us (29%)
  other arithmetic  6.36 us (4%)
  local copies, waits for them, and re-layouts  4.41 us (3%)
    ppermute x27, waiting for transfers between devices, over_all(): return lax.ppermute(x, ('seq', 'head'), pairs)  58.2 us
    ppermute x27, starting transfers between devices, over_all(): return lax.ppermute(x, ('seq', 'head'), pairs)  51.8 us
    pallas_call x2, Pallas kernels, attend(): pl.pallas_call(functools.partial(attend_kernel, foreign, groups, n_y, n_s...  25.5 us
    pallas_call x2, Pallas kernels, project(): pl.pallas_call(body, grid_spec=pltpu.PrefetchScalarGridSpec(num_scalar_pr...  15.2 us
    pallas_call x1, Pallas kernels, own(): pl.pallas_call(functools.partial(own_kernel, groups), grid=(1,), in_specs...  6.29 us
    convert_element_type x2, other arithmetic, sum_one(): a = (first + jnp.where(core == 0, extra, 0.0)).astype(BF)  3.47 us
  transfers between devices with their start and end apart: 27, of which 11 were waited for; matrix products, arithmetic and copies ran while one was open for 4% of the time, Pallas kernels for 25%

profile of v3, /device:TPU:1, one launch (start us, length us, event | category | flops | bytes accessed | tf_op | source)
XLA Modules:
  0.0 170.7 jit_solution(4901377642014715522)
XLA Ops:
  0.0 1.4 collective-permute-start.10
  1.4 0.6 stack.27.info
  2.0 2.6 %prep.1.kv_ref.own_ref = bf16[2048,128]{1,0:T(8,128)(2,1)} custom-call(s32[13]{0:T(128)} %stack.27.info, bf16[1024,1024]{1,0:T(8,128)(2,1)} %k_ref.1, bf16[1024,1024]{1,0:T(8,128)(2,1)} %v_ref.1), custom_call_target="tpu_custom_call" | custom-call | tf_op jit(solution)/shard_map/prep/pallas_call | solution.py:37
  4.7 6.5 %collective-permute-start = (bf16[2048,128]{1,0:T(8,128)(2,1)}, bf16[2048,128]{1,0:T(8,128)(2,1)}, u32[]{:S(2)}, u32[]{:S(2)}) collective-permute-start(bf16[2048,128]{1,0:T(8,128)(2,1)} %prep.1.kv_ref.own_ref), channel_id=1, source_target_pairs={{0,112},{1,49},{2,114},{3,51},{4,116},{5,53},{6,118},{7,55},{8,120... | collective-permute-start | bytes 1572872 | tf_op jit(solution)/shard_map/ppermute | solution.py:334
  11.2 2.2 %collective-permute-start.1 = (bf16[2048,128]{1,0:T(8,128)(2,1)}, bf16[2048,128]{1,0:T(8,128)(2,1)}, u32[]{:S(2)}, u32[]{:S(2)}) collective-permute-start(bf16[2048,128]{1,0:T(8,128)(2,1)} %prep.1.kv_ref.own_ref), channel_id=1, source_target_pairs={{0,96},{1,33},{2,98},{3,35},{4,100},{5,37},{6,102},{7,39},{8,104},... | collective-permute-start | bytes 1572872 | tf_op jit(solution)/shard_map/ppermute | solution.py:334
  13.3 1.9 %collective-permute-start.2 = (bf16[2048,128]{1,0:T(8,128)(2,1)}, bf16[2048,128]{1,0:T(8,128)(2,1)}, u32[]{:S(2)}, u32[]{:S(2)}) collective-permute-start(bf16[2048,128]{1,0:T(8,128)(2,1)} %prep.1.kv_ref.own_ref), channel_id=1, source_target_pairs={{0,80},{1,17},{2,82},{3,19},{4,84},{5,21},{6,86},{7,23},{8,88},{9,... | collective-permute-start | bytes 1572872 | tf_op jit(solution)/shard_map/ppermute | solution.py:334
  15.3 1.5 collective-permute-start.3
  16.8 6.3 %own.1 = (bf16[256,2048]{1,0:T(8,128)(2,1)}, f32[144,2048]{1,0:T(8,128)}, f32[8,2048]{1,0:T(8,128)}) custom-call(bf16[16,2,32,512]{3,2,1,0:T(8,128)(2,1)} %bitcast.12, bf16[2048,128]{1,0:T(8,128)(2,1)} %prep.1.kv_ref.own_ref), custom_call_target="tpu_custom_call" | custom-call | flops 2147483648 | bytes 8388608 | tf_op jit(solution)/shard_map/own/pallas_call | solution.py:103
  23.1 0.7 collective-permute-done.refs_3_.refs_1_
  23.8 5.4 %collective-permute-start.5 = (bf16[2048,128]{1,0:T(8,128)(2,1)}, bf16[2048,128]{1,0:T(8,128)(2,1)}, u32[]{:S(2)}, u32[]{:S(2)}) collective-permute-start(bf16[2048,128]{1,0:T(8,128)(2,1)} %collective-permute-done.refs_3_.refs_1_), channel_id=1, source_target_pairs={{0,1},{1,0},{2,3},{3,2},{4,5},{5,4},{6,7},{7,6},{8,9},{9,8},{10,11... | collective-permute-start | bytes 1572872 | tf_op jit(solution)/shard_map/ppermute | solution.py:334
  29.1 4.9 %collective-permute-done.1.refs_4_.refs_2_ = bf16[2048,128]{1,0:T(8,128)(2,1)} collective-permute-done((bf16[2048,128]{1,0:T(8,128)(2,1)}, bf16[2048,128]{1,0:T(8,128)(2,1)}, u32[]{:S(2)}, u32[]{:S(2)}) %collective-permute-start.1) | collective-permute-done | bytes 524320 | tf_op jit(solution)/shard_map/ppermute | solution.py:334
  34.0 6.5 %collective-permute-start.6 = (bf16[2048,128]{1,0:T(8,128)(2,1)}, bf16[2048,128]{1,0:T(8,128)(2,1)}, u32[]{:S(2)}, u32[]{:S(2)}) collective-permute-start(bf16[2048,128]{1,0:T(8,128)(2,1)} %collective-permute-done.1.refs_4_.refs_2_), channel_id=1, source_target_pairs={{0,1},{1,0},{2,3},{3,2},{4,5},{5,4},{6,7},{7,6},{8,9},{9,8},{10,11... | collective-permute-start | bytes 1572872 | tf_op jit(solution)/shard_map/ppermute | solution.py:334
  40.6 0.7 collective-permute-start.8
  41.3 1.9 %slice_bitcast_fusion = bf16[16,32,512]{2,1,0:T(8,128)(2,1)} fusion(bf16[16,2,32,512]{3,2,1,0:T(8,128)(2,1)} %bitcast.13), kind=kLoop, calls=%fused_computation.15 | loop fusion | bytes 1048576 | tf_op jit(solution)/shard_map/squeeze | solution.py:355
  43.2 1.2 collective-permute-start.4
  44.4 3.7 %attend_own.1 = (bf16[512,512]{1,0:T(8,128)(2,1)}, bf16[512,512]{1,0:T(8,128)(2,1)}) custom-call(s32[13]{0:T(128)} %stack.27.info, bf16[2048,128]{1,0:T(8,128)(2,1)} %prep.1.kv_ref.own_ref, bf16[256,2048]{1,0:T(8,128)(2,1)} %get-tuple-element.39.refs_0_, f32[144,2048]{1,0:T(8,128)} %get-tuple-element.40.refs_1_, f32[8,2048]{1,0:T(8,128)} %get-tuple-element.36.refs_2_, ...), custom_call_target="tpu_custom_call" | custom-call | flops 4294967296 | bytes 4194304 | tf_op jit(solution)/shard_map/attend_own/pallas_call | solution.py:249
  48.2 0.4 collective-permute-start.9
  48.5 12.2 %collective-permute-done.4.refs_0_ = bf16[16,32,512]{2,1,0:T(8,128)(2,1)} collective-permute-done((bf16[16,32,512]{2,1,0:T(8,128)(2,1)}, bf16[16,32,512]{2,1,0:T(8,128)(2,1)}, u32[]{:S(2)}, u32[]{:S(2)}) %collective-permute-start.4) | collective-permute-done | bytes 524320 | tf_op jit(solution)/shard_map/ppermute | solution.py:334
  60.7 7.6 %project.2 = (bf16[128,3072]{1,0:T(8,128)(2,1)}, bf16[128,3072]{1,0:T(8,128)(2,1)}, bf16[128,3072]{1,0:T(8,128)(2,1)}, bf16[128,3072]{1,0:T(8,128)(2,1)}) custom-call(s32[13]{0:T(128)} %stack.27.info, bf16[512,512]{1,0:T(8,128)(2,1)} %get-tuple-element.45.a, bf16[512,512]{1,0:T(8,128)(2,1)} %collective-permute-done.9.b, bf16[512,6144]{1,0:T(8,128)(2,1)} %wa.3, ...), custom_call_target="tpu_custom_call" | custom-call | flops 3221225472 | bytes 12582912 | tf_op jit(solution)/shard_map/project/pallas_call | solution.py:291
  68.2 1.0 collective-permute-start.11
  69.2 0.5 collective-permute-start.12
  69.8 1.6 collective-permute-start.13
  71.3 21.8 %attend_foreign.1 = (bf16[512,512]{1,0:T(8,128)(2,1)}, bf16[512,512]{1,0:T(8,128)(2,1)}) custom-call(s32[13]{0:T(128)} %stack.27.info, bf16[2048,128]{1,0:T(8,128)(2,1)} %prep.1.kv_ref.own_ref, bf16[16,32,512]{2,1,0:T(8,128)(2,1)} %collective-permute-done.4.refs_0_, bf16[2048,128]{1,0:T(8,128)(2,1)} %collective-permute-done.refs_3_.refs_1_, ...), custom_call_target="tpu_custom_call" | custom-call | flops 4294967296 | bytes 4194304 | tf_op jit(solution)/shard_map/attend_foreign/pallas_call | solution.py:249
  93.2 5.0 %collective-permute-start.17 = (bf16[512,512]{1,0:T(8,128)(2,1)}, bf16[512,512]{1,0:T(8,128)(2,1)}, u32[]{:S(2)}, u32[]{:S(2)}) collective-permute-start(bf16[512,512]{1,0:T(8,128)(2,1)} %get-tuple-element.56), channel_id=1, source_target_pairs={{0,1},{1,0},{2,3},{3,2},{4,5},{5,4},{6,7},{7,6},{8,9},{9,8},{10,11... | collective-permute-start | bytes 1572872 | tf_op jit(solution)/shard_map/ppermute | solution.py:334
  98.2 2.8 %fusion.2 = (bf16[128,3072]{1,0:T(8,128)(2,1)S(1)}, bf16[128,3072]{1,0:T(8,128)(2,1)S(1)}) fusion(bf16[128,3072]{1,0:T(8,128)(2,1)} %collective-permute-done.12, bf16[128,3072]{1,0:T(8,128)(2,1)} %collective-permute-done.13, bf16[128,3072]{1,0:T(8,128)(2,1)} %collective-permute-done.11, bf16[128,3072]{1,0:T(8,128)(2,1)} %get-tuple-element.50, pred[]{:T(512)S(6)} %eq.7, ...), kind=kLoop, calls=%fused_computation.6 | loop fusion | flops 4718592 | bytes 5505025 | tf_op jit(solution)/shard_map/convert_element_type | solution.py:367
  101.0 0.8 slice.62
  101.8 0.9 fusion.9
  102.7 2.7 %collective-permute-start.15 = (bf16[64,3072]{1,0:T(8,128)(2,1)}, bf16[64,3072]{1,0:T(8,128)(2,1)}, u32[]{:S(2)}, u32[]{:S(2)}) collective-permute-start(bf16[64,3072]{1,0:T(8,128)(2,1)} %get-tuple-element.75), channel_id=1, source_target_pairs={{1,13},{3,15},{5,1},{7,3},{9,5},{11,7},{13,9},{15,11},{17,29},{19,... | collective-permute-start | bytes 1179656 | tf_op jit(solution)/shard_map/ppermute | solution.py:334
  105.4 3.3 %collective-permute-start.16 = (bf16[64,3072]{1,0:T(8,128)(2,1)}, bf16[64,3072]{1,0:T(8,128)(2,1)}, u32[]{:S(2)}, u32[]{:S(2)}) collective-permute-start(bf16[64,3072]{1,0:T(8,128)(2,1)} %get-tuple-element.76), channel_id=1, source_target_pairs={{1,9},{3,11},{5,13},{7,15},{9,1},{11,3},{13,5},{15,7},{17,25},{19,... | collective-permute-start | bytes 1179656 | tf_op jit(solution)/shard_map/ppermute | solution.py:334
  108.8 7.6 %project.3 = (bf16[128,3072]{1,0:T(8,128)(2,1)}, bf16[128,3072]{1,0:T(8,128)(2,1)}, bf16[128,3072]{1,0:T(8,128)(2,1)}, bf16[128,3072]{1,0:T(8,128)(2,1)}) custom-call(s32[13]{0:T(128)} %stack.27.info, bf16[512,512]{1,0:T(8,128)(2,1)} %get-tuple-element.49.a, bf16[512,512]{1,0:T(8,128)(2,1)} %collective-permute-done.17.b, bf16[512,6144]{1,0:T(8,128)(2,1)} %wa.3, ...), custom_call_target="tpu_custom_call" | custom-call | flops 3221225472 | bytes 12582912 | tf_op jit(solution)/shard_map/project/pallas_call | solution.py:291
  116.5 3.5 %collective-permute-done.14 = bf16[64,3072]{1,0:T(8,128)(2,1)} collective-permute-done((bf16[64,3072]{1,0:T(8,128)(2,1)}, bf16[64,3072]{1,0:T(8,128)(2,1)}, u32[]{:S(2)}, u32[]{:S(2)}) %collective-permute-start.14) | collective-permute-done | bytes 393248 | tf_op jit(solution)/shard_map/ppermute | solution.py:334
  120.0 1.5 add_convert_fusion.1
  121.5 1.0 collective-permute-start.19
  122.5 0.7 collective-permute-start.21
  123.2 0.9 collective-permute-start.20
  124.2 1.4 collective-permute-done.18
  125.6 7.3 %collective-permute-done.19 = bf16[128,3072]{1,0:T(8,128)(2,1)S(1)} collective-permute-done((bf16[128,3072]{1,0:T(8,128)(2,1)}, bf16[128,3072]{1,0:T(8,128)(2,1)S(1)}, u32[]{:S(2)}, u32[]{:S(2)}) %collective-permute-start.19) | collective-permute-done | bytes 786464 | tf_op jit(solution)/shard_map/ppermute | solution.py:334
  132.9 8.1 %collective-permute-done.20 = bf16[128,3072]{1,0:T(8,128)(2,1)S(1)} collective-permute-done((bf16[128,3072]{1,0:T(8,128)(2,1)}, bf16[128,3072]{1,0:T(8,128)(2,1)S(1)}, u32[]{:S(2)}, u32[]{:S(2)}) %collective-permute-start.20) | collective-permute-done | bytes 786464 | tf_op jit(solution)/shard_map/ppermute | solution.py:334
  141.1 0.7 fusion.6
  141.8 2.8 %collective-permute-start.23 = (bf16[64,3072]{1,0:T(8,128)(2,1)S(1)}, bf16[64,3072]{1,0:T(8,128)(2,1)S(1)}, u32[]{:S(2)}, u32[]{:S(2)}) collective-permute-start(bf16[64,3072]{1,0:T(8,128)(2,1)S(1)} %get-tuple-element.71), channel_id=1, source_target_pairs={{1,13},{3,15},{5,1},{7,3},{9,5},{11,7},{13,9},{15,11},{17,29},{19,... | collective-permute-start | bytes 1179656 | tf_op jit(solution)/shard_map/ppermute | solution.py:334
  144.6 3.3 %collective-permute-start.24 = (bf16[64,3072]{1,0:T(8,128)(2,1)S(1)}, bf16[64,3072]{1,0:T(8,128)(2,1)S(1)}, u32[]{:S(2)}, u32[]{:S(2)}) collective-permute-start(bf16[64,3072]{1,0:T(8,128)(2,1)S(1)} %get-tuple-element.72), channel_id=1, source_target_pairs={{1,9},{3,11},{5,13},{7,15},{9,1},{11,3},{13,5},{15,7},{17,25},{19,... | collective-permute-start | bytes 1179656 | tf_op jit(solution)/shard_map/ppermute | solution.py:334
  147.9 0.9 collective-permute-start.22
  148.9 1.5 collective-permute-done.23
  150.4 4.4 %collective-permute-done.24 = bf16[64,3072]{1,0:T(8,128)(2,1)S(1)} collective-permute-done((bf16[64,3072]{1,0:T(8,128)(2,1)S(1)}, bf16[64,3072]{1,0:T(8,128)(2,1)S(1)}, u32[]{:S(2)}, u32[]{:S(2)}) %collective-permute-start.24) | collective-permute-done | bytes 393248 | tf_op jit(solution)/shard_map/ppermute | solution.py:334
  154.8 4.1 %collective-permute-done.22 = bf16[64,3072]{1,0:T(8,128)(2,1)S(1)} collective-permute-done((bf16[64,3072]{1,0:T(8,128)(2,1)S(1)}, bf16[64,3072]{1,0:T(8,128)(2,1)S(1)}, u32[]{:S(2)}, u32[]{:S(2)}) %collective-permute-start.22) | collective-permute-done | bytes 393248 | tf_op jit(solution)/shard_map/ppermute | solution.py:334
  159.2 0.3 collective-permute-start.25
  159.5 10.0 %collective-permute-done.26 = bf16[32,3072]{1,0:T(8,128)(2,1)S(1)} collective-permute-done((bf16[32,3072]{1,0:T(8,128)(2,1)S(1)}, bf16[32,3072]{1,0:T(8,128)(2,1)S(1)}, u32[]{:S(2)}, u32[]{:S(2)}) %collective-permute-start.26) | collective-permute-done | bytes 196640 | tf_op jit(solution)/shard_map/ppermute | solution.py:334
  169.7 0.9 pad_maximum_fusion
  (34 shorter events, 0.8 us)
Async XLA Ops:
  0.0 60.7 %collective-permute-start.10 = (bf16[512,6144]{1,0:T(8,128)(2,1)}, bf16[512,6144]{1,0:T(8,128)(2,1)}, u32[]{:S(2)}, u32[]{:S(2)}) collective-permute-start(bf16[512,6144]{1,0:T(8,128)(2,1)} %wa.3), channel_id=1, source_target_pairs={{0,1},{1,0},{2,3},{3,2},{4,5},{5,4},{6,7},{7,6},{8,9},{9,8},{10,11... | collective-permute-start | bytes 18874376 | tf_op jit(solution)/shard_map/ppermute | solution.py:334
  4.7 19.1 %collective-permute-start = (bf16[2048,128]{1,0:T(8,128)(2,1)}, bf16[2048,128]{1,0:T(8,128)(2,1)}, u32[]{:S(2)}, u32[]{:S(2)}) collective-permute-start(bf16[2048,128]{1,0:T(8,128)(2,1)} %prep.1.kv_ref.own_ref), channel_id=1, source_target_pairs={{0,112},{1,49},{2,114},{3,51},{4,116},{5,53},{6,118},{7,55},{8,120... | collective-permute-start | bytes 1572872 | tf_op jit(solution)/shard_map/ppermute | solution.py:334
  11.2 22.8 %collective-permute-start.1 = (bf16[2048,128]{1,0:T(8,128)(2,1)}, bf16[2048,128]{1,0:T(8,128)(2,1)}, u32[]{:S(2)}, u32[]{:S(2)}) collective-permute-start(bf16[2048,128]{1,0:T(8,128)(2,1)} %prep.1.kv_ref.own_ref), channel_id=1, source_target_pairs={{0,96},{1,33},{2,98},{3,35},{4,100},{5,37},{6,102},{7,39},{8,104},... | collective-permute-start | bytes 1572872 | tf_op jit(solution)/shard_map/ppermute | solution.py:334
  13.3 27.2 %collective-permute-start.2 = (bf16[2048,128]{1,0:T(8,128)(2,1)}, bf16[2048,128]{1,0:T(8,128)(2,1)}, u32[]{:S(2)}, u32[]{:S(2)}) collective-permute-start(bf16[2048,128]{1,0:T(8,128)(2,1)} %prep.1.kv_ref.own_ref), channel_id=1, source_target_pairs={{0,80},{1,17},{2,82},{3,19},{4,84},{5,21},{6,86},{7,23},{8,88},{9,... | collective-permute-start | bytes 1572872 | tf_op jit(solution)/shard_map/ppermute | solution.py:334
  15.3 25.3 %collective-permute-start.3 = (bf16[2048,128]{1,0:T(8,128)(2,1)}, bf16[2048,128]{1,0:T(8,128)(2,1)}, u32[]{:S(2)}, u32[]{:S(2)}) collective-permute-start(bf16[2048,128]{1,0:T(8,128)(2,1)} %prep.1.kv_ref.own_ref), channel_id=1, source_target_pairs={{0,64},{2,66},{4,68},{6,70},{8,72},{10,74},{12,76},{14,78},{16,80}... | collective-permute-start | bytes 1572872 | tf_op jit(solution)/shard_map/ppermute | solution.py:334
  23.8 19.4 %collective-permute-start.5 = (bf16[2048,128]{1,0:T(8,128)(2,1)}, bf16[2048,128]{1,0:T(8,128)(2,1)}, u32[]{:S(2)}, u32[]{:S(2)}) collective-permute-start(bf16[2048,128]{1,0:T(8,128)(2,1)} %collective-permute-done.refs_3_.refs_1_), channel_id=1, source_target_pairs={{0,1},{1,0},{2,3},{3,2},{4,5},{5,4},{6,7},{7,6},{8,9},{9,8},{10,11... | collective-permute-start | bytes 1572872 | tf_op jit(solution)/shard_map/ppermute | solution.py:334
  34.0 10.4 %collective-permute-start.6 = (bf16[2048,128]{1,0:T(8,128)(2,1)}, bf16[2048,128]{1,0:T(8,128)(2,1)}, u32[]{:S(2)}, u32[]{:S(2)}) collective-permute-start(bf16[2048,128]{1,0:T(8,128)(2,1)} %collective-permute-done.1.refs_4_.refs_2_), channel_id=1, source_target_pairs={{0,1},{1,0},{2,3},{3,2},{4,5},{5,4},{6,7},{7,6},{8,9},{9,8},{10,11... | collective-permute-start | bytes 1572872 | tf_op jit(solution)/shard_map/ppermute | solution.py:334
  40.6 3.9 %collective-permute-start.7 = (bf16[2048,128]{1,0:T(8,128)(2,1)}, bf16[2048,128]{1,0:T(8,128)(2,1)}, u32[]{:S(2)}, u32[]{:S(2)}) collective-permute-start(bf16[2048,128]{1,0:T(8,128)(2,1)} %collective-permute-done.2.refs_5_.refs_3_), channel_id=1, source_target_pairs={{0,1},{1,0},{2,3},{3,2},{4,5},{5,4},{6,7},{7,6},{8,9},{9,8},{10,11... | collective-permute-start | bytes 1572872 | tf_op jit(solution)/shard_map/ppermute | solution.py:334
  40.6 3.9 %collective-permute-start.8 = (bf16[2048,128]{1,0:T(8,128)(2,1)}, bf16[2048,128]{1,0:T(8,128)(2,1)}, u32[]{:S(2)}, u32[]{:S(2)}) collective-permute-start(bf16[2048,128]{1,0:T(8,128)(2,1)} %collective-permute-done.3.refs_6_.refs_4_), channel_id=1, source_target_pairs={{0,1},{1,0},{2,3},{3,2},{4,5},{5,4},{6,7},{7,6},{8,9},{9,8},{10,11... | collective-permute-start | bytes 1572872 | tf_op jit(solution)/shard_map/ppermute | solution.py:334
  43.2 17.5 %collective-permute-start.4 = (bf16[16,32,512]{2,1,0:T(8,128)(2,1)}, bf16[16,32,512]{2,1,0:T(8,128)(2,1)}, u32[]{:S(2)}, u32[]{:S(2)}) collective-permute-start(bf16[16,32,512]{2,1,0:T(8,128)(2,1)} %slice_bitcast_fusion), channel_id=1, source_target_pairs={{0,112},{1,113},{2,114},{3,115},{4,116},{5,117},{6,118},{7,119},{8... | collective-permute-start | bytes 1572872 | tf_op jit(solution)/shard_map/ppermute | solution.py:334
  48.2 12.5 %collective-permute-start.9 = (bf16[512,512]{1,0:T(8,128)(2,1)}, bf16[512,512]{1,0:T(8,128)(2,1)}, u32[]{:S(2)}, u32[]{:S(2)}) collective-permute-start(bf16[512,512]{1,0:T(8,128)(2,1)} %get-tuple-element.46), channel_id=1, source_target_pairs={{0,1},{1,0},{2,3},{3,2},{4,5},{5,4},{6,7},{7,6},{8,9},{9,8},{10,11... | collective-permute-start | bytes 1572872 | tf_op jit(solution)/shard_map/ppermute | solution.py:334
  68.2 29.9 %collective-permute-start.11 = (bf16[128,3072]{1,0:T(8,128)(2,1)}, bf16[128,3072]{1,0:T(8,128)(2,1)}, u32[]{:S(2)}, u32[]{:S(2)}) collective-permute-start(bf16[128,3072]{1,0:T(8,128)(2,1)} %get-tuple-element.51), channel_id=1, source_target_pairs={{0,4},{1,3},{2,6},{3,1},{4,8},{5,7},{6,10},{7,5},{8,12},{9,11},{10... | collective-permute-start | bytes 2359304 | tf_op jit(solution)/shard_map/ppermute | solution.py:334
  69.2 28.9 %collective-permute-start.12 = (bf16[128,3072]{1,0:T(8,128)(2,1)}, bf16[128,3072]{1,0:T(8,128)(2,1)}, u32[]{:S(2)}, u32[]{:S(2)}) collective-permute-start(bf16[128,3072]{1,0:T(8,128)(2,1)} %get-tuple-element.52), channel_id=1, source_target_pairs={{0,12},{1,3},{2,14},{3,1},{4,0},{5,7},{6,2},{7,5},{8,4},{9,11},{10... | collective-permute-start | bytes 2359304 | tf_op jit(solution)/shard_map/ppermute | solution.py:334
  69.8 28.4 %collective-permute-start.13 = (bf16[128,3072]{1,0:T(8,128)(2,1)}, bf16[128,3072]{1,0:T(8,128)(2,1)}, u32[]{:S(2)}, u32[]{:S(2)}) collective-permute-start(bf16[128,3072]{1,0:T(8,128)(2,1)} %get-tuple-element.54), channel_id=1, source_target_pairs={{0,8},{2,10},{4,12},{6,14},{8,0},{10,2},{12,4},{14,6},{16,24},{18,... | collective-permute-start | bytes 2359304 | tf_op jit(solution)/shard_map/ppermute | solution.py:334
  93.2 15.6 %collective-permute-start.17 = (bf16[512,512]{1,0:T(8,128)(2,1)}, bf16[512,512]{1,0:T(8,128)(2,1)}, u32[]{:S(2)}, u32[]{:S(2)}) collective-permute-start(bf16[512,512]{1,0:T(8,128)(2,1)} %get-tuple-element.56), channel_id=1, source_target_pairs={{0,1},{1,0},{2,3},{3,2},{4,5},{5,4},{6,7},{7,6},{8,9},{9,8},{10,11... | collective-permute-start | bytes 1572872 | tf_op jit(solution)/shard_map/ppermute | solution.py:334
  100.9 1.8 %copy-start = (bf16[128,3072]{1,0:T(8,128)(2,1)}, bf16[128,3072]{1,0:T(8,128)(2,1)S(1)}, u32[]{:S(2)}) copy-start(bf16[128,3072]{1,0:T(8,128)(2,1)S(1)} %get-tuple-element.73) | copy-start | bytes 2359300
  102.7 13.7 %collective-permute-start.15 = (bf16[64,3072]{1,0:T(8,128)(2,1)}, bf16[64,3072]{1,0:T(8,128)(2,1)}, u32[]{:S(2)}, u32[]{:S(2)}) collective-permute-start(bf16[64,3072]{1,0:T(8,128)(2,1)} %get-tuple-element.75), channel_id=1, source_target_pairs={{1,13},{3,15},{5,1},{7,3},{9,5},{11,7},{13,9},{15,11},{17,29},{19,... | collective-permute-start | bytes 1179656 | tf_op jit(solution)/shard_map/ppermute | solution.py:334
  105.4 11.1 %collective-permute-start.16 = (bf16[64,3072]{1,0:T(8,128)(2,1)}, bf16[64,3072]{1,0:T(8,128)(2,1)}, u32[]{:S(2)}, u32[]{:S(2)}) collective-permute-start(bf16[64,3072]{1,0:T(8,128)(2,1)} %get-tuple-element.76), channel_id=1, source_target_pairs={{1,9},{3,11},{5,13},{7,15},{9,1},{11,3},{13,5},{15,7},{17,25},{19,... | collective-permute-start | bytes 1179656 | tf_op jit(solution)/shard_map/ppermute | solution.py:334
  108.7 11.2 %collective-permute-start.14 = (bf16[64,3072]{1,0:T(8,128)(2,1)}, bf16[64,3072]{1,0:T(8,128)(2,1)}, u32[]{:S(2)}, u32[]{:S(2)}) collective-permute-start(bf16[64,3072]{1,0:T(8,128)(2,1)} %slice.62), channel_id=1, source_target_pairs={{0,2},{1,5},{2,0},{3,7},{4,6},{5,9},{6,4},{7,11},{8,10},{9,13},{10... | collective-permute-start | bytes 1179656 | tf_op jit(solution)/shard_map/ppermute | solution.py:334
  116.4 6.0 %copy-start.2 = (bf16[128,3072]{1,0:T(8,128)(2,1)S(1)}, bf16[128,3072]{1,0:T(8,128)(2,1)}, u32[]{:S(2)}) copy-start(bf16[128,3072]{1,0:T(8,128)(2,1)} %get-tuple-element.66) | copy-start | bytes 2359300
  116.4 24.6 %copy-start.1 = (bf16[128,3072]{1,0:T(8,128)(2,1)S(1)}, bf16[128,3072]{1,0:T(8,128)(2,1)}, u32[]{:S(2)}) copy-start(bf16[128,3072]{1,0:T(8,128)(2,1)} %get-tuple-element.59) | copy-start | bytes 2359300
  121.5 11.4 %collective-permute-start.19 = (bf16[128,3072]{1,0:T(8,128)(2,1)}, bf16[128,3072]{1,0:T(8,128)(2,1)S(1)}, u32[]{:S(2)}, u32[]{:S(2)}) collective-permute-start(bf16[128,3072]{1,0:T(8,128)(2,1)} %get-tuple-element.61), channel_id=1, source_target_pairs={{0,4},{1,3},{2,6},{3,1},{4,8},{5,7},{6,10},{7,5},{8,12},{9,11},{10... | collective-permute-start | bytes 2359304 | tf_op jit(solution)/shard_map/ppermute | solution.py:334
  122.5 10.4 %collective-permute-start.21 = (bf16[128,3072]{1,0:T(8,128)(2,1)S(1)}, bf16[128,3072]{1,0:T(8,128)(2,1)S(1)}, u32[]{:S(2)}, u32[]{:S(2)}) collective-permute-start(bf16[128,3072]{1,0:T(8,128)(2,1)S(1)} %copy-done.2), channel_id=1, source_target_pairs={{0,8},{2,10},{4,12},{6,14},{8,0},{10,2},{12,4},{14,6},{16,24},{18,... | collective-permute-start | bytes 2359304 | tf_op jit(solution)/shard_map/ppermute | solution.py:334
  123.2 17.9 %collective-permute-start.20 = (bf16[128,3072]{1,0:T(8,128)(2,1)}, bf16[128,3072]{1,0:T(8,128)(2,1)S(1)}, u32[]{:S(2)}, u32[]{:S(2)}) collective-permute-start(bf16[128,3072]{1,0:T(8,128)(2,1)} %get-tuple-element.63), channel_id=1, source_target_pairs={{0,12},{1,3},{2,14},{3,1},{4,0},{5,7},{6,2},{7,5},{8,4},{9,11},{10... | collective-permute-start | bytes 2359304 | tf_op jit(solution)/shard_map/ppermute | solution.py:334
  124.1 1.5 collective-permute-start.18
  141.8 8.5 %collective-permute-start.23 = (bf16[64,3072]{1,0:T(8,128)(2,1)S(1)}, bf16[64,3072]{1,0:T(8,128)(2,1)S(1)}, u32[]{:S(2)}, u32[]{:S(2)}) collective-permute-start(bf16[64,3072]{1,0:T(8,128)(2,1)S(1)} %get-tuple-element.71), channel_id=1, source_target_pairs={{1,13},{3,15},{5,1},{7,3},{9,5},{11,7},{13,9},{15,11},{17,29},{19,... | collective-permute-start | bytes 1179656 | tf_op jit(solution)/shard_map/ppermute | solution.py:334
  144.6 10.1 %collective-permute-start.24 = (bf16[64,3072]{1,0:T(8,128)(2,1)S(1)}, bf16[64,3072]{1,0:T(8,128)(2,1)S(1)}, u32[]{:S(2)}, u32[]{:S(2)}) collective-permute-start(bf16[64,3072]{1,0:T(8,128)(2,1)S(1)} %get-tuple-element.72), channel_id=1, source_target_pairs={{1,9},{3,11},{5,13},{7,15},{9,1},{11,3},{13,5},{15,7},{17,25},{19,... | collective-permute-start | bytes 1179656 | tf_op jit(solution)/shard_map/ppermute | solution.py:334
  147.9 10.9 %collective-permute-start.22 = (bf16[64,3072]{1,0:T(8,128)(2,1)S(1)}, bf16[64,3072]{1,0:T(8,128)(2,1)S(1)}, u32[]{:S(2)}, u32[]{:S(2)}) collective-permute-start(bf16[64,3072]{1,0:T(8,128)(2,1)S(1)} %slice.68), channel_id=1, source_target_pairs={{0,2},{1,5},{2,0},{3,7},{4,6},{5,9},{6,4},{7,11},{8,10},{9,13},{10... | collective-permute-start | bytes 1179656 | tf_op jit(solution)/shard_map/ppermute | solution.py:334
  159.1 10.4 %collective-permute-start.26 = (bf16[32,3072]{1,0:T(8,128)(2,1)S(1)}, bf16[32,3072]{1,0:T(8,128)(2,1)S(1)}, u32[]{:S(2)}, u32[]{:S(2)}) collective-permute-start(bf16[32,3072]{1,0:T(8,128)(2,1)S(1)} %get-tuple-element.80), channel_id=1, source_target_pairs={{0,113},{1,112},{2,115},{3,114},{4,117},{5,116},{6,119},{7,118},{8... | collective-permute-start | bytes 589832 | tf_op jit(solution)/shard_map/ppermute | solution.py:334
  159.2 10.3 %collective-permute-start.25 = (bf16[32,3072]{1,0:T(8,128)(2,1)S(1)}, bf16[32,3072]{1,0:T(8,128)(2,1)S(1)}, u32[]{:S(2)}, u32[]{:S(2)}) collective-permute-start(bf16[32,3072]{1,0:T(8,128)(2,1)S(1)} %get-tuple-element.79), channel_id=1, source_target_pairs={{0,112},{1,113},{2,114},{3,115},{4,116},{5,117},{6,118},{7,119},{8... | collective-permute-start | bytes 589832 | tf_op jit(solution)/shard_map/ppermute | solution.py:334

commit v4 on v3

--- a/solution.py
+++ b/solution.py
@@ -129,7 +129,7 @@
     ops = n_seq // 2
     inputs = 1 if foreign else 3
     mine, other = refs[inputs : inputs + ops], refs[inputs + ops : inputs + 2 * ops]
-    o_ref, peer_ref, q_buf, kv_buf, qt_ref, acc_ref, m_ref, mx_ref, count, sems = refs[inputs + 2 * ops :]
+    o_ref, q_buf, kv_buf, qt_ref, acc_ref, m_ref, mx_ref, count, sems = refs[inputs + 2 * ops :]
     place, core, partner = info[0], info[2], info[5]
     rows = own_ref.shape[0] // 2
     cols = qt_ref.shape[1]
@@ -230,13 +230,8 @@
         for g in range(groups):
             ry = (g // 4 + n_y - info[3]) % n_y
             rz = (g // 2 % 2) ^ info[4]
-            by_y = ((ry * 2 + rz) * 2 + g % 2) * sub
-            by_z = (((ry // 2 * 2 + rz) * 2 + ry % 2) * 2 + g % 2) * sub
-            piece = o[g * sub : (g + 1) * sub, :]
-            here = pl.multiple_of(jnp.where(core == 0, by_y, by_z), sub)
-            there = pl.multiple_of(jnp.where(core == 0, by_z, by_y), sub)
-            o_ref[pl.ds(here, sub), h * DH : (h + 1) * DH] = piece
-            peer_ref[pl.ds(there, sub), h * DH : (h + 1) * DH] = piece
+            dst = pl.multiple_of(((ry * 2 + rz) * 2 + g % 2) * sub, sub)
+            o_ref[pl.ds(dst, sub), h * DH : (h + 1) * DH] = o[g * sub : (g + 1) * sub, :]
 
 
 def attend(info, kv, state, q_shape, mine, other, n_y, n_seq):
@@ -252,7 +247,7 @@
             num_scalar_prefetch=1,
             grid=(1,),
             in_specs=[any_space] * (1 + len(state) + 2 * len(mine)),
-            out_specs=[out, out],
+            out_specs=out,
             scratch_shapes=[
                 pltpu.VMEM(q_shape, BF),
                 pltpu.VMEM((len(SLOTS) + 1, *kv.shape), BF),
@@ -264,7 +259,7 @@
                 pltpu.SemaphoreType.DMA((len(SLOTS) + 4,)),
             ],
         ),
-        out_shape=[jax.ShapeDtypeStruct((qb, width), BF)] * 2,
+        out_shape=jax.ShapeDtypeStruct((qb, width), BF),
         name="attend_foreign" if foreign else "attend_own",
         cost_estimate=pl.CostEstimate(
             flops=2 * cols * kv.shape[0] * 4 * DH, bytes_accessed=4 << 20, transcendentals=0
@@ -354,49 +349,26 @@
     other = [swap_core(after(x, state[2])) for x in mine]
     q_far = over_all(after(q4[:, 1], state[2], *mine), lambda s, y, z, c: (n_seq - 1 - s, y, z, c))
 
-    def stage_one(parts):
-        return [
-            over_all(parts[1], lambda s, y, z, c: (s, y, 1 - z, c) if c else (s, y + 1, z, c)),
-            over_all(parts[3], lambda s, y, z, c: (s, y, 1 - z, c) if c else (s, y - 1, z, c)),
-            over_all(parts[2], lambda s, y, z, c: None if c else (s, y + 2, z, c)),
-        ]
-
-    def sum_one(parts, got):
-        first = parts[0].astype(F32) + got[0].astype(F32)
-        extra = got[1].astype(F32) + got[2].astype(F32)
-        a = (first + jnp.where(core == 0, extra, 0.0)).astype(BF)
-        b = add(parts[2], got[1])
-        n = a.shape[0] // 2
-        return a[:n], a[n:], b[:n], b[n:]
-
-    def stage_two(total):
-        return [
-            over_all(total[1], lambda s, y, z, c: (s, y + 1, z, c) if c else (s, y, 1 - z, c)),
-            over_all(total[3], lambda s, y, z, c: (s, y - 1, z, c) if c else None),
-            over_all(total[2], lambda s, y, z, c: (s, y + 2, z, c) if c else None),
-        ]
-
-    half = (n_head, sub, width)
-    near, near_peer = attend(info, kv, state, half, mine, other, n_y, n_seq)
-    near_far = swap_core(near_peer)
-    parts_n = project(after(info, q_far), near, near_far, w_out, w_other, n_y, cols // 4)
-    got_n = stage_one(parts_n)
-    far, far_peer = attend(after(info, parts_n[0]), kv, [q_far], half, mine, other, n_y, n_seq)
-    far_far = swap_core(far_peer)
-    total_n = sum_one([after(p, far) for p in parts_n], got_n)
-    got2_n = stage_two(total_n)
-    parts_f = project(after(info, *total_n), far, far_far, w_out, w_other, n_y, cols // 4)
-    done_n = add(total_n[0], *got2_n).reshape(2, sub, cols // 2)
+    ways = [(2, 1), (1, 0), (3, 0), (0, 1), (2, 0), (1, 1), (3, 1)]
+
+    def scatter(parts):
+        return [over_all(parts[a * 2 + b], lambda s, y, z, c, a=a, b=b: (s, y + a, z ^ b, c)) for a, b in ways]
 
     def by_core(x, same):
         return jnp.where((core == 0) == same, x[0], x[1])
 
-    parts_f = [after(p, done_n) for p in parts_f]
-    got_f = stage_one(parts_f)
+    half = (n_head, sub, width)
+    near = attend(info, kv, state, half, mine, other, n_y, n_seq)
+    near_far = swap_core(near)
+    parts_n = project(after(info, q_far), near, near_far, w_out, w_other, 2 * n_y, cols // 4)
+    got_n = scatter(parts_n)
+    far = attend(after(info, parts_n[0]), kv, [q_far], half, mine, other, n_y, n_seq)
+    far_far = swap_core(after(far, *got_n[:4]))
+    parts_f = project(info, far, far_far, w_out, w_other, 2 * n_y, cols // 4)
+    got_f = scatter(parts_f)
+    done_n = add(after(parts_n[0], parts_f[0]), *got_n).reshape(2, sub, cols // 2)
     own_other = swap_core(by_core(done_n, False))
-    total_f = sum_one([after(p, own_other) for p in parts_f], got_f)
-    got2_f = stage_two(total_f)
-    done_f = add(total_f[0], *got2_f).reshape(2, sub, cols // 2)
+    done_f = add(after(parts_f[0], own_other), *got_f).reshape(2, sub, cols // 2)
     home = over_all(by_core(done_f, True), lambda s, y, z, c: (n_seq - 1 - s, y, z, c))
     home_other = over_all(by_core(done_f, False), lambda s, y, z, c: (n_seq - 1 - s, y, z, 1 - c))
     here = jnp.concatenate([by_core(done_n, True), home], axis=0)

time: 173 us -> 184 us (1.064)
  starting transfers between devices: 51.8 us -> 60.4 us
  waiting for transfers between devices: 58.2 us -> 65.9 us
  other arithmetic: 6.36 us -> 3.94 us
    ppermute x27 -> x29, starting transfers between devices: 51.8 us -> 60.4 us  [over_all(): return lax.ppermute(x, ('seq', 'head'), pairs)]
    ppermute x27 -> x29, waiting for transfers between devices: 58.2 us -> 65.9 us  [over_all(): return lax.ppermute(x, ('seq', 'head'), pairs)]
    convert_element_type x2 -> x0, other arithmetic: 3.47 us -> none  [sum_one(): a = (first + jnp.where(core == 0, extra, 0.0)).astype(BF)]
    slice x4 -> x0, local copies, waits for them, and re-layouts: 1.85 us -> none  [sum_one(): return (a[:n], a[n:], b[:n], b[n:])]
  transfers between devices with their start and end apart: 27 -> 29, of which waited for: 11 -> 12; matrix products, arithmetic and copies ran while one was open for 4% -> 3% of each run, Pallas kernels for 25% -> 23%
where the time goes in v4:
time: 184 us; the launch traced here: 182 us
  waiting for transfers between devices  65.9 us (36%)
  starting transfers between devices  60.4 us (33%)
  Pallas kernels  49 us (27%)
  other arithmetic  3.94 us (2%)
  local copies, waits for them, and re-layouts  2.58 us (1%)
    ppermute x29, waiting for transfers between devices, over_all(): return lax.ppermute(x, ('seq', 'head'), pairs)  65.9 us
    ppermute x29, starting transfers between devices, over_all(): return lax.ppermute(x, ('seq', 'head'), pairs)  60.4 us
    pallas_call x2, Pallas kernels, attend(): pl.pallas_call(functools.partial(attend_kernel, foreign, groups, n_y, n_s...  24.8 us
    pallas_call x2, Pallas kernels, project(): pl.pallas_call(body, grid_spec=pltpu.PrefetchScalarGridSpec(num_scalar_pr...  15.2 us
    pallas_call x1, Pallas kernels, own(): pl.pallas_call(functools.partial(own_kernel, groups), grid=(1,), in_specs...  6.35 us
  transfers between devices with their start and end apart: 29, of which 12 were waited for; matrix products, arithmetic and copies ran while one was open for 3% of the time, Pallas kernels for 23%

profile of v4, /device:TPU:1, one launch (start us, length us, event | category | flops | bytes accessed | tf_op | source)
XLA Modules:
  0.0 182.0 jit_solution(8208352773302345650)
XLA Ops:
  0.0 1.4 collective-permute-start.10
  1.4 0.6 stack.27.info
  2.1 2.6 %prep.1.kv_ref.own_ref = bf16[2048,128]{1,0:T(8,128)(2,1)} custom-call(s32[13]{0:T(128)} %stack.27.info, bf16[1024,1024]{1,0:T(8,128)(2,1)} %k_ref.1, bf16[1024,1024]{1,0:T(8,128)(2,1)} %v_ref.1), custom_call_target="tpu_custom_call" | custom-call | tf_op jit(solution)/shard_map/prep/pallas_call | solution.py:37
  4.7 6.5 %collective-permute-start = (bf16[2048,128]{1,0:T(8,128)(2,1)}, bf16[2048,128]{1,0:T(8,128)(2,1)}, u32[]{:S(2)}, u32[]{:S(2)}) collective-permute-start(bf16[2048,128]{1,0:T(8,128)(2,1)} %prep.1.kv_ref.own_ref), channel_id=1, source_target_pairs={{0,112},{1,49},{2,114},{3,51},{4,116},{5,53},{6,118},{7,55},{8,120... | collective-permute-start | bytes 1572872 | tf_op jit(solution)/shard_map/ppermute | solution.py:329
  11.2 2.2 %collective-permute-start.1 = (bf16[2048,128]{1,0:T(8,128)(2,1)}, bf16[2048,128]{1,0:T(8,128)(2,1)}, u32[]{:S(2)}, u32[]{:S(2)}) collective-permute-start(bf16[2048,128]{1,0:T(8,128)(2,1)} %prep.1.kv_ref.own_ref), channel_id=1, source_target_pairs={{0,96},{1,33},{2,98},{3,35},{4,100},{5,37},{6,102},{7,39},{8,104},... | collective-permute-start | bytes 1572872 | tf_op jit(solution)/shard_map/ppermute | solution.py:329
  13.4 2.0 %collective-permute-start.2 = (bf16[2048,128]{1,0:T(8,128)(2,1)}, bf16[2048,128]{1,0:T(8,128)(2,1)}, u32[]{:S(2)}, u32[]{:S(2)}) collective-permute-start(bf16[2048,128]{1,0:T(8,128)(2,1)} %prep.1.kv_ref.own_ref), channel_id=1, source_target_pairs={{0,80},{1,17},{2,82},{3,19},{4,84},{5,21},{6,86},{7,23},{8,88},{9,... | collective-permute-start | bytes 1572872 | tf_op jit(solution)/shard_map/ppermute | solution.py:329
  15.3 1.5 collective-permute-start.3
  16.8 6.3 %own.1 = (bf16[256,2048]{1,0:T(8,128)(2,1)}, f32[144,2048]{1,0:T(8,128)}, f32[8,2048]{1,0:T(8,128)}) custom-call(bf16[16,2,32,512]{3,2,1,0:T(8,128)(2,1)} %bitcast.11, bf16[2048,128]{1,0:T(8,128)(2,1)} %prep.1.kv_ref.own_ref), custom_call_target="tpu_custom_call" | custom-call | flops 2147483648 | bytes 8388608 | tf_op jit(solution)/shard_map/own/pallas_call | solution.py:103
  23.1 0.6 collective-permute-done.refs_3_.refs_1_
  23.8 5.4 %collective-permute-start.5 = (bf16[2048,128]{1,0:T(8,128)(2,1)}, bf16[2048,128]{1,0:T(8,128)(2,1)}, u32[]{:S(2)}, u32[]{:S(2)}) collective-permute-start(bf16[2048,128]{1,0:T(8,128)(2,1)} %collective-permute-done.refs_3_.refs_1_), channel_id=1, source_target_pairs={{0,1},{1,0},{2,3},{3,2},{4,5},{5,4},{6,7},{7,6},{8,9},{9,8},{10,11... | collective-permute-start | bytes 1572872 | tf_op jit(solution)/shard_map/ppermute | solution.py:329
  29.2 4.8 %collective-permute-done.1.refs_4_.refs_2_ = bf16[2048,128]{1,0:T(8,128)(2,1)} collective-permute-done((bf16[2048,128]{1,0:T(8,128)(2,1)}, bf16[2048,128]{1,0:T(8,128)(2,1)}, u32[]{:S(2)}, u32[]{:S(2)}) %collective-permute-start.1) | collective-permute-done | bytes 524320 | tf_op jit(solution)/shard_map/ppermute | solution.py:329
  34.0 6.5 %collective-permute-start.6 = (bf16[2048,128]{1,0:T(8,128)(2,1)}, bf16[2048,128]{1,0:T(8,128)(2,1)}, u32[]{:S(2)}, u32[]{:S(2)}) collective-permute-start(bf16[2048,128]{1,0:T(8,128)(2,1)} %collective-permute-done.1.refs_4_.refs_2_), channel_id=1, source_target_pairs={{0,1},{1,0},{2,3},{3,2},{4,5},{5,4},{6,7},{7,6},{8,9},{9,8},{10,11... | collective-permute-start | bytes 1572872 | tf_op jit(solution)/shard_map/ppermute | solution.py:329
  40.6 0.7 collective-permute-start.8
  41.3 1.9 %slice_bitcast_fusion = bf16[16,32,512]{2,1,0:T(8,128)(2,1)} fusion(bf16[16,2,32,512]{3,2,1,0:T(8,128)(2,1)} %bitcast.12), kind=kLoop, calls=%fused_computation.3 | loop fusion | bytes 1048576 | tf_op jit(solution)/shard_map/squeeze | solution.py:350
  43.2 1.2 collective-permute-start.4
  44.4 3.4 %attend_own.1.a = bf16[512,512]{1,0:T(8,128)(2,1)} custom-call(s32[13]{0:T(128)} %stack.27.info, bf16[2048,128]{1,0:T(8,128)(2,1)} %prep.1.kv_ref.own_ref, bf16[256,2048]{1,0:T(8,128)(2,1)} %get-tuple-element.37.refs_0_, f32[144,2048]{1,0:T(8,128)} %get-tuple-element.38.refs_1_, f32[8,2048]{1,0:T(8,128)} %get-tuple-element.34.refs_2_, ...), custom_call_target="tpu_custom_call" | custom-call | flops 4294967296 | bytes 4194304 | tf_op jit(solution)/shard_map/attend_own/pallas_call | solution.py:244
  47.8 0.4 collective-permute-start.9
  48.2 12.5 %collective-permute-done.4.refs_0_ = bf16[16,32,512]{2,1,0:T(8,128)(2,1)} collective-permute-done((bf16[16,32,512]{2,1,0:T(8,128)(2,1)}, bf16[16,32,512]{2,1,0:T(8,128)(2,1)}, u32[]{:S(2)}, u32[]{:S(2)}) %collective-permute-start.4) | collective-permute-done | bytes 524320 | tf_op jit(solution)/shard_map/ppermute | solution.py:329
  60.7 7.6 %project.2 = (bf16[64,3072]{1,0:T(8,128)(2,1)}, bf16[64,3072]{1,0:T(8,128)(2,1)}, bf16[64,3072]{1,0:T(8,128)(2,1)}, bf16[64,3072]{1,0:T(8,128)(2,1)}, bf16[64,30...) custom-call(s32[13]{0:T(128)} %stack.27.info, ...), custom_call_target="tpu_custom_call" | custom-call | flops 3221225472 | bytes 12582912 | tf_op jit(solution)/shard_map/project/pallas_call | solution.py:286
  68.3 3.6 %collective-permute-start.11 = (bf16[64,3072]{1,0:T(8,128)(2,1)}, bf16[64,3072]{1,0:T(8,128)(2,1)}, u32[]{:S(2)}, u32[]{:S(2)}) collective-permute-start(bf16[64,3072]{1,0:T(8,128)(2,1)} %get-tuple-element.45), channel_id=1, source_target_pairs={{0,10},{1,11},{2,8},{3,9},{4,14},{5,15},{6,12},{7,13},{8,2},{9,3},... | collective-permute-start | bytes 1179656 | tf_op jit(solution)/shard_map/ppermute | solution.py:329
  71.9 0.4 collective-permute-start.12
  72.3 2.3 %collective-permute-start.13 = (bf16[64,3072]{1,0:T(8,128)(2,1)}, bf16[64,3072]{1,0:T(8,128)(2,1)}, u32[]{:S(2)}, u32[]{:S(2)}) collective-permute-start(bf16[64,3072]{1,0:T(8,128)(2,1)} %get-tuple-element.47), channel_id=1, source_target_pairs={{0,12},{1,13},{2,14},{3,15},{4,0},{5,1},{6,2},{7,3},{8,4},{9,5},{1... | collective-permute-start | bytes 1179656 | tf_op jit(solution)/shard_map/ppermute | solution.py:329
  74.6 0.5 collective-permute-start.14
  75.2 21.5 %attend_foreign.1.a = bf16[512,512]{1,0:T(8,128)(2,1)} custom-call(s32[13]{0:T(128)} %stack.27.info, bf16[2048,128]{1,0:T(8,128)(2,1)} %prep.1.kv_ref.own_ref, bf16[16,32,512]{2,1,0:T(8,128)(2,1)} %collective-permute-done.4.refs_0_, bf16[2048,128]{1,0:T(8,128)(2,1)} %collective-permute-done.refs_3_.refs_1_, ...), custom_call_target="tpu_custom_call" | custom-call | flops 4294967296 | bytes 4194304 | tf_op jit(solution)/shard_map/attend_foreign/pallas_call | solution.py:244
  96.7 2.0 %collective-permute-start.15 = (bf16[512,512]{1,0:T(8,128)(2,1)}, bf16[512,512]{1,0:T(8,128)(2,1)}, u32[]{:S(2)}, u32[]{:S(2)}) collective-permute-start(bf16[512,512]{1,0:T(8,128)(2,1)} %attend_foreign.1.a), channel_id=1, source_target_pairs={{0,1},{1,0},{2,3},{3,2},{4,5},{5,4},{6,7},{7,6},{8,9},{9,8},{10,11... | collective-permute-start | bytes 1572872 | tf_op jit(solution)/shard_map/ppermute | solution.py:329
  98.7 0.9 collective-permute-start.17
  99.6 2.6 %collective-permute-start.18 = (bf16[64,3072]{1,0:T(8,128)(2,1)}, bf16[64,3072]{1,0:T(8,128)(2,1)}, u32[]{:S(2)}, u32[]{:S(2)}) collective-permute-start(bf16[64,3072]{1,0:T(8,128)(2,1)} %get-tuple-element.54), channel_id=1, source_target_pairs={{0,14},{1,15},{2,12},{3,13},{4,2},{5,3},{6,0},{7,1},{8,6},{9,7},{1... | collective-permute-start | bytes 1179656 | tf_op jit(solution)/shard_map/ppermute | solution.py:329
  102.2 7.5 %project.3 = (bf16[64,3072]{1,0:T(8,128)(2,1)}, bf16[64,3072]{1,0:T(8,128)(2,1)}, bf16[64,3072]{1,0:T(8,128)(2,1)}, bf16[64,3072]{1,0:T(8,128)(2,1)}, bf16[64,30...) custom-call(s32[13]{0:T(128)} %stack.27.info, ...), custom_call_target="tpu_custom_call" | custom-call | flops 3221225472 | bytes 12582912 | tf_op jit(solution)/shard_map/project/pallas_call | solution.py:286
  109.8 2.5 %collective-permute-start.20 = (bf16[64,3072]{1,0:T(8,128)(2,1)}, bf16[64,3072]{1,0:T(8,128)(2,1)S(1)}, u32[]{:S(2)}, u32[]{:S(2)}) collective-permute-start(bf16[64,3072]{1,0:T(8,128)(2,1)} %get-tuple-element.56), channel_id=1, source_target_pairs={{0,10},{1,11},{2,8},{3,9},{4,14},{5,15},{6,12},{7,13},{8,2},{9,3},... | collective-permute-start | bytes 1179656 | tf_op jit(solution)/shard_map/ppermute | solution.py:329
  112.4 13.4 %collective-permute-done.17 = bf16[64,3072]{1,0:T(8,128)(2,1)} collective-permute-done((bf16[64,3072]{1,0:T(8,128)(2,1)}, bf16[64,3072]{1,0:T(8,128)(2,1)}, u32[]{:S(2)}, u32[]{:S(2)}) %collective-permute-start.17) | collective-permute-done | bytes 393248 | tf_op jit(solution)/shard_map/ppermute | solution.py:329
  125.8 2.3 %add_convert_fusion.1 = bf16[64,3072]{1,0:T(8,128)(2,1)S(1)} fusion(bf16[64,3072]{1,0:T(8,128)(2,1)} %collective-permute-done.18, bf16[64,3072]{1,0:T(8,128)(2,1)} %collective-permute-done.17, bf16[64,3072]{1,0:T(8,128)(2,1)} %collective-permute-done.16, bf16[64,3072]{1,0:T(8,128)(2,1)} %collective-permute-done.14, ...), kind=kLoop, calls=%fused_computation.2 | loop fusion | flops 3145728 | bytes 3538944 | tf_op jit(solution)/shard_map/convert_element_type | solution.py:307
  128.2 1.3 collective-permute-start.19
  129.4 5.0 %collective-permute-start.22 = (bf16[64,3072]{1,0:T(8,128)(2,1)S(1)}, bf16[64,3072]{1,0:T(8,128)(2,1)S(1)}, u32[]{:S(2)}, u32[]{:S(2)}) collective-permute-start(bf16[64,3072]{1,0:T(8,128)(2,1)S(1)} %copy-done.5), channel_id=1, source_target_pairs={{0,12},{1,13},{2,14},{3,15},{4,0},{5,1},{6,2},{7,3},{8,4},{9,5},{1... | collective-permute-start | bytes 1179656 | tf_op jit(solution)/shard_map/ppermute | solution.py:329
  134.4 0.5 collective-permute-start.23
  134.9 1.9 %collective-permute-done.20 = bf16[64,3072]{1,0:T(8,128)(2,1)S(1)} collective-permute-done((bf16[64,3072]{1,0:T(8,128)(2,1)}, bf16[64,3072]{1,0:T(8,128)(2,1)S(1)}, u32[]{:S(2)}, u32[]{:S(2)}) %collective-permute-start.20) | collective-permute-done | bytes 393248 | tf_op jit(solution)/shard_map/ppermute | solution.py:329
  136.8 4.1 %collective-permute-done.21 = bf16[64,3072]{1,0:T(8,128)(2,1)S(1)} collective-permute-done((bf16[64,3072]{1,0:T(8,128)(2,1)}, bf16[64,3072]{1,0:T(8,128)(2,1)S(1)}, u32[]{:S(2)}, u32[]{:S(2)}) %collective-permute-start.21) | collective-permute-done | bytes 393248 | tf_op jit(solution)/shard_map/ppermute | solution.py:329
  140.9 4.6 %collective-permute-start.26 = (bf16[64,3072]{1,0:T(8,128)(2,1)S(1)}, bf16[64,3072]{1,0:T(8,128)(2,1)S(1)}, u32[]{:S(2)}, u32[]{:S(2)}) collective-permute-start(bf16[64,3072]{1,0:T(8,128)(2,1)S(1)} %copy-done.1), channel_id=1, source_target_pairs={{0,14},{1,15},{2,12},{3,13},{4,2},{5,3},{6,0},{7,1},{8,6},{9,7},{1... | collective-permute-start | bytes 1179656 | tf_op jit(solution)/shard_map/ppermute | solution.py:329
  145.5 5.6 %collective-permute-done.22 = bf16[64,3072]{1,0:T(8,128)(2,1)S(1)} collective-permute-done((bf16[64,3072]{1,0:T(8,128)(2,1)S(1)}, bf16[64,3072]{1,0:T(8,128)(2,1)S(1)}, u32[]{:S(2)}, u32[]{:S(2)}) %collective-permute-start.22) | collective-permute-done | bytes 393248 | tf_op jit(solution)/shard_map/ppermute | solution.py:329
  151.1 2.0 %collective-permute-done.24 = bf16[64,3072]{1,0:T(8,128)(2,1)S(1)} collective-permute-done((bf16[64,3072]{1,0:T(8,128)(2,1)S(1)}, bf16[64,3072]{1,0:T(8,128)(2,1)S(1)}, u32[]{:S(2)}, u32[]{:S(2)}) %collective-permute-start.24) | collective-permute-done | bytes 393248 | tf_op jit(solution)/shard_map/ppermute | solution.py:329
  153.1 10.1 %collective-permute-done.25 = bf16[64,3072]{1,0:T(8,128)(2,1)S(1)} collective-permute-done((bf16[64,3072]{1,0:T(8,128)(2,1)S(1)}, bf16[64,3072]{1,0:T(8,128)(2,1)S(1)}, u32[]{:S(2)}, u32[]{:S(2)}) %collective-permute-start.25) | collective-permute-done | bytes 393248 | tf_op jit(solution)/shard_map/ppermute | solution.py:329
  163.2 0.5 collective-permute-done.26
  163.7 0.5 add_convert_fusion
  164.2 6.2 %collective-permute-start.28 = (bf16[32,3072]{1,0:T(8,128)(2,1)S(1)}, bf16[32,3072]{1,0:T(8,128)(2,1)S(1)}, u32[]{:S(2)}, u32[]{:S(2)}) collective-permute-start(bf16[32,3072]{1,0:T(8,128)(2,1)S(1)} %get-tuple-element.68), channel_id=1, source_target_pairs={{0,113},{1,112},{2,115},{3,114},{4,117},{5,116},{6,119},{7,118},{8... | collective-permute-start | bytes 589832 | tf_op jit(solution)/shard_map/ppermute | solution.py:329
  170.4 0.1 collective-permute-start.27
  170.5 5.1 %collective-permute-done.28 = bf16[32,3072]{1,0:T(8,128)(2,1)S(1)} collective-permute-done((bf16[32,3072]{1,0:T(8,128)(2,1)S(1)}, bf16[32,3072]{1,0:T(8,128)(2,1)S(1)}, u32[]{:S(2)}, u32[]{:S(2)}) %collective-permute-start.28) | collective-permute-done | bytes 196640 | tf_op jit(solution)/shard_map/ppermute | solution.py:329
  175.6 5.3 %collective-permute-done.27 = bf16[32,3072]{1,0:T(8,128)(2,1)S(1)} collective-permute-done((bf16[32,3072]{1,0:T(8,128)(2,1)S(1)}, bf16[32,3072]{1,0:T(8,128)(2,1)S(1)}, u32[]{:S(2)}, u32[]{:S(2)}) %collective-permute-start.27) | collective-permute-done | bytes 196640 | tf_op jit(solution)/shard_map/ppermute | solution.py:329
  180.9 0.1 broadcast_select_fusion.1
  181.1 0.9 pad_maximum_fusion
  (38 shorter events, 0.2 us)
Async XLA Ops:
  0.0 60.7 %collective-permute-start.10 = (bf16[512,6144]{1,0:T(8,128)(2,1)}, bf16[512,6144]{1,0:T(8,128)(2,1)}, u32[]{:S(2)}, u32[]{:S(2)}) collective-permute-start(bf16[512,6144]{1,0:T(8,128)(2,1)} %wa.3), channel_id=1, source_target_pairs={{0,1},{1,0},{2,3},{3,2},{4,5},{5,4},{6,7},{7,6},{8,9},{9,8},{10,11... | collective-permute-start | bytes 18874376 | tf_op jit(solution)/shard_map/ppermute | solution.py:329
  4.7 19.1 %collective-permute-start = (bf16[2048,128]{1,0:T(8,128)(2,1)}, bf16[2048,128]{1,0:T(8,128)(2,1)}, u32[]{:S(2)}, u32[]{:S(2)}) collective-permute-start(bf16[2048,128]{1,0:T(8,128)(2,1)} %prep.1.kv_ref.own_ref), channel_id=1, source_target_pairs={{0,112},{1,49},{2,114},{3,51},{4,116},{5,53},{6,118},{7,55},{8,120... | collective-permute-start | bytes 1572872 | tf_op jit(solution)/shard_map/ppermute | solution.py:329
  11.2 22.8 %collective-permute-start.1 = (bf16[2048,128]{1,0:T(8,128)(2,1)}, bf16[2048,128]{1,0:T(8,128)(2,1)}, u32[]{:S(2)}, u32[]{:S(2)}) collective-permute-start(bf16[2048,128]{1,0:T(8,128)(2,1)} %prep.1.kv_ref.own_ref), channel_id=1, source_target_pairs={{0,96},{1,33},{2,98},{3,35},{4,100},{5,37},{6,102},{7,39},{8,104},... | collective-permute-start | bytes 1572872 | tf_op jit(solution)/shard_map/ppermute | solution.py:329
  13.4 27.2 %collective-permute-start.2 = (bf16[2048,128]{1,0:T(8,128)(2,1)}, bf16[2048,128]{1,0:T(8,128)(2,1)}, u32[]{:S(2)}, u32[]{:S(2)}) collective-permute-start(bf16[2048,128]{1,0:T(8,128)(2,1)} %prep.1.kv_ref.own_ref), channel_id=1, source_target_pairs={{0,80},{1,17},{2,82},{3,19},{4,84},{5,21},{6,86},{7,23},{8,88},{9,... | collective-permute-start | bytes 1572872 | tf_op jit(solution)/shard_map/ppermute | solution.py:329
  15.3 25.3 %collective-permute-start.3 = (bf16[2048,128]{1,0:T(8,128)(2,1)}, bf16[2048,128]{1,0:T(8,128)(2,1)}, u32[]{:S(2)}, u32[]{:S(2)}) collective-permute-start(bf16[2048,128]{1,0:T(8,128)(2,1)} %prep.1.kv_ref.own_ref), channel_id=1, source_target_pairs={{0,64},{2,66},{4,68},{6,70},{8,72},{10,74},{12,76},{14,78},{16,80}... | collective-permute-start | bytes 1572872 | tf_op jit(solution)/shard_map/ppermute | solution.py:329
  23.8 19.4 %collective-permute-start.5 = (bf16[2048,128]{1,0:T(8,128)(2,1)}, bf16[2048,128]{1,0:T(8,128)(2,1)}, u32[]{:S(2)}, u32[]{:S(2)}) collective-permute-start(bf16[2048,128]{1,0:T(8,128)(2,1)} %collective-permute-done.refs_3_.refs_1_), channel_id=1, source_target_pairs={{0,1},{1,0},{2,3},{3,2},{4,5},{5,4},{6,7},{7,6},{8,9},{9,8},{10,11... | collective-permute-start | bytes 1572872 | tf_op jit(solution)/shard_map/ppermute | solution.py:329
  34.0 10.4 %collective-permute-start.6 = (bf16[2048,128]{1,0:T(8,128)(2,1)}, bf16[2048,128]{1,0:T(8,128)(2,1)}, u32[]{:S(2)}, u32[]{:S(2)}) collective-permute-start(bf16[2048,128]{1,0:T(8,128)(2,1)} %collective-permute-done.1.refs_4_.refs_2_), channel_id=1, source_target_pairs={{0,1},{1,0},{2,3},{3,2},{4,5},{5,4},{6,7},{7,6},{8,9},{9,8},{10,11... | collective-permute-start | bytes 1572872 | tf_op jit(solution)/shard_map/ppermute | solution.py:329
  40.6 3.9 %collective-permute-start.7 = (bf16[2048,128]{1,0:T(8,128)(2,1)}, bf16[2048,128]{1,0:T(8,128)(2,1)}, u32[]{:S(2)}, u32[]{:S(2)}) collective-permute-start(bf16[2048,128]{1,0:T(8,128)(2,1)} %collective-permute-done.2.refs_5_.refs_3_), channel_id=1, source_target_pairs={{0,1},{1,0},{2,3},{3,2},{4,5},{5,4},{6,7},{7,6},{8,9},{9,8},{10,11... | collective-permute-start | bytes 1572872 | tf_op jit(solution)/shard_map/ppermute | solution.py:329
  40.6 3.9 %collective-permute-start.8 = (bf16[2048,128]{1,0:T(8,128)(2,1)}, bf16[2048,128]{1,0:T(8,128)(2,1)}, u32[]{:S(2)}, u32[]{:S(2)}) collective-permute-start(bf16[2048,128]{1,0:T(8,128)(2,1)} %collective-permute-done.3.refs_6_.refs_4_), channel_id=1, source_target_pairs={{0,1},{1,0},{2,3},{3,2},{4,5},{5,4},{6,7},{7,6},{8,9},{9,8},{10,11... | collective-permute-start | bytes 1572872 | tf_op jit(solution)/shard_map/ppermute | solution.py:329
  43.2 17.5 %collective-permute-start.4 = (bf16[16,32,512]{2,1,0:T(8,128)(2,1)}, bf16[16,32,512]{2,1,0:T(8,128)(2,1)}, u32[]{:S(2)}, u32[]{:S(2)}) collective-permute-start(bf16[16,32,512]{2,1,0:T(8,128)(2,1)} %slice_bitcast_fusion), channel_id=1, source_target_pairs={{0,112},{1,113},{2,114},{3,115},{4,116},{5,117},{6,118},{7,119},{8... | collective-permute-start | bytes 1572872 | tf_op jit(solution)/shard_map/ppermute | solution.py:329
  47.8 12.9 %collective-permute-start.9 = (bf16[512,512]{1,0:T(8,128)(2,1)}, bf16[512,512]{1,0:T(8,128)(2,1)}, u32[]{:S(2)}, u32[]{:S(2)}) collective-permute-start(bf16[512,512]{1,0:T(8,128)(2,1)} %attend_own.1.a), channel_id=1, source_target_pairs={{0,1},{1,0},{2,3},{3,2},{4,5},{5,4},{6,7},{7,6},{8,9},{9,8},{10,11... | collective-permute-start | bytes 1572872 | tf_op jit(solution)/shard_map/ppermute | solution.py:329
  68.3 28.4 %collective-permute-start.11 = (bf16[64,3072]{1,0:T(8,128)(2,1)}, bf16[64,3072]{1,0:T(8,128)(2,1)}, u32[]{:S(2)}, u32[]{:S(2)}) collective-permute-start(bf16[64,3072]{1,0:T(8,128)(2,1)} %get-tuple-element.45), channel_id=1, source_target_pairs={{0,10},{1,11},{2,8},{3,9},{4,14},{5,15},{6,12},{7,13},{8,2},{9,3},... | collective-permute-start | bytes 1179656 | tf_op jit(solution)/shard_map/ppermute | solution.py:329
  71.9 24.7 %collective-permute-start.12 = (bf16[64,3072]{1,0:T(8,128)(2,1)}, bf16[64,3072]{1,0:T(8,128)(2,1)}, u32[]{:S(2)}, u32[]{:S(2)}) collective-permute-start(bf16[64,3072]{1,0:T(8,128)(2,1)} %get-tuple-element.46), channel_id=1, source_target_pairs={{0,4},{1,5},{2,6},{3,7},{4,8},{5,9},{6,10},{7,11},{8,12},{9,13},{1... | collective-permute-start | bytes 1179656 | tf_op jit(solution)/shard_map/ppermute | solution.py:329
  72.3 24.4 %collective-permute-start.13 = (bf16[64,3072]{1,0:T(8,128)(2,1)}, bf16[64,3072]{1,0:T(8,128)(2,1)}, u32[]{:S(2)}, u32[]{:S(2)}) collective-permute-start(bf16[64,3072]{1,0:T(8,128)(2,1)} %get-tuple-element.47), channel_id=1, source_target_pairs={{0,12},{1,13},{2,14},{3,15},{4,0},{5,1},{6,2},{7,3},{8,4},{9,5},{1... | collective-permute-start | bytes 1179656 | tf_op jit(solution)/shard_map/ppermute | solution.py:329
  74.6 22.1 %collective-permute-start.14 = (bf16[64,3072]{1,0:T(8,128)(2,1)}, bf16[64,3072]{1,0:T(8,128)(2,1)}, u32[]{:S(2)}, u32[]{:S(2)}) collective-permute-start(bf16[64,3072]{1,0:T(8,128)(2,1)} %get-tuple-element.48), channel_id=1, source_target_pairs={{0,2},{1,3},{2,0},{3,1},{4,6},{5,7},{6,4},{7,5},{8,10},{9,11},{10,... | collective-permute-start | bytes 1179656 | tf_op jit(solution)/shard_map/ppermute | solution.py:329
  96.7 5.5 %collective-permute-start.15 = (bf16[512,512]{1,0:T(8,128)(2,1)}, bf16[512,512]{1,0:T(8,128)(2,1)}, u32[]{:S(2)}, u32[]{:S(2)}) collective-permute-start(bf16[512,512]{1,0:T(8,128)(2,1)} %attend_foreign.1.a), channel_id=1, source_target_pairs={{0,1},{1,0},{2,3},{3,2},{4,5},{5,4},{6,7},{7,6},{8,9},{9,8},{10,11... | collective-permute-start | bytes 1572872 | tf_op jit(solution)/shard_map/ppermute | solution.py:329
  98.7 13.7 %collective-permute-start.16 = (bf16[64,3072]{1,0:T(8,128)(2,1)}, bf16[64,3072]{1,0:T(8,128)(2,1)}, u32[]{:S(2)}, u32[]{:S(2)}) collective-permute-start(bf16[64,3072]{1,0:T(8,128)(2,1)} %get-tuple-element.52), channel_id=1, source_target_pairs={{0,8},{1,9},{2,10},{3,11},{4,12},{5,13},{6,14},{7,15},{8,0},{9,1},... | collective-permute-start | bytes 1179656 | tf_op jit(solution)/shard_map/ppermute | solution.py:329
  98.7 27.1 %collective-permute-start.17 = (bf16[64,3072]{1,0:T(8,128)(2,1)}, bf16[64,3072]{1,0:T(8,128)(2,1)}, u32[]{:S(2)}, u32[]{:S(2)}) collective-permute-start(bf16[64,3072]{1,0:T(8,128)(2,1)} %get-tuple-element.53), channel_id=1, source_target_pairs={{0,6},{1,7},{2,4},{3,5},{4,10},{5,11},{6,8},{7,9},{8,14},{9,15},{1... | collective-permute-start | bytes 1179656 | tf_op jit(solution)/shard_map/ppermute | solution.py:329
  99.6 26.2 %collective-permute-start.18 = (bf16[64,3072]{1,0:T(8,128)(2,1)}, bf16[64,3072]{1,0:T(8,128)(2,1)}, u32[]{:S(2)}, u32[]{:S(2)}) collective-permute-start(bf16[64,3072]{1,0:T(8,128)(2,1)} %get-tuple-element.54), channel_id=1, source_target_pairs={{0,14},{1,15},{2,12},{3,13},{4,2},{5,3},{6,0},{7,1},{8,6},{9,7},{1... | collective-permute-start | bytes 1179656 | tf_op jit(solution)/shard_map/ppermute | solution.py:329
  109.8 27.0 %collective-permute-start.20 = (bf16[64,3072]{1,0:T(8,128)(2,1)}, bf16[64,3072]{1,0:T(8,128)(2,1)S(1)}, u32[]{:S(2)}, u32[]{:S(2)}) collective-permute-start(bf16[64,3072]{1,0:T(8,128)(2,1)} %get-tuple-element.56), channel_id=1, source_target_pairs={{0,10},{1,11},{2,8},{3,9},{4,14},{5,15},{6,12},{7,13},{8,2},{9,3},... | collective-permute-start | bytes 1179656 | tf_op jit(solution)/shard_map/ppermute | solution.py:329
  112.3 17.1 %copy-start.5 = (bf16[64,3072]{1,0:T(8,128)(2,1)S(1)}, bf16[64,3072]{1,0:T(8,128)(2,1)}, u32[]{:S(2)}) copy-start(bf16[64,3072]{1,0:T(8,128)(2,1)} %get-tuple-element.58) | copy-start | bytes 1179652
  112.3 22.1 %copy-start.4 = (bf16[64,3072]{1,0:T(8,128)(2,1)S(1)}, bf16[64,3072]{1,0:T(8,128)(2,1)}, u32[]{:S(2)}) copy-start(bf16[64,3072]{1,0:T(8,128)(2,1)} %get-tuple-element.59) | copy-start | bytes 1179652
  112.3 22.7 %copy-start.3 = (bf16[64,3072]{1,0:T(8,128)(2,1)S(1)}, bf16[64,3072]{1,0:T(8,128)(2,1)}, u32[]{:S(2)}) copy-start(bf16[64,3072]{1,0:T(8,128)(2,1)} %get-tuple-element.60) | copy-start | bytes 1179652
  112.3 24.6 %copy-start.2 = (bf16[64,3072]{1,0:T(8,128)(2,1)S(1)}, bf16[64,3072]{1,0:T(8,128)(2,1)}, u32[]{:S(2)}) copy-start(bf16[64,3072]{1,0:T(8,128)(2,1)} %get-tuple-element.61) | copy-start | bytes 1179652
  112.3 28.6 %copy-start.1 = (bf16[64,3072]{1,0:T(8,128)(2,1)S(1)}, bf16[64,3072]{1,0:T(8,128)(2,1)}, u32[]{:S(2)}) copy-start(bf16[64,3072]{1,0:T(8,128)(2,1)} %get-tuple-element.62) | copy-start | bytes 1179652
  112.3 51.4 %copy-start = (bf16[64,3072]{1,0:T(8,128)(2,1)S(1)}, bf16[64,3072]{1,0:T(8,128)(2,1)}, u32[]{:S(2)}) copy-start(bf16[64,3072]{1,0:T(8,128)(2,1)} %get-tuple-element.55) | copy-start | bytes 1179652
  112.3 28.6 %collective-permute-start.21 = (bf16[64,3072]{1,0:T(8,128)(2,1)}, bf16[64,3072]{1,0:T(8,128)(2,1)S(1)}, u32[]{:S(2)}, u32[]{:S(2)}) collective-permute-start(bf16[64,3072]{1,0:T(8,128)(2,1)} %get-tuple-element.57), channel_id=1, source_target_pairs={{0,4},{1,5},{2,6},{3,7},{4,8},{5,9},{6,10},{7,11},{8,12},{9,13},{1... | collective-permute-start | bytes 1179656 | tf_op jit(solution)/shard_map/ppermute | solution.py:329
  128.2 6.8 %collective-permute-start.19 = (bf16[32,3072]{1,0:T(8,128)(2,1)S(1)}, bf16[32,3072]{1,0:T(8,128)(2,1)S(1)}, u32[]{:S(2)}, u32[]{:S(2)}) collective-permute-start(bf16[32,3072]{1,0:T(8,128)(2,1)S(1)} %get-tuple-element.66), channel_id=1, source_target_pairs={{0,1},{1,0},{2,3},{3,2},{4,5},{5,4},{6,7},{7,6},{8,9},{9,8},{10,11... | collective-permute-start | bytes 589832 | tf_op jit(solution)/shard_map/ppermute | solution.py:329
  129.4 21.7 %collective-permute-start.22 = (bf16[64,3072]{1,0:T(8,128)(2,1)S(1)}, bf16[64,3072]{1,0:T(8,128)(2,1)S(1)}, u32[]{:S(2)}, u32[]{:S(2)}) collective-permute-start(bf16[64,3072]{1,0:T(8,128)(2,1)S(1)} %copy-done.5), channel_id=1, source_target_pairs={{0,12},{1,13},{2,14},{3,15},{4,0},{5,1},{6,2},{7,3},{8,4},{9,5},{1... | collective-permute-start | bytes 1179656 | tf_op jit(solution)/shard_map/ppermute | solution.py:329
  134.4 16.7 %collective-permute-start.23 = (bf16[64,3072]{1,0:T(8,128)(2,1)S(1)}, bf16[64,3072]{1,0:T(8,128)(2,1)S(1)}, u32[]{:S(2)}, u32[]{:S(2)}) collective-permute-start(bf16[64,3072]{1,0:T(8,128)(2,1)S(1)} %copy-done.4), channel_id=1, source_target_pairs={{0,2},{1,3},{2,0},{3,1},{4,6},{5,7},{6,4},{7,5},{8,10},{9,11},{10,... | collective-permute-start | bytes 1179656 | tf_op jit(solution)/shard_map/ppermute | solution.py:329
  134.9 18.1 %collective-permute-start.24 = (bf16[64,3072]{1,0:T(8,128)(2,1)S(1)}, bf16[64,3072]{1,0:T(8,128)(2,1)S(1)}, u32[]{:S(2)}, u32[]{:S(2)}) collective-permute-start(bf16[64,3072]{1,0:T(8,128)(2,1)S(1)} %copy-done.3), channel_id=1, source_target_pairs={{0,8},{1,9},{2,10},{3,11},{4,12},{5,13},{6,14},{7,15},{8,0},{9,1},... | collective-permute-start | bytes 1179656 | tf_op jit(solution)/shard_map/ppermute | solution.py:329
  136.8 26.3 %collective-permute-start.25 = (bf16[64,3072]{1,0:T(8,128)(2,1)S(1)}, bf16[64,3072]{1,0:T(8,128)(2,1)S(1)}, u32[]{:S(2)}, u32[]{:S(2)}) collective-permute-start(bf16[64,3072]{1,0:T(8,128)(2,1)S(1)} %copy-done.2), channel_id=1, source_target_pairs={{0,6},{1,7},{2,4},{3,5},{4,10},{5,11},{6,8},{7,9},{8,14},{9,15},{1... | collective-permute-start | bytes 1179656 | tf_op jit(solution)/shard_map/ppermute | solution.py:329
  140.9 22.7 %collective-permute-start.26 = (bf16[64,3072]{1,0:T(8,128)(2,1)S(1)}, bf16[64,3072]{1,0:T(8,128)(2,1)S(1)}, u32[]{:S(2)}, u32[]{:S(2)}) collective-permute-start(bf16[64,3072]{1,0:T(8,128)(2,1)S(1)} %copy-done.1), channel_id=1, source_target_pairs={{0,14},{1,15},{2,12},{3,13},{4,2},{5,3},{6,0},{7,1},{8,6},{9,7},{1... | collective-permute-start | bytes 1179656 | tf_op jit(solution)/shard_map/ppermute | solution.py:329
  164.2 11.4 %collective-permute-start.28 = (bf16[32,3072]{1,0:T(8,128)(2,1)S(1)}, bf16[32,3072]{1,0:T(8,128)(2,1)S(1)}, u32[]{:S(2)}, u32[]{:S(2)}) collective-permute-start(bf16[32,3072]{1,0:T(8,128)(2,1)S(1)} %get-tuple-element.68), channel_id=1, source_target_pairs={{0,113},{1,112},{2,115},{3,114},{4,117},{5,116},{6,119},{7,118},{8... | collective-permute-start | bytes 589832 | tf_op jit(solution)/shard_map/ppermute | solution.py:329
  170.4 10.5 %collective-permute-start.27 = (bf16[32,3072]{1,0:T(8,128)(2,1)S(1)}, bf16[32,3072]{1,0:T(8,128)(2,1)S(1)}, u32[]{:S(2)}, u32[]{:S(2)}) collective-permute-start(bf16[32,3072]{1,0:T(8,128)(2,1)S(1)} %get-tuple-element.67), channel_id=1, source_target_pairs={{0,112},{1,113},{2,114},{3,115},{4,116},{5,117},{6,118},{7,119},{8... | collective-permute-start | bytes 589832 | tf_op jit(solution)/shard_map/ppermute | solution.py:329

commit v5 on v3

--- a/solution.py
+++ b/solution.py
@@ -129,7 +129,9 @@
     ops = n_seq // 2
     inputs = 1 if foreign else 3
     mine, other = refs[inputs : inputs + ops], refs[inputs + ops : inputs + 2 * ops]
-    o_ref, peer_ref, q_buf, kv_buf, qt_ref, acc_ref, m_ref, mx_ref, count, sems = refs[inputs + 2 * ops :]
+    o_ref, first_ref, second_ref, q_buf, kv_buf, qt_ref, acc_ref, m_ref, mx_ref, peer_buf, count, sems = refs[
+        inputs + 2 * ops :
+    ]
     place, core, partner = info[0], info[2], info[5]
     rows = own_ref.shape[0] // 2
     cols = qt_ref.shape[1]
@@ -236,7 +238,9 @@
             here = pl.multiple_of(jnp.where(core == 0, by_y, by_z), sub)
             there = pl.multiple_of(jnp.where(core == 0, by_z, by_y), sub)
             o_ref[pl.ds(here, sub), h * DH : (h + 1) * DH] = piece
-            peer_ref[pl.ds(there, sub), h * DH : (h + 1) * DH] = piece
+            peer_buf[pl.ds(there, sub), h * DH : (h + 1) * DH] = piece
+    first_ref[...] = peer_buf[: qb // 2, :]
+    second_ref[...] = peer_buf[qb // 2 :, :]
 
 
 def attend(info, kv, state, q_shape, mine, other, n_y, n_seq):
@@ -246,13 +250,14 @@
     cols = qb * width // DH
     any_space = pl.BlockSpec(memory_space=pltpu.HBM)
     out = pl.BlockSpec((qb, width), lambda i, info: (0, 0))
+    part = pl.BlockSpec((qb // 2, width), lambda i, info: (0, 0))
     return pl.pallas_call(
         functools.partial(attend_kernel, foreign, groups, n_y, n_seq),
         grid_spec=pltpu.PrefetchScalarGridSpec(
             num_scalar_prefetch=1,
             grid=(1,),
             in_specs=[any_space] * (1 + len(state) + 2 * len(mine)),
-            out_specs=[out, out],
+            out_specs=[out, part, part],
             scratch_shapes=[
                 pltpu.VMEM(q_shape, BF),
                 pltpu.VMEM((len(SLOTS) + 1, *kv.shape), BF),
@@ -260,11 +265,12 @@
                 pltpu.VMEM((2, DH + 16, cols), F32),
                 pltpu.VMEM((8, cols), F32),
                 pltpu.VMEM((8, cols), F32),
+                pltpu.VMEM((qb, width), BF),
                 pltpu.SMEM((1,), jnp.int32),
                 pltpu.SemaphoreType.DMA((len(SLOTS) + 4,)),
             ],
         ),
-        out_shape=[jax.ShapeDtypeStruct((qb, width), BF)] * 2,
+        out_shape=[jax.ShapeDtypeStruct((rows, width), BF) for rows in (qb, qb // 2, qb // 2)],
         name="attend_foreign" if foreign else "attend_own",
         cost_estimate=pl.CostEstimate(
             flops=2 * cols * kv.shape[0] * 4 * DH, bytes_accessed=4 << 20, transcendentals=0
@@ -273,36 +279,49 @@
     )(info, kv, *state, *mine, *other)
 
 
-def project(info, mine, other, w, w_other, parts, tile):
+def project(info, mine, other, w, w_other, parts, tile, sums=()):
     rows, width = mine.shape
     n = w.shape[1] // 2
     steps = n // tile
 
-    def body(info, a, b, wa, wb, *outs):
+    def body(info, a, b0, b1, wa, wb, *refs):
+        outs = refs[len(sums) :]
+        b = jnp.concatenate([b0[...], b1[...]], axis=0)
         s = jnp.dot(a[...], wa[...], preferred_element_type=F32) + jnp.dot(
-            b[...], wb[...], preferred_element_type=F32
+            b, wb[...], preferred_element_type=F32
         )
-        part = s.shape[0] // len(outs)
-        for i, o in enumerate(outs):
+        part = s.shape[0] // parts
+        for i, o in enumerate(outs[:parts]):
             o[...] = s[i * part : (i + 1) * part].astype(BF)
+        if sums:
+            p0, p2, g0, g1, g2 = [ref[...].astype(F32) for ref in refs[: len(sums)]]
+            first = p0 + g0 + jnp.where(info[2] == 0, g1 + g2, 0.0)
+            second = p2 + g1
+            half = part // 2
+            for o, x in zip(outs[parts:], (first[:half], first[half:], second[:half], second[half:]), strict=True):
+                o[...] = x.astype(BF)
 
     whole = pl.BlockSpec((rows, width), lambda i, info: (0, 0))
+    part = pl.BlockSpec((rows // 2, width), lambda i, info: (0, 0))
     weights = pl.BlockSpec((width, tile), lambda i, info: (0, info[2] * steps + i))
+
+    def strip(r):
+        return pl.BlockSpec((r, tile), lambda i, info: (0, i))
+
+    sizes = [rows // parts] * parts + [rows // parts // 2] * (4 if sums else 0)
     return pl.pallas_call(
         body,
         grid_spec=pltpu.PrefetchScalarGridSpec(
             num_scalar_prefetch=1,
             grid=(steps,),
-            in_specs=[whole, whole, weights, weights],
-            out_specs=[pl.BlockSpec((rows // parts, tile), lambda i, info: (0, i))] * parts,
+            in_specs=[whole, part, part, weights, weights] + [strip(x.shape[0]) for x in sums],
+            out_specs=[strip(r) for r in sizes],
         ),
-        out_shape=[jax.ShapeDtypeStruct((rows // parts, n), BF)] * parts,
-        name="project",
-        cost_estimate=pl.CostEstimate(
-            flops=4 * rows * width * n, bytes_accessed=4 * width * n + 4 * rows * n, transcendentals=0
-        ),
+        out_shape=[jax.ShapeDtypeStruct((r, n), BF) for r in sizes],
+        name="project_and_sum" if sums else "project",
+        cost_estimate=pl.CostEstimate(flops=0, bytes_accessed=0, transcendentals=0),
         compiler_params=PARAMS,
-    )(info, mine, other, w, w_other)
+    )(info, mine, *other, w, w_other, *sums)
 
 
 def add(*terms):
@@ -376,27 +395,26 @@
             over_all(total[2], lambda s, y, z, c: (s, y + 2, z, c) if c else None),
         ]
 
-    half = (n_head, sub, width)
-    near, near_peer = attend(info, kv, state, half, mine, other, n_y, n_seq)
-    near_far = swap_core(near_peer)
-    parts_n = project(after(info, q_far), near, near_far, w_out, w_other, n_y, cols // 4)
-    got_n = stage_one(parts_n)
-    far, far_peer = attend(after(info, parts_n[0]), kv, [q_far], half, mine, other, n_y, n_seq)
-    far_far = swap_core(far_peer)
-    total_n = sum_one([after(p, far) for p in parts_n], got_n)
-    got2_n = stage_two(total_n)
-    parts_f = project(after(info, *total_n), far, far_far, w_out, w_other, n_y, cols // 4)
-    done_n = add(total_n[0], *got2_n).reshape(2, sub, cols // 2)
-
     def by_core(x, same):
         return jnp.where((core == 0) == same, x[0], x[1])
 
-    parts_f = [after(p, done_n) for p in parts_f]
+    half = (n_head, sub, width)
+    near, *near_peer = attend(info, kv, state, half, mine, other, n_y, n_seq)
+    near_far = [swap_core(x) for x in near_peer]
+    parts_n = project(info, near, near_far, w_out, w_other, n_y, cols // 4)
+    got_n = stage_one(parts_n)
+    far, *far_peer = attend(after(info, parts_n[0]), kv, [q_far], half, mine, other, n_y, n_seq)
+    far_far = [swap_core(x) for x in far_peer]
+    *parts_f, a0, a1, b0, b1 = project(
+        info, far, far_far, w_out, w_other, n_y, cols // 4, (parts_n[0], parts_n[2], *got_n)
+    )
     got_f = stage_one(parts_f)
-    own_other = swap_core(by_core(done_n, False))
-    total_f = sum_one([after(p, own_other) for p in parts_f], got_f)
+    total_f = sum_one(parts_f, got_f)
+    got2_n = stage_two((a0, a1, after(b0, total_f[0]), b1))
     got2_f = stage_two(total_f)
     done_f = add(total_f[0], *got2_f).reshape(2, sub, cols // 2)
+    done_n = add(after(a0, total_f[0]), *got2_n).reshape(2, sub, cols // 2)
+    own_other = swap_core(by_core(done_n, False))
     home = over_all(by_core(done_f, True), lambda s, y, z, c: (n_seq - 1 - s, y, z, c))
     home_other = over_all(by_core(done_f, False), lambda s, y, z, c: (n_seq - 1 - s, y, z, 1 - c))
     here = jnp.concatenate([by_core(done_n, True), home], axis=0)

time: 173 us -> 164 us (0.948)
  the two profiles are of different devices: /device:TPU:1 before, /device:TPU:8 now
where the time goes in v5:
time: 164 us; the launch traced here: 162 us
  starting transfers between devices  60.3 us (37%)
  Pallas kernels  51.8 us (32%)
  waiting for transfers between devices  43.6 us (27%)
  other arithmetic  3.64 us (2%)
  local copies, waits for them, and re-layouts  2.64 us (2%)
    ppermute x29, starting transfers between devices, over_all(): return lax.ppermute(x, ('seq', 'head'), pairs)  60.3 us
    ppermute x29, waiting for transfers between devices, over_all(): return lax.ppermute(x, ('seq', 'head'), pairs)  43.6 us
    pallas_call x2, Pallas kernels, attend(): pl.pallas_call(functools.partial(attend_kernel, foreign, groups, n_y, n_s...  25.7 us
    pallas_call x2, Pallas kernels, project(): pl.pallas_call(body, grid_spec=pltpu.PrefetchScalarGridSpec(num_scalar_pr...  17.2 us
    pallas_call x1, Pallas kernels, own(): pl.pallas_call(functools.partial(own_kernel, groups), grid=(1,), in_specs...  6.32 us
  transfers between devices with their start and end apart: 29, of which 11 were waited for; matrix products, arithmetic and copies ran while one was open for 3% of the time, Pallas kernels for 26%

profile of v5, /device:TPU:8, one launch (start us, length us, event | category | flops | bytes accessed | tf_op | source)
XLA Modules:
  0.0 162.3 jit_solution(1912687561481470632)
XLA Ops:
  0.0 0.6 stack.27.info
  0.6 2.6 %prep.1.kv_ref.own_ref = bf16[2048,128]{1,0:T(8,128)(2,1)} custom-call(s32[13]{0:T(128)} %stack.27.info, bf16[1024,1024]{1,0:T(8,128)(2,1)} %k_ref.1, bf16[1024,1024]{1,0:T(8,128)(2,1)} %v_ref.1), custom_call_target="tpu_custom_call" | custom-call | tf_op jit(solution)/shard_map/prep/pallas_call | solution.py:37
  3.2 8.0 %collective-permute-start = (bf16[2048,128]{1,0:T(8,128)(2,1)}, bf16[2048,128]{1,0:T(8,128)(2,1)}, u32[]{:S(2)}, u32[]{:S(2)}) collective-permute-start(bf16[2048,128]{1,0:T(8,128)(2,1)} %prep.1.kv_ref.own_ref), channel_id=1, source_target_pairs={{0,112},{1,49},{2,114},{3,51},{4,116},{5,53},{6,118},{7,55},{8,120... | collective-permute-start | bytes 1572872 | tf_op jit(solution)/shard_map/ppermute | solution.py:353
  11.2 2.4 %collective-permute-start.1 = (bf16[2048,128]{1,0:T(8,128)(2,1)}, bf16[2048,128]{1,0:T(8,128)(2,1)}, u32[]{:S(2)}, u32[]{:S(2)}) collective-permute-start(bf16[2048,128]{1,0:T(8,128)(2,1)} %prep.1.kv_ref.own_ref), channel_id=1, source_target_pairs={{0,96},{1,33},{2,98},{3,35},{4,100},{5,37},{6,102},{7,39},{8,104},... | collective-permute-start | bytes 1572872 | tf_op jit(solution)/shard_map/ppermute | solution.py:353
  13.6 1.9 %collective-permute-start.2 = (bf16[2048,128]{1,0:T(8,128)(2,1)}, bf16[2048,128]{1,0:T(8,128)(2,1)}, u32[]{:S(2)}, u32[]{:S(2)}) collective-permute-start(bf16[2048,128]{1,0:T(8,128)(2,1)} %prep.1.kv_ref.own_ref), channel_id=1, source_target_pairs={{0,80},{1,17},{2,82},{3,19},{4,84},{5,21},{6,86},{7,23},{8,88},{9,... | collective-permute-start | bytes 1572872 | tf_op jit(solution)/shard_map/ppermute | solution.py:353
  15.5 5.8 %collective-permute-start.3 = (bf16[2048,128]{1,0:T(8,128)(2,1)}, bf16[2048,128]{1,0:T(8,128)(2,1)}, u32[]{:S(2)}, u32[]{:S(2)}) collective-permute-start(bf16[2048,128]{1,0:T(8,128)(2,1)} %prep.1.kv_ref.own_ref), channel_id=1, source_target_pairs={{0,64},{2,66},{4,68},{6,70},{8,72},{10,74},{12,76},{14,78},{16,80}... | collective-permute-start | bytes 1572872 | tf_op jit(solution)/shard_map/ppermute | solution.py:353
  21.3 6.3 %own.1 = (bf16[256,2048]{1,0:T(8,128)(2,1)}, f32[144,2048]{1,0:T(8,128)}, f32[8,2048]{1,0:T(8,128)}) custom-call(bf16[16,2,32,512]{3,2,1,0:T(8,128)(2,1)} %bitcast.11, bf16[2048,128]{1,0:T(8,128)(2,1)} %prep.1.kv_ref.own_ref), custom_call_target="tpu_custom_call" | custom-call | flops 2147483648 | bytes 8388608 | tf_op jit(solution)/shard_map/own/pallas_call | solution.py:103
  27.6 11.4 %collective-permute-done.1.refs_4_.refs_2_ = bf16[2048,128]{1,0:T(8,128)(2,1)} collective-permute-done((bf16[2048,128]{1,0:T(8,128)(2,1)}, bf16[2048,128]{1,0:T(8,128)(2,1)}, u32[]{:S(2)}, u32[]{:S(2)}) %collective-permute-start.1) | collective-permute-done | bytes 524320 | tf_op jit(solution)/shard_map/ppermute | solution.py:353
  39.1 0.5 collective-permute-start.6
  39.6 0.2 collective-permute-done.3.refs_6_.refs_4_
  39.8 1.9 %slice_bitcast_fusion = bf16[16,32,512]{2,1,0:T(8,128)(2,1)} fusion(bf16[16,2,32,512]{3,2,1,0:T(8,128)(2,1)} %bitcast.12), kind=kLoop, calls=%fused_computation.9 | loop fusion | bytes 1048576 | tf_op jit(solution)/shard_map/squeeze | solution.py:374
  41.7 1.5 collective-permute-start.11
  43.2 3.8 %attend_own.1 = (bf16[512,512]{1,0:T(8,128)(2,1)}, bf16[256,512]{1,0:T(8,128)(2,1)}, bf16[256,512]{1,0:T(8,128)(2,1)}) custom-call(s32[13]{0:T(128)} %stack.27.info, bf16[2048,128]{1,0:T(8,128)(2,1)} %prep.1.kv_ref.own_ref, bf16[256,2048]{1,0:T(8,128)(2,1)} %get-tuple-element.34.refs_0_, f32[144,2048]{1,0:T(8,128)} %get-tuple-element.35.refs_1_, ...), custom_call_target="tpu_custom_call" | custom-call | flops 4294967296 | bytes 4194304 | tf_op jit(solution)/shard_map/attend_own/pallas_call | solution.py:254
  47.0 0.3 collective-permute-start.8
  47.3 0.3 collective-permute-start.9
  47.6 1.4 collective-permute-done.8.b0
  49.0 0.4 collective-permute-done.9.b1
  49.3 7.5 %project.1 = (bf16[128,3072]{1,0:T(8,128)(2,1)}, bf16[128,3072]{1,0:T(8,128)(2,1)}, bf16[128,3072]{1,0:T(8,128)(2,1)}, bf16[128,3072]{1,0:T(8,128)(2,1)}) custom-call(s32[13]{0:T(128)} %stack.27.info, bf16[512,512]{1,0:T(8,128)(2,1)} %get-tuple-element.41.a, bf16[256,512]{1,0:T(8,128)(2,1)} %collective-permute-done.8.b0, ...), custom_call_target="tpu_custom_call" | custom-call | tf_op jit(solution)/shard_map/project/pallas_call | solution.py:312
  56.9 1.6 %collective-permute-start.14 = (bf16[128,3072]{1,0:T(8,128)(2,1)}, bf16[128,3072]{1,0:T(8,128)(2,1)}, u32[]{:S(2)}, u32[]{:S(2)}) collective-permute-start(bf16[128,3072]{1,0:T(8,128)(2,1)} %get-tuple-element.51), channel_id=1, source_target_pairs={{0,4},{1,3},{2,6},{3,1},{4,8},{5,7},{6,10},{7,5},{8,12},{9,11},{10... | collective-permute-start | bytes 2359304 | tf_op jit(solution)/shard_map/ppermute | solution.py:353
  58.5 0.4 collective-permute-start.15
  59.0 4.2 %collective-permute-start.16 = (bf16[128,3072]{1,0:T(8,128)(2,1)}, bf16[128,3072]{1,0:T(8,128)(2,1)}, u32[]{:S(2)}, u32[]{:S(2)}) collective-permute-start(bf16[128,3072]{1,0:T(8,128)(2,1)} %get-tuple-element.50.refs_1_), channel_id=1, source_target_pairs={{0,8},{2,10},{4,12},{6,14},{8,0},{10,2},{12,4},{14,6},{16,24},{18,... | collective-permute-start | bytes 2359304 | tf_op jit(solution)/shard_map/ppermute | solution.py:353
  63.2 21.9 %attend_foreign.1 = (bf16[512,512]{1,0:T(8,128)(2,1)}, bf16[256,512]{1,0:T(8,128)(2,1)}, bf16[256,512]{1,0:T(8,128)(2,1)}) custom-call(s32[13]{0:T(128)} %stack.27.info, bf16[2048,128]{1,0:T(8,128)(2,1)} %prep.1.kv_ref.own_ref, bf16[16,32,512]{2,1,0:T(8,128)(2,1)} %collective-permute-done.11.refs_0_, bf16[2048,128]{1,0:T(8,128)(2,1)} %collective-permute-done.refs_3_.refs_1_, ...), custom_call_target="tpu_custom_call" | custom-call | flops 4294967296 | bytes 4194304 | tf_op jit(solution)/shard_map/attend_foreign/pallas_call | solution.py:254
  85.1 0.1 collective-permute-start.12
  85.2 0.5 collective-permute-start.13
  85.7 1.4 collective-permute-done.12.b0
  87.0 0.4 collective-permute-done.13.b1
  87.4 9.6 %project_and_sum.1 = (bf16[128,3072]{1,0:T(8,128)(2,1)}, bf16[128,3072]{1,0:T(8,128)(2,1)}, bf16[128,3072]{1,0:T(8,128)(2,1)}, bf16[128,3072]{1,0:T(8,128)(2,1)}...) custom-call(s32[13]{0:T(128)} %stack.27.info, ...), custom_call_target="tpu_custom_call" | custom-call | tf_op jit(solution)/shard_map/project_and_sum/pallas_call | solution.py:312
  97.1 0.9 collective-permute-start.17
  98.0 1.2 collective-permute-start.18
  99.2 3.3 %collective-permute-start.19 = (bf16[128,3072]{1,0:T(8,128)(2,1)}, bf16[128,3072]{1,0:T(8,128)(2,1)S(1)}, u32[]{:S(2)}, u32[]{:S(2)}) collective-permute-start(bf16[128,3072]{1,0:T(8,128)(2,1)} %get-tuple-element.57), channel_id=1, source_target_pairs={{0,8},{2,10},{4,12},{6,14},{8,0},{10,2},{12,4},{14,6},{16,24},{18,... | collective-permute-start | bytes 2359304 | tf_op jit(solution)/shard_map/ppermute | solution.py:353
  102.5 1.0 collective-permute-start.20
  103.5 0.7 collective-permute-start.21
  104.1 9.4 %collective-permute-done.17 = bf16[128,3072]{1,0:T(8,128)(2,1)S(1)} collective-permute-done((bf16[128,3072]{1,0:T(8,128)(2,1)}, bf16[128,3072]{1,0:T(8,128)(2,1)S(1)}, u32[]{:S(2)}, u32[]{:S(2)}) %collective-permute-start.17) | collective-permute-done | bytes 786464 | tf_op jit(solution)/shard_map/ppermute | solution.py:353
  113.5 0.8 collective-permute-done.18
  114.4 9.0 %collective-permute-done.19 = bf16[128,3072]{1,0:T(8,128)(2,1)S(1)} collective-permute-done((bf16[128,3072]{1,0:T(8,128)(2,1)}, bf16[128,3072]{1,0:T(8,128)(2,1)S(1)}, u32[]{:S(2)}, u32[]{:S(2)}) %collective-permute-start.19) | collective-permute-done | bytes 786464 | tf_op jit(solution)/shard_map/ppermute | solution.py:353
  123.4 2.1 %fusion.3 = (bf16[128,3072]{1,0:T(8,128)(2,1)S(1)}, bf16[128,3072]{1,0:T(8,128)(2,1)S(1)}) fusion(bf16[128,3072]{1,0:T(8,128)(2,1)S(1)} %collective-permute-done.18, bf16[128,3072]{1,0:T(8,128)(2,1)} %get-tuple-element.57, bf16[128,3072]{1,0:T(8,128)(2,1)S(1)} %collective-permute-done.19, pred[]{:T(512)S(6)} %eq.7, ...), kind=kLoop, calls=%fused_computation.5 | loop fusion | flops 4718592 | bytes 5505025 | tf_op jit(solution)/shard_map/convert_element_type | solution.py:331
  125.5 1.0 collective-permute-start.23
  126.5 0.7 collective-permute-start.22
  127.3 0.7 collective-permute-start.24
  128.0 0.7 collective-permute-start.25
  128.7 0.2 add_convert_fusion.1
  128.9 5.5 %collective-permute-start.27 = (bf16[32,3072]{1,0:T(8,128)(2,1)S(1)}, bf16[32,3072]{1,0:T(8,128)(2,1)S(1)}, u32[]{:S(2)}, u32[]{:S(2)}) collective-permute-start(bf16[32,3072]{1,0:T(8,128)(2,1)S(1)} %get-tuple-element.72), channel_id=1, source_target_pairs={{0,1},{1,0},{2,3},{3,2},{4,5},{5,4},{6,7},{7,6},{8,9},{9,8},{10,11... | collective-permute-start | bytes 589832 | tf_op jit(solution)/shard_map/ppermute | solution.py:353
  134.5 0.2 add_convert_fusion
  134.7 17.2 %collective-permute-start.28 = (bf16[32,3072]{1,0:T(8,128)(2,1)S(1)}, bf16[32,3072]{1,0:T(8,128)(2,1)S(1)}, u32[]{:S(2)}, u32[]{:S(2)}) collective-permute-start(bf16[32,3072]{1,0:T(8,128)(2,1)S(1)} %get-tuple-element.74), channel_id=1, source_target_pairs={{0,113},{1,112},{2,115},{3,114},{4,117},{5,116},{6,119},{7,118},{8... | collective-permute-start | bytes 589832 | tf_op jit(solution)/shard_map/ppermute | solution.py:353
  151.9 4.8 %collective-permute-done.28 = bf16[32,3072]{1,0:T(8,128)(2,1)S(1)} collective-permute-done((bf16[32,3072]{1,0:T(8,128)(2,1)S(1)}, bf16[32,3072]{1,0:T(8,128)(2,1)S(1)}, u32[]{:S(2)}, u32[]{:S(2)}) %collective-permute-start.28) | collective-permute-done | bytes 196640 | tf_op jit(solution)/shard_map/ppermute | solution.py:353
  156.7 4.5 %collective-permute-done.26 = bf16[32,3072]{1,0:T(8,128)(2,1)S(1)} collective-permute-done((bf16[32,3072]{1,0:T(8,128)(2,1)S(1)}, bf16[32,3072]{1,0:T(8,128)(2,1)S(1)}, u32[]{:S(2)}, u32[]{:S(2)}) %collective-permute-start.26) | collective-permute-done | bytes 196640 | tf_op jit(solution)/shard_map/ppermute | solution.py:353
  161.2 0.1 broadcast_select_fusion.1
  161.3 0.9 pad_maximum_fusion
  (33 shorter events, 0.2 us)
Async XLA Ops:
  0.0 49.3 %collective-permute-start.10 = (bf16[512,6144]{1,0:T(8,128)(2,1)}, bf16[512,6144]{1,0:T(8,128)(2,1)}, u32[]{:S(2)}, u32[]{:S(2)}) collective-permute-start(bf16[512,6144]{1,0:T(8,128)(2,1)} %wa.3), channel_id=1, source_target_pairs={{0,1},{1,0},{2,3},{3,2},{4,5},{5,4},{6,7},{7,6},{8,9},{9,8},{10,11... | collective-permute-start | bytes 18874376 | tf_op jit(solution)/shard_map/ppermute | solution.py:353
  3.2 24.4 %collective-permute-start = (bf16[2048,128]{1,0:T(8,128)(2,1)}, bf16[2048,128]{1,0:T(8,128)(2,1)}, u32[]{:S(2)}, u32[]{:S(2)}) collective-permute-start(bf16[2048,128]{1,0:T(8,128)(2,1)} %prep.1.kv_ref.own_ref), channel_id=1, source_target_pairs={{0,112},{1,49},{2,114},{3,51},{4,116},{5,53},{6,118},{7,55},{8,120... | collective-permute-start | bytes 1572872 | tf_op jit(solution)/shard_map/ppermute | solution.py:353
  11.2 27.8 %collective-permute-start.1 = (bf16[2048,128]{1,0:T(8,128)(2,1)}, bf16[2048,128]{1,0:T(8,128)(2,1)}, u32[]{:S(2)}, u32[]{:S(2)}) collective-permute-start(bf16[2048,128]{1,0:T(8,128)(2,1)} %prep.1.kv_ref.own_ref), channel_id=1, source_target_pairs={{0,96},{1,33},{2,98},{3,35},{4,100},{5,37},{6,102},{7,39},{8,104},... | collective-permute-start | bytes 1572872 | tf_op jit(solution)/shard_map/ppermute | solution.py:353
  13.6 25.4 %collective-permute-start.2 = (bf16[2048,128]{1,0:T(8,128)(2,1)}, bf16[2048,128]{1,0:T(8,128)(2,1)}, u32[]{:S(2)}, u32[]{:S(2)}) collective-permute-start(bf16[2048,128]{1,0:T(8,128)(2,1)} %prep.1.kv_ref.own_ref), channel_id=1, source_target_pairs={{0,80},{1,17},{2,82},{3,19},{4,84},{5,21},{6,86},{7,23},{8,88},{9,... | collective-permute-start | bytes 1572872 | tf_op jit(solution)/shard_map/ppermute | solution.py:353
  15.5 24.2 %collective-permute-start.3 = (bf16[2048,128]{1,0:T(8,128)(2,1)}, bf16[2048,128]{1,0:T(8,128)(2,1)}, u32[]{:S(2)}, u32[]{:S(2)}) collective-permute-start(bf16[2048,128]{1,0:T(8,128)(2,1)} %prep.1.kv_ref.own_ref), channel_id=1, source_target_pairs={{0,64},{2,66},{4,68},{6,70},{8,72},{10,74},{12,76},{14,78},{16,80}... | collective-permute-start | bytes 1572872 | tf_op jit(solution)/shard_map/ppermute | solution.py:353
  27.6 14.1 %collective-permute-start.4 = (bf16[2048,128]{1,0:T(8,128)(2,1)}, bf16[2048,128]{1,0:T(8,128)(2,1)}, u32[]{:S(2)}, u32[]{:S(2)}) collective-permute-start(bf16[2048,128]{1,0:T(8,128)(2,1)} %collective-permute-done.refs_3_.refs_1_), channel_id=1, source_target_pairs={{0,1},{1,0},{2,3},{3,2},{4,5},{5,4},{6,7},{7,6},{8,9},{9,8},{10,11... | collective-permute-start | bytes 1572872 | tf_op jit(solution)/shard_map/ppermute | solution.py:353
  39.1 4.2 %collective-permute-start.5 = (bf16[2048,128]{1,0:T(8,128)(2,1)}, bf16[2048,128]{1,0:T(8,128)(2,1)}, u32[]{:S(2)}, u32[]{:S(2)}) collective-permute-start(bf16[2048,128]{1,0:T(8,128)(2,1)} %collective-permute-done.1.refs_4_.refs_2_), channel_id=1, source_target_pairs={{0,1},{1,0},{2,3},{3,2},{4,5},{5,4},{6,7},{7,6},{8,9},{9,8},{10,11... | collective-permute-start | bytes 1572872 | tf_op jit(solution)/shard_map/ppermute | solution.py:353
  39.1 4.2 %collective-permute-start.6 = (bf16[2048,128]{1,0:T(8,128)(2,1)}, bf16[2048,128]{1,0:T(8,128)(2,1)}, u32[]{:S(2)}, u32[]{:S(2)}) collective-permute-start(bf16[2048,128]{1,0:T(8,128)(2,1)} %collective-permute-done.2.refs_5_.refs_3_), channel_id=1, source_target_pairs={{0,1},{1,0},{2,3},{3,2},{4,5},{5,4},{6,7},{7,6},{8,9},{9,8},{10,11... | collective-permute-start | bytes 1572872 | tf_op jit(solution)/shard_map/ppermute | solution.py:353
  39.8 3.4 %collective-permute-start.7 = (bf16[2048,128]{1,0:T(8,128)(2,1)}, bf16[2048,128]{1,0:T(8,128)(2,1)}, u32[]{:S(2)}, u32[]{:S(2)}) collective-permute-start(bf16[2048,128]{1,0:T(8,128)(2,1)} %collective-permute-done.3.refs_6_.refs_4_), channel_id=1, source_target_pairs={{0,1},{1,0},{2,3},{3,2},{4,5},{5,4},{6,7},{7,6},{8,9},{9,8},{10,11... | collective-permute-start | bytes 1572872 | tf_op jit(solution)/shard_map/ppermute | solution.py:353
  41.7 21.5 %collective-permute-start.11 = (bf16[16,32,512]{2,1,0:T(8,128)(2,1)}, bf16[16,32,512]{2,1,0:T(8,128)(2,1)}, u32[]{:S(2)}, u32[]{:S(2)}) collective-permute-start(bf16[16,32,512]{2,1,0:T(8,128)(2,1)} %slice_bitcast_fusion), channel_id=1, source_target_pairs={{0,112},{1,113},{2,114},{3,115},{4,116},{5,117},{6,118},{7,119},{8... | collective-permute-start | bytes 1572872 | tf_op jit(solution)/shard_map/ppermute | solution.py:353
  47.0 2.0 %collective-permute-start.8 = (bf16[256,512]{1,0:T(8,128)(2,1)}, bf16[256,512]{1,0:T(8,128)(2,1)}, u32[]{:S(2)}, u32[]{:S(2)}) collective-permute-start(bf16[256,512]{1,0:T(8,128)(2,1)} %get-tuple-element.42), channel_id=1, source_target_pairs={{0,1},{1,0},{2,3},{3,2},{4,5},{5,4},{6,7},{7,6},{8,9},{9,8},{10,11... | collective-permute-start | bytes 786440 | tf_op jit(solution)/shard_map/ppermute | solution.py:353
  47.3 2.0 %collective-permute-start.9 = (bf16[256,512]{1,0:T(8,128)(2,1)}, bf16[256,512]{1,0:T(8,128)(2,1)}, u32[]{:S(2)}, u32[]{:S(2)}) collective-permute-start(bf16[256,512]{1,0:T(8,128)(2,1)} %get-tuple-element.43), channel_id=1, source_target_pairs={{0,1},{1,0},{2,3},{3,2},{4,5},{5,4},{6,7},{7,6},{8,9},{9,8},{10,11... | collective-permute-start | bytes 786440 | tf_op jit(solution)/shard_map/ppermute | solution.py:353
  56.9 30.5 %collective-permute-start.14 = (bf16[128,3072]{1,0:T(8,128)(2,1)}, bf16[128,3072]{1,0:T(8,128)(2,1)}, u32[]{:S(2)}, u32[]{:S(2)}) collective-permute-start(bf16[128,3072]{1,0:T(8,128)(2,1)} %get-tuple-element.51), channel_id=1, source_target_pairs={{0,4},{1,3},{2,6},{3,1},{4,8},{5,7},{6,10},{7,5},{8,12},{9,11},{10... | collective-permute-start | bytes 2359304 | tf_op jit(solution)/shard_map/ppermute | solution.py:353
  58.5 28.9 %collective-permute-start.15 = (bf16[128,3072]{1,0:T(8,128)(2,1)}, bf16[128,3072]{1,0:T(8,128)(2,1)}, u32[]{:S(2)}, u32[]{:S(2)}) collective-permute-start(bf16[128,3072]{1,0:T(8,128)(2,1)} %get-tuple-element.52), channel_id=1, source_target_pairs={{0,12},{1,3},{2,14},{3,1},{4,0},{5,7},{6,2},{7,5},{8,4},{9,11},{10... | collective-permute-start | bytes 2359304 | tf_op jit(solution)/shard_map/ppermute | solution.py:353
  59.0 28.5 %collective-permute-start.16 = (bf16[128,3072]{1,0:T(8,128)(2,1)}, bf16[128,3072]{1,0:T(8,128)(2,1)}, u32[]{:S(2)}, u32[]{:S(2)}) collective-permute-start(bf16[128,3072]{1,0:T(8,128)(2,1)} %get-tuple-element.50.refs_1_), channel_id=1, source_target_pairs={{0,8},{2,10},{4,12},{6,14},{8,0},{10,2},{12,4},{14,6},{16,24},{18,... | collective-permute-start | bytes 2359304 | tf_op jit(solution)/shard_map/ppermute | solution.py:353
  85.1 2.0 %collective-permute-start.12 = (bf16[256,512]{1,0:T(8,128)(2,1)}, bf16[256,512]{1,0:T(8,128)(2,1)}, u32[]{:S(2)}, u32[]{:S(2)}) collective-permute-start(bf16[256,512]{1,0:T(8,128)(2,1)} %get-tuple-element.48), channel_id=1, source_target_pairs={{0,1},{1,0},{2,3},{3,2},{4,5},{5,4},{6,7},{7,6},{8,9},{9,8},{10,11... | collective-permute-start | bytes 786440 | tf_op jit(solution)/shard_map/ppermute | solution.py:353
  85.2 2.2 %collective-permute-start.13 = (bf16[256,512]{1,0:T(8,128)(2,1)}, bf16[256,512]{1,0:T(8,128)(2,1)}, u32[]{:S(2)}, u32[]{:S(2)}) collective-permute-start(bf16[256,512]{1,0:T(8,128)(2,1)} %get-tuple-element.49), channel_id=1, source_target_pairs={{0,1},{1,0},{2,3},{3,2},{4,5},{5,4},{6,7},{7,6},{8,9},{9,8},{10,11... | collective-permute-start | bytes 786440 | tf_op jit(solution)/shard_map/ppermute | solution.py:353
  97.1 16.5 %collective-permute-start.17 = (bf16[128,3072]{1,0:T(8,128)(2,1)}, bf16[128,3072]{1,0:T(8,128)(2,1)S(1)}, u32[]{:S(2)}, u32[]{:S(2)}) collective-permute-start(bf16[128,3072]{1,0:T(8,128)(2,1)} %get-tuple-element.55), channel_id=1, source_target_pairs={{0,4},{1,3},{2,6},{3,1},{4,8},{5,7},{6,10},{7,5},{8,12},{9,11},{10... | collective-permute-start | bytes 2359304 | tf_op jit(solution)/shard_map/ppermute | solution.py:353
  98.0 16.4 %collective-permute-start.18 = (bf16[128,3072]{1,0:T(8,128)(2,1)}, bf16[128,3072]{1,0:T(8,128)(2,1)S(1)}, u32[]{:S(2)}, u32[]{:S(2)}) collective-permute-start(bf16[128,3072]{1,0:T(8,128)(2,1)} %get-tuple-element.56), channel_id=1, source_target_pairs={{0,12},{1,3},{2,14},{3,1},{4,0},{5,7},{6,2},{7,5},{8,4},{9,11},{10... | collective-permute-start | bytes 2359304 | tf_op jit(solution)/shard_map/ppermute | solution.py:353
  99.2 24.2 %collective-permute-start.19 = (bf16[128,3072]{1,0:T(8,128)(2,1)}, bf16[128,3072]{1,0:T(8,128)(2,1)S(1)}, u32[]{:S(2)}, u32[]{:S(2)}) collective-permute-start(bf16[128,3072]{1,0:T(8,128)(2,1)} %get-tuple-element.57), channel_id=1, source_target_pairs={{0,8},{2,10},{4,12},{6,14},{8,0},{10,2},{12,4},{14,6},{16,24},{18,... | collective-permute-start | bytes 2359304 | tf_op jit(solution)/shard_map/ppermute | solution.py:353
  102.5 25.5 %collective-permute-start.20 = (bf16[64,3072]{1,0:T(8,128)(2,1)}, bf16[64,3072]{1,0:T(8,128)(2,1)S(1)}, u32[]{:S(2)}, u32[]{:S(2)}) collective-permute-start(bf16[64,3072]{1,0:T(8,128)(2,1)} %get-tuple-element.59), channel_id=1, source_target_pairs={{0,2},{1,5},{2,0},{3,7},{4,6},{5,9},{6,4},{7,11},{8,10},{9,13},{10... | collective-permute-start | bytes 1179656 | tf_op jit(solution)/shard_map/ppermute | solution.py:353
  103.5 25.2 %collective-permute-start.21 = (bf16[64,3072]{1,0:T(8,128)(2,1)}, bf16[64,3072]{1,0:T(8,128)(2,1)S(1)}, u32[]{:S(2)}, u32[]{:S(2)}) collective-permute-start(bf16[64,3072]{1,0:T(8,128)(2,1)} %get-tuple-element.60), channel_id=1, source_target_pairs={{1,13},{3,15},{5,1},{7,3},{9,5},{11,7},{13,9},{15,11},{17,29},{19,... | collective-permute-start | bytes 1179656 | tf_op jit(solution)/shard_map/ppermute | solution.py:353
  123.4 3.1 %copy-start.1 = (bf16[64,3072]{1,0:T(8,128)(2,1)S(1)}, bf16[64,3072]{1,0:T(8,128)(2,1)}, u32[]{:S(2)}) copy-start(bf16[64,3072]{1,0:T(8,128)(2,1)} %get-tuple-element.62) | copy-start | bytes 1179652
  125.5 3.2 %copy-start = (bf16[64,3072]{1,0:T(8,128)(2,1)S(1)}, bf16[64,3072]{1,0:T(8,128)(2,1)}, u32[]{:S(2)}) copy-start(bf16[64,3072]{1,0:T(8,128)(2,1)} %get-tuple-element.58) | copy-start | bytes 1179652
  125.5 9.0 %collective-permute-start.23 = (bf16[64,3072]{1,0:T(8,128)(2,1)S(1)}, bf16[64,3072]{1,0:T(8,128)(2,1)S(1)}, u32[]{:S(2)}, u32[]{:S(2)}) collective-permute-start(bf16[64,3072]{1,0:T(8,128)(2,1)S(1)} %fusion.4), channel_id=1, source_target_pairs={{0,2},{1,5},{2,0},{3,7},{4,6},{5,9},{6,4},{7,11},{8,10},{9,13},{10... | collective-permute-start | bytes 1179656 | tf_op jit(solution)/shard_map/ppermute | solution.py:353
  126.5 2.2 %collective-permute-start.22 = (bf16[64,3072]{1,0:T(8,128)(2,1)S(1)}, bf16[64,3072]{1,0:T(8,128)(2,1)S(1)}, u32[]{:S(2)}, u32[]{:S(2)}) collective-permute-start(bf16[64,3072]{1,0:T(8,128)(2,1)S(1)} %copy-done.1), channel_id=1, source_target_pairs={{1,9},{3,11},{5,13},{7,15},{9,1},{11,3},{13,5},{15,7},{17,25},{19,... | collective-permute-start | bytes 1179656 | tf_op jit(solution)/shard_map/ppermute | solution.py:353
  127.3 7.2 %collective-permute-start.24 = (bf16[64,3072]{1,0:T(8,128)(2,1)S(1)}, bf16[64,3072]{1,0:T(8,128)(2,1)S(1)}, u32[]{:S(2)}, u32[]{:S(2)}) collective-permute-start(bf16[64,3072]{1,0:T(8,128)(2,1)S(1)} %get-tuple-element.67), channel_id=1, source_target_pairs={{1,13},{3,15},{5,1},{7,3},{9,5},{11,7},{13,9},{15,11},{17,29},{19,... | collective-permute-start | bytes 1179656 | tf_op jit(solution)/shard_map/ppermute | solution.py:353
  128.0 6.5 %collective-permute-start.25 = (bf16[64,3072]{1,0:T(8,128)(2,1)S(1)}, bf16[64,3072]{1,0:T(8,128)(2,1)S(1)}, u32[]{:S(2)}, u32[]{:S(2)}) collective-permute-start(bf16[64,3072]{1,0:T(8,128)(2,1)S(1)} %get-tuple-element.68), channel_id=1, source_target_pairs={{1,9},{3,11},{5,13},{7,15},{9,1},{11,3},{13,5},{15,7},{17,25},{19,... | collective-permute-start | bytes 1179656 | tf_op jit(solution)/shard_map/ppermute | solution.py:353
  128.9 23.0 %collective-permute-start.27 = (bf16[32,3072]{1,0:T(8,128)(2,1)S(1)}, bf16[32,3072]{1,0:T(8,128)(2,1)S(1)}, u32[]{:S(2)}, u32[]{:S(2)}) collective-permute-start(bf16[32,3072]{1,0:T(8,128)(2,1)S(1)} %get-tuple-element.72), channel_id=1, source_target_pairs={{0,1},{1,0},{2,3},{3,2},{4,5},{5,4},{6,7},{7,6},{8,9},{9,8},{10,11... | collective-permute-start | bytes 589832 | tf_op jit(solution)/shard_map/ppermute | solution.py:353
  134.7 22.0 %collective-permute-start.28 = (bf16[32,3072]{1,0:T(8,128)(2,1)S(1)}, bf16[32,3072]{1,0:T(8,128)(2,1)S(1)}, u32[]{:S(2)}, u32[]{:S(2)}) collective-permute-start(bf16[32,3072]{1,0:T(8,128)(2,1)S(1)} %get-tuple-element.74), channel_id=1, source_target_pairs={{0,113},{1,112},{2,115},{3,114},{4,117},{5,116},{6,119},{7,118},{8... | collective-permute-start | bytes 589832 | tf_op jit(solution)/shard_map/ppermute | solution.py:353
  151.9 9.3 %collective-permute-start.26 = (bf16[32,3072]{1,0:T(8,128)(2,1)S(1)}, bf16[32,3072]{1,0:T(8,128)(2,1)S(1)}, u32[]{:S(2)}, u32[]{:S(2)}) collective-permute-start(bf16[32,3072]{1,0:T(8,128)(2,1)S(1)} %get-tuple-element.73), channel_id=1, source_target_pairs={{0,112},{1,113},{2,114},{3,115},{4,116},{5,117},{6,118},{7,119},{8... | collective-permute-start | bytes 589832 | tf_op jit(solution)/shard_map/ppermute | solution.py:353

commit v6 on v5

--- a/solution.py
+++ b/solution.py
@@ -24,14 +24,16 @@
     return lax.optimization_barrier((x, *deps))[0]
 
 
-def prep_kernel(info, k_ref, v_ref, kv_ref):
+def prep_kernel(info, k_ref, v_ref, q_ref, kv_ref, away_ref):
+    away_ref[...] = q_ref[:, 0]
     rows = k_ref.shape[0]
     kv_ref[0:rows, :] = k_ref[...]
     for t in range(rows // DH):
         kv_ref[rows + t * DH : rows + (t + 1) * DH, :] = v_ref[t * DH : (t + 1) * DH, :].T
 
 
-def prep(info, keys, values):
+def prep(info, keys, values, q4):
+    groups, _, sub, width = q4.shape
     rows = keys.shape[0]
     col = pl.BlockSpec((rows, DH), lambda i, info: (0, info[1]))
     return pl.pallas_call(
@@ -39,13 +41,19 @@
         grid_spec=pltpu.PrefetchScalarGridSpec(
             num_scalar_prefetch=1,
             grid=(1,),
-            in_specs=[col, col],
-            out_specs=pl.BlockSpec((2 * rows, DH), lambda i, info: (0, 0)),
+            in_specs=[col, col, pl.BlockSpec((groups, 1, sub, width), lambda i, info: (0, 1, 0, 0))],
+            out_specs=[
+                pl.BlockSpec((2 * rows, DH), lambda i, info: (0, 0)),
+                pl.BlockSpec((groups, sub, width), lambda i, info: (0, 0, 0)),
+            ],
         ),
-        out_shape=jax.ShapeDtypeStruct((2 * rows, DH), BF),
+        out_shape=[
+            jax.ShapeDtypeStruct((2 * rows, DH), BF),
+            jax.ShapeDtypeStruct((groups, sub, width), BF),
+        ],
         name="prep",
         compiler_params=PARAMS,
-    )(info, keys, values)
+    )(info, keys, values, q4)
 
 
 def keys_of(kv):
@@ -230,7 +238,7 @@
         o = acc_ref[last, :, h * qb : (h + 1) * qb]
         o = (o[0:DH] * (1.0 / o[DH : DH + 1])).astype(BF).T
         for g in range(groups):
-            ry = (g // 4 + n_y - info[3]) % n_y
+            ry = (g // 4) ^ info[3]
             rz = (g // 2 % 2) ^ info[4]
             by_y = ((ry * 2 + rz) * 2 + g % 2) * sub
             by_z = (((ry // 2 * 2 + rz) * 2 + ry % 2) * 2 + g % 2) * sub
@@ -367,17 +375,17 @@
     sub = rows // n_head // 2
     q4 = queries.reshape(n_head, 2, sub, width)
     w_other = swap_core(w_out)
-    kv = prep(info, keys, values)
+    kv, q_away = prep(info, keys, values, q4)
     mine = [fetch(kv, pair) for pair in FETCH]
     state = own(q4, kv)
     other = [swap_core(after(x, state[2])) for x in mine]
-    q_far = over_all(after(q4[:, 1], state[2], *mine), lambda s, y, z, c: (n_seq - 1 - s, y, z, c))
+    q_far = over_all(after(q_away, state[2], *mine), lambda s, y, z, c: (n_seq - 1 - s, y, z, c))
 
     def stage_one(parts):
         return [
-            over_all(parts[1], lambda s, y, z, c: (s, y, 1 - z, c) if c else (s, y + 1, z, c)),
-            over_all(parts[3], lambda s, y, z, c: (s, y, 1 - z, c) if c else (s, y - 1, z, c)),
-            over_all(parts[2], lambda s, y, z, c: None if c else (s, y + 2, z, c)),
+            over_all(parts[1], lambda s, y, z, c: (s, y, 1 - z, c) if c else (s, y ^ 1, z, c)),
+            over_all(parts[3], lambda s, y, z, c: (s, y, 1 - z, c) if c else (s, y ^ 3, z, c)),
+            over_all(parts[2], lambda s, y, z, c: None if c else (s, y ^ 2, z, c)),
         ]
 
     def sum_one(parts, got):
@@ -390,9 +398,9 @@
 
     def stage_two(total):
         return [
-            over_all(total[1], lambda s, y, z, c: (s, y + 1, z, c) if c else (s, y, 1 - z, c)),
-            over_all(total[3], lambda s, y, z, c: (s, y - 1, z, c) if c else None),
-            over_all(total[2], lambda s, y, z, c: (s, y + 2, z, c) if c else None),
+            over_all(total[1], lambda s, y, z, c: (s, y ^ 1, z, c) if c else (s, y, 1 - z, c)),
+            over_all(total[3], lambda s, y, z, c: (s, y ^ 3, z, c) if c else None),
+            over_all(total[2], lambda s, y, z, c: (s, y ^ 2, z, c) if c else None),
         ]
 
     def by_core(x, same):

time: 164 us -> 165 us (level)
  the two profiles are of different devices: /device:TPU:8 before, /device:TPU:1 now
where the time goes in v6:
time: 165 us; the launch traced here: 162 us
  starting transfers between devices  62.8 us (38%)
  Pallas kernels  51.9 us (31%)
  waiting for transfers between devices  42.4 us (26%)
  other arithmetic  3.64 us (2%)
    ppermute x29, starting transfers between devices, over_all(): return lax.ppermute(x, ('seq', 'head'), pairs)  62.8 us
    ppermute x29, waiting for transfers between devices, over_all(): return lax.ppermute(x, ('seq', 'head'), pairs)  42.4 us
    pallas_call x2, Pallas kernels, attend(): pl.pallas_call(functools.partial(attend_kernel, foreign, groups, n_y, n_s...  25.5 us
    pallas_call x2, Pallas kernels, project(): pl.pallas_call(body, grid_spec=pltpu.PrefetchScalarGridSpec(num_scalar_pr...  17.2 us
    pallas_call x1, Pallas kernels, own(): pl.pallas_call(functools.partial(own_kernel, groups), grid=(1,), in_specs...  6.28 us
  transfers between devices with their start and end apart: 29, of which 13 were waited for; matrix products, arithmetic and copies ran while one was open for 2% of the time, Pallas kernels for 26%

profile of v6, /device:TPU:1, one launch (start us, length us, event | category | flops | bytes accessed | tf_op | source)
XLA Modules:
  0.0 161.7 jit_solution(17316756118052332495)
XLA Ops:
  0.0 1.4 collective-permute-start.10
  1.4 0.7 stack.27.info
  2.1 2.9 %prep.1 = (bf16[2048,128]{1,0:T(8,128)(2,1)}, bf16[16,32,512]{2,1,0:T(8,128)(2,1)}) custom-call(s32[13]{0:T(128)} %stack.27.info, bf16[1024,1024]{1,0:T(8,128)(2,1)} %k_ref.1, bf16[1024,1024]{1,0:T(8,128)(2,1)} %v_ref.1, bf16[16,2,32,512]{3,2,1,0:T(8,128)(2,1)} %bitcast.7), custom_call_target="tpu_custom_call" | custom-call | tf_op jit(solution)/shard_map/prep/pallas_call | solution.py:39
  5.0 6.5 %collective-permute-start = (bf16[2048,128]{1,0:T(8,128)(2,1)}, bf16[2048,128]{1,0:T(8,128)(2,1)}, u32[]{:S(2)}, u32[]{:S(2)}) collective-permute-start(bf16[2048,128]{1,0:T(8,128)(2,1)} %get-tuple-element.36.kv_ref.own_ref), channel_id=1, source_target_pairs={{0,112},{1,49},{2,114},{3,51},{4,116},{5,53},{6,118},{7,55},{8,120... | collective-permute-start | bytes 1572872 | tf_op jit(solution)/shard_map/ppermute | solution.py:361
  11.5 2.2 %collective-permute-start.1 = (bf16[2048,128]{1,0:T(8,128)(2,1)}, bf16[2048,128]{1,0:T(8,128)(2,1)}, u32[]{:S(2)}, u32[]{:S(2)}) collective-permute-start(bf16[2048,128]{1,0:T(8,128)(2,1)} %get-tuple-element.36.kv_ref.own_ref), channel_id=1, source_target_pairs={{0,96},{1,33},{2,98},{3,35},{4,100},{5,37},{6,102},{7,39},{8,104},... | collective-permute-start | bytes 1572872 | tf_op jit(solution)/shard_map/ppermute | solution.py:361
  13.7 1.9 %collective-permute-start.2 = (bf16[2048,128]{1,0:T(8,128)(2,1)}, bf16[2048,128]{1,0:T(8,128)(2,1)}, u32[]{:S(2)}, u32[]{:S(2)}) collective-permute-start(bf16[2048,128]{1,0:T(8,128)(2,1)} %get-tuple-element.36.kv_ref.own_ref), channel_id=1, source_target_pairs={{0,80},{1,17},{2,82},{3,19},{4,84},{5,21},{6,86},{7,23},{8,88},{9,... | collective-permute-start | bytes 1572872 | tf_op jit(solution)/shard_map/ppermute | solution.py:361
  15.7 1.5 collective-permute-start.3
  17.1 6.3 %own.1 = (bf16[256,2048]{1,0:T(8,128)(2,1)}, f32[144,2048]{1,0:T(8,128)}, f32[8,2048]{1,0:T(8,128)}) custom-call(bf16[16,2,32,512]{3,2,1,0:T(8,128)(2,1)} %bitcast.8, bf16[2048,128]{1,0:T(8,128)(2,1)} %get-tuple-element.36.kv_ref.own_ref), custom_call_target="tpu_custom_call" | custom-call | flops 2147483648 | bytes 8388608 | tf_op jit(solution)/shard_map/own/pallas_call | solution.py:111
  23.4 0.7 collective-permute-done.refs_3_.refs_1_
  24.1 5.3 %collective-permute-start.4 = (bf16[2048,128]{1,0:T(8,128)(2,1)}, bf16[2048,128]{1,0:T(8,128)(2,1)}, u32[]{:S(2)}, u32[]{:S(2)}) collective-permute-start(bf16[2048,128]{1,0:T(8,128)(2,1)} %collective-permute-done.refs_3_.refs_1_), channel_id=1, source_target_pairs={{0,1},{1,0},{2,3},{3,2},{4,5},{5,4},{6,7},{7,6},{8,9},{9,8},{10,11... | collective-permute-start | bytes 1572872 | tf_op jit(solution)/shard_map/ppermute | solution.py:361
  29.5 4.9 %collective-permute-done.1.refs_4_.refs_2_ = bf16[2048,128]{1,0:T(8,128)(2,1)} collective-permute-done((bf16[2048,128]{1,0:T(8,128)(2,1)}, bf16[2048,128]{1,0:T(8,128)(2,1)}, u32[]{:S(2)}, u32[]{:S(2)}) %collective-permute-start.1) | collective-permute-done | bytes 524320 | tf_op jit(solution)/shard_map/ppermute | solution.py:361
  34.4 6.5 %collective-permute-start.5 = (bf16[2048,128]{1,0:T(8,128)(2,1)}, bf16[2048,128]{1,0:T(8,128)(2,1)}, u32[]{:S(2)}, u32[]{:S(2)}) collective-permute-start(bf16[2048,128]{1,0:T(8,128)(2,1)} %collective-permute-done.1.refs_4_.refs_2_), channel_id=1, source_target_pairs={{0,1},{1,0},{2,3},{3,2},{4,5},{5,4},{6,7},{7,6},{8,9},{9,8},{10,11... | collective-permute-start | bytes 1572872 | tf_op jit(solution)/shard_map/ppermute | solution.py:361
  40.9 0.7 collective-permute-start.7
  41.7 1.2 collective-permute-start.11
  42.9 0.7 collective-permute-done.6.refs_9_.refs_7_
  43.6 0.7 collective-permute-done.7.refs_10_.refs_8_
  44.3 3.7 %attend_own.1 = (bf16[512,512]{1,0:T(8,128)(2,1)}, bf16[256,512]{1,0:T(8,128)(2,1)}, bf16[256,512]{1,0:T(8,128)(2,1)}) custom-call(s32[13]{0:T(128)} %stack.27.info, bf16[2048,128]{1,0:T(8,128)(2,1)} %get-tuple-element.36.kv_ref.own_ref, bf16[256,2048]{1,0:T(8,128)(2,1)} %get-tuple-element.37.refs_0_, f32[144,2048]{1,0:T(8,128)} %get-tuple-element.38.refs_1_, ...), custom_call_target="tpu_custom_call" | custom-call | flops 4294967296 | bytes 4194304 | tf_op jit(solution)/shard_map/attend_own/pallas_call | solution.py:262
  48.0 0.5 collective-permute-start.8
  48.6 1.4 collective-permute-done.8.b0
  50.0 0.4 collective-permute-done.9.b1
  50.3 7.6 %project.1 = (bf16[128,3072]{1,0:T(8,128)(2,1)}, bf16[128,3072]{1,0:T(8,128)(2,1)}, bf16[128,3072]{1,0:T(8,128)(2,1)}, bf16[128,3072]{1,0:T(8,128)(2,1)}) custom-call(s32[13]{0:T(128)} %stack.27.info, bf16[512,512]{1,0:T(8,128)(2,1)} %get-tuple-element.44.a, bf16[256,512]{1,0:T(8,128)(2,1)} %collective-permute-done.8.b0, ...), custom_call_target="tpu_custom_call" | custom-call | tf_op jit(solution)/shard_map/project/pallas_call | solution.py:320
  57.9 0.8 collective-permute-start.14
  58.7 0.7 collective-permute-start.15
  59.4 1.5 collective-permute-start.16
  61.0 21.8 %attend_foreign.1 = (bf16[512,512]{1,0:T(8,128)(2,1)}, bf16[256,512]{1,0:T(8,128)(2,1)}, bf16[256,512]{1,0:T(8,128)(2,1)}) custom-call(s32[13]{0:T(128)} %stack.27.info, bf16[2048,128]{1,0:T(8,128)(2,1)} %get-tuple-element.36.kv_ref.own_ref, bf16[16,32,512]{2,1,0:T(8,128)(2,1)} %collective-permute-done.11.refs_0_, ...), custom_call_target="tpu_custom_call" | custom-call | flops 4294967296 | bytes 4194304 | tf_op jit(solution)/shard_map/attend_foreign/pallas_call | solution.py:262
  82.8 3.9 %collective-permute-start.12 = (bf16[256,512]{1,0:T(8,128)(2,1)}, bf16[256,512]{1,0:T(8,128)(2,1)}, u32[]{:S(2)}, u32[]{:S(2)}) collective-permute-start(bf16[256,512]{1,0:T(8,128)(2,1)} %get-tuple-element.52), channel_id=1, source_target_pairs={{0,1},{1,0},{2,3},{3,2},{4,5},{5,4},{6,7},{7,6},{8,9},{9,8},{10,11... | collective-permute-start | bytes 786440 | tf_op jit(solution)/shard_map/ppermute | solution.py:361
  86.7 1.4 collective-permute-done.12.b0
  88.1 0.4 collective-permute-done.13.b1
  88.5 9.6 %project_and_sum.1 = (bf16[128,3072]{1,0:T(8,128)(2,1)}, bf16[128,3072]{1,0:T(8,128)(2,1)}, bf16[128,3072]{1,0:T(8,128)(2,1)}, bf16[128,3072]{1,0:T(8,128)(2,1)}...) custom-call(s32[13]{0:T(128)} %stack.27.info, ...), custom_call_target="tpu_custom_call" | custom-call | tf_op jit(solution)/shard_map/project_and_sum/pallas_call | solution.py:320
  98.2 0.8 collective-permute-start.17
  99.0 0.7 collective-permute-start.18
  99.7 0.7 collective-permute-start.19
  100.4 1.0 collective-permute-start.20
  101.4 4.0 %collective-permute-start.21 = (bf16[64,3072]{1,0:T(8,128)(2,1)}, bf16[64,3072]{1,0:T(8,128)(2,1)S(1)}, u32[]{:S(2)}, u32[]{:S(2)}) collective-permute-start(bf16[64,3072]{1,0:T(8,128)(2,1)} %get-tuple-element.64), channel_id=1, source_target_pairs={{1,13},{3,15},{5,9},{7,11},{9,5},{11,7},{13,1},{15,3},{17,29},{19,... | collective-permute-start | bytes 1179656 | tf_op jit(solution)/shard_map/ppermute | solution.py:361
  105.4 5.6 %collective-permute-done.17 = bf16[128,3072]{1,0:T(8,128)(2,1)S(1)} collective-permute-done((bf16[128,3072]{1,0:T(8,128)(2,1)}, bf16[128,3072]{1,0:T(8,128)(2,1)S(1)}, u32[]{:S(2)}, u32[]{:S(2)}) %collective-permute-start.17) | collective-permute-done | bytes 786464 | tf_op jit(solution)/shard_map/ppermute | solution.py:361
  111.0 11.2 %collective-permute-done.18 = bf16[128,3072]{1,0:T(8,128)(2,1)S(1)} collective-permute-done((bf16[128,3072]{1,0:T(8,128)(2,1)}, bf16[128,3072]{1,0:T(8,128)(2,1)S(1)}, u32[]{:S(2)}, u32[]{:S(2)}) %collective-permute-start.18) | collective-permute-done | bytes 786464 | tf_op jit(solution)/shard_map/ppermute | solution.py:361
  122.2 2.1 %fusion.3 = (bf16[128,3072]{1,0:T(8,128)(2,1)S(1)}, bf16[128,3072]{1,0:T(8,128)(2,1)S(1)}) fusion(bf16[128,3072]{1,0:T(8,128)(2,1)S(1)} %collective-permute-done.18, bf16[128,3072]{1,0:T(8,128)(2,1)} %get-tuple-element.61, bf16[128,3072]{1,0:T(8,128)(2,1)S(1)} %collective-permute-done.19, pred[]{:T(512)S(6)} %eq.7, ...), kind=kLoop, calls=%fused_computation.5 | loop fusion | flops 4718592 | bytes 5505025 | tf_op jit(solution)/shard_map/convert_element_type | solution.py:339
  124.4 1.0 collective-permute-start.23
  125.4 4.5 %collective-permute-start.22 = (bf16[64,3072]{1,0:T(8,128)(2,1)S(1)}, bf16[64,3072]{1,0:T(8,128)(2,1)S(1)}, u32[]{:S(2)}, u32[]{:S(2)}) collective-permute-start(bf16[64,3072]{1,0:T(8,128)(2,1)S(1)} %copy-done.1), channel_id=1, source_target_pairs={{1,9},{3,11},{5,13},{7,15},{9,1},{11,3},{13,5},{15,7},{17,25},{19,... | collective-permute-start | bytes 1179656 | tf_op jit(solution)/shard_map/ppermute | solution.py:361
  130.0 2.2 %collective-permute-start.24 = (bf16[64,3072]{1,0:T(8,128)(2,1)S(1)}, bf16[64,3072]{1,0:T(8,128)(2,1)S(1)}, u32[]{:S(2)}, u32[]{:S(2)}) collective-permute-start(bf16[64,3072]{1,0:T(8,128)(2,1)S(1)} %get-tuple-element.71), channel_id=1, source_target_pairs={{1,13},{3,15},{5,9},{7,11},{9,5},{11,7},{13,1},{15,3},{17,29},{19,... | collective-permute-start | bytes 1179656 | tf_op jit(solution)/shard_map/ppermute | solution.py:361
  132.2 3.2 %collective-permute-start.25 = (bf16[64,3072]{1,0:T(8,128)(2,1)S(1)}, bf16[64,3072]{1,0:T(8,128)(2,1)S(1)}, u32[]{:S(2)}, u32[]{:S(2)}) collective-permute-start(bf16[64,3072]{1,0:T(8,128)(2,1)S(1)} %get-tuple-element.72), channel_id=1, source_target_pairs={{1,9},{3,11},{5,13},{7,15},{9,1},{11,3},{13,5},{15,7},{17,25},{19,... | collective-permute-start | bytes 1179656 | tf_op jit(solution)/shard_map/ppermute | solution.py:361
  135.5 2.0 %collective-permute-done.22 = bf16[64,3072]{1,0:T(8,128)(2,1)S(1)} collective-permute-done((bf16[64,3072]{1,0:T(8,128)(2,1)S(1)}, bf16[64,3072]{1,0:T(8,128)(2,1)S(1)}, u32[]{:S(2)}, u32[]{:S(2)}) %collective-permute-start.22) | collective-permute-done | bytes 393248 | tf_op jit(solution)/shard_map/ppermute | solution.py:361
  137.5 0.2 add_convert_fusion.1
  137.8 8.0 %collective-permute-done.24 = bf16[64,3072]{1,0:T(8,128)(2,1)S(1)} collective-permute-done((bf16[64,3072]{1,0:T(8,128)(2,1)S(1)}, bf16[64,3072]{1,0:T(8,128)(2,1)S(1)}, u32[]{:S(2)}, u32[]{:S(2)}) %collective-permute-start.24) | collective-permute-done | bytes 393248 | tf_op jit(solution)/shard_map/ppermute | solution.py:361
  146.0 1.6 collective-permute-start.28
  147.6 8.0 %collective-permute-start.26 = (bf16[32,3072]{1,0:T(8,128)(2,1)S(1)}, bf16[32,3072]{1,0:T(8,128)(2,1)S(1)}, u32[]{:S(2)}, u32[]{:S(2)}) collective-permute-start(bf16[32,3072]{1,0:T(8,128)(2,1)S(1)} %get-tuple-element.77), channel_id=1, source_target_pairs={{0,112},{1,113},{2,114},{3,115},{4,116},{5,117},{6,118},{7,119},{8... | collective-permute-start | bytes 589832 | tf_op jit(solution)/shard_map/ppermute | solution.py:361
  155.6 5.0 %collective-permute-done.26 = bf16[32,3072]{1,0:T(8,128)(2,1)S(1)} collective-permute-done((bf16[32,3072]{1,0:T(8,128)(2,1)S(1)}, bf16[32,3072]{1,0:T(8,128)(2,1)S(1)}, u32[]{:S(2)}, u32[]{:S(2)}) %collective-permute-start.26) | collective-permute-done | bytes 196640 | tf_op jit(solution)/shard_map/ppermute | solution.py:361
  160.8 0.9 pad_maximum_fusion
  (32 shorter events, 0.9 us)
Async XLA Ops:
  0.0 50.3 %collective-permute-start.10 = (bf16[512,6144]{1,0:T(8,128)(2,1)}, bf16[512,6144]{1,0:T(8,128)(2,1)}, u32[]{:S(2)}, u32[]{:S(2)}) collective-permute-start(bf16[512,6144]{1,0:T(8,128)(2,1)} %wa.3), channel_id=1, source_target_pairs={{0,1},{1,0},{2,3},{3,2},{4,5},{5,4},{6,7},{7,6},{8,9},{9,8},{10,11... | collective-permute-start | bytes 18874376 | tf_op jit(solution)/shard_map/ppermute | solution.py:361
  5.0 19.1 %collective-permute-start = (bf16[2048,128]{1,0:T(8,128)(2,1)}, bf16[2048,128]{1,0:T(8,128)(2,1)}, u32[]{:S(2)}, u32[]{:S(2)}) collective-permute-start(bf16[2048,128]{1,0:T(8,128)(2,1)} %get-tuple-element.36.kv_ref.own_ref), channel_id=1, source_target_pairs={{0,112},{1,49},{2,114},{3,51},{4,116},{5,53},{6,118},{7,55},{8,120... | collective-permute-start | bytes 1572872 | tf_op jit(solution)/shard_map/ppermute | solution.py:361
  11.5 22.8 %collective-permute-start.1 = (bf16[2048,128]{1,0:T(8,128)(2,1)}, bf16[2048,128]{1,0:T(8,128)(2,1)}, u32[]{:S(2)}, u32[]{:S(2)}) collective-permute-start(bf16[2048,128]{1,0:T(8,128)(2,1)} %get-tuple-element.36.kv_ref.own_ref), channel_id=1, source_target_pairs={{0,96},{1,33},{2,98},{3,35},{4,100},{5,37},{6,102},{7,39},{8,104},... | collective-permute-start | bytes 1572872 | tf_op jit(solution)/shard_map/ppermute | solution.py:361
  13.7 27.2 %collective-permute-start.2 = (bf16[2048,128]{1,0:T(8,128)(2,1)}, bf16[2048,128]{1,0:T(8,128)(2,1)}, u32[]{:S(2)}, u32[]{:S(2)}) collective-permute-start(bf16[2048,128]{1,0:T(8,128)(2,1)} %get-tuple-element.36.kv_ref.own_ref), channel_id=1, source_target_pairs={{0,80},{1,17},{2,82},{3,19},{4,84},{5,21},{6,86},{7,23},{8,88},{9,... | collective-permute-start | bytes 1572872 | tf_op jit(solution)/shard_map/ppermute | solution.py:361
  15.7 25.3 %collective-permute-start.3 = (bf16[2048,128]{1,0:T(8,128)(2,1)}, bf16[2048,128]{1,0:T(8,128)(2,1)}, u32[]{:S(2)}, u32[]{:S(2)}) collective-permute-start(bf16[2048,128]{1,0:T(8,128)(2,1)} %get-tuple-element.36.kv_ref.own_ref), channel_id=1, source_target_pairs={{0,64},{2,66},{4,68},{6,70},{8,72},{10,74},{12,76},{14,78},{16,80}... | collective-permute-start | bytes 1572872 | tf_op jit(solution)/shard_map/ppermute | solution.py:361
  24.1 17.5 %collective-permute-start.4 = (bf16[2048,128]{1,0:T(8,128)(2,1)}, bf16[2048,128]{1,0:T(8,128)(2,1)}, u32[]{:S(2)}, u32[]{:S(2)}) collective-permute-start(bf16[2048,128]{1,0:T(8,128)(2,1)} %collective-permute-done.refs_3_.refs_1_), channel_id=1, source_target_pairs={{0,1},{1,0},{2,3},{3,2},{4,5},{5,4},{6,7},{7,6},{8,9},{9,8},{10,11... | collective-permute-start | bytes 1572872 | tf_op jit(solution)/shard_map/ppermute | solution.py:361
  34.4 8.5 %collective-permute-start.5 = (bf16[2048,128]{1,0:T(8,128)(2,1)}, bf16[2048,128]{1,0:T(8,128)(2,1)}, u32[]{:S(2)}, u32[]{:S(2)}) collective-permute-start(bf16[2048,128]{1,0:T(8,128)(2,1)} %collective-permute-done.1.refs_4_.refs_2_), channel_id=1, source_target_pairs={{0,1},{1,0},{2,3},{3,2},{4,5},{5,4},{6,7},{7,6},{8,9},{9,8},{10,11... | collective-permute-start | bytes 1572872 | tf_op jit(solution)/shard_map/ppermute | solution.py:361
  40.9 2.6 %collective-permute-start.6 = (bf16[2048,128]{1,0:T(8,128)(2,1)}, bf16[2048,128]{1,0:T(8,128)(2,1)}, u32[]{:S(2)}, u32[]{:S(2)}) collective-permute-start(bf16[2048,128]{1,0:T(8,128)(2,1)} %collective-permute-done.2.refs_5_.refs_3_), channel_id=1, source_target_pairs={{0,1},{1,0},{2,3},{3,2},{4,5},{5,4},{6,7},{7,6},{8,9},{9,8},{10,11... | collective-permute-start | bytes 1572872 | tf_op jit(solution)/shard_map/ppermute | solution.py:361
  40.9 3.4 %collective-permute-start.7 = (bf16[2048,128]{1,0:T(8,128)(2,1)}, bf16[2048,128]{1,0:T(8,128)(2,1)}, u32[]{:S(2)}, u32[]{:S(2)}) collective-permute-start(bf16[2048,128]{1,0:T(8,128)(2,1)} %collective-permute-done.3.refs_6_.refs_4_), channel_id=1, source_target_pairs={{0,1},{1,0},{2,3},{3,2},{4,5},{5,4},{6,7},{7,6},{8,9},{9,8},{10,11... | collective-permute-start | bytes 1572872 | tf_op jit(solution)/shard_map/ppermute | solution.py:361
  41.7 19.3 %collective-permute-start.11 = (bf16[16,32,512]{2,1,0:T(8,128)(2,1)}, bf16[16,32,512]{2,1,0:T(8,128)(2,1)}, u32[]{:S(2)}, u32[]{:S(2)}) collective-permute-start(bf16[16,32,512]{2,1,0:T(8,128)(2,1)} %get-tuple-element.50), channel_id=1, source_target_pairs={{0,112},{1,113},{2,114},{3,115},{4,116},{5,117},{6,118},{7,119},{8... | collective-permute-start | bytes 1572872 | tf_op jit(solution)/shard_map/ppermute | solution.py:361
  48.0 2.0 %collective-permute-start.8 = (bf16[256,512]{1,0:T(8,128)(2,1)}, bf16[256,512]{1,0:T(8,128)(2,1)}, u32[]{:S(2)}, u32[]{:S(2)}) collective-permute-start(bf16[256,512]{1,0:T(8,128)(2,1)} %get-tuple-element.45), channel_id=1, source_target_pairs={{0,1},{1,0},{2,3},{3,2},{4,5},{5,4},{6,7},{7,6},{8,9},{9,8},{10,11... | collective-permute-start | bytes 786440 | tf_op jit(solution)/shard_map/ppermute | solution.py:361
  48.5 1.9 %collective-permute-start.9 = (bf16[256,512]{1,0:T(8,128)(2,1)}, bf16[256,512]{1,0:T(8,128)(2,1)}, u32[]{:S(2)}, u32[]{:S(2)}) collective-permute-start(bf16[256,512]{1,0:T(8,128)(2,1)} %get-tuple-element.46), channel_id=1, source_target_pairs={{0,1},{1,0},{2,3},{3,2},{4,5},{5,4},{6,7},{7,6},{8,9},{9,8},{10,11... | collective-permute-start | bytes 786440 | tf_op jit(solution)/shard_map/ppermute | solution.py:361
  57.9 30.6 %collective-permute-start.14 = (bf16[128,3072]{1,0:T(8,128)(2,1)}, bf16[128,3072]{1,0:T(8,128)(2,1)}, u32[]{:S(2)}, u32[]{:S(2)}) collective-permute-start(bf16[128,3072]{1,0:T(8,128)(2,1)} %get-tuple-element.55), channel_id=1, source_target_pairs={{0,4},{1,3},{2,6},{3,1},{4,0},{5,7},{6,2},{7,5},{8,12},{9,11},{10,... | collective-permute-start | bytes 2359304 | tf_op jit(solution)/shard_map/ppermute | solution.py:361
  58.7 29.8 %collective-permute-start.15 = (bf16[128,3072]{1,0:T(8,128)(2,1)}, bf16[128,3072]{1,0:T(8,128)(2,1)}, u32[]{:S(2)}, u32[]{:S(2)}) collective-permute-start(bf16[128,3072]{1,0:T(8,128)(2,1)} %get-tuple-element.56), channel_id=1, source_target_pairs={{0,12},{1,3},{2,14},{3,1},{4,8},{5,7},{6,10},{7,5},{8,4},{9,11},{1... | collective-permute-start | bytes 2359304 | tf_op jit(solution)/shard_map/ppermute | solution.py:361
  59.4 29.1 %collective-permute-start.16 = (bf16[128,3072]{1,0:T(8,128)(2,1)}, bf16[128,3072]{1,0:T(8,128)(2,1)}, u32[]{:S(2)}, u32[]{:S(2)}) collective-permute-start(bf16[128,3072]{1,0:T(8,128)(2,1)} %get-tuple-element.54.refs_1_), channel_id=1, source_target_pairs={{0,8},{2,10},{4,12},{6,14},{8,0},{10,2},{12,4},{14,6},{16,24},{18,... | collective-permute-start | bytes 2359304 | tf_op jit(solution)/shard_map/ppermute | solution.py:361
  82.8 5.4 %collective-permute-start.12 = (bf16[256,512]{1,0:T(8,128)(2,1)}, bf16[256,512]{1,0:T(8,128)(2,1)}, u32[]{:S(2)}, u32[]{:S(2)}) collective-permute-start(bf16[256,512]{1,0:T(8,128)(2,1)} %get-tuple-element.52), channel_id=1, source_target_pairs={{0,1},{1,0},{2,3},{3,2},{4,5},{5,4},{6,7},{7,6},{8,9},{9,8},{10,11... | collective-permute-start | bytes 786440 | tf_op jit(solution)/shard_map/ppermute | solution.py:361
  86.6 1.9 %collective-permute-start.13 = (bf16[256,512]{1,0:T(8,128)(2,1)}, bf16[256,512]{1,0:T(8,128)(2,1)}, u32[]{:S(2)}, u32[]{:S(2)}) collective-permute-start(bf16[256,512]{1,0:T(8,128)(2,1)} %get-tuple-element.53), channel_id=1, source_target_pairs={{0,1},{1,0},{2,3},{3,2},{4,5},{5,4},{6,7},{7,6},{8,9},{9,8},{10,11... | collective-permute-start | bytes 786440 | tf_op jit(solution)/shard_map/ppermute | solution.py:361
  98.2 12.9 %collective-permute-start.17 = (bf16[128,3072]{1,0:T(8,128)(2,1)}, bf16[128,3072]{1,0:T(8,128)(2,1)S(1)}, u32[]{:S(2)}, u32[]{:S(2)}) collective-permute-start(bf16[128,3072]{1,0:T(8,128)(2,1)} %get-tuple-element.59), channel_id=1, source_target_pairs={{0,4},{1,3},{2,6},{3,1},{4,0},{5,7},{6,2},{7,5},{8,12},{9,11},{10,... | collective-permute-start | bytes 2359304 | tf_op jit(solution)/shard_map/ppermute | solution.py:361
  99.0 23.2 %collective-permute-start.18 = (bf16[128,3072]{1,0:T(8,128)(2,1)}, bf16[128,3072]{1,0:T(8,128)(2,1)S(1)}, u32[]{:S(2)}, u32[]{:S(2)}) collective-permute-start(bf16[128,3072]{1,0:T(8,128)(2,1)} %get-tuple-element.60), channel_id=1, source_target_pairs={{0,12},{1,3},{2,14},{3,1},{4,8},{5,7},{6,10},{7,5},{8,4},{9,11},{1... | collective-permute-start | bytes 2359304 | tf_op jit(solution)/shard_map/ppermute | solution.py:361
  99.7 22.5 %collective-permute-start.19 = (bf16[128,3072]{1,0:T(8,128)(2,1)}, bf16[128,3072]{1,0:T(8,128)(2,1)S(1)}, u32[]{:S(2)}, u32[]{:S(2)}) collective-permute-start(bf16[128,3072]{1,0:T(8,128)(2,1)} %get-tuple-element.61), channel_id=1, source_target_pairs={{0,8},{2,10},{4,12},{6,14},{8,0},{10,2},{12,4},{14,6},{16,24},{18,... | collective-permute-start | bytes 2359304 | tf_op jit(solution)/shard_map/ppermute | solution.py:361
  100.4 31.8 %collective-permute-start.20 = (bf16[64,3072]{1,0:T(8,128)(2,1)}, bf16[64,3072]{1,0:T(8,128)(2,1)S(1)}, u32[]{:S(2)}, u32[]{:S(2)}) collective-permute-start(bf16[64,3072]{1,0:T(8,128)(2,1)} %get-tuple-element.63), channel_id=1, source_target_pairs={{0,2},{1,5},{2,0},{3,7},{4,6},{5,1},{6,4},{7,3},{8,10},{9,13},{10,... | collective-permute-start | bytes 1179656 | tf_op jit(solution)/shard_map/ppermute | solution.py:361
  101.4 34.0 %collective-permute-start.21 = (bf16[64,3072]{1,0:T(8,128)(2,1)}, bf16[64,3072]{1,0:T(8,128)(2,1)S(1)}, u32[]{:S(2)}, u32[]{:S(2)}) collective-permute-start(bf16[64,3072]{1,0:T(8,128)(2,1)} %get-tuple-element.64), channel_id=1, source_target_pairs={{1,13},{3,15},{5,9},{7,11},{9,5},{11,7},{13,1},{15,3},{17,29},{19,... | collective-permute-start | bytes 1179656 | tf_op jit(solution)/shard_map/ppermute | solution.py:361
  122.2 3.2 %copy-start.1 = (bf16[64,3072]{1,0:T(8,128)(2,1)S(1)}, bf16[64,3072]{1,0:T(8,128)(2,1)}, u32[]{:S(2)}) copy-start(bf16[64,3072]{1,0:T(8,128)(2,1)} %get-tuple-element.66) | copy-start | bytes 1179652
  124.3 13.1 %copy-start = (bf16[64,3072]{1,0:T(8,128)(2,1)S(1)}, bf16[64,3072]{1,0:T(8,128)(2,1)}, u32[]{:S(2)}) copy-start(bf16[64,3072]{1,0:T(8,128)(2,1)} %get-tuple-element.62) | copy-start | bytes 1179652
  124.4 13.4 %collective-permute-start.23 = (bf16[64,3072]{1,0:T(8,128)(2,1)S(1)}, bf16[64,3072]{1,0:T(8,128)(2,1)S(1)}, u32[]{:S(2)}, u32[]{:S(2)}) collective-permute-start(bf16[64,3072]{1,0:T(8,128)(2,1)S(1)} %fusion.4), channel_id=1, source_target_pairs={{0,2},{1,5},{2,0},{3,7},{4,6},{5,1},{6,4},{7,3},{8,10},{9,13},{10,... | collective-permute-start | bytes 1179656 | tf_op jit(solution)/shard_map/ppermute | solution.py:361
  125.4 12.1 %collective-permute-start.22 = (bf16[64,3072]{1,0:T(8,128)(2,1)S(1)}, bf16[64,3072]{1,0:T(8,128)(2,1)S(1)}, u32[]{:S(2)}, u32[]{:S(2)}) collective-permute-start(bf16[64,3072]{1,0:T(8,128)(2,1)S(1)} %copy-done.1), channel_id=1, source_target_pairs={{1,9},{3,11},{5,13},{7,15},{9,1},{11,3},{13,5},{15,7},{17,25},{19,... | collective-permute-start | bytes 1179656 | tf_op jit(solution)/shard_map/ppermute | solution.py:361
  130.0 15.8 %collective-permute-start.24 = (bf16[64,3072]{1,0:T(8,128)(2,1)S(1)}, bf16[64,3072]{1,0:T(8,128)(2,1)S(1)}, u32[]{:S(2)}, u32[]{:S(2)}) collective-permute-start(bf16[64,3072]{1,0:T(8,128)(2,1)S(1)} %get-tuple-element.71), channel_id=1, source_target_pairs={{1,13},{3,15},{5,9},{7,11},{9,5},{11,7},{13,1},{15,3},{17,29},{19,... | collective-permute-start | bytes 1179656 | tf_op jit(solution)/shard_map/ppermute | solution.py:361
  132.2 13.6 %collective-permute-start.25 = (bf16[64,3072]{1,0:T(8,128)(2,1)S(1)}, bf16[64,3072]{1,0:T(8,128)(2,1)S(1)}, u32[]{:S(2)}, u32[]{:S(2)}) collective-permute-start(bf16[64,3072]{1,0:T(8,128)(2,1)S(1)} %get-tuple-element.72), channel_id=1, source_target_pairs={{1,9},{3,11},{5,13},{7,15},{9,1},{11,3},{13,5},{15,7},{17,25},{19,... | collective-permute-start | bytes 1179656 | tf_op jit(solution)/shard_map/ppermute | solution.py:361
  137.7 17.9 %collective-permute-start.27 = (bf16[32,3072]{1,0:T(8,128)(2,1)S(1)}, bf16[32,3072]{1,0:T(8,128)(2,1)S(1)}, u32[]{:S(2)}, u32[]{:S(2)}) collective-permute-start(bf16[32,3072]{1,0:T(8,128)(2,1)S(1)} %get-tuple-element.76), channel_id=1, source_target_pairs={{0,1},{1,0},{2,3},{3,2},{4,5},{5,4},{6,7},{7,6},{8,9},{9,8},{10,11... | collective-permute-start | bytes 589832 | tf_op jit(solution)/shard_map/ppermute | solution.py:361
  146.0 9.6 %collective-permute-start.28 = (bf16[32,3072]{1,0:T(8,128)(2,1)S(1)}, bf16[32,3072]{1,0:T(8,128)(2,1)S(1)}, u32[]{:S(2)}, u32[]{:S(2)}) collective-permute-start(bf16[32,3072]{1,0:T(8,128)(2,1)S(1)} %get-tuple-element.78), channel_id=1, source_target_pairs={{0,113},{1,112},{2,115},{3,114},{4,117},{5,116},{6,119},{7,118},{8... | collective-permute-start | bytes 589832 | tf_op jit(solution)/shard_map/ppermute | solution.py:361
  147.6 13.0 %collective-permute-start.26 = (bf16[32,3072]{1,0:T(8,128)(2,1)S(1)}, bf16[32,3072]{1,0:T(8,128)(2,1)S(1)}, u32[]{:S(2)}, u32[]{:S(2)}) collective-permute-start(bf16[32,3072]{1,0:T(8,128)(2,1)S(1)} %get-tuple-element.77), channel_id=1, source_target_pairs={{0,112},{1,113},{2,114},{3,115},{4,116},{5,117},{6,118},{7,119},{8... | collective-permute-start | bytes 589832 | tf_op jit(solution)/shard_map/ppermute | solution.py:361

commit v7 on v5

--- a/solution.py
+++ b/solution.py
@@ -14,7 +14,7 @@
 LIMIT = 60.0
 BF = jnp.bfloat16
 F32 = jnp.float32
-PARAMS = pltpu.CompilerParams(vmem_limit_bytes=64 << 20)
+PARAMS = pltpu.CompilerParams(vmem_limit_bytes=28 << 20)
 FETCH = ((7, 3), (6, 2), (5, 1), (4, None))
 SLOTS = [d for pair in FETCH for d in pair if d is not None]
 TABLE = 6
@@ -44,7 +44,7 @@
         ),
         out_shape=jax.ShapeDtypeStruct((2 * rows, DH), BF),
         name="prep",
-        compiler_params=PARAMS,
+        compiler_params=pltpu.CompilerParams(vmem_limit_bytes=64 << 20),
     )(info, keys, values)
 
 
@@ -88,7 +88,8 @@
         m_ref[:, c] = jnp.broadcast_to(top, (8, qb))
 
 
-def own_kernel(groups, q_ref, kv_ref, qt_ref, acc_ref, m_ref):
+def own_kernel(groups, q_ref, away_ref, kv_ref, qt_ref, acc_ref, m_ref, send_ref):
+    send_ref[...] = away_ref[:, 0]
     _, _, sub, width = q_ref.shape
     for h in range(width // DH):
         load_queries(q_ref[:, 0, :, h * DH : (h + 1) * DH].reshape(groups * sub, DH), h, qt_ref)
@@ -105,24 +106,27 @@
         grid=(1,),
         in_specs=[
             pl.BlockSpec((groups, 1, sub, width), lambda i: (0, 0, 0, 0)),
+            pl.BlockSpec((groups, 1, sub, width), lambda i: (0, 1, 0, 0)),
             pl.BlockSpec(kv.shape, lambda i: (0, 0)),
         ],
         out_specs=[
             pl.BlockSpec((2 * DH, cols), lambda i: (0, 0)),
             pl.BlockSpec((DH + 16, cols), lambda i: (0, 0)),
             pl.BlockSpec((8, cols), lambda i: (0, 0)),
+            pl.BlockSpec((groups, sub, width), lambda i: (0, 0, 0)),
         ],
         out_shape=[
             jax.ShapeDtypeStruct((2 * DH, cols), BF),
             jax.ShapeDtypeStruct((DH + 16, cols), F32),
             jax.ShapeDtypeStruct((8, cols), F32),
+            jax.ShapeDtypeStruct((groups, sub, width), BF),
         ],
         name="own",
         cost_estimate=pl.CostEstimate(
             flops=2 * cols * kv.shape[0] * 2 * DH, bytes_accessed=8 << 20, transcendentals=0
         ),
         compiler_params=PARAMS,
-    )(q4, kv)
+    )(q4, q4, kv)
 
 
 def attend_kernel(foreign, groups, n_y, n_seq, info, own_ref, *refs):
@@ -140,6 +144,7 @@
     sub = qb // groups
     half = cols // 4
     limit = partner if foreign else place
+    y_first = core == (0 if foreign else 1)
     n = len(SLOTS)
     if foreign:
         state = [pltpu.make_async_copy(refs[0], q_buf, sems.at[n + 1])]
@@ -230,13 +235,13 @@
         o = acc_ref[last, :, h * qb : (h + 1) * qb]
         o = (o[0:DH] * (1.0 / o[DH : DH + 1])).astype(BF).T
         for g in range(groups):
-            ry = (g // 4 + n_y - info[3]) % n_y
+            ry = (g // 4) ^ info[3]
             rz = (g // 2 % 2) ^ info[4]
             by_y = ((ry * 2 + rz) * 2 + g % 2) * sub
             by_z = (((ry // 2 * 2 + rz) * 2 + ry % 2) * 2 + g % 2) * sub
             piece = o[g * sub : (g + 1) * sub, :]
-            here = pl.multiple_of(jnp.where(core == 0, by_y, by_z), sub)
-            there = pl.multiple_of(jnp.where(core == 0, by_z, by_y), sub)
+            here = pl.multiple_of(jnp.where(y_first, by_y, by_z), sub)
+            there = pl.multiple_of(jnp.where(y_first, by_z, by_y), sub)
             o_ref[pl.ds(here, sub), h * DH : (h + 1) * DH] = piece
             peer_buf[pl.ds(there, sub), h * DH : (h + 1) * DH] = piece
     first_ref[...] = peer_buf[: qb // 2, :]
@@ -248,7 +253,7 @@
     groups, sub, width = q_shape
     qb = groups * sub
     cols = qb * width // DH
-    any_space = pl.BlockSpec(memory_space=pltpu.HBM)
+    any_space = pl.BlockSpec(memory_space=pl.ANY)
     out = pl.BlockSpec((qb, width), lambda i, info: (0, 0))
     part = pl.BlockSpec((qb // 2, width), lambda i, info: (0, 0))
     return pl.pallas_call(
@@ -295,7 +300,7 @@
             o[...] = s[i * part : (i + 1) * part].astype(BF)
         if sums:
             p0, p2, g0, g1, g2 = [ref[...].astype(F32) for ref in refs[: len(sums)]]
-            first = p0 + g0 + jnp.where(info[2] == 0, g1 + g2, 0.0)
+            first = p0 + g0 + jnp.where(info[2] == 1, g1 + g2, 0.0)
             second = p2 + g1
             half = part // 2
             for o, x in zip(outs[parts:], (first[:half], first[half:], second[:half], second[half:]), strict=True):
@@ -369,15 +374,15 @@
     w_other = swap_core(w_out)
     kv = prep(info, keys, values)
     mine = [fetch(kv, pair) for pair in FETCH]
-    state = own(q4, kv)
+    *state, q_away = own(q4, kv)
     other = [swap_core(after(x, state[2])) for x in mine]
-    q_far = over_all(after(q4[:, 1], state[2], *mine), lambda s, y, z, c: (n_seq - 1 - s, y, z, c))
-
-    def stage_one(parts):
+    q_far = over_all(after(q_away, state[2], *mine), lambda s, y, z, c: (n_seq - 1 - s, y, z, c))
+
+    def stage_one(parts, first):
         return [
-            over_all(parts[1], lambda s, y, z, c: (s, y, 1 - z, c) if c else (s, y + 1, z, c)),
-            over_all(parts[3], lambda s, y, z, c: (s, y, 1 - z, c) if c else (s, y - 1, z, c)),
-            over_all(parts[2], lambda s, y, z, c: None if c else (s, y + 2, z, c)),
+            over_all(parts[1], lambda s, y, z, c: (s, y ^ 1, z, c) if c == first else (s, y, 1 - z, c)),
+            over_all(parts[3], lambda s, y, z, c: (s, y ^ 3, z, c) if c == first else (s, y, 1 - z, c)),
+            over_all(parts[2], lambda s, y, z, c: (s, y ^ 2, z, c) if c == first else None),
         ]
 
     def sum_one(parts, got):
@@ -388,11 +393,11 @@
         n = a.shape[0] // 2
         return a[:n], a[n:], b[:n], b[n:]
 
-    def stage_two(total):
+    def stage_two(total, first):
         return [
-            over_all(total[1], lambda s, y, z, c: (s, y + 1, z, c) if c else (s, y, 1 - z, c)),
-            over_all(total[3], lambda s, y, z, c: (s, y - 1, z, c) if c else None),
-            over_all(total[2], lambda s, y, z, c: (s, y + 2, z, c) if c else None),
+            over_all(total[1], lambda s, y, z, c: (s, y, 1 - z, c) if c == first else (s, y ^ 1, z, c)),
+            over_all(total[3], lambda s, y, z, c: None if c == first else (s, y ^ 3, z, c)),
+            over_all(total[2], lambda s, y, z, c: None if c == first else (s, y ^ 2, z, c)),
         ]
 
     def by_core(x, same):
@@ -402,16 +407,16 @@
     near, *near_peer = attend(info, kv, state, half, mine, other, n_y, n_seq)
     near_far = [swap_core(x) for x in near_peer]
     parts_n = project(info, near, near_far, w_out, w_other, n_y, cols // 4)
-    got_n = stage_one(parts_n)
+    got_n = stage_one(parts_n, 1)
     far, *far_peer = attend(after(info, parts_n[0]), kv, [q_far], half, mine, other, n_y, n_seq)
     far_far = [swap_core(x) for x in far_peer]
     *parts_f, a0, a1, b0, b1 = project(
         info, far, far_far, w_out, w_other, n_y, cols // 4, (parts_n[0], parts_n[2], *got_n)
     )
-    got_f = stage_one(parts_f)
+    got_f = stage_one(parts_f, 0)
     total_f = sum_one(parts_f, got_f)
-    got2_n = stage_two((a0, a1, after(b0, total_f[0]), b1))
-    got2_f = stage_two(total_f)
+    got2_n = stage_two((a0, a1, after(b0, total_f[0]), b1), 1)
+    got2_f = stage_two(total_f, 0)
     done_f = add(total_f[0], *got2_f).reshape(2, sub, cols // 2)
     done_n = add(after(a0, total_f[0]), *got2_n).reshape(2, sub, cols // 2)
     own_other = swap_core(by_core(done_n, False))

time: 164 us -> 156 us (0.951)
  the two profiles are of different devices: /device:TPU:8 before, /device:TPU:1 now
where the time goes in v7:
time: 156 us; the launch traced here: 154 us
  starting transfers between devices  69.4 us (44%)
  Pallas kernels  41.6 us (27%)
  waiting for transfers between devices  33.7 us (22%)
  local copies, waits for them, and re-layouts  5.19 us (3%)
  other arithmetic  3.88 us (2%)
    ppermute x29, starting transfers between devices, over_all(): return lax.ppermute(x, ('seq', 'head'), pairs)  69.4 us
    ppermute x29, waiting for transfers between devices, over_all(): return lax.ppermute(x, ('seq', 'head'), pairs)  33.7 us
    pallas_call x2, Pallas kernels, attend(): pl.pallas_call(functools.partial(attend_kernel, foreign, groups, n_y, n_s...  21.9 us
    pallas_call x2, Pallas kernels, project(): pl.pallas_call(body, grid_spec=pltpu.PrefetchScalarGridSpec(num_scalar_pr...  13 us
    unnamed x21, local copies, waits for them, and re-layouts  4.52 us
    pallas_call x1, Pallas kernels, own(): pl.pallas_call(functools.partial(own_kernel, groups), grid=(1,), in_specs...  4.16 us
  transfers between devices with their start and end apart: 29, of which 13 were waited for; matrix products, arithmetic and copies ran while one was open for 2% of the time, Pallas kernels for 22%

profile of v7, /device:TPU:1, one launch (start us, length us, event | category | flops | bytes accessed | tf_op | source)
XLA Modules:
  0.0 154.1 jit_solution(8231492202485689882)
XLA Ops:
  0.0 1.4 collective-permute-start.10
  1.4 0.6 stack.27.info
  2.0 2.6 %prep.1.kv_ref.own_ref = bf16[2048,128]{1,0:T(8,128)(2,1)} custom-call(s32[13]{0:T(128)} %stack.27.info, bf16[1024,1024]{1,0:T(8,128)(2,1)} %k_ref.1, bf16[1024,1024]{1,0:T(8,128)(2,1)} %v_ref.1), custom_call_target="tpu_custom_call" | custom-call | tf_op jit(solution)/shard_map/prep/pallas_call | solution.py:37
  4.6 6.5 %collective-permute-start = (bf16[2048,128]{1,0:T(8,128)(2,1)}, bf16[2048,128]{1,0:T(8,128)(2,1)S(1)}, u32[]{:S(2)}, u32[]{:S(2)}) collective-permute-start(bf16[2048,128]{1,0:T(8,128)(2,1)} %prep.1.kv_ref.own_ref), channel_id=1, source_target_pairs={{0,112},{1,49},{2,114},{3,51},{4,116},{5,53},{6,118},{7,55},{8,120... | collective-permute-start | bytes 1572872 | tf_op jit(solution)/shard_map/ppermute | solution.py:358
  11.1 2.2 %collective-permute-start.1 = (bf16[2048,128]{1,0:T(8,128)(2,1)}, bf16[2048,128]{1,0:T(8,128)(2,1)S(1)}, u32[]{:S(2)}, u32[]{:S(2)}) collective-permute-start(bf16[2048,128]{1,0:T(8,128)(2,1)} %prep.1.kv_ref.own_ref), channel_id=1, source_target_pairs={{0,96},{1,33},{2,98},{3,35},{4,100},{5,37},{6,102},{7,39},{8,104},... | collective-permute-start | bytes 1572872 | tf_op jit(solution)/shard_map/ppermute | solution.py:358
  13.3 1.9 %collective-permute-start.2 = (bf16[2048,128]{1,0:T(8,128)(2,1)}, bf16[2048,128]{1,0:T(8,128)(2,1)S(1)}, u32[]{:S(2)}, u32[]{:S(2)}) collective-permute-start(bf16[2048,128]{1,0:T(8,128)(2,1)} %prep.1.kv_ref.own_ref), channel_id=1, source_target_pairs={{0,80},{1,17},{2,82},{3,19},{4,84},{5,21},{6,86},{7,23},{8,88},{9,... | collective-permute-start | bytes 1572872 | tf_op jit(solution)/shard_map/ppermute | solution.py:358
  15.3 0.7 collective-permute-start.3
  16.0 1.0 copy-done
  17.0 1.2 copy-done.3
  18.2 4.2 %own.1 = (bf16[256,2048]{1,0:T(8,128)(2,1)S(1)}, f32[144,2048]{1,0:T(8,128)S(1)}, f32[8,2048]{1,0:T(8,128)S(1)}, bf16[16,32,512]{2,1,0:T(8,128)(2,1)S(1)}) custom-call(bf16[16,2,32,512]{3,2,1,0:T(8,128)(2,1)S(1)} %bitcast.9, bf16[16,2,32,512]{3,2,1,0:T(8,128)(2,1)S(1)} %bitcast.10, bf16[2048,128]{1,0:T(8,128)(2,1)S(1)} %copy-done), custom_call_target="tpu_custom_call" | custom-call | flops 2147483648 | bytes 8388608 | tf_op jit(solution)/shard_map/own/pallas_call | solution.py:104
  22.4 1.2 collective-permute-done.refs_3_.refs_1_
  23.6 4.9 %collective-permute-start.4 = (bf16[2048,128]{1,0:T(8,128)(2,1)S(1)}, bf16[2048,128]{1,0:T(8,128)(2,1)S(1)}, u32[]{:S(2)}, u32[]{:S(2)}) collective-permute-start(bf16[2048,128]{1,0:T(8,128)(2,1)S(1)} %collective-permute-done.refs_3_.refs_1_), channel_id=1, source_target_pairs={{0,1},{1,0},{2,3},{3,2},{4,5},{5,4},{6,7},{7,6},{8,9},{9,8},{10,11... | collective-permute-start | bytes 1572872 | tf_op jit(solution)/shard_map/ppermute | solution.py:358
  28.5 5.3 %collective-permute-done.1.refs_4_.refs_2_ = bf16[2048,128]{1,0:T(8,128)(2,1)S(1)} collective-permute-done((bf16[2048,128]{1,0:T(8,128)(2,1)}, bf16[2048,128]{1,0:T(8,128)(2,1)S(1)}, u32[]{:S(2)}, u32[]{:S(2)}) %collective-permute-start.1) | collective-permute-done | bytes 524320 | tf_op jit(solution)/shard_map/ppermute | solution.py:358
  33.9 7.0 %collective-permute-start.5 = (bf16[2048,128]{1,0:T(8,128)(2,1)S(1)}, bf16[2048,128]{1,0:T(8,128)(2,1)S(1)}, u32[]{:S(2)}, u32[]{:S(2)}) collective-permute-start(bf16[2048,128]{1,0:T(8,128)(2,1)S(1)} %collective-permute-done.1.refs_4_.refs_2_), channel_id=1, source_target_pairs={{0,1},{1,0},{2,3},{3,2},{4,5},{5,4},{6,7},{7,6},{8,9},{9,8},{10,11... | collective-permute-start | bytes 1572872 | tf_op jit(solution)/shard_map/ppermute | solution.py:358
  40.9 0.5 collective-permute-start.7
  41.4 1.0 collective-permute-start.11
  42.4 0.7 collective-permute-done.6.refs_9_.refs_7_
  43.2 0.7 collective-permute-done.7.refs_10_.refs_8_
  43.9 1.7 %attend_own.1 = (bf16[512,512]{1,0:T(8,128)(2,1)S(1)}, bf16[256,512]{1,0:T(8,128)(2,1)S(1)}, bf16[256,512]{1,0:T(8,128)(2,1)S(1)}) custom-call(s32[13]{0:T(128)S(1)} %copy-done.2, bf16[2048,128]{1,0:T(8,128)(2,1)S(1)} %copy-done.1, bf16[256,2048]{1,0:T(8,128)(2,1)S(1)} %get-tuple-element.35.refs_0_, f32[144,2048]{1,0:T(8,128)S(1)} %get-tuple-element.36.refs_1_, ...), custom_call_target="tpu_custom_call" | custom-call | flops 4294967296 | bytes 4194304 | tf_op jit(solution)/shard_map/attend_own/pallas_call | solution.py:259
  45.7 0.5 collective-permute-start.8
  46.4 0.9 collective-permute-done.8.b0
  47.7 5.9 %project.1 = (bf16[128,3072]{1,0:T(8,128)(2,1)S(1)}, bf16[128,3072]{1,0:T(8,128)(2,1)S(1)}, bf16[128,3072]{1,0:T(8,128)(2,1)S(1)}, bf16[128,3072]{1,0:T(8,128)(2,1)S(1)}) custom-call(s32[13]{0:T(128)S(1)} %copy-done.2, bf16[512,512]{1,0:T(8,128)(2,1)S(1)} %get-tuple-element.42.a, bf16[256,512]{1,0:T(8,128)(2,1)S(1)} %collective-permute-done.8.b0, ...), custom_call_target="tpu_custom_call" | custom-call | tf_op jit(solution)/shard_map/project/pallas_call | solution.py:317
  53.6 1.4 collective-permute-start.14
  55.0 1.9 %collective-permute-start.15 = (bf16[128,3072]{1,0:T(8,128)(2,1)S(1)}, bf16[128,3072]{1,0:T(8,128)(2,1)S(1)}, u32[]{:S(2)}, u32[]{:S(2)}) collective-permute-start(bf16[128,3072]{1,0:T(8,128)(2,1)S(1)} %get-tuple-element.54), channel_id=1, source_target_pairs={{0,2},{1,13},{2,0},{3,15},{4,6},{5,9},{6,4},{7,11},{8,10},{9,5},{1... | collective-permute-start | bytes 2359304 | tf_op jit(solution)/shard_map/ppermute | solution.py:358
  56.9 2.6 %collective-permute-start.16 = (bf16[128,3072]{1,0:T(8,128)(2,1)S(1)}, bf16[128,3072]{1,0:T(8,128)(2,1)S(1)}, u32[]{:S(2)}, u32[]{:S(2)}) collective-permute-start(bf16[128,3072]{1,0:T(8,128)(2,1)S(1)} %get-tuple-element.52.refs_1_), channel_id=1, source_target_pairs={{1,9},{3,11},{5,13},{7,15},{9,1},{11,3},{13,5},{15,7},{17,25},{19,... | collective-permute-start | bytes 2359304 | tf_op jit(solution)/shard_map/ppermute | solution.py:358
  59.5 20.2 %attend_foreign.1 = (bf16[512,512]{1,0:T(8,128)(2,1)S(1)}, bf16[256,512]{1,0:T(8,128)(2,1)S(1)}, bf16[256,512]{1,0:T(8,128)(2,1)S(1)}) custom-call(s32[13]{0:T(128)S(1)} %copy-done.2, bf16[2048,128]{1,0:T(8,128)(2,1)S(1)} %copy-done.1, bf16[16,32,512]{2,1,0:T(8,128)(2,1)S(1)} %collective-permute-done.11.refs_0_, ...), custom_call_target="tpu_custom_call" | custom-call | flops 4294967296 | bytes 4194304 | tf_op jit(solution)/shard_map/attend_foreign/pallas_call | solution.py:259
  79.8 0.5 collective-permute-start.13
  80.3 1.0 collective-permute-done.12.b0
  81.7 7.0 %project_and_sum.1 = (bf16[128,3072]{1,0:T(8,128)(2,1)S(1)}, bf16[128,3072]{1,0:T(8,128)(2,1)S(1)}, bf16[128,3072]{1,0:T(8,128)(2,1)S(1)}, bf16[128,3072]{1,0:T(...) custom-call(s32[13]{0:T(128)S(1)} %copy-done.2, ...), custom_call_target="tpu_custom_call" | custom-call | tf_op jit(solution)/shard_map/project_and_sum/pallas_call | solution.py:317
  88.8 0.7 copy-done.4
  89.5 0.7 copy-done.6
  90.2 0.7 copy-done.7
  91.4 1.1 collective-permute-start.18
  92.5 1.6 %collective-permute-start.19 = (bf16[128,3072]{1,0:T(8,128)(2,1)S(1)}, bf16[128,3072]{1,0:T(8,128)(2,1)}, u32[]{:S(2)}, u32[]{:S(2)}) collective-permute-start(bf16[128,3072]{1,0:T(8,128)(2,1)S(1)} %get-tuple-element.59), channel_id=1, source_target_pairs={{0,8},{2,10},{4,12},{6,14},{8,0},{10,2},{12,4},{14,6},{16,24},{18,... | collective-permute-start | bytes 2359304 | tf_op jit(solution)/shard_map/ppermute | solution.py:358
  94.4 0.7 collective-permute-start.21
  95.0 7.2 %collective-permute-done.17 = bf16[128,3072]{1,0:T(8,128)(2,1)} collective-permute-done((bf16[128,3072]{1,0:T(8,128)(2,1)S(1)}, bf16[128,3072]{1,0:T(8,128)(2,1)}, u32[]{:S(2)}, u32[]{:S(2)}) %collective-permute-start.17) | collective-permute-done | bytes 786464 | tf_op jit(solution)/shard_map/ppermute | solution.py:358
  102.2 8.4 %collective-permute-done.18 = bf16[128,3072]{1,0:T(8,128)(2,1)} collective-permute-done((bf16[128,3072]{1,0:T(8,128)(2,1)S(1)}, bf16[128,3072]{1,0:T(8,128)(2,1)}, u32[]{:S(2)}, u32[]{:S(2)}) %collective-permute-start.18) | collective-permute-done | bytes 786464 | tf_op jit(solution)/shard_map/ppermute | solution.py:358
  110.7 2.3 %fusion.3 = (bf16[128,3072]{1,0:T(8,128)(2,1)S(1)}, bf16[128,3072]{1,0:T(8,128)(2,1)S(1)}) fusion(bf16[128,3072]{1,0:T(8,128)(2,1)} %collective-permute-done.18, bf16[128,3072]{1,0:T(8,128)(2,1)S(1)} %get-tuple-element.59, bf16[128,3072]{1,0:T(8,128)(2,1)} %collective-permute-done.19, pred[]{:T(512)S(6)} %eq.7, bf16[128,3072]{1,0:T(8,128)(2,1)} %collective-permute-done.17, ...), kind=kLoop, calls=%fused_computation.5 | loop fusion | flops 4718592 | bytes 5505025 | tf_op jit(solution)/shard_map/convert_element_type | solution.py:336
  113.0 1.7 %collective-permute-start.23 = (bf16[64,3072]{1,0:T(8,128)(2,1)S(1)}, bf16[64,3072]{1,0:T(8,128)(2,1)S(1)}, u32[]{:S(2)}, u32[]{:S(2)}) collective-permute-start(bf16[64,3072]{1,0:T(8,128)(2,1)S(1)} %fusion.4), channel_id=1, source_target_pairs={{0,2},{1,5},{2,0},{3,7},{4,6},{5,1},{6,4},{7,3},{8,10},{9,13},{10,... | collective-permute-start | bytes 1179656 | tf_op jit(solution)/shard_map/ppermute | solution.py:358
  114.8 0.7 collective-permute-start.22
  115.5 2.9 %collective-permute-start.24 = (bf16[64,3072]{1,0:T(8,128)(2,1)S(1)}, bf16[64,3072]{1,0:T(8,128)(2,1)S(1)}, u32[]{:S(2)}, u32[]{:S(2)}) collective-permute-start(bf16[64,3072]{1,0:T(8,128)(2,1)S(1)} %get-tuple-element.69), channel_id=1, source_target_pairs={{1,13},{3,15},{5,9},{7,11},{9,5},{11,7},{13,1},{15,3},{17,29},{19,... | collective-permute-start | bytes 1179656 | tf_op jit(solution)/shard_map/ppermute | solution.py:358
  118.5 2.7 %collective-permute-start.25 = (bf16[64,3072]{1,0:T(8,128)(2,1)S(1)}, bf16[64,3072]{1,0:T(8,128)(2,1)S(1)}, u32[]{:S(2)}, u32[]{:S(2)}) collective-permute-start(bf16[64,3072]{1,0:T(8,128)(2,1)S(1)} %get-tuple-element.70), channel_id=1, source_target_pairs={{1,9},{3,11},{5,13},{7,15},{9,1},{11,3},{13,5},{15,7},{17,25},{19,... | collective-permute-start | bytes 1179656 | tf_op jit(solution)/shard_map/ppermute | solution.py:358
  121.4 12.4 %collective-permute-start.27 = (bf16[32,3072]{1,0:T(8,128)(2,1)S(1)}, bf16[32,3072]{1,0:T(8,128)(2,1)S(1)}, u32[]{:S(2)}, u32[]{:S(2)}) collective-permute-start(bf16[32,3072]{1,0:T(8,128)(2,1)S(1)} %get-tuple-element.74), channel_id=1, source_target_pairs={{0,1},{1,0},{2,3},{3,2},{4,5},{5,4},{6,7},{7,6},{8,9},{9,8},{10,11... | collective-permute-start | bytes 589832 | tf_op jit(solution)/shard_map/ppermute | solution.py:358
  134.1 10.4 %collective-permute-start.28 = (bf16[32,3072]{1,0:T(8,128)(2,1)S(1)}, bf16[32,3072]{1,0:T(8,128)(2,1)S(1)}, u32[]{:S(2)}, u32[]{:S(2)}) collective-permute-start(bf16[32,3072]{1,0:T(8,128)(2,1)S(1)} %get-tuple-element.76), channel_id=1, source_target_pairs={{0,113},{1,112},{2,115},{3,114},{4,117},{5,116},{6,119},{7,118},{8... | collective-permute-start | bytes 589832 | tf_op jit(solution)/shard_map/ppermute | solution.py:358
  144.5 1.2 collective-permute-start.26
  145.7 3.8 %collective-permute-done.28 = bf16[32,3072]{1,0:T(8,128)(2,1)S(1)} collective-permute-done((bf16[32,3072]{1,0:T(8,128)(2,1)S(1)}, bf16[32,3072]{1,0:T(8,128)(2,1)S(1)}, u32[]{:S(2)}, u32[]{:S(2)}) %collective-permute-start.28) | collective-permute-done | bytes 196640 | tf_op jit(solution)/shard_map/ppermute | solution.py:358
  149.5 3.5 %collective-permute-done.26 = bf16[32,3072]{1,0:T(8,128)(2,1)S(1)} collective-permute-done((bf16[32,3072]{1,0:T(8,128)(2,1)S(1)}, bf16[32,3072]{1,0:T(8,128)(2,1)S(1)}, u32[]{:S(2)}, u32[]{:S(2)}) %collective-permute-start.26) | collective-permute-done | bytes 196640 | tf_op jit(solution)/shard_map/ppermute | solution.py:358
  153.2 0.9 pad_maximum_fusion
  (49 shorter events, 2.7 us)
Async XLA Ops:
  0.0 47.7 %collective-permute-start.10 = (bf16[512,6144]{1,0:T(8,128)(2,1)}, bf16[512,6144]{1,0:T(8,128)(2,1)}, u32[]{:S(2)}, u32[]{:S(2)}) collective-permute-start(bf16[512,6144]{1,0:T(8,128)(2,1)} %wa.3), channel_id=1, source_target_pairs={{0,1},{1,0},{2,3},{3,2},{4,5},{5,4},{6,7},{7,6},{8,9},{9,8},{10,11... | collective-permute-start | bytes 18874376 | tf_op jit(solution)/shard_map/ppermute | solution.py:358
  4.6 19.0 %collective-permute-start = (bf16[2048,128]{1,0:T(8,128)(2,1)}, bf16[2048,128]{1,0:T(8,128)(2,1)S(1)}, u32[]{:S(2)}, u32[]{:S(2)}) collective-permute-start(bf16[2048,128]{1,0:T(8,128)(2,1)} %prep.1.kv_ref.own_ref), channel_id=1, source_target_pairs={{0,112},{1,49},{2,114},{3,51},{4,116},{5,53},{6,118},{7,55},{8,120... | collective-permute-start | bytes 1572872 | tf_op jit(solution)/shard_map/ppermute | solution.py:358
  11.1 22.7 %collective-permute-start.1 = (bf16[2048,128]{1,0:T(8,128)(2,1)}, bf16[2048,128]{1,0:T(8,128)(2,1)S(1)}, u32[]{:S(2)}, u32[]{:S(2)}) collective-permute-start(bf16[2048,128]{1,0:T(8,128)(2,1)} %prep.1.kv_ref.own_ref), channel_id=1, source_target_pairs={{0,96},{1,33},{2,98},{3,35},{4,100},{5,37},{6,102},{7,39},{8,104},... | collective-permute-start | bytes 1572872 | tf_op jit(solution)/shard_map/ppermute | solution.py:358
  13.3 27.6 %collective-permute-start.2 = (bf16[2048,128]{1,0:T(8,128)(2,1)}, bf16[2048,128]{1,0:T(8,128)(2,1)S(1)}, u32[]{:S(2)}, u32[]{:S(2)}) collective-permute-start(bf16[2048,128]{1,0:T(8,128)(2,1)} %prep.1.kv_ref.own_ref), channel_id=1, source_target_pairs={{0,80},{1,17},{2,82},{3,19},{4,84},{5,21},{6,86},{7,23},{8,88},{9,... | collective-permute-start | bytes 1572872 | tf_op jit(solution)/shard_map/ppermute | solution.py:358
  15.3 25.6 %collective-permute-start.3 = (bf16[2048,128]{1,0:T(8,128)(2,1)}, bf16[2048,128]{1,0:T(8,128)(2,1)S(1)}, u32[]{:S(2)}, u32[]{:S(2)}) collective-permute-start(bf16[2048,128]{1,0:T(8,128)(2,1)} %prep.1.kv_ref.own_ref), channel_id=1, source_target_pairs={{0,64},{2,66},{4,68},{6,70},{8,72},{10,74},{12,76},{14,78},{16,80}... | collective-permute-start | bytes 1572872 | tf_op jit(solution)/shard_map/ppermute | solution.py:358
  16.0 1.0 copy-start
  17.0 1.2 copy-start.3
  18.2 25.7 %copy-start.1 = (bf16[2048,128]{1,0:T(8,128)(2,1)S(1)}, bf16[2048,128]{1,0:T(8,128)(2,1)}, u32[]{:S(2)}) copy-start(bf16[2048,128]{1,0:T(8,128)(2,1)} %prep.1.kv_ref.own_ref) | copy-start | bytes 1572868
  18.2 25.7 %copy-start.2 = (s32[13]{0:T(128)S(1)}, s32[13]{0:T(128)}, u32[]{:S(2)}) copy-start(s32[13]{0:T(128)} %stack.27.info) | copy-start | bytes 160
  23.6 17.8 %collective-permute-start.4 = (bf16[2048,128]{1,0:T(8,128)(2,1)S(1)}, bf16[2048,128]{1,0:T(8,128)(2,1)S(1)}, u32[]{:S(2)}, u32[]{:S(2)}) collective-permute-start(bf16[2048,128]{1,0:T(8,128)(2,1)S(1)} %collective-permute-done.refs_3_.refs_1_), channel_id=1, source_target_pairs={{0,1},{1,0},{2,3},{3,2},{4,5},{5,4},{6,7},{7,6},{8,9},{9,8},{10,11... | collective-permute-start | bytes 1572872 | tf_op jit(solution)/shard_map/ppermute | solution.py:358
  33.9 8.6 %collective-permute-start.5 = (bf16[2048,128]{1,0:T(8,128)(2,1)S(1)}, bf16[2048,128]{1,0:T(8,128)(2,1)S(1)}, u32[]{:S(2)}, u32[]{:S(2)}) collective-permute-start(bf16[2048,128]{1,0:T(8,128)(2,1)S(1)} %collective-permute-done.1.refs_4_.refs_2_), channel_id=1, source_target_pairs={{0,1},{1,0},{2,3},{3,2},{4,5},{5,4},{6,7},{7,6},{8,9},{9,8},{10,11... | collective-permute-start | bytes 1572872 | tf_op jit(solution)/shard_map/ppermute | solution.py:358
  40.9 2.3 %collective-permute-start.6 = (bf16[2048,128]{1,0:T(8,128)(2,1)S(1)}, bf16[2048,128]{1,0:T(8,128)(2,1)S(1)}, u32[]{:S(2)}, u32[]{:S(2)}) collective-permute-start(bf16[2048,128]{1,0:T(8,128)(2,1)S(1)} %collective-permute-done.2.refs_5_.refs_3_), channel_id=1, source_target_pairs={{0,1},{1,0},{2,3},{3,2},{4,5},{5,4},{6,7},{7,6},{8,9},{9,8},{10,11... | collective-permute-start | bytes 1572872 | tf_op jit(solution)/shard_map/ppermute | solution.py:358
  40.9 3.0 %collective-permute-start.7 = (bf16[2048,128]{1,0:T(8,128)(2,1)S(1)}, bf16[2048,128]{1,0:T(8,128)(2,1)S(1)}, u32[]{:S(2)}, u32[]{:S(2)}) collective-permute-start(bf16[2048,128]{1,0:T(8,128)(2,1)S(1)} %collective-permute-done.3.refs_6_.refs_4_), channel_id=1, source_target_pairs={{0,1},{1,0},{2,3},{3,2},{4,5},{5,4},{6,7},{7,6},{8,9},{9,8},{10,11... | collective-permute-start | bytes 1572872 | tf_op jit(solution)/shard_map/ppermute | solution.py:358
  41.4 18.1 %collective-permute-start.11 = (bf16[16,32,512]{2,1,0:T(8,128)(2,1)S(1)}, bf16[16,32,512]{2,1,0:T(8,128)(2,1)S(1)}, u32[]{:S(2)}, u32[]{:S(2)}) collective-permute-start(bf16[16,32,512]{2,1,0:T(8,128)(2,1)S(1)} %get-tuple-element.48), channel_id=1, source_target_pairs={{0,112},{1,113},{2,114},{3,115},{4,116},{5,117},{6,118},{7,119},{8... | collective-permute-start | bytes 1572872 | tf_op jit(solution)/shard_map/ppermute | solution.py:358
  43.9 3.7 %slice-start = ((s8[6291456]{0:T(1024)(128)(4,1)}), s8[4194304]{0:T(1024)(128)(4,1)S(1)}, s32[]{:S(2)}) async-start(s8[6291456]{0:T(1024)(128)(4,1)} %bitcast.7), calls=%async_computation | async-start | bytes 8388608
  43.9 3.7 %slice-start.1 = ((s8[6291456]{0:T(1024)(128)(4,1)}), s8[2097152]{0:T(1024)(128)(4,1)S(1)}, s32[]{:S(2)}) async-start(s8[6291456]{0:T(1024)(128)(4,1)} %bitcast.7), calls=%async_computation.1 | async-start | bytes 4194304
  45.7 1.6 %collective-permute-start.8 = (bf16[256,512]{1,0:T(8,128)(2,1)S(1)}, bf16[256,512]{1,0:T(8,128)(2,1)S(1)}, u32[]{:S(2)}, u32[]{:S(2)}) collective-permute-start(bf16[256,512]{1,0:T(8,128)(2,1)S(1)} %get-tuple-element.43), channel_id=1, source_target_pairs={{0,1},{1,0},{2,3},{3,2},{4,5},{5,4},{6,7},{7,6},{8,9},{9,8},{10,11... | collective-permute-start | bytes 786440 | tf_op jit(solution)/shard_map/ppermute | solution.py:358
  46.1 1.5 collective-permute-start.9
  53.6 28.1 %collective-permute-start.14 = (bf16[128,3072]{1,0:T(8,128)(2,1)S(1)}, bf16[128,3072]{1,0:T(8,128)(2,1)S(1)}, u32[]{:S(2)}, u32[]{:S(2)}) collective-permute-start(bf16[128,3072]{1,0:T(8,128)(2,1)S(1)} %get-tuple-element.53), channel_id=1, source_target_pairs={{0,2},{1,5},{2,0},{3,7},{4,6},{5,1},{6,4},{7,3},{8,10},{9,13},{10,... | collective-permute-start | bytes 2359304 | tf_op jit(solution)/shard_map/ppermute | solution.py:358
  55.0 26.7 %collective-permute-start.15 = (bf16[128,3072]{1,0:T(8,128)(2,1)S(1)}, bf16[128,3072]{1,0:T(8,128)(2,1)S(1)}, u32[]{:S(2)}, u32[]{:S(2)}) collective-permute-start(bf16[128,3072]{1,0:T(8,128)(2,1)S(1)} %get-tuple-element.54), channel_id=1, source_target_pairs={{0,2},{1,13},{2,0},{3,15},{4,6},{5,9},{6,4},{7,11},{8,10},{9,5},{1... | collective-permute-start | bytes 2359304 | tf_op jit(solution)/shard_map/ppermute | solution.py:358
  56.9 24.8 %collective-permute-start.16 = (bf16[128,3072]{1,0:T(8,128)(2,1)S(1)}, bf16[128,3072]{1,0:T(8,128)(2,1)S(1)}, u32[]{:S(2)}, u32[]{:S(2)}) collective-permute-start(bf16[128,3072]{1,0:T(8,128)(2,1)S(1)} %get-tuple-element.52.refs_1_), channel_id=1, source_target_pairs={{1,9},{3,11},{5,13},{7,15},{9,1},{11,3},{13,5},{15,7},{17,25},{19,... | collective-permute-start | bytes 2359304 | tf_op jit(solution)/shard_map/ppermute | solution.py:358
  79.7 1.6 %collective-permute-start.12 = (bf16[256,512]{1,0:T(8,128)(2,1)S(1)}, bf16[256,512]{1,0:T(8,128)(2,1)S(1)}, u32[]{:S(2)}, u32[]{:S(2)}) collective-permute-start(bf16[256,512]{1,0:T(8,128)(2,1)S(1)} %get-tuple-element.50), channel_id=1, source_target_pairs={{0,1},{1,0},{2,3},{3,2},{4,5},{5,4},{6,7},{7,6},{8,9},{9,8},{10,11... | collective-permute-start | bytes 786440 | tf_op jit(solution)/shard_map/ppermute | solution.py:358
  79.8 1.9 %collective-permute-start.13 = (bf16[256,512]{1,0:T(8,128)(2,1)S(1)}, bf16[256,512]{1,0:T(8,128)(2,1)S(1)}, u32[]{:S(2)}, u32[]{:S(2)}) collective-permute-start(bf16[256,512]{1,0:T(8,128)(2,1)S(1)} %get-tuple-element.51), channel_id=1, source_target_pairs={{0,1},{1,0},{2,3},{3,2},{4,5},{5,4},{6,7},{7,6},{8,9},{9,8},{10,11... | collective-permute-start | bytes 786440 | tf_op jit(solution)/shard_map/ppermute | solution.py:358
  88.8 0.7 copy-start.4
  89.5 0.7 copy-start.6
  90.2 0.7 copy-start.7
  91.0 11.2 %collective-permute-start.17 = (bf16[128,3072]{1,0:T(8,128)(2,1)S(1)}, bf16[128,3072]{1,0:T(8,128)(2,1)}, u32[]{:S(2)}, u32[]{:S(2)}) collective-permute-start(bf16[128,3072]{1,0:T(8,128)(2,1)S(1)} %get-tuple-element.57), channel_id=1, source_target_pairs={{0,4},{1,3},{2,6},{3,1},{4,0},{5,7},{6,2},{7,5},{8,12},{9,11},{10,... | collective-permute-start | bytes 2359304 | tf_op jit(solution)/shard_map/ppermute | solution.py:358
  91.4 19.3 %collective-permute-start.18 = (bf16[128,3072]{1,0:T(8,128)(2,1)S(1)}, bf16[128,3072]{1,0:T(8,128)(2,1)}, u32[]{:S(2)}, u32[]{:S(2)}) collective-permute-start(bf16[128,3072]{1,0:T(8,128)(2,1)S(1)} %get-tuple-element.58), channel_id=1, source_target_pairs={{0,12},{1,3},{2,14},{3,1},{4,8},{5,7},{6,10},{7,5},{8,4},{9,11},{1... | collective-permute-start | bytes 2359304 | tf_op jit(solution)/shard_map/ppermute | solution.py:358
  92.5 18.2 %collective-permute-start.19 = (bf16[128,3072]{1,0:T(8,128)(2,1)S(1)}, bf16[128,3072]{1,0:T(8,128)(2,1)}, u32[]{:S(2)}, u32[]{:S(2)}) collective-permute-start(bf16[128,3072]{1,0:T(8,128)(2,1)S(1)} %get-tuple-element.59), channel_id=1, source_target_pairs={{0,8},{2,10},{4,12},{6,14},{8,0},{10,2},{12,4},{14,6},{16,24},{18,... | collective-permute-start | bytes 2359304 | tf_op jit(solution)/shard_map/ppermute | solution.py:358
  94.0 24.5 %collective-permute-start.20 = (bf16[64,3072]{1,0:T(8,128)(2,1)}, bf16[64,3072]{1,0:T(8,128)(2,1)S(1)}, u32[]{:S(2)}, u32[]{:S(2)}) collective-permute-start(bf16[64,3072]{1,0:T(8,128)(2,1)} %copy-done.7), channel_id=1, source_target_pairs={{0,4},{1,3},{2,6},{3,1},{4,0},{5,7},{6,2},{7,5},{8,12},{9,11},{10,... | collective-permute-start | bytes 1179656 | tf_op jit(solution)/shard_map/ppermute | solution.py:358
  94.4 26.8 %collective-permute-start.21 = (bf16[64,3072]{1,0:T(8,128)(2,1)}, bf16[64,3072]{1,0:T(8,128)(2,1)S(1)}, u32[]{:S(2)}, u32[]{:S(2)}) collective-permute-start(bf16[64,3072]{1,0:T(8,128)(2,1)} %copy-done.6), channel_id=1, source_target_pairs={{0,12},{2,14},{4,8},{6,10},{8,4},{10,6},{12,0},{14,2},{16,28},{18,... | collective-permute-start | bytes 1179656 | tf_op jit(solution)/shard_map/ppermute | solution.py:358
  110.7 4.1 %copy-start.5 = (bf16[64,3072]{1,0:T(8,128)(2,1)S(1)}, bf16[64,3072]{1,0:T(8,128)(2,1)}, u32[]{:S(2)}) copy-start(bf16[64,3072]{1,0:T(8,128)(2,1)} %copy-done.4) | copy-start | bytes 1179652
  113.0 20.8 %collective-permute-start.23 = (bf16[64,3072]{1,0:T(8,128)(2,1)S(1)}, bf16[64,3072]{1,0:T(8,128)(2,1)S(1)}, u32[]{:S(2)}, u32[]{:S(2)}) collective-permute-start(bf16[64,3072]{1,0:T(8,128)(2,1)S(1)} %fusion.4), channel_id=1, source_target_pairs={{0,2},{1,5},{2,0},{3,7},{4,6},{5,1},{6,4},{7,3},{8,10},{9,13},{10,... | collective-permute-start | bytes 1179656 | tf_op jit(solution)/shard_map/ppermute | solution.py:358
  114.8 6.4 %collective-permute-start.22 = (bf16[64,3072]{1,0:T(8,128)(2,1)S(1)}, bf16[64,3072]{1,0:T(8,128)(2,1)S(1)}, u32[]{:S(2)}, u32[]{:S(2)}) collective-permute-start(bf16[64,3072]{1,0:T(8,128)(2,1)S(1)} %copy-done.5), channel_id=1, source_target_pairs={{0,8},{2,10},{4,12},{6,14},{8,0},{10,2},{12,4},{14,6},{16,24},{18,... | collective-permute-start | bytes 1179656 | tf_op jit(solution)/shard_map/ppermute | solution.py:358
  115.5 18.3 %collective-permute-start.24 = (bf16[64,3072]{1,0:T(8,128)(2,1)S(1)}, bf16[64,3072]{1,0:T(8,128)(2,1)S(1)}, u32[]{:S(2)}, u32[]{:S(2)}) collective-permute-start(bf16[64,3072]{1,0:T(8,128)(2,1)S(1)} %get-tuple-element.69), channel_id=1, source_target_pairs={{1,13},{3,15},{5,9},{7,11},{9,5},{11,7},{13,1},{15,3},{17,29},{19,... | collective-permute-start | bytes 1179656 | tf_op jit(solution)/shard_map/ppermute | solution.py:358
  118.5 15.4 %collective-permute-start.25 = (bf16[64,3072]{1,0:T(8,128)(2,1)S(1)}, bf16[64,3072]{1,0:T(8,128)(2,1)S(1)}, u32[]{:S(2)}, u32[]{:S(2)}) collective-permute-start(bf16[64,3072]{1,0:T(8,128)(2,1)S(1)} %get-tuple-element.70), channel_id=1, source_target_pairs={{1,9},{3,11},{5,13},{7,15},{9,1},{11,3},{13,5},{15,7},{17,25},{19,... | collective-permute-start | bytes 1179656 | tf_op jit(solution)/shard_map/ppermute | solution.py:358
  121.4 24.2 %collective-permute-start.27 = (bf16[32,3072]{1,0:T(8,128)(2,1)S(1)}, bf16[32,3072]{1,0:T(8,128)(2,1)S(1)}, u32[]{:S(2)}, u32[]{:S(2)}) collective-permute-start(bf16[32,3072]{1,0:T(8,128)(2,1)S(1)} %get-tuple-element.74), channel_id=1, source_target_pairs={{0,1},{1,0},{2,3},{3,2},{4,5},{5,4},{6,7},{7,6},{8,9},{9,8},{10,11... | collective-permute-start | bytes 589832 | tf_op jit(solution)/shard_map/ppermute | solution.py:358
  134.1 15.4 %collective-permute-start.28 = (bf16[32,3072]{1,0:T(8,128)(2,1)S(1)}, bf16[32,3072]{1,0:T(8,128)(2,1)S(1)}, u32[]{:S(2)}, u32[]{:S(2)}) collective-permute-start(bf16[32,3072]{1,0:T(8,128)(2,1)S(1)} %get-tuple-element.76), channel_id=1, source_target_pairs={{0,113},{1,112},{2,115},{3,114},{4,117},{5,116},{6,119},{7,118},{8... | collective-permute-start | bytes 589832 | tf_op jit(solution)/shard_map/ppermute | solution.py:358
  144.5 8.5 %collective-permute-start.26 = (bf16[32,3072]{1,0:T(8,128)(2,1)S(1)}, bf16[32,3072]{1,0:T(8,128)(2,1)S(1)}, u32[]{:S(2)}, u32[]{:S(2)}) collective-permute-start(bf16[32,3072]{1,0:T(8,128)(2,1)S(1)} %get-tuple-element.75), channel_id=1, source_target_pairs={{0,112},{1,113},{2,114},{3,115},{4,116},{5,117},{6,118},{7,119},{8... | collective-permute-start | bytes 589832 | tf_op jit(solution)/shard_map/ppermute | solution.py:358

commit v8 on v7

--- a/solution.py
+++ b/solution.py
@@ -14,7 +14,7 @@
 LIMIT = 60.0
 BF = jnp.bfloat16
 F32 = jnp.float32
-PARAMS = pltpu.CompilerParams(vmem_limit_bytes=28 << 20)
+PARAMS = pltpu.CompilerParams(vmem_limit_bytes=22 << 20)
 FETCH = ((7, 3), (6, 2), (5, 1), (4, None))
 SLOTS = [d for pair in FETCH for d in pair if d is not None]
 TABLE = 6
@@ -60,32 +60,38 @@
 
 
 def load_queries(q, h, qt_ref):
-    qb = q.shape[0]
+    heads = KV_HEADS // 2
     scaled = q.astype(F32) * (DH**-0.5 * LOG2E)
     high = scaled.astype(BF)
     low = (scaled - high.astype(F32)).astype(BF)
-    qt_ref[0:DH, h * qb : (h + 1) * qb] = high.T
-    qt_ref[DH : 2 * DH, h * qb : (h + 1) * qb] = low.T
-
-
-def exact_block(kv, behind, second, groups, qt_ref, acc, m_ref):
+    high, low = high.T, low.T
+    for seg in range(q.shape[0] // DH):
+        c = slice((seg * heads + h) * DH, (seg * heads + h + 1) * DH)
+        rows = slice(seg * DH, (seg + 1) * DH)
+        qt_ref[0:DH, c] = high[:, rows]
+        qt_ref[DH : 2 * DH, c] = low[:, rows]
+
+
+def diagonal_block(kv, second, groups, qt_ref, acc, m_ref):
     rows = kv.shape[0] // 2
-    heads = KV_HEADS // 2
-    qb = qt_ref.shape[1] // heads
-    sub = qb // groups
+    cols = qt_ref.shape[1]
+    width = KV_HEADS // 2 * DH
+    segs = cols // width
+    quarter = rows // segs
+    sub = segs * DH // groups
     kk, vt = keys_of(kv), values_of(kv)
-    j = lax.broadcasted_iota(jnp.int32, (rows, qb), 1)
-    pos = behind * rows + j // sub * (rows // groups) + second * sub + j % sub
-    allowed = lax.broadcasted_iota(jnp.int32, (rows, qb), 0) <= pos
-    for h in range(heads):
-        c = slice(h * qb, (h + 1) * qb)
-        s = jnp.where(allowed, jnp.dot(kk, qt_ref[:, c], preferred_element_type=F32), NEG)
-        m = m_ref[0:1, c]
-        top = jnp.maximum(m, jnp.max(s, axis=0, keepdims=True))
-        acc[:, c] = acc[:, c] * jnp.exp2(m - top) + jnp.dot(
-            vt, jnp.exp2(s - top).astype(BF), preferred_element_type=F32
-        )
-        m_ref[:, c] = jnp.broadcast_to(top, (8, qb))
+    j = lax.broadcasted_iota(jnp.int32, (quarter, width), 1) % DH
+    pos = j // sub * (rows // groups) + second * sub + j % sub
+    allowed = lax.broadcasted_iota(jnp.int32, (quarter, width), 0) <= pos
+    for seg in range(segs):
+        c = slice(seg * width, (seg + 1) * width)
+        n = (seg + 1) * quarter
+        s = jnp.dot(kk[:n], qt_ref[:, c], preferred_element_type=F32)
+        last = jnp.where(allowed, s[n - quarter :], NEG)
+        s = last if seg == 0 else jnp.concatenate([s[: n - quarter], last], axis=0)
+        m = jnp.max(s, axis=0, keepdims=True)
+        acc[:, c] = jnp.dot(vt[:, :n], jnp.exp2(s - m).astype(BF), preferred_element_type=F32)
+        m_ref[:, c] = jnp.broadcast_to(m, (8, width))
 
 
 def own_kernel(groups, q_ref, away_ref, kv_ref, qt_ref, acc_ref, m_ref, send_ref):
@@ -93,9 +99,7 @@
     _, _, sub, width = q_ref.shape
     for h in range(width // DH):
         load_queries(q_ref[:, 0, :, h * DH : (h + 1) * DH].reshape(groups * sub, DH), h, qt_ref)
-    acc_ref[...] = jnp.zeros_like(acc_ref)
-    m_ref[...] = jnp.full_like(m_ref, NEG)
-    exact_block(kv_ref, 0, 0, groups, qt_ref, acc_ref, m_ref)
+    diagonal_block(kv_ref, 0, groups, qt_ref, acc_ref, m_ref)
 
 
 def own(q4, kv):
@@ -188,11 +192,8 @@
     if foreign:
         for h in range(heads):
             load_queries(q_buf[:, :, h * DH : (h + 1) * DH].reshape(qb, DH), h, qt_ref)
-        acc_ref[0] = jnp.zeros(acc_ref.shape[1:], F32)
-        m_ref[...] = jnp.full_like(m_ref, NEG)
-
         wait(1)
-        exact_block(kv_buf.at[1], 0, 1, groups, qt_ref, acc_ref.at[0], m_ref)
+        diagonal_block(kv_buf.at[1], 1, groups, qt_ref, acc_ref.at[0], m_ref)
 
     def scores(kk, c0):
         return jnp.dot(kk, qt_ref[:, c0 : c0 + half], preferred_element_type=F32)
@@ -231,19 +232,22 @@
 
     lax.fori_loop(0, n + 1, add_block, 0)
     last = count[0] % 2
-    for h in range(heads):
-        o = acc_ref[last, :, h * qb : (h + 1) * qb]
-        o = (o[0:DH] * (1.0 / o[DH : DH + 1])).astype(BF).T
-        for g in range(groups):
-            ry = (g // 4) ^ info[3]
-            rz = (g // 2 % 2) ^ info[4]
-            by_y = ((ry * 2 + rz) * 2 + g % 2) * sub
-            by_z = (((ry // 2 * 2 + rz) * 2 + ry % 2) * 2 + g % 2) * sub
-            piece = o[g * sub : (g + 1) * sub, :]
-            here = pl.multiple_of(jnp.where(y_first, by_y, by_z), sub)
-            there = pl.multiple_of(jnp.where(y_first, by_z, by_y), sub)
-            o_ref[pl.ds(here, sub), h * DH : (h + 1) * DH] = piece
-            peer_buf[pl.ds(there, sub), h * DH : (h + 1) * DH] = piece
+    per_seg = groups * DH // qb
+    for seg in range(qb // DH):
+        for h in range(heads):
+            o = acc_ref[last, :, (seg * heads + h) * DH : (seg * heads + h + 1) * DH]
+            o = (o[0:DH] * (1.0 / o[DH : DH + 1])).astype(BF).T
+            for k in range(per_seg):
+                g = seg * per_seg + k
+                ry = (g // 4) ^ info[3]
+                rz = (g // 2 % 2) ^ info[4]
+                by_y = ((ry * 2 + rz) * 2 + g % 2) * sub
+                by_z = (((ry // 2 * 2 + rz) * 2 + ry % 2) * 2 + g % 2) * sub
+                piece = o[k * sub : (k + 1) * sub, :]
+                here = pl.multiple_of(jnp.where(y_first, by_y, by_z), sub)
+                there = pl.multiple_of(jnp.where(y_first, by_z, by_y), sub)
+                o_ref[pl.ds(here, sub), h * DH : (h + 1) * DH] = piece
+                peer_buf[pl.ds(there, sub), h * DH : (h + 1) * DH] = piece
     first_ref[...] = peer_buf[: qb // 2, :]
     second_ref[...] = peer_buf[qb // 2 :, :]
 
@@ -418,8 +422,8 @@
     got2_n = stage_two((a0, a1, after(b0, total_f[0]), b1), 1)
     got2_f = stage_two(total_f, 0)
     done_f = add(total_f[0], *got2_f).reshape(2, sub, cols // 2)
-    done_n = add(after(a0, total_f[0]), *got2_n).reshape(2, sub, cols // 2)
-    own_other = swap_core(by_core(done_n, False))
+    done_n = add(after(a0, by_core(done_f, True)), *got2_n).reshape(2, sub, cols // 2)
+    own_other = swap_core(after(by_core(done_n, False), done_f))
     home = over_all(by_core(done_f, True), lambda s, y, z, c: (n_seq - 1 - s, y, z, c))
     home_other = over_all(by_core(done_f, False), lambda s, y, z, c: (n_seq - 1 - s, y, z, 1 - c))
     here = jnp.concatenate([by_core(done_n, True), home], axis=0)

time: 156 us -> 163 us (1.045)
  waiting for transfers between devices: 33.7 us -> 52.4 us
  starting transfers between devices: 69.4 us -> 60.9 us
  Pallas kernels: 41.6 us -> 38.6 us
    ppermute x29, waiting for transfers between devices: 33.7 us -> 52.4 us  [over_all(): return lax.ppermute(x, ('seq', 'head'), pairs)]
    ppermute x29, starting transfers between devices: 69.4 us -> 60.9 us  [over_all(): return lax.ppermute(x, ('seq', 'head'), pairs)]
    convert_element_type x0 -> x1, other arithmetic: none -> 2.29 us  [sum_one(): a = (first + jnp.where(core == 0, extra, 0.0)).astype(BF)]
    unnamed x21 -> x25, local copies, waits for them, and re-layouts: 4.52 us -> 4.52 us
  transfers between devices with their start and end apart: 29 -> 29, of which waited for: 13 -> 14; matrix products, arithmetic and copies ran while one was open for 2% -> 1% of each run, Pallas kernels for 22% -> 19%
where the time goes in v8:
time: 163 us; the launch traced here: 162 us
  starting transfers between devices  60.9 us (37%)
  waiting for transfers between devices  52.4 us (32%)
  Pallas kernels  38.6 us (24%)
  local copies, waits for them, and re-layouts  5.26 us (3%)
  other arithmetic  5.06 us (3%)
    ppermute x29, starting transfers between devices, over_all(): return lax.ppermute(x, ('seq', 'head'), pairs)  60.9 us
    ppermute x29, waiting for transfers between devices, over_all(): return lax.ppermute(x, ('seq', 'head'), pairs)  52.4 us
    pallas_call x2, Pallas kernels, attend(): pl.pallas_call(functools.partial(attend_kernel, foreign, groups, n_y, n_s...  20.5 us
    pallas_call x2, Pallas kernels, project(): pl.pallas_call(body, grid_spec=pltpu.PrefetchScalarGridSpec(num_scalar_pr...  12.9 us
    unnamed x25, local copies, waits for them, and re-layouts  4.52 us
  transfers between devices with their start and end apart: 29, of which 14 were waited for; matrix products, arithmetic and copies ran while one was open for 1% of the time, Pallas kernels for 19%

profile of v8, /device:TPU:1, one launch (start us, length us, event | category | flops | bytes accessed | tf_op | source)
XLA Modules:
  0.0 162.5 jit_solution(6949687411475657535)
XLA Ops:
  0.0 1.4 collective-permute-start.10
  1.4 0.6 stack.27.info
  2.1 2.6 %prep.1.kv_ref.own_ref = bf16[2048,128]{1,0:T(8,128)(2,1)} custom-call(s32[13]{0:T(128)} %stack.27.info, bf16[1024,1024]{1,0:T(8,128)(2,1)} %k_ref.1, bf16[1024,1024]{1,0:T(8,128)(2,1)} %v_ref.1), custom_call_target="tpu_custom_call" | custom-call | tf_op jit(solution)/shard_map/prep/pallas_call | solution.py:37
  4.7 6.5 %collective-permute-start = (bf16[2048,128]{1,0:T(8,128)(2,1)}, bf16[2048,128]{1,0:T(8,128)(2,1)S(1)}, u32[]{:S(2)}, u32[]{:S(2)}) collective-permute-start(bf16[2048,128]{1,0:T(8,128)(2,1)} %prep.1.kv_ref.own_ref), channel_id=1, source_target_pairs={{0,112},{1,49},{2,114},{3,51},{4,116},{5,53},{6,118},{7,55},{8,120... | collective-permute-start | bytes 1572872 | tf_op jit(solution)/shard_map/ppermute | solution.py:362
  11.2 2.2 %collective-permute-start.1 = (bf16[2048,128]{1,0:T(8,128)(2,1)}, bf16[2048,128]{1,0:T(8,128)(2,1)S(1)}, u32[]{:S(2)}, u32[]{:S(2)}) collective-permute-start(bf16[2048,128]{1,0:T(8,128)(2,1)} %prep.1.kv_ref.own_ref), channel_id=1, source_target_pairs={{0,96},{1,33},{2,98},{3,35},{4,100},{5,37},{6,102},{7,39},{8,104},... | collective-permute-start | bytes 1572872 | tf_op jit(solution)/shard_map/ppermute | solution.py:362
  13.4 1.9 %collective-permute-start.2 = (bf16[2048,128]{1,0:T(8,128)(2,1)}, bf16[2048,128]{1,0:T(8,128)(2,1)S(1)}, u32[]{:S(2)}, u32[]{:S(2)}) collective-permute-start(bf16[2048,128]{1,0:T(8,128)(2,1)} %prep.1.kv_ref.own_ref), channel_id=1, source_target_pairs={{0,80},{1,17},{2,82},{3,19},{4,84},{5,21},{6,86},{7,23},{8,88},{9,... | collective-permute-start | bytes 1572872 | tf_op jit(solution)/shard_map/ppermute | solution.py:362
  15.3 0.7 collective-permute-start.3
  16.0 1.0 copy-done
  17.1 1.2 copy-done.3
  18.3 2.6 %own.1 = (bf16[256,2048]{1,0:T(8,128)(2,1)S(1)}, f32[144,2048]{1,0:T(8,128)S(1)}, f32[8,2048]{1,0:T(8,128)S(1)}, bf16[16,32,512]{2,1,0:T(8,128)(2,1)S(1)}) custom-call(bf16[16,2,32,512]{3,2,1,0:T(8,128)(2,1)S(1)} %bitcast.9, bf16[16,2,32,512]{3,2,1,0:T(8,128)(2,1)S(1)} %bitcast.10, bf16[2048,128]{1,0:T(8,128)(2,1)S(1)} %copy-done), custom_call_target="tpu_custom_call" | custom-call | flops 2147483648 | bytes 8388608 | tf_op jit(solution)/shard_map/own/pallas_call | solution.py:108
  20.9 2.7 %collective-permute-done.refs_3_.refs_1_ = bf16[2048,128]{1,0:T(8,128)(2,1)S(1)} collective-permute-done((bf16[2048,128]{1,0:T(8,128)(2,1)}, bf16[2048,128]{1,0:T(8,128)(2,1)S(1)}, u32[]{:S(2)}, u32[]{:S(2)}) %collective-permute-start) | collective-permute-done | bytes 524320 | tf_op jit(solution)/shard_map/ppermute | solution.py:362
  23.7 4.8 %collective-permute-start.4 = (bf16[2048,128]{1,0:T(8,128)(2,1)S(1)}, bf16[2048,128]{1,0:T(8,128)(2,1)S(1)}, u32[]{:S(2)}, u32[]{:S(2)}) collective-permute-start(bf16[2048,128]{1,0:T(8,128)(2,1)S(1)} %collective-permute-done.refs_3_.refs_1_), channel_id=1, source_target_pairs={{0,1},{1,0},{2,3},{3,2},{4,5},{5,4},{6,7},{7,6},{8,9},{9,8},{10,11... | collective-permute-start | bytes 1572872 | tf_op jit(solution)/shard_map/ppermute | solution.py:362
  28.5 5.4 %collective-permute-done.1.refs_4_.refs_2_ = bf16[2048,128]{1,0:T(8,128)(2,1)S(1)} collective-permute-done((bf16[2048,128]{1,0:T(8,128)(2,1)}, bf16[2048,128]{1,0:T(8,128)(2,1)S(1)}, u32[]{:S(2)}, u32[]{:S(2)}) %collective-permute-start.1) | collective-permute-done | bytes 524320 | tf_op jit(solution)/shard_map/ppermute | solution.py:362
  33.9 7.0 %collective-permute-start.5 = (bf16[2048,128]{1,0:T(8,128)(2,1)S(1)}, bf16[2048,128]{1,0:T(8,128)(2,1)S(1)}, u32[]{:S(2)}, u32[]{:S(2)}) collective-permute-start(bf16[2048,128]{1,0:T(8,128)(2,1)S(1)} %collective-permute-done.1.refs_4_.refs_2_), channel_id=1, source_target_pairs={{0,1},{1,0},{2,3},{3,2},{4,5},{5,4},{6,7},{7,6},{8,9},{9,8},{10,11... | collective-permute-start | bytes 1572872 | tf_op jit(solution)/shard_map/ppermute | solution.py:362
  41.0 0.5 collective-permute-start.7
  41.5 1.0 collective-permute-start.11
  42.5 0.7 collective-permute-done.6.refs_9_.refs_7_
  43.2 0.7 collective-permute-done.7.refs_10_.refs_8_
  44.0 1.6 attend_own.1
  46.2 1.0 collective-permute-done.8.b0
  47.6 5.9 %project.1 = (bf16[128,3072]{1,0:T(8,128)(2,1)S(1)}, bf16[128,3072]{1,0:T(8,128)(2,1)S(1)}, bf16[128,3072]{1,0:T(8,128)(2,1)S(1)}, bf16[128,3072]{1,0:T(8,128)(2,1)S(1)}) custom-call(s32[13]{0:T(128)S(1)} %copy-done.2, bf16[512,512]{1,0:T(8,128)(2,1)S(1)} %get-tuple-element.42.a, bf16[256,512]{1,0:T(8,128)(2,1)S(1)} %collective-permute-done.8.b0, ...), custom_call_target="tpu_custom_call" | custom-call | tf_op jit(solution)/shard_map/project/pallas_call | solution.py:321
  53.5 1.4 collective-permute-start.14
  54.9 1.9 %collective-permute-start.15 = (bf16[128,3072]{1,0:T(8,128)(2,1)S(1)}, bf16[128,3072]{1,0:T(8,128)(2,1)S(1)}, u32[]{:S(2)}, u32[]{:S(2)}) collective-permute-start(bf16[128,3072]{1,0:T(8,128)(2,1)S(1)} %get-tuple-element.54), channel_id=1, source_target_pairs={{0,2},{1,13},{2,0},{3,15},{4,6},{5,9},{6,4},{7,11},{8,10},{9,5},{1... | collective-permute-start | bytes 2359304 | tf_op jit(solution)/shard_map/ppermute | solution.py:362
  56.8 2.6 %collective-permute-start.16 = (bf16[128,3072]{1,0:T(8,128)(2,1)S(1)}, bf16[128,3072]{1,0:T(8,128)(2,1)S(1)}, u32[]{:S(2)}, u32[]{:S(2)}) collective-permute-start(bf16[128,3072]{1,0:T(8,128)(2,1)S(1)} %get-tuple-element.52.refs_1_), channel_id=1, source_target_pairs={{1,9},{3,11},{5,13},{7,15},{9,1},{11,3},{13,5},{15,7},{17,25},{19,... | collective-permute-start | bytes 2359304 | tf_op jit(solution)/shard_map/ppermute | solution.py:362
  59.5 18.9 %attend_foreign.1 = (bf16[512,512]{1,0:T(8,128)(2,1)S(1)}, bf16[256,512]{1,0:T(8,128)(2,1)S(1)}, bf16[256,512]{1,0:T(8,128)(2,1)S(1)}) custom-call(s32[13]{0:T(128)S(1)} %copy-done.2, bf16[2048,128]{1,0:T(8,128)(2,1)S(1)} %copy-done.1, bf16[16,32,512]{2,1,0:T(8,128)(2,1)S(1)} %collective-permute-done.11.refs_0_, ...), custom_call_target="tpu_custom_call" | custom-call | flops 4294967296 | bytes 4194304 | tf_op jit(solution)/shard_map/attend_foreign/pallas_call | solution.py:263
  78.4 0.5 collective-permute-start.13
  78.9 1.0 collective-permute-done.12.b0
  80.4 6.9 %project_and_sum.1 = (bf16[128,3072]{1,0:T(8,128)(2,1)S(1)}, bf16[128,3072]{1,0:T(8,128)(2,1)S(1)}, bf16[128,3072]{1,0:T(8,128)(2,1)S(1)}, bf16[128,3072]{1,0:T(...) custom-call(s32[13]{0:T(128)S(1)} %copy-done.2, ...), custom_call_target="tpu_custom_call" | custom-call | tf_op jit(solution)/shard_map/project_and_sum/pallas_call | solution.py:321
  87.3 0.7 copy-done.4
  88.1 0.7 copy-done.6
  88.8 0.7 copy-done.8
  89.9 1.1 collective-permute-start.18
  91.0 1.6 collective-permute-start.19
  92.6 8.2 %collective-permute-done.17 = bf16[128,3072]{1,0:T(8,128)(2,1)} collective-permute-done((bf16[128,3072]{1,0:T(8,128)(2,1)S(1)}, bf16[128,3072]{1,0:T(8,128)(2,1)}, u32[]{:S(2)}, u32[]{:S(2)}) %collective-permute-start.17) | collective-permute-done | bytes 786464 | tf_op jit(solution)/shard_map/ppermute | solution.py:362
  100.8 8.4 %collective-permute-done.18 = bf16[128,3072]{1,0:T(8,128)(2,1)} collective-permute-done((bf16[128,3072]{1,0:T(8,128)(2,1)S(1)}, bf16[128,3072]{1,0:T(8,128)(2,1)}, u32[]{:S(2)}, u32[]{:S(2)}) %collective-permute-start.18) | collective-permute-done | bytes 786464 | tf_op jit(solution)/shard_map/ppermute | solution.py:362
  109.2 2.3 %fusion.2 = (bf16[128,3072]{1,0:T(8,128)(2,1)S(1)}, bf16[128,3072]{1,0:T(8,128)(2,1)S(1)}) fusion(bf16[128,3072]{1,0:T(8,128)(2,1)} %collective-permute-done.18, bf16[128,3072]{1,0:T(8,128)(2,1)} %collective-permute-done.19, bf16[128,3072]{1,0:T(8,128)(2,1)} %collective-permute-done.17, bf16[128,3072]{1,0:T(8,128)(2,1)S(1)} %get-tuple-element.56, pred[]{:T(512)S(6)} %eq.7, ...), kind=kLoop, calls=%fused_computation.4 | loop fusion | flops 4718592 | bytes 5505025 | tf_op jit(solution)/shard_map/convert_element_type | solution.py:395
  111.6 6.2 %collective-permute-start.21 = (bf16[64,3072]{1,0:T(8,128)(2,1)S(1)}, bf16[64,3072]{1,0:T(8,128)(2,1)}, u32[]{:S(2)}, u32[]{:S(2)}) collective-permute-start(bf16[64,3072]{1,0:T(8,128)(2,1)S(1)} %get-tuple-element.69), channel_id=1, source_target_pairs={{1,13},{3,15},{5,9},{7,11},{9,5},{11,7},{13,1},{15,3},{17,29},{19,... | collective-permute-start | bytes 1179656 | tf_op jit(solution)/shard_map/ppermute | solution.py:362
  117.8 1.9 %collective-permute-start.22 = (bf16[64,3072]{1,0:T(8,128)(2,1)S(1)}, bf16[64,3072]{1,0:T(8,128)(2,1)}, u32[]{:S(2)}, u32[]{:S(2)}) collective-permute-start(bf16[64,3072]{1,0:T(8,128)(2,1)S(1)} %get-tuple-element.70), channel_id=1, source_target_pairs={{1,9},{3,11},{5,13},{7,15},{9,1},{11,3},{13,5},{15,7},{17,25},{19,... | collective-permute-start | bytes 1179656 | tf_op jit(solution)/shard_map/ppermute | solution.py:362
  119.8 0.7 collective-permute-start.20
  120.4 0.7 collective-permute-start.25
  121.2 8.2 %collective-permute-done.21 = bf16[64,3072]{1,0:T(8,128)(2,1)} collective-permute-done((bf16[64,3072]{1,0:T(8,128)(2,1)S(1)}, bf16[64,3072]{1,0:T(8,128)(2,1)}, u32[]{:S(2)}, u32[]{:S(2)}) %collective-permute-start.21) | collective-permute-done | bytes 393248 | tf_op jit(solution)/shard_map/ppermute | solution.py:362
  129.4 0.7 collective-permute-start.24
  130.1 4.6 %collective-permute-done.20 = bf16[64,3072]{1,0:T(8,128)(2,1)} collective-permute-done((bf16[64,3072]{1,0:T(8,128)(2,1)S(1)}, bf16[64,3072]{1,0:T(8,128)(2,1)}, u32[]{:S(2)}, u32[]{:S(2)}) %collective-permute-start.20) | collective-permute-done | bytes 393248 | tf_op jit(solution)/shard_map/ppermute | solution.py:362
  134.7 1.4 add_convert_fusion.1
  136.5 2.7 %collective-permute-start.27 = (bf16[32,3072]{1,0:T(8,128)(2,1)S(1)}, bf16[32,3072]{1,0:T(8,128)(2,1)S(1)}, u32[]{:S(2)}, u32[]{:S(2)}) collective-permute-start(bf16[32,3072]{1,0:T(8,128)(2,1)S(1)} %get-tuple-element.72), channel_id=1, source_target_pairs={{0,1},{1,0},{2,3},{3,2},{4,5},{5,4},{6,7},{7,6},{8,9},{9,8},{10,11... | collective-permute-start | bytes 589832 | tf_op jit(solution)/shard_map/ppermute | solution.py:362
  139.2 11.7 %collective-permute-start.26 = (bf16[32,3072]{1,0:T(8,128)(2,1)S(1)}, bf16[32,3072]{1,0:T(8,128)(2,1)S(1)}, u32[]{:S(2)}, u32[]{:S(2)}) collective-permute-start(bf16[32,3072]{1,0:T(8,128)(2,1)S(1)} %get-tuple-element.74), channel_id=1, source_target_pairs={{0,112},{1,113},{2,114},{3,115},{4,116},{5,117},{6,118},{7,119},{8... | collective-permute-start | bytes 589832 | tf_op jit(solution)/shard_map/ppermute | solution.py:362
  151.0 10.4 %collective-permute-done.28 = bf16[32,3072]{1,0:T(8,128)(2,1)S(1)} collective-permute-done((bf16[32,3072]{1,0:T(8,128)(2,1)S(1)}, bf16[32,3072]{1,0:T(8,128)(2,1)S(1)}, u32[]{:S(2)}, u32[]{:S(2)}) %collective-permute-start.28) | collective-permute-done | bytes 196640 | tf_op jit(solution)/shard_map/ppermute | solution.py:362
  161.6 0.9 pad_maximum_fusion
  (53 shorter events, 2.6 us)
Async XLA Ops:
  0.0 47.6 %collective-permute-start.10 = (bf16[512,6144]{1,0:T(8,128)(2,1)}, bf16[512,6144]{1,0:T(8,128)(2,1)}, u32[]{:S(2)}, u32[]{:S(2)}) collective-permute-start(bf16[512,6144]{1,0:T(8,128)(2,1)} %wa.3), channel_id=1, source_target_pairs={{0,1},{1,0},{2,3},{3,2},{4,5},{5,4},{6,7},{7,6},{8,9},{9,8},{10,11... | collective-permute-start | bytes 18874376 | tf_op jit(solution)/shard_map/ppermute | solution.py:362
  4.7 19.0 %collective-permute-start = (bf16[2048,128]{1,0:T(8,128)(2,1)}, bf16[2048,128]{1,0:T(8,128)(2,1)S(1)}, u32[]{:S(2)}, u32[]{:S(2)}) collective-permute-start(bf16[2048,128]{1,0:T(8,128)(2,1)} %prep.1.kv_ref.own_ref), channel_id=1, source_target_pairs={{0,112},{1,49},{2,114},{3,51},{4,116},{5,53},{6,118},{7,55},{8,120... | collective-permute-start | bytes 1572872 | tf_op jit(solution)/shard_map/ppermute | solution.py:362
  11.2 22.7 %collective-permute-start.1 = (bf16[2048,128]{1,0:T(8,128)(2,1)}, bf16[2048,128]{1,0:T(8,128)(2,1)S(1)}, u32[]{:S(2)}, u32[]{:S(2)}) collective-permute-start(bf16[2048,128]{1,0:T(8,128)(2,1)} %prep.1.kv_ref.own_ref), channel_id=1, source_target_pairs={{0,96},{1,33},{2,98},{3,35},{4,100},{5,37},{6,102},{7,39},{8,104},... | collective-permute-start | bytes 1572872 | tf_op jit(solution)/shard_map/ppermute | solution.py:362
  13.4 27.6 %collective-permute-start.2 = (bf16[2048,128]{1,0:T(8,128)(2,1)}, bf16[2048,128]{1,0:T(8,128)(2,1)S(1)}, u32[]{:S(2)}, u32[]{:S(2)}) collective-permute-start(bf16[2048,128]{1,0:T(8,128)(2,1)} %prep.1.kv_ref.own_ref), channel_id=1, source_target_pairs={{0,80},{1,17},{2,82},{3,19},{4,84},{5,21},{6,86},{7,23},{8,88},{9,... | collective-permute-start | bytes 1572872 | tf_op jit(solution)/shard_map/ppermute | solution.py:362
  15.3 25.6 %collective-permute-start.3 = (bf16[2048,128]{1,0:T(8,128)(2,1)}, bf16[2048,128]{1,0:T(8,128)(2,1)S(1)}, u32[]{:S(2)}, u32[]{:S(2)}) collective-permute-start(bf16[2048,128]{1,0:T(8,128)(2,1)} %prep.1.kv_ref.own_ref), channel_id=1, source_target_pairs={{0,64},{2,66},{4,68},{6,70},{8,72},{10,74},{12,76},{14,78},{16,80}... | collective-permute-start | bytes 1572872 | tf_op jit(solution)/shard_map/ppermute | solution.py:362
  16.0 1.0 copy-start
  17.1 1.2 copy-start.3
  18.3 25.7 %copy-start.1 = (bf16[2048,128]{1,0:T(8,128)(2,1)S(1)}, bf16[2048,128]{1,0:T(8,128)(2,1)}, u32[]{:S(2)}) copy-start(bf16[2048,128]{1,0:T(8,128)(2,1)} %prep.1.kv_ref.own_ref) | copy-start | bytes 1572868
  18.3 25.7 %copy-start.2 = (s32[13]{0:T(128)S(1)}, s32[13]{0:T(128)}, u32[]{:S(2)}) copy-start(s32[13]{0:T(128)} %stack.27.info) | copy-start | bytes 160
  23.7 17.8 %collective-permute-start.4 = (bf16[2048,128]{1,0:T(8,128)(2,1)S(1)}, bf16[2048,128]{1,0:T(8,128)(2,1)S(1)}, u32[]{:S(2)}, u32[]{:S(2)}) collective-permute-start(bf16[2048,128]{1,0:T(8,128)(2,1)S(1)} %collective-permute-done.refs_3_.refs_1_), channel_id=1, source_target_pairs={{0,1},{1,0},{2,3},{3,2},{4,5},{5,4},{6,7},{7,6},{8,9},{9,8},{10,11... | collective-permute-start | bytes 1572872 | tf_op jit(solution)/shard_map/ppermute | solution.py:362
  33.9 8.6 %collective-permute-start.5 = (bf16[2048,128]{1,0:T(8,128)(2,1)S(1)}, bf16[2048,128]{1,0:T(8,128)(2,1)S(1)}, u32[]{:S(2)}, u32[]{:S(2)}) collective-permute-start(bf16[2048,128]{1,0:T(8,128)(2,1)S(1)} %collective-permute-done.1.refs_4_.refs_2_), channel_id=1, source_target_pairs={{0,1},{1,0},{2,3},{3,2},{4,5},{5,4},{6,7},{7,6},{8,9},{9,8},{10,11... | collective-permute-start | bytes 1572872 | tf_op jit(solution)/shard_map/ppermute | solution.py:362
  41.0 2.3 %collective-permute-start.6 = (bf16[2048,128]{1,0:T(8,128)(2,1)S(1)}, bf16[2048,128]{1,0:T(8,128)(2,1)S(1)}, u32[]{:S(2)}, u32[]{:S(2)}) collective-permute-start(bf16[2048,128]{1,0:T(8,128)(2,1)S(1)} %collective-permute-done.2.refs_5_.refs_3_), channel_id=1, source_target_pairs={{0,1},{1,0},{2,3},{3,2},{4,5},{5,4},{6,7},{7,6},{8,9},{9,8},{10,11... | collective-permute-start | bytes 1572872 | tf_op jit(solution)/shard_map/ppermute | solution.py:362
  41.0 3.0 %collective-permute-start.7 = (bf16[2048,128]{1,0:T(8,128)(2,1)S(1)}, bf16[2048,128]{1,0:T(8,128)(2,1)S(1)}, u32[]{:S(2)}, u32[]{:S(2)}) collective-permute-start(bf16[2048,128]{1,0:T(8,128)(2,1)S(1)} %collective-permute-done.3.refs_6_.refs_4_), channel_id=1, source_target_pairs={{0,1},{1,0},{2,3},{3,2},{4,5},{5,4},{6,7},{7,6},{8,9},{9,8},{10,11... | collective-permute-start | bytes 1572872 | tf_op jit(solution)/shard_map/ppermute | solution.py:362
  41.5 18.0 %collective-permute-start.11 = (bf16[16,32,512]{2,1,0:T(8,128)(2,1)S(1)}, bf16[16,32,512]{2,1,0:T(8,128)(2,1)S(1)}, u32[]{:S(2)}, u32[]{:S(2)}) collective-permute-start(bf16[16,32,512]{2,1,0:T(8,128)(2,1)S(1)} %get-tuple-element.48), channel_id=1, source_target_pairs={{0,112},{1,113},{2,114},{3,115},{4,116},{5,117},{6,118},{7,119},{8... | collective-permute-start | bytes 1572872 | tf_op jit(solution)/shard_map/ppermute | solution.py:362
  44.0 3.6 %slice-start = ((s8[6291456]{0:T(1024)(128)(4,1)}), s8[4194304]{0:T(1024)(128)(4,1)S(1)}, s32[]{:S(2)}) async-start(s8[6291456]{0:T(1024)(128)(4,1)} %bitcast.7), calls=%async_computation | async-start | bytes 8388608
  44.0 3.6 %slice-start.1 = ((s8[6291456]{0:T(1024)(128)(4,1)}), s8[2097152]{0:T(1024)(128)(4,1)S(1)}, s32[]{:S(2)}) async-start(s8[6291456]{0:T(1024)(128)(4,1)} %bitcast.7), calls=%async_computation.1 | async-start | bytes 4194304
  45.6 1.6 collective-permute-start.8
  46.1 1.5 collective-permute-start.9
  53.5 26.8 %collective-permute-start.14 = (bf16[128,3072]{1,0:T(8,128)(2,1)S(1)}, bf16[128,3072]{1,0:T(8,128)(2,1)S(1)}, u32[]{:S(2)}, u32[]{:S(2)}) collective-permute-start(bf16[128,3072]{1,0:T(8,128)(2,1)S(1)} %get-tuple-element.53), channel_id=1, source_target_pairs={{0,2},{1,5},{2,0},{3,7},{4,6},{5,1},{6,4},{7,3},{8,10},{9,13},{10,... | collective-permute-start | bytes 2359304 | tf_op jit(solution)/shard_map/ppermute | solution.py:362
  54.9 25.4 %collective-permute-start.15 = (bf16[128,3072]{1,0:T(8,128)(2,1)S(1)}, bf16[128,3072]{1,0:T(8,128)(2,1)S(1)}, u32[]{:S(2)}, u32[]{:S(2)}) collective-permute-start(bf16[128,3072]{1,0:T(8,128)(2,1)S(1)} %get-tuple-element.54), channel_id=1, source_target_pairs={{0,2},{1,13},{2,0},{3,15},{4,6},{5,9},{6,4},{7,11},{8,10},{9,5},{1... | collective-permute-start | bytes 2359304 | tf_op jit(solution)/shard_map/ppermute | solution.py:362
  56.8 23.5 %collective-permute-start.16 = (bf16[128,3072]{1,0:T(8,128)(2,1)S(1)}, bf16[128,3072]{1,0:T(8,128)(2,1)S(1)}, u32[]{:S(2)}, u32[]{:S(2)}) collective-permute-start(bf16[128,3072]{1,0:T(8,128)(2,1)S(1)} %get-tuple-element.52.refs_1_), channel_id=1, source_target_pairs={{1,9},{3,11},{5,13},{7,15},{9,1},{11,3},{13,5},{15,7},{17,25},{19,... | collective-permute-start | bytes 2359304 | tf_op jit(solution)/shard_map/ppermute | solution.py:362
  78.4 1.6 collective-permute-start.12
  78.4 1.9 %collective-permute-start.13 = (bf16[256,512]{1,0:T(8,128)(2,1)S(1)}, bf16[256,512]{1,0:T(8,128)(2,1)S(1)}, u32[]{:S(2)}, u32[]{:S(2)}) collective-permute-start(bf16[256,512]{1,0:T(8,128)(2,1)S(1)} %get-tuple-element.51), channel_id=1, source_target_pairs={{0,1},{1,0},{2,3},{3,2},{4,5},{5,4},{6,7},{7,6},{8,9},{9,8},{10,11... | collective-permute-start | bytes 786440 | tf_op jit(solution)/shard_map/ppermute | solution.py:362
  87.3 0.7 copy-start.4
  88.1 0.7 copy-start.6
  88.8 0.7 copy-start.8
  89.5 11.2 %collective-permute-start.17 = (bf16[128,3072]{1,0:T(8,128)(2,1)S(1)}, bf16[128,3072]{1,0:T(8,128)(2,1)}, u32[]{:S(2)}, u32[]{:S(2)}) collective-permute-start(bf16[128,3072]{1,0:T(8,128)(2,1)S(1)} %get-tuple-element.57), channel_id=1, source_target_pairs={{0,4},{1,3},{2,6},{3,1},{4,0},{5,7},{6,2},{7,5},{8,12},{9,11},{10,... | collective-permute-start | bytes 2359304 | tf_op jit(solution)/shard_map/ppermute | solution.py:362
  89.9 19.3 %collective-permute-start.18 = (bf16[128,3072]{1,0:T(8,128)(2,1)S(1)}, bf16[128,3072]{1,0:T(8,128)(2,1)}, u32[]{:S(2)}, u32[]{:S(2)}) collective-permute-start(bf16[128,3072]{1,0:T(8,128)(2,1)S(1)} %get-tuple-element.58), channel_id=1, source_target_pairs={{0,12},{1,3},{2,14},{3,1},{4,8},{5,7},{6,10},{7,5},{8,4},{9,11},{1... | collective-permute-start | bytes 2359304 | tf_op jit(solution)/shard_map/ppermute | solution.py:362
  91.0 18.2 %collective-permute-start.19 = (bf16[128,3072]{1,0:T(8,128)(2,1)S(1)}, bf16[128,3072]{1,0:T(8,128)(2,1)}, u32[]{:S(2)}, u32[]{:S(2)}) collective-permute-start(bf16[128,3072]{1,0:T(8,128)(2,1)S(1)} %get-tuple-element.59), channel_id=1, source_target_pairs={{0,8},{2,10},{4,12},{6,14},{8,0},{10,2},{12,4},{14,6},{16,24},{18,... | collective-permute-start | bytes 2359304 | tf_op jit(solution)/shard_map/ppermute | solution.py:362
  111.5 8.9 %copy-start.9 = (bf16[64,3072]{1,0:T(8,128)(2,1)S(1)}, bf16[64,3072]{1,0:T(8,128)(2,1)}, u32[]{:S(2)}) copy-start(bf16[64,3072]{1,0:T(8,128)(2,1)} %copy-done.8) | copy-start | bytes 1179652
  111.5 9.6 %copy-start.7 = (bf16[64,3072]{1,0:T(8,128)(2,1)S(1)}, bf16[64,3072]{1,0:T(8,128)(2,1)}, u32[]{:S(2)}) copy-start(bf16[64,3072]{1,0:T(8,128)(2,1)} %copy-done.6) | copy-start | bytes 1179652
  111.5 17.9 %copy-start.5 = (bf16[64,3072]{1,0:T(8,128)(2,1)S(1)}, bf16[64,3072]{1,0:T(8,128)(2,1)}, u32[]{:S(2)}) copy-start(bf16[64,3072]{1,0:T(8,128)(2,1)} %copy-done.4) | copy-start | bytes 1179652
  111.6 17.8 %collective-permute-start.21 = (bf16[64,3072]{1,0:T(8,128)(2,1)S(1)}, bf16[64,3072]{1,0:T(8,128)(2,1)}, u32[]{:S(2)}, u32[]{:S(2)}) collective-permute-start(bf16[64,3072]{1,0:T(8,128)(2,1)S(1)} %get-tuple-element.69), channel_id=1, source_target_pairs={{1,13},{3,15},{5,9},{7,11},{9,5},{11,7},{13,1},{15,3},{17,29},{19,... | collective-permute-start | bytes 1179656 | tf_op jit(solution)/shard_map/ppermute | solution.py:362
  117.8 12.2 %collective-permute-start.22 = (bf16[64,3072]{1,0:T(8,128)(2,1)S(1)}, bf16[64,3072]{1,0:T(8,128)(2,1)}, u32[]{:S(2)}, u32[]{:S(2)}) collective-permute-start(bf16[64,3072]{1,0:T(8,128)(2,1)S(1)} %get-tuple-element.70), channel_id=1, source_target_pairs={{1,9},{3,11},{5,13},{7,15},{9,1},{11,3},{13,5},{15,7},{17,25},{19,... | collective-permute-start | bytes 1179656 | tf_op jit(solution)/shard_map/ppermute | solution.py:362
  119.8 14.9 %collective-permute-start.20 = (bf16[64,3072]{1,0:T(8,128)(2,1)S(1)}, bf16[64,3072]{1,0:T(8,128)(2,1)}, u32[]{:S(2)}, u32[]{:S(2)}) collective-permute-start(bf16[64,3072]{1,0:T(8,128)(2,1)S(1)} %slice.43), channel_id=1, source_target_pairs={{0,2},{1,5},{2,0},{3,7},{4,6},{5,1},{6,4},{7,3},{8,10},{9,13},{10,... | collective-permute-start | bytes 1179656 | tf_op jit(solution)/shard_map/ppermute | solution.py:362
  120.4 15.7 %collective-permute-start.25 = (bf16[64,3072]{1,0:T(8,128)(2,1)S(1)}, bf16[64,3072]{1,0:T(8,128)(2,1)S(1)}, u32[]{:S(2)}, u32[]{:S(2)}) collective-permute-start(bf16[64,3072]{1,0:T(8,128)(2,1)S(1)} %copy-done.9), channel_id=1, source_target_pairs={{0,8},{2,10},{4,12},{6,14},{8,0},{10,2},{12,4},{14,6},{16,24},{18,... | collective-permute-start | bytes 1179656 | tf_op jit(solution)/shard_map/ppermute | solution.py:362
  121.1 15.0 %collective-permute-start.23 = (bf16[64,3072]{1,0:T(8,128)(2,1)S(1)}, bf16[64,3072]{1,0:T(8,128)(2,1)S(1)}, u32[]{:S(2)}, u32[]{:S(2)}) collective-permute-start(bf16[64,3072]{1,0:T(8,128)(2,1)S(1)} %copy-done.7), channel_id=1, source_target_pairs={{0,4},{1,3},{2,6},{3,1},{4,0},{5,7},{6,2},{7,5},{8,12},{9,11},{10,... | collective-permute-start | bytes 1179656 | tf_op jit(solution)/shard_map/ppermute | solution.py:362
  129.4 6.8 %collective-permute-start.24 = (bf16[64,3072]{1,0:T(8,128)(2,1)S(1)}, bf16[64,3072]{1,0:T(8,128)(2,1)S(1)}, u32[]{:S(2)}, u32[]{:S(2)}) collective-permute-start(bf16[64,3072]{1,0:T(8,128)(2,1)S(1)} %copy-done.5), channel_id=1, source_target_pairs={{0,12},{2,14},{4,8},{6,10},{8,4},{10,6},{12,0},{14,2},{16,28},{18,... | collective-permute-start | bytes 1179656 | tf_op jit(solution)/shard_map/ppermute | solution.py:362
  136.5 14.5 %collective-permute-start.27 = (bf16[32,3072]{1,0:T(8,128)(2,1)S(1)}, bf16[32,3072]{1,0:T(8,128)(2,1)S(1)}, u32[]{:S(2)}, u32[]{:S(2)}) collective-permute-start(bf16[32,3072]{1,0:T(8,128)(2,1)S(1)} %get-tuple-element.72), channel_id=1, source_target_pairs={{0,1},{1,0},{2,3},{3,2},{4,5},{5,4},{6,7},{7,6},{8,9},{9,8},{10,11... | collective-permute-start | bytes 589832 | tf_op jit(solution)/shard_map/ppermute | solution.py:362
  139.2 22.2 %collective-permute-start.26 = (bf16[32,3072]{1,0:T(8,128)(2,1)S(1)}, bf16[32,3072]{1,0:T(8,128)(2,1)S(1)}, u32[]{:S(2)}, u32[]{:S(2)}) collective-permute-start(bf16[32,3072]{1,0:T(8,128)(2,1)S(1)} %get-tuple-element.74), channel_id=1, source_target_pairs={{0,112},{1,113},{2,114},{3,115},{4,116},{5,117},{6,118},{7,119},{8... | collective-permute-start | bytes 589832 | tf_op jit(solution)/shard_map/ppermute | solution.py:362
  150.9 10.5 %collective-permute-start.28 = (bf16[32,3072]{1,0:T(8,128)(2,1)S(1)}, bf16[32,3072]{1,0:T(8,128)(2,1)S(1)}, u32[]{:S(2)}, u32[]{:S(2)}) collective-permute-start(bf16[32,3072]{1,0:T(8,128)(2,1)S(1)} %get-tuple-element.73), channel_id=1, source_target_pairs={{0,113},{1,112},{2,115},{3,114},{4,117},{5,116},{6,119},{7,118},{8... | collective-permute-start | bytes 589832 | tf_op jit(solution)/shard_map/ppermute | solution.py:362

commit v9 on v8

--- a/solution.py
+++ b/solution.py
@@ -288,49 +288,36 @@
     )(info, kv, *state, *mine, *other)
 
 
-def project(info, mine, other, w, w_other, parts, tile, sums=()):
+def project(info, mine, other, w, w_other, parts, tile):
     rows, width = mine.shape
     n = w.shape[1] // 2
     steps = n // tile
 
-    def body(info, a, b0, b1, wa, wb, *refs):
-        outs = refs[len(sums) :]
+    def body(info, a, b0, b1, wa, wb, *outs):
         b = jnp.concatenate([b0[...], b1[...]], axis=0)
         s = jnp.dot(a[...], wa[...], preferred_element_type=F32) + jnp.dot(
             b, wb[...], preferred_element_type=F32
         )
         part = s.shape[0] // parts
-        for i, o in enumerate(outs[:parts]):
+        for i, o in enumerate(outs):
             o[...] = s[i * part : (i + 1) * part].astype(BF)
-        if sums:
-            p0, p2, g0, g1, g2 = [ref[...].astype(F32) for ref in refs[: len(sums)]]
-            first = p0 + g0 + jnp.where(info[2] == 1, g1 + g2, 0.0)
-            second = p2 + g1
-            half = part // 2
-            for o, x in zip(outs[parts:], (first[:half], first[half:], second[:half], second[half:]), strict=True):
-                o[...] = x.astype(BF)
 
     whole = pl.BlockSpec((rows, width), lambda i, info: (0, 0))
-    part = pl.BlockSpec((rows // 2, width), lambda i, info: (0, 0))
+    half = pl.BlockSpec((rows // 2, width), lambda i, info: (0, 0))
     weights = pl.BlockSpec((width, tile), lambda i, info: (0, info[2] * steps + i))
-
-    def strip(r):
-        return pl.BlockSpec((r, tile), lambda i, info: (0, i))
-
-    sizes = [rows // parts] * parts + [rows // parts // 2] * (4 if sums else 0)
     return pl.pallas_call(
         body,
         grid_spec=pltpu.PrefetchScalarGridSpec(
             num_scalar_prefetch=1,
             grid=(steps,),
-            in_specs=[whole, part, part, weights, weights] + [strip(x.shape[0]) for x in sums],
-            out_specs=[strip(r) for r in sizes],
+            in_specs=[whole, half, half, weights, weights],
+            out_specs=[pl.BlockSpec((rows // parts, tile), lambda i, info: (0, i))] * parts,
         ),
-        out_shape=[jax.ShapeDtypeStruct((r, n), BF) for r in sizes],
-        name="project_and_sum" if sums else "project",
+        out_shape=[jax.ShapeDtypeStruct((rows // parts, n), BF)] * parts,
+        name="project",
         cost_estimate=pl.CostEstimate(flops=0, bytes_accessed=0, transcendentals=0),
         compiler_params=PARAMS,
-    )(info, mine, *other, w, w_other, *sums)
+    )(info, mine, *other, w, w_other)
 
 
 def add(*terms):
@@ -389,10 +376,10 @@
             over_all(parts[2], lambda s, y, z, c: (s, y ^ 2, z, c) if c == first else None),
         ]
 
-    def sum_one(parts, got):
-        first = parts[0].astype(F32) + got[0].astype(F32)
+    def sum_one(parts, got, first):
+        along_y = parts[0].astype(F32) + got[0].astype(F32)
         extra = got[1].astype(F32) + got[2].astype(F32)
-        a = (first + jnp.where(core == 0, extra, 0.0)).astype(BF)
+        a = (along_y + jnp.where(core == first, extra, 0.0)).astype(BF)
         b = add(parts[2], got[1])
         n = a.shape[0] // 2
         return a[:n], a[n:], b[:n], b[n:]
@@ -414,15 +401,14 @@
     got_n = stage_one(parts_n, 1)
     far, *far_peer = attend(after(info, parts_n[0]), kv, [q_far], half, mine, other, n_y, n_seq)
     far_far = [swap_core(x) for x in far_peer]
-    *parts_f, a0, a1, b0, b1 = project(
-        info, far, far_far, w_out, w_other, n_y, cols // 4, (parts_n[0], parts_n[2], *got_n)
-    )
+    parts_f = project(info, far, far_far, w_out, w_other, n_y, cols // 4)
     got_f = stage_one(parts_f, 0)
-    total_f = sum_one(parts_f, got_f)
-    got2_n = stage_two((a0, a1, after(b0, total_f[0]), b1), 1)
+    total_n = sum_one([after(p, parts_f[0]) for p in parts_n], got_n, 1)
+    total_f = sum_one(parts_f, got_f, 0)
+    got2_n = stage_two((total_n[0], total_n[1], after(total_n[2], total_f[0]), total_n[3]), 1)
     got2_f = stage_two(total_f, 0)
     done_f = add(total_f[0], *got2_f).reshape(2, sub, cols // 2)
-    done_n = add(after(a0, by_core(done_f, True)), *got2_n).reshape(2, sub, cols // 2)
+    done_n = add(after(total_n[0], total_f[0]), *got2_n).reshape(2, sub, cols // 2)
     own_other = swap_core(after(by_core(done_n, False), done_f))
     home = over_all(by_core(done_f, True), lambda s, y, z, c: (n_seq - 1 - s, y, z, c))
     home_other = over_all(by_core(done_f, False), lambda s, y, z, c: (n_seq - 1 - s, y, z, 1 - c))

time: 163 us -> 149 us (0.914)
  starting transfers between devices: 60.9 us -> 50.3 us
  waiting for transfers between devices: 52.4 us -> 49.3 us
    ppermute x29, starting transfers between devices: 60.9 us -> 50.3 us  [over_all(): return lax.ppermute(x, ('seq', 'head'), pairs)]
    ppermute x29, waiting for transfers between devices: 52.4 us -> 49.3 us  [over_all(): return lax.ppermute(x, ('seq', 'head'), pairs)]
    unnamed x25 -> x15, local copies, waits for them, and re-layouts: 4.52 us -> 5.08 us
  transfers between devices with their start and end apart: 29 -> 29, of which waited for: 14 -> 13; matrix products, arithmetic and copies ran while one was open for 1% -> 3% of each run, Pallas kernels for 19% -> 26%
where the time goes in v9:
time: 149 us
  starting transfers between devices  50.3 us (34%)
  waiting for transfers between devices  49.3 us (33%)
  Pallas kernels  39 us (26%)
  local copies, waits for them, and re-layouts  5.95 us (4%)
  other arithmetic  4.52 us (3%)
    ppermute x29, starting transfers between devices, over_all(): return lax.ppermute(x, ('seq', 'head'), pairs)  50.3 us
    ppermute x29, waiting for transfers between devices, over_all(): return lax.ppermute(x, ('seq', 'head'), pairs)  49.3 us
    pallas_call x2, Pallas kernels, attend(): pl.pallas_call(functools.partial(attend_kernel, foreign, groups, n_y, n_s...  21.3 us
    pallas_call x2, Pallas kernels, project(): pl.pallas_call(body, grid_spec=pltpu.PrefetchScalarGridSpec(num_scalar_pr...  12.4 us
    unnamed x15, local copies, waits for them, and re-layouts  5.08 us
  transfers between devices with their start and end apart: 29, of which 13 were waited for; matrix products, arithmetic and copies ran while one was open for 3% of the time, Pallas kernels for 26%

profile of v9, /device:TPU:1, one launch (start us, length us, event | category | flops | bytes accessed | tf_op | source)
XLA Modules:
  0.0 149.3 jit_solution(3531288911006869580)
XLA Ops:
  0.0 1.4 collective-permute-start.10
  1.4 0.7 stack.27.info
  2.1 2.6 %prep.1.kv_ref.own_ref = bf16[2048,128]{1,0:T(8,128)(2,1)} custom-call(s32[13]{0:T(128)} %stack.27.info, bf16[1024,1024]{1,0:T(8,128)(2,1)} %k_ref.1, bf16[1024,1024]{1,0:T(8,128)(2,1)} %v_ref.1), custom_call_target="tpu_custom_call" | custom-call | tf_op jit(solution)/shard_map/prep/pallas_call | solution.py:37
  4.7 0.7 collective-permute-start.3
  5.4 5.6 %collective-permute-start.2 = (bf16[2048,128]{1,0:T(8,128)(2,1)}, bf16[2048,128]{1,0:T(8,128)(2,1)S(1)}, u32[]{:S(2)}, u32[]{:S(2)}) collective-permute-start(bf16[2048,128]{1,0:T(8,128)(2,1)} %prep.1.kv_ref.own_ref), channel_id=1, source_target_pairs={{0,80},{1,17},{2,82},{3,19},{4,84},{5,21},{6,86},{7,23},{8,88},{9,... | collective-permute-start | bytes 1572872 | tf_op jit(solution)/shard_map/ppermute | solution.py:349
  11.0 3.1 %collective-permute-start.1 = (bf16[2048,128]{1,0:T(8,128)(2,1)}, bf16[2048,128]{1,0:T(8,128)(2,1)S(1)}, u32[]{:S(2)}, u32[]{:S(2)}) collective-permute-start(bf16[2048,128]{1,0:T(8,128)(2,1)} %prep.1.kv_ref.own_ref), channel_id=1, source_target_pairs={{0,96},{1,33},{2,98},{3,35},{4,100},{5,37},{6,102},{7,39},{8,104},... | collective-permute-start | bytes 1572872 | tf_op jit(solution)/shard_map/ppermute | solution.py:349
  14.1 1.9 %collective-permute-start = (bf16[2048,128]{1,0:T(8,128)(2,1)}, bf16[2048,128]{1,0:T(8,128)(2,1)S(1)}, u32[]{:S(2)}, u32[]{:S(2)}) collective-permute-start(bf16[2048,128]{1,0:T(8,128)(2,1)} %prep.1.kv_ref.own_ref), channel_id=1, source_target_pairs={{0,112},{1,49},{2,114},{3,51},{4,116},{5,53},{6,118},{7,55},{8,120... | collective-permute-start | bytes 1572872 | tf_op jit(solution)/shard_map/ppermute | solution.py:349
  16.1 1.0 copy-done.1
  17.1 1.2 copy-done.4
  18.3 2.6 %own.1 = (bf16[256,2048]{1,0:T(8,128)(2,1)S(1)}, f32[144,2048]{1,0:T(8,128)S(1)}, f32[8,2048]{1,0:T(8,128)S(1)}, bf16[16,32,512]{2,1,0:T(8,128)(2,1)S(1)}) custom-call(bf16[16,2,32,512]{3,2,1,0:T(8,128)(2,1)S(1)} %bitcast.9, bf16[16,2,32,512]{3,2,1,0:T(8,128)(2,1)S(1)} %bitcast.10, bf16[2048,128]{1,0:T(8,128)(2,1)S(1)} %copy-done.1), custom_call_target="tpu_custom_call" | custom-call | flops 2147483648 | bytes 8388608 | tf_op jit(solution)/shard_map/own/pallas_call | solution.py:108
  21.0 6.1 %collective-permute-done.1.refs_4_.refs_2_ = bf16[2048,128]{1,0:T(8,128)(2,1)S(1)} collective-permute-done((bf16[2048,128]{1,0:T(8,128)(2,1)}, bf16[2048,128]{1,0:T(8,128)(2,1)S(1)}, u32[]{:S(2)}, u32[]{:S(2)}) %collective-permute-start.1) | collective-permute-done | bytes 524320 | tf_op jit(solution)/shard_map/ppermute | solution.py:349
  27.1 13.9 %collective-permute-done.refs_3_.refs_1_ = bf16[2048,128]{1,0:T(8,128)(2,1)S(1)} collective-permute-done((bf16[2048,128]{1,0:T(8,128)(2,1)}, bf16[2048,128]{1,0:T(8,128)(2,1)S(1)}, u32[]{:S(2)}, u32[]{:S(2)}) %collective-permute-start) | collective-permute-done | bytes 524320 | tf_op jit(solution)/shard_map/ppermute | solution.py:349
  41.0 1.3 collective-permute-start.4
  42.3 0.5 collective-permute-start.6
  42.8 1.0 collective-permute-done.4.refs_7_.refs_5_
  43.8 1.7 %collective-permute-start.11 = (bf16[16,32,512]{2,1,0:T(8,128)(2,1)S(1)}, bf16[16,32,512]{2,1,0:T(8,128)(2,1)S(1)}, u32[]{:S(2)}, u32[]{:S(2)}) collective-permute-start(bf16[16,32,512]{2,1,0:T(8,128)(2,1)S(1)} %get-tuple-element.46), channel_id=1, source_target_pairs={{0,112},{1,113},{2,114},{3,115},{4,116},{5,117},{6,118},{7,119},{8... | collective-permute-start | bytes 1572872 | tf_op jit(solution)/shard_map/ppermute | solution.py:349
  45.6 0.5 collective-permute-done.7.refs_10_.refs_8_
  46.1 1.6 %attend_own.1 = (bf16[512,512]{1,0:T(8,128)(2,1)S(1)}, bf16[256,512]{1,0:T(8,128)(2,1)S(1)}, bf16[256,512]{1,0:T(8,128)(2,1)S(1)}) custom-call(s32[13]{0:T(128)S(1)} %copy-done.3, bf16[2048,128]{1,0:T(8,128)(2,1)S(1)} %copy-done.2, bf16[256,2048]{1,0:T(8,128)(2,1)S(1)} %get-tuple-element.33.refs_0_, f32[144,2048]{1,0:T(8,128)S(1)} %get-tuple-element.34.refs_1_, ...), custom_call_target="tpu_custom_call" | custom-call | flops 4294967296 | bytes 4194304 | tf_op jit(solution)/shard_map/attend_own/pallas_call | solution.py:263
  47.7 0.5 collective-permute-start.8
  48.3 1.0 collective-permute-done.8.b0
  49.3 0.4 collective-permute-done.9.b1
  49.7 6.5 %project.2 = (bf16[128,3072]{1,0:T(8,128)(2,1)S(1)}, bf16[128,3072]{1,0:T(8,128)(2,1)}, bf16[128,3072]{1,0:T(8,128)(2,1)S(1)}, bf16[128,3072]{1,0:T(8,128)(2,1)S(1)}) custom-call(s32[13]{0:T(128)S(1)} %copy-done.3, bf16[512,512]{1,0:T(8,128)(2,1)S(1)} %get-tuple-element.40.a, bf16[256,512]{1,0:T(8,128)(2,1)S(1)} %collective-permute-done.8.b0, ...), custom_call_target="tpu_custom_call" | custom-call | tf_op jit(solution)/shard_map/project/pallas_call | solution.py:308
  56.2 1.3 collective-permute-start.14
  57.5 1.9 %collective-permute-start.15 = (bf16[128,3072]{1,0:T(8,128)(2,1)S(1)}, bf16[128,3072]{1,0:T(8,128)(2,1)}, u32[]{:S(2)}, u32[]{:S(2)}) collective-permute-start(bf16[128,3072]{1,0:T(8,128)(2,1)S(1)} %get-tuple-element.53), channel_id=1, source_target_pairs={{0,2},{1,13},{2,0},{3,15},{4,6},{5,9},{6,4},{7,11},{8,10},{9,5},{1... | collective-permute-start | bytes 2359304 | tf_op jit(solution)/shard_map/ppermute | solution.py:349
  59.4 2.6 %collective-permute-start.16 = (bf16[128,3072]{1,0:T(8,128)(2,1)S(1)}, bf16[128,3072]{1,0:T(8,128)(2,1)}, u32[]{:S(2)}, u32[]{:S(2)}) collective-permute-start(bf16[128,3072]{1,0:T(8,128)(2,1)S(1)} %get-tuple-element.59), channel_id=1, source_target_pairs={{1,9},{3,11},{5,13},{7,15},{9,1},{11,3},{13,5},{15,7},{17,25},{19,... | collective-permute-start | bytes 2359304 | tf_op jit(solution)/shard_map/ppermute | solution.py:349
  62.1 19.7 %attend_foreign.1 = (bf16[512,512]{1,0:T(8,128)(2,1)S(1)}, bf16[256,512]{1,0:T(8,128)(2,1)}, bf16[256,512]{1,0:T(8,128)(2,1)}) custom-call(s32[13]{0:T(128)S(1)} %copy-done.3, bf16[2048,128]{1,0:T(8,128)(2,1)S(1)} %copy-done.2, bf16[16,32,512]{2,1,0:T(8,128)(2,1)S(1)} %collective-permute-done.11.refs_0_, ...), custom_call_target="tpu_custom_call" | custom-call | flops 4294967296 | bytes 4194304 | tf_op jit(solution)/shard_map/attend_foreign/pallas_call | solution.py:263
  81.8 0.5 collective-permute-start.13
  82.3 1.2 collective-permute-done.12.b0
  84.0 2.8 %copy-done = bf16[512,6144]{1,0:T(8,128)(2,1)S(1)} copy-done((bf16[512,6144]{1,0:T(8,128)(2,1)S(1)}, bf16[512,6144]{1,0:T(8,128)(2,1)}, u32[]{:S(2)}) %copy-start) | copy-done | bytes 6291480
  86.7 5.9 %project.3 = (bf16[128,3072]{1,0:T(8,128)(2,1)S(1)}, bf16[128,3072]{1,0:T(8,128)(2,1)S(1)}, bf16[128,3072]{1,0:T(8,128)(2,1)S(1)}, bf16[128,3072]{1,0:T(8,128)(2,1)S(1)}) custom-call(s32[13]{0:T(128)S(1)} %copy-done.3, bf16[512,512]{1,0:T(8,128)(2,1)S(1)} %get-tuple-element.47.a, bf16[256,512]{1,0:T(8,128)(2,1)S(1)} %collective-permute-done.12.b0, ...), custom_call_target="tpu_custom_call" | custom-call | tf_op jit(solution)/shard_map/project/pallas_call | solution.py:308
  92.6 1.6 %collective-permute-start.17 = (bf16[128,3072]{1,0:T(8,128)(2,1)S(1)}, bf16[128,3072]{1,0:T(8,128)(2,1)S(1)}, u32[]{:S(2)}, u32[]{:S(2)}) collective-permute-start(bf16[128,3072]{1,0:T(8,128)(2,1)S(1)} %get-tuple-element.55), channel_id=1, source_target_pairs={{0,4},{1,3},{2,6},{3,1},{4,0},{5,7},{6,2},{7,5},{8,12},{9,11},{10,... | collective-permute-start | bytes 2359304 | tf_op jit(solution)/shard_map/ppermute | solution.py:349
  94.3 0.7 collective-permute-start.19
  95.1 2.3 %fusion.2 = (bf16[128,3072]{1,0:T(8,128)(2,1)S(1)}, bf16[128,3072]{1,0:T(8,128)(2,1)S(1)}) fusion(bf16[128,3072]{1,0:T(8,128)(2,1)} %collective-permute-done.15, bf16[128,3072]{1,0:T(8,128)(2,1)} %collective-permute-done.16, bf16[128,3072]{1,0:T(8,128)(2,1)} %collective-permute-done.14, bf16[128,3072]{1,0:T(8,128)(2,1)S(1)} %get-tuple-element.51, ...), kind=kLoop, calls=%fused_computation.6 | loop fusion | flops 4718592 | bytes 5505025 | tf_op jit(solution)/shard_map/convert_element_type | solution.py:382
  97.4 1.4 collective-permute-start.20
  98.9 0.7 collective-permute-start.21
  99.6 4.3 %collective-permute-done.17 = bf16[128,3072]{1,0:T(8,128)(2,1)S(1)} collective-permute-done((bf16[128,3072]{1,0:T(8,128)(2,1)S(1)}, bf16[128,3072]{1,0:T(8,128)(2,1)S(1)}, u32[]{:S(2)}, u32[]{:S(2)}) %collective-permute-start.17) | collective-permute-done | bytes 786464 | tf_op jit(solution)/shard_map/ppermute | solution.py:349
  103.9 8.4 %collective-permute-done.18 = bf16[128,3072]{1,0:T(8,128)(2,1)S(1)} collective-permute-done((bf16[128,3072]{1,0:T(8,128)(2,1)S(1)}, bf16[128,3072]{1,0:T(8,128)(2,1)S(1)}, u32[]{:S(2)}, u32[]{:S(2)}) %collective-permute-start.18) | collective-permute-done | bytes 786464 | tf_op jit(solution)/shard_map/ppermute | solution.py:349
  112.3 0.7 fusion.7
  113.1 0.7 collective-permute-start.22
  113.8 4.0 %collective-permute-start.24 = (bf16[64,3072]{1,0:T(8,128)(2,1)S(1)}, bf16[64,3072]{1,0:T(8,128)(2,1)S(1)}, u32[]{:S(2)}, u32[]{:S(2)}) collective-permute-start(bf16[64,3072]{1,0:T(8,128)(2,1)S(1)} %get-tuple-element.65), channel_id=1, source_target_pairs={{1,13},{3,15},{5,9},{7,11},{9,5},{11,7},{13,1},{15,3},{17,29},{19,... | collective-permute-start | bytes 1179656 | tf_op jit(solution)/shard_map/ppermute | solution.py:349
  117.8 2.2 %collective-permute-start.25 = (bf16[64,3072]{1,0:T(8,128)(2,1)S(1)}, bf16[64,3072]{1,0:T(8,128)(2,1)S(1)}, u32[]{:S(2)}, u32[]{:S(2)}) collective-permute-start(bf16[64,3072]{1,0:T(8,128)(2,1)S(1)} %get-tuple-element.66), channel_id=1, source_target_pairs={{1,9},{3,11},{5,13},{7,15},{9,1},{11,3},{13,5},{15,7},{17,25},{19,... | collective-permute-start | bytes 1179656 | tf_op jit(solution)/shard_map/ppermute | solution.py:349
  120.1 0.9 collective-permute-start.23
  121.2 10.0 %collective-permute-start.27 = (bf16[32,3072]{1,0:T(8,128)(2,1)S(1)}, bf16[32,3072]{1,0:T(8,128)(2,1)S(1)}, u32[]{:S(2)}, u32[]{:S(2)}) collective-permute-start(bf16[32,3072]{1,0:T(8,128)(2,1)S(1)} %get-tuple-element.76), channel_id=1, source_target_pairs={{0,1},{1,0},{2,3},{3,2},{4,5},{5,4},{6,7},{7,6},{8,9},{9,8},{10,11... | collective-permute-start | bytes 589832 | tf_op jit(solution)/shard_map/ppermute | solution.py:349
  131.2 0.8 collective-permute-done.24
  132.0 2.5 %collective-permute-done.23 = bf16[64,3072]{1,0:T(8,128)(2,1)S(1)} collective-permute-done((bf16[64,3072]{1,0:T(8,128)(2,1)S(1)}, bf16[64,3072]{1,0:T(8,128)(2,1)S(1)}, u32[]{:S(2)}, u32[]{:S(2)}) %collective-permute-start.23) | collective-permute-done | bytes 393248 | tf_op jit(solution)/shard_map/ppermute | solution.py:349
  134.8 4.7 %collective-permute-start.26 = (bf16[32,3072]{1,0:T(8,128)(2,1)S(1)}, bf16[32,3072]{1,0:T(8,128)(2,1)S(1)}, u32[]{:S(2)}, u32[]{:S(2)}) collective-permute-start(bf16[32,3072]{1,0:T(8,128)(2,1)S(1)} %get-tuple-element.77), channel_id=1, source_target_pairs={{0,112},{1,113},{2,114},{3,115},{4,116},{5,117},{6,118},{7,119},{8... | collective-permute-start | bytes 589832 | tf_op jit(solution)/shard_map/ppermute | solution.py:349
  139.5 8.7 %collective-permute-done.28 = bf16[32,3072]{1,0:T(8,128)(2,1)S(1)} collective-permute-done((bf16[32,3072]{1,0:T(8,128)(2,1)S(1)}, bf16[32,3072]{1,0:T(8,128)(2,1)S(1)}, u32[]{:S(2)}, u32[]{:S(2)}) %collective-permute-start.28) | collective-permute-done | bytes 196640 | tf_op jit(solution)/shard_map/ppermute | solution.py:349
  148.3 0.9 pad_maximum_fusion
  (46 shorter events, 1.6 us)
Async XLA Ops:
  0.0 49.7 %collective-permute-start.10 = (bf16[512,6144]{1,0:T(8,128)(2,1)}, bf16[512,6144]{1,0:T(8,128)(2,1)}, u32[]{:S(2)}, u32[]{:S(2)}) collective-permute-start(bf16[512,6144]{1,0:T(8,128)(2,1)} %wa.3), channel_id=1, source_target_pairs={{0,1},{1,0},{2,3},{3,2},{4,5},{5,4},{6,7},{7,6},{8,9},{9,8},{10,11... | collective-permute-start | bytes 18874376 | tf_op jit(solution)/shard_map/ppermute | solution.py:349
  4.7 16.3 %collective-permute-start.3 = (bf16[2048,128]{1,0:T(8,128)(2,1)}, bf16[2048,128]{1,0:T(8,128)(2,1)S(1)}, u32[]{:S(2)}, u32[]{:S(2)}) collective-permute-start(bf16[2048,128]{1,0:T(8,128)(2,1)} %prep.1.kv_ref.own_ref), channel_id=1, source_target_pairs={{0,64},{2,66},{4,68},{6,70},{8,72},{10,74},{12,76},{14,78},{16,80}... | collective-permute-start | bytes 1572872 | tf_op jit(solution)/shard_map/ppermute | solution.py:349
  5.4 15.6 %collective-permute-start.2 = (bf16[2048,128]{1,0:T(8,128)(2,1)}, bf16[2048,128]{1,0:T(8,128)(2,1)S(1)}, u32[]{:S(2)}, u32[]{:S(2)}) collective-permute-start(bf16[2048,128]{1,0:T(8,128)(2,1)} %prep.1.kv_ref.own_ref), channel_id=1, source_target_pairs={{0,80},{1,17},{2,82},{3,19},{4,84},{5,21},{6,86},{7,23},{8,88},{9,... | collective-permute-start | bytes 1572872 | tf_op jit(solution)/shard_map/ppermute | solution.py:349
  11.0 16.1 %collective-permute-start.1 = (bf16[2048,128]{1,0:T(8,128)(2,1)}, bf16[2048,128]{1,0:T(8,128)(2,1)S(1)}, u32[]{:S(2)}, u32[]{:S(2)}) collective-permute-start(bf16[2048,128]{1,0:T(8,128)(2,1)} %prep.1.kv_ref.own_ref), channel_id=1, source_target_pairs={{0,96},{1,33},{2,98},{3,35},{4,100},{5,37},{6,102},{7,39},{8,104},... | collective-permute-start | bytes 1572872 | tf_op jit(solution)/shard_map/ppermute | solution.py:349
  14.1 26.9 %collective-permute-start = (bf16[2048,128]{1,0:T(8,128)(2,1)}, bf16[2048,128]{1,0:T(8,128)(2,1)S(1)}, u32[]{:S(2)}, u32[]{:S(2)}) collective-permute-start(bf16[2048,128]{1,0:T(8,128)(2,1)} %prep.1.kv_ref.own_ref), channel_id=1, source_target_pairs={{0,112},{1,49},{2,114},{3,51},{4,116},{5,53},{6,118},{7,55},{8,120... | collective-permute-start | bytes 1572872 | tf_op jit(solution)/shard_map/ppermute | solution.py:349
  16.1 1.1 copy-start.1
  17.1 1.2 copy-start.4
  18.3 27.8 %copy-start.2 = (bf16[2048,128]{1,0:T(8,128)(2,1)S(1)}, bf16[2048,128]{1,0:T(8,128)(2,1)}, u32[]{:S(2)}) copy-start(bf16[2048,128]{1,0:T(8,128)(2,1)} %prep.1.kv_ref.own_ref) | copy-start | bytes 1572868
  18.3 27.8 %copy-start.3 = (s32[13]{0:T(128)S(1)}, s32[13]{0:T(128)}, u32[]{:S(2)}) copy-start(s32[13]{0:T(128)} %stack.27.info) | copy-start | bytes 160
  41.0 2.8 %collective-permute-start.4 = (bf16[2048,128]{1,0:T(8,128)(2,1)S(1)}, bf16[2048,128]{1,0:T(8,128)(2,1)S(1)}, u32[]{:S(2)}, u32[]{:S(2)}) collective-permute-start(bf16[2048,128]{1,0:T(8,128)(2,1)S(1)} %collective-permute-done.refs_3_.refs_1_), channel_id=1, source_target_pairs={{0,1},{1,0},{2,3},{3,2},{4,5},{5,4},{6,7},{7,6},{8,9},{9,8},{10,11... | collective-permute-start | bytes 1572872 | tf_op jit(solution)/shard_map/ppermute | solution.py:349
  42.3 3.3 %collective-permute-start.5 = (bf16[2048,128]{1,0:T(8,128)(2,1)S(1)}, bf16[2048,128]{1,0:T(8,128)(2,1)S(1)}, u32[]{:S(2)}, u32[]{:S(2)}) collective-permute-start(bf16[2048,128]{1,0:T(8,128)(2,1)S(1)} %collective-permute-done.1.refs_4_.refs_2_), channel_id=1, source_target_pairs={{0,1},{1,0},{2,3},{3,2},{4,5},{5,4},{6,7},{7,6},{8,9},{9,8},{10,11... | collective-permute-start | bytes 1572872 | tf_op jit(solution)/shard_map/ppermute | solution.py:349
  42.3 3.3 %collective-permute-start.6 = (bf16[2048,128]{1,0:T(8,128)(2,1)S(1)}, bf16[2048,128]{1,0:T(8,128)(2,1)S(1)}, u32[]{:S(2)}, u32[]{:S(2)}) collective-permute-start(bf16[2048,128]{1,0:T(8,128)(2,1)S(1)} %collective-permute-done.2.refs_5_.refs_3_), channel_id=1, source_target_pairs={{0,1},{1,0},{2,3},{3,2},{4,5},{5,4},{6,7},{7,6},{8,9},{9,8},{10,11... | collective-permute-start | bytes 1572872 | tf_op jit(solution)/shard_map/ppermute | solution.py:349
  42.8 3.3 %collective-permute-start.7 = (bf16[2048,128]{1,0:T(8,128)(2,1)S(1)}, bf16[2048,128]{1,0:T(8,128)(2,1)S(1)}, u32[]{:S(2)}, u32[]{:S(2)}) collective-permute-start(bf16[2048,128]{1,0:T(8,128)(2,1)S(1)} %collective-permute-done.3.refs_6_.refs_4_), channel_id=1, source_target_pairs={{0,1},{1,0},{2,3},{3,2},{4,5},{5,4},{6,7},{7,6},{8,9},{9,8},{10,11... | collective-permute-start | bytes 1572872 | tf_op jit(solution)/shard_map/ppermute | solution.py:349
  43.8 18.2 %collective-permute-start.11 = (bf16[16,32,512]{2,1,0:T(8,128)(2,1)S(1)}, bf16[16,32,512]{2,1,0:T(8,128)(2,1)S(1)}, u32[]{:S(2)}, u32[]{:S(2)}) collective-permute-start(bf16[16,32,512]{2,1,0:T(8,128)(2,1)S(1)} %get-tuple-element.46), channel_id=1, source_target_pairs={{0,112},{1,113},{2,114},{3,115},{4,116},{5,117},{6,118},{7,119},{8... | collective-permute-start | bytes 1572872 | tf_op jit(solution)/shard_map/ppermute | solution.py:349
  46.1 3.6 %slice-start = ((s8[6291456]{0:T(1024)(128)(4,1)}), s8[4194304]{0:T(1024)(128)(4,1)S(1)}, s32[]{:S(2)}) async-start(s8[6291456]{0:T(1024)(128)(4,1)} %bitcast.7), calls=%async_computation | async-start | bytes 8388608
  46.1 3.6 %slice-start.1 = ((s8[6291456]{0:T(1024)(128)(4,1)}), s8[2097152]{0:T(1024)(128)(4,1)S(1)}, s32[]{:S(2)}) async-start(s8[6291456]{0:T(1024)(128)(4,1)} %bitcast.7), calls=%async_computation.1 | async-start | bytes 4194304
  47.7 1.6 %collective-permute-start.8 = (bf16[256,512]{1,0:T(8,128)(2,1)S(1)}, bf16[256,512]{1,0:T(8,128)(2,1)S(1)}, u32[]{:S(2)}, u32[]{:S(2)}) collective-permute-start(bf16[256,512]{1,0:T(8,128)(2,1)S(1)} %get-tuple-element.41), channel_id=1, source_target_pairs={{0,1},{1,0},{2,3},{3,2},{4,5},{5,4},{6,7},{7,6},{8,9},{9,8},{10,11... | collective-permute-start | bytes 786440 | tf_op jit(solution)/shard_map/ppermute | solution.py:349
  48.2 1.5 %collective-permute-start.9 = (bf16[256,512]{1,0:T(8,128)(2,1)S(1)}, bf16[256,512]{1,0:T(8,128)(2,1)S(1)}, u32[]{:S(2)}, u32[]{:S(2)}) collective-permute-start(bf16[256,512]{1,0:T(8,128)(2,1)S(1)} %get-tuple-element.42), channel_id=1, source_target_pairs={{0,1},{1,0},{2,3},{3,2},{4,5},{5,4},{6,7},{7,6},{8,9},{9,8},{10,11... | collective-permute-start | bytes 786440 | tf_op jit(solution)/shard_map/ppermute | solution.py:349
  56.2 38.1 %collective-permute-start.14 = (bf16[128,3072]{1,0:T(8,128)(2,1)}, bf16[128,3072]{1,0:T(8,128)(2,1)}, u32[]{:S(2)}, u32[]{:S(2)}) collective-permute-start(bf16[128,3072]{1,0:T(8,128)(2,1)} %get-tuple-element.52), channel_id=1, source_target_pairs={{0,2},{1,5},{2,0},{3,7},{4,6},{5,1},{6,4},{7,3},{8,10},{9,13},{10,... | collective-permute-start | bytes 2359304 | tf_op jit(solution)/shard_map/ppermute | solution.py:349
  57.5 37.5 %collective-permute-start.15 = (bf16[128,3072]{1,0:T(8,128)(2,1)S(1)}, bf16[128,3072]{1,0:T(8,128)(2,1)}, u32[]{:S(2)}, u32[]{:S(2)}) collective-permute-start(bf16[128,3072]{1,0:T(8,128)(2,1)S(1)} %get-tuple-element.53), channel_id=1, source_target_pairs={{0,2},{1,13},{2,0},{3,15},{4,6},{5,9},{6,4},{7,11},{8,10},{9,5},{1... | collective-permute-start | bytes 2359304 | tf_op jit(solution)/shard_map/ppermute | solution.py:349
  59.4 35.6 %collective-permute-start.16 = (bf16[128,3072]{1,0:T(8,128)(2,1)S(1)}, bf16[128,3072]{1,0:T(8,128)(2,1)}, u32[]{:S(2)}, u32[]{:S(2)}) collective-permute-start(bf16[128,3072]{1,0:T(8,128)(2,1)S(1)} %get-tuple-element.59), channel_id=1, source_target_pairs={{1,9},{3,11},{5,13},{7,15},{9,1},{11,3},{13,5},{15,7},{17,25},{19,... | collective-permute-start | bytes 2359304 | tf_op jit(solution)/shard_map/ppermute | solution.py:349
  81.8 1.8 %collective-permute-start.12 = (bf16[256,512]{1,0:T(8,128)(2,1)}, bf16[256,512]{1,0:T(8,128)(2,1)S(1)}, u32[]{:S(2)}, u32[]{:S(2)}) collective-permute-start(bf16[256,512]{1,0:T(8,128)(2,1)} %get-tuple-element.48), channel_id=1, source_target_pairs={{0,1},{1,0},{2,3},{3,2},{4,5},{5,4},{6,7},{7,6},{8,9},{9,8},{10,11... | collective-permute-start | bytes 786440 | tf_op jit(solution)/shard_map/ppermute | solution.py:349
  81.8 2.1 %collective-permute-start.13 = (bf16[256,512]{1,0:T(8,128)(2,1)}, bf16[256,512]{1,0:T(8,128)(2,1)S(1)}, u32[]{:S(2)}, u32[]{:S(2)}) collective-permute-start(bf16[256,512]{1,0:T(8,128)(2,1)} %get-tuple-element.49), channel_id=1, source_target_pairs={{0,1},{1,0},{2,3},{3,2},{4,5},{5,4},{6,7},{7,6},{8,9},{9,8},{10,11... | collective-permute-start | bytes 786440 | tf_op jit(solution)/shard_map/ppermute | solution.py:349
  84.0 2.8 %copy-start = (bf16[512,6144]{1,0:T(8,128)(2,1)S(1)}, bf16[512,6144]{1,0:T(8,128)(2,1)}, u32[]{:S(2)}) copy-start(bf16[512,6144]{1,0:T(8,128)(2,1)} %wa.3) | copy-start | bytes 18874372
  92.6 11.3 %collective-permute-start.17 = (bf16[128,3072]{1,0:T(8,128)(2,1)S(1)}, bf16[128,3072]{1,0:T(8,128)(2,1)S(1)}, u32[]{:S(2)}, u32[]{:S(2)}) collective-permute-start(bf16[128,3072]{1,0:T(8,128)(2,1)S(1)} %get-tuple-element.55), channel_id=1, source_target_pairs={{0,4},{1,3},{2,6},{3,1},{4,0},{5,7},{6,2},{7,5},{8,12},{9,11},{10,... | collective-permute-start | bytes 2359304 | tf_op jit(solution)/shard_map/ppermute | solution.py:349
  94.2 18.1 %collective-permute-start.18 = (bf16[128,3072]{1,0:T(8,128)(2,1)S(1)}, bf16[128,3072]{1,0:T(8,128)(2,1)S(1)}, u32[]{:S(2)}, u32[]{:S(2)}) collective-permute-start(bf16[128,3072]{1,0:T(8,128)(2,1)S(1)} %get-tuple-element.56), channel_id=1, source_target_pairs={{0,12},{1,3},{2,14},{3,1},{4,8},{5,7},{6,10},{7,5},{8,4},{9,11},{1... | collective-permute-start | bytes 2359304 | tf_op jit(solution)/shard_map/ppermute | solution.py:349
  94.3 18.0 %collective-permute-start.19 = (bf16[128,3072]{1,0:T(8,128)(2,1)S(1)}, bf16[128,3072]{1,0:T(8,128)(2,1)S(1)}, u32[]{:S(2)}, u32[]{:S(2)}) collective-permute-start(bf16[128,3072]{1,0:T(8,128)(2,1)S(1)} %get-tuple-element.57), channel_id=1, source_target_pairs={{0,8},{2,10},{4,12},{6,14},{8,0},{10,2},{12,4},{14,6},{16,24},{18,... | collective-permute-start | bytes 2359304 | tf_op jit(solution)/shard_map/ppermute | solution.py:349
  97.4 22.6 %collective-permute-start.20 = (bf16[64,3072]{1,0:T(8,128)(2,1)S(1)}, bf16[64,3072]{1,0:T(8,128)(2,1)S(1)}, u32[]{:S(2)}, u32[]{:S(2)}) collective-permute-start(bf16[64,3072]{1,0:T(8,128)(2,1)S(1)} %get-tuple-element.70), channel_id=1, source_target_pairs={{0,4},{1,3},{2,6},{3,1},{4,0},{5,7},{6,2},{7,5},{8,12},{9,11},{10,... | collective-permute-start | bytes 1179656 | tf_op jit(solution)/shard_map/ppermute | solution.py:349
  98.9 22.1 %collective-permute-start.21 = (bf16[64,3072]{1,0:T(8,128)(2,1)S(1)}, bf16[64,3072]{1,0:T(8,128)(2,1)S(1)}, u32[]{:S(2)}, u32[]{:S(2)}) collective-permute-start(bf16[64,3072]{1,0:T(8,128)(2,1)S(1)} %get-tuple-element.73), channel_id=1, source_target_pairs={{0,12},{2,14},{4,8},{6,10},{8,4},{10,6},{12,0},{14,2},{16,28},{18,... | collective-permute-start | bytes 1179656 | tf_op jit(solution)/shard_map/ppermute | solution.py:349
  113.1 7.9 %collective-permute-start.22 = (bf16[64,3072]{1,0:T(8,128)(2,1)S(1)}, bf16[64,3072]{1,0:T(8,128)(2,1)S(1)}, u32[]{:S(2)}, u32[]{:S(2)}) collective-permute-start(bf16[64,3072]{1,0:T(8,128)(2,1)S(1)} %get-tuple-element.60), channel_id=1, source_target_pairs={{0,8},{2,10},{4,12},{6,14},{8,0},{10,2},{12,4},{14,6},{16,24},{18,... | collective-permute-start | bytes 1179656 | tf_op jit(solution)/shard_map/ppermute | solution.py:349
  113.8 18.2 %collective-permute-start.24 = (bf16[64,3072]{1,0:T(8,128)(2,1)S(1)}, bf16[64,3072]{1,0:T(8,128)(2,1)S(1)}, u32[]{:S(2)}, u32[]{:S(2)}) collective-permute-start(bf16[64,3072]{1,0:T(8,128)(2,1)S(1)} %get-tuple-element.65), channel_id=1, source_target_pairs={{1,13},{3,15},{5,9},{7,11},{9,5},{11,7},{13,1},{15,3},{17,29},{19,... | collective-permute-start | bytes 1179656 | tf_op jit(solution)/shard_map/ppermute | solution.py:349
  117.8 14.2 %collective-permute-start.25 = (bf16[64,3072]{1,0:T(8,128)(2,1)S(1)}, bf16[64,3072]{1,0:T(8,128)(2,1)S(1)}, u32[]{:S(2)}, u32[]{:S(2)}) collective-permute-start(bf16[64,3072]{1,0:T(8,128)(2,1)S(1)} %get-tuple-element.66), channel_id=1, source_target_pairs={{1,9},{3,11},{5,13},{7,15},{9,1},{11,3},{13,5},{15,7},{17,25},{19,... | collective-permute-start | bytes 1179656 | tf_op jit(solution)/shard_map/ppermute | solution.py:349
  120.1 14.4 %collective-permute-start.23 = (bf16[64,3072]{1,0:T(8,128)(2,1)S(1)}, bf16[64,3072]{1,0:T(8,128)(2,1)S(1)}, u32[]{:S(2)}, u32[]{:S(2)}) collective-permute-start(bf16[64,3072]{1,0:T(8,128)(2,1)S(1)} %fusion.8), channel_id=1, source_target_pairs={{0,2},{1,5},{2,0},{3,7},{4,6},{5,1},{6,4},{7,3},{8,10},{9,13},{10,... | collective-permute-start | bytes 1179656 | tf_op jit(solution)/shard_map/ppermute | solution.py:349
  121.2 18.2 %collective-permute-start.27 = (bf16[32,3072]{1,0:T(8,128)(2,1)S(1)}, bf16[32,3072]{1,0:T(8,128)(2,1)S(1)}, u32[]{:S(2)}, u32[]{:S(2)}) collective-permute-start(bf16[32,3072]{1,0:T(8,128)(2,1)S(1)} %get-tuple-element.76), channel_id=1, source_target_pairs={{0,1},{1,0},{2,3},{3,2},{4,5},{5,4},{6,7},{7,6},{8,9},{9,8},{10,11... | collective-permute-start | bytes 589832 | tf_op jit(solution)/shard_map/ppermute | solution.py:349
  134.8 13.4 %collective-permute-start.26 = (bf16[32,3072]{1,0:T(8,128)(2,1)S(1)}, bf16[32,3072]{1,0:T(8,128)(2,1)S(1)}, u32[]{:S(2)}, u32[]{:S(2)}) collective-permute-start(bf16[32,3072]{1,0:T(8,128)(2,1)S(1)} %get-tuple-element.77), channel_id=1, source_target_pairs={{0,112},{1,113},{2,114},{3,115},{4,116},{5,117},{6,118},{7,119},{8... | collective-permute-start | bytes 589832 | tf_op jit(solution)/shard_map/ppermute | solution.py:349
  139.4 8.7 %collective-permute-start.28 = (bf16[32,3072]{1,0:T(8,128)(2,1)S(1)}, bf16[32,3072]{1,0:T(8,128)(2,1)S(1)}, u32[]{:S(2)}, u32[]{:S(2)}) collective-permute-start(bf16[32,3072]{1,0:T(8,128)(2,1)S(1)} %get-tuple-element.78), channel_id=1, source_target_pairs={{0,113},{1,112},{2,115},{3,114},{4,117},{5,116},{6,119},{7,118},{8... | collective-permute-start | bytes 589832 | tf_op jit(solution)/shard_map/ppermute | solution.py:349

commit v10 on v9

--- a/solution.py
+++ b/solution.py
@@ -14,7 +14,7 @@
 LIMIT = 60.0
 BF = jnp.bfloat16
 F32 = jnp.float32
-PARAMS = pltpu.CompilerParams(vmem_limit_bytes=22 << 20)
+PARAMS = pltpu.CompilerParams(vmem_limit_bytes=17 << 20)
 FETCH = ((7, 3), (6, 2), (5, 1), (4, None))
 SLOTS = [d for pair in FETCH for d in pair if d is not None]
 TABLE = 6

time: 149 us -> 150 us (level)
  no operation moved by 1% of the time
where the time goes in v10:
time: 150 us; the launch traced here: 149 us
  waiting for transfers between devices  50 us (33%)
  starting transfers between devices  49.4 us (33%)
  Pallas kernels  39 us (26%)
  local copies, waits for them, and re-layouts  5.95 us (4%)
  other arithmetic  4.53 us (3%)
    ppermute x29, waiting for transfers between devices, over_all(): return lax.ppermute(x, ('seq', 'head'), pairs)  50 us
    ppermute x29, starting transfers between devices, over_all(): return lax.ppermute(x, ('seq', 'head'), pairs)  49.4 us
    pallas_call x2, Pallas kernels, attend(): pl.pallas_call(functools.partial(attend_kernel, foreign, groups, n_y, n_s...  21.3 us
    pallas_call x2, Pallas kernels, project(): pl.pallas_call(body, grid_spec=pltpu.PrefetchScalarGridSpec(num_scalar_pr...  12.4 us
    unnamed x15, local copies, waits for them, and re-layouts  5.08 us
  transfers between devices with their start and end apart: 29, of which 13 were waited for; matrix products, arithmetic and copies ran while one was open for 3% of the time, Pallas kernels for 26%

profile of v10, /device:TPU:1, one launch (start us, length us, event | category | flops | bytes accessed | tf_op | source)
XLA Modules:
  0.0 149.2 jit_solution(11766333705721634687)
XLA Ops:
  0.0 1.4 collective-permute-start.10
  1.4 0.7 stack.27.info
  2.1 2.6 %prep.1.kv_ref.own_ref = bf16[2048,128]{1,0:T(8,128)(2,1)} custom-call(s32[13]{0:T(128)} %stack.27.info, bf16[1024,1024]{1,0:T(8,128)(2,1)} %k_ref.1, bf16[1024,1024]{1,0:T(8,128)(2,1)} %v_ref.1), custom_call_target="tpu_custom_call" | custom-call | tf_op jit(solution)/shard_map/prep/pallas_call | solution.py:37
  4.7 0.7 collective-permute-start.3
  5.4 5.6 %collective-permute-start.2 = (bf16[2048,128]{1,0:T(8,128)(2,1)}, bf16[2048,128]{1,0:T(8,128)(2,1)S(1)}, u32[]{:S(2)}, u32[]{:S(2)}) collective-permute-start(bf16[2048,128]{1,0:T(8,128)(2,1)} %prep.1.kv_ref.own_ref), channel_id=1, source_target_pairs={{0,80},{1,17},{2,82},{3,19},{4,84},{5,21},{6,86},{7,23},{8,88},{9,... | collective-permute-start | bytes 1572872 | tf_op jit(solution)/shard_map/ppermute | solution.py:349
  11.0 3.1 %collective-permute-start.1 = (bf16[2048,128]{1,0:T(8,128)(2,1)}, bf16[2048,128]{1,0:T(8,128)(2,1)S(1)}, u32[]{:S(2)}, u32[]{:S(2)}) collective-permute-start(bf16[2048,128]{1,0:T(8,128)(2,1)} %prep.1.kv_ref.own_ref), channel_id=1, source_target_pairs={{0,96},{1,33},{2,98},{3,35},{4,100},{5,37},{6,102},{7,39},{8,104},... | collective-permute-start | bytes 1572872 | tf_op jit(solution)/shard_map/ppermute | solution.py:349
  14.1 1.9 %collective-permute-start = (bf16[2048,128]{1,0:T(8,128)(2,1)}, bf16[2048,128]{1,0:T(8,128)(2,1)S(1)}, u32[]{:S(2)}, u32[]{:S(2)}) collective-permute-start(bf16[2048,128]{1,0:T(8,128)(2,1)} %prep.1.kv_ref.own_ref), channel_id=1, source_target_pairs={{0,112},{1,49},{2,114},{3,51},{4,116},{5,53},{6,118},{7,55},{8,120... | collective-permute-start | bytes 1572872 | tf_op jit(solution)/shard_map/ppermute | solution.py:349
  16.1 1.0 copy-done.1
  17.1 1.2 copy-done.4
  18.3 2.6 %own.1 = (bf16[256,2048]{1,0:T(8,128)(2,1)S(1)}, f32[144,2048]{1,0:T(8,128)S(1)}, f32[8,2048]{1,0:T(8,128)S(1)}, bf16[16,32,512]{2,1,0:T(8,128)(2,1)S(1)}) custom-call(bf16[16,2,32,512]{3,2,1,0:T(8,128)(2,1)S(1)} %bitcast.9, bf16[16,2,32,512]{3,2,1,0:T(8,128)(2,1)S(1)} %bitcast.10, bf16[2048,128]{1,0:T(8,128)(2,1)S(1)} %copy-done.1), custom_call_target="tpu_custom_call" | custom-call | flops 2147483648 | bytes 8388608 | tf_op jit(solution)/shard_map/own/pallas_call | solution.py:108
  21.0 6.1 %collective-permute-done.1.refs_4_.refs_2_ = bf16[2048,128]{1,0:T(8,128)(2,1)S(1)} collective-permute-done((bf16[2048,128]{1,0:T(8,128)(2,1)}, bf16[2048,128]{1,0:T(8,128)(2,1)S(1)}, u32[]{:S(2)}, u32[]{:S(2)}) %collective-permute-start.1) | collective-permute-done | bytes 524320 | tf_op jit(solution)/shard_map/ppermute | solution.py:349
  27.1 13.9 %collective-permute-done.refs_3_.refs_1_ = bf16[2048,128]{1,0:T(8,128)(2,1)S(1)} collective-permute-done((bf16[2048,128]{1,0:T(8,128)(2,1)}, bf16[2048,128]{1,0:T(8,128)(2,1)S(1)}, u32[]{:S(2)}, u32[]{:S(2)}) %collective-permute-start) | collective-permute-done | bytes 524320 | tf_op jit(solution)/shard_map/ppermute | solution.py:349
  41.0 1.3 collective-permute-start.4
  42.3 0.5 collective-permute-start.6
  42.8 1.0 collective-permute-done.4.refs_7_.refs_5_
  43.8 1.7 %collective-permute-start.11 = (bf16[16,32,512]{2,1,0:T(8,128)(2,1)S(1)}, bf16[16,32,512]{2,1,0:T(8,128)(2,1)S(1)}, u32[]{:S(2)}, u32[]{:S(2)}) collective-permute-start(bf16[16,32,512]{2,1,0:T(8,128)(2,1)S(1)} %get-tuple-element.46), channel_id=1, source_target_pairs={{0,112},{1,113},{2,114},{3,115},{4,116},{5,117},{6,118},{7,119},{8... | collective-permute-start | bytes 1572872 | tf_op jit(solution)/shard_map/ppermute | solution.py:349
  45.6 0.5 collective-permute-done.7.refs_10_.refs_8_
  46.1 1.6 %attend_own.1 = (bf16[512,512]{1,0:T(8,128)(2,1)S(1)}, bf16[256,512]{1,0:T(8,128)(2,1)S(1)}, bf16[256,512]{1,0:T(8,128)(2,1)S(1)}) custom-call(s32[13]{0:T(128)S(1)} %copy-done.3, bf16[2048,128]{1,0:T(8,128)(2,1)S(1)} %copy-done.2, bf16[256,2048]{1,0:T(8,128)(2,1)S(1)} %get-tuple-element.33.refs_0_, f32[144,2048]{1,0:T(8,128)S(1)} %get-tuple-element.34.refs_1_, ...), custom_call_target="tpu_custom_call" | custom-call | flops 4294967296 | bytes 4194304 | tf_op jit(solution)/shard_map/attend_own/pallas_call | solution.py:263
  47.7 0.5 collective-permute-start.8
  48.3 1.0 collective-permute-done.8.b0
  49.3 0.4 collective-permute-done.9.b1
  49.7 6.5 %project.2 = (bf16[128,3072]{1,0:T(8,128)(2,1)S(1)}, bf16[128,3072]{1,0:T(8,128)(2,1)}, bf16[128,3072]{1,0:T(8,128)(2,1)S(1)}, bf16[128,3072]{1,0:T(8,128)(2,1)S(1)}) custom-call(s32[13]{0:T(128)S(1)} %copy-done.3, bf16[512,512]{1,0:T(8,128)(2,1)S(1)} %get-tuple-element.40.a, bf16[256,512]{1,0:T(8,128)(2,1)S(1)} %collective-permute-done.8.b0, ...), custom_call_target="tpu_custom_call" | custom-call | tf_op jit(solution)/shard_map/project/pallas_call | solution.py:308
  56.2 1.3 collective-permute-start.14
  57.5 1.9 %collective-permute-start.15 = (bf16[128,3072]{1,0:T(8,128)(2,1)S(1)}, bf16[128,3072]{1,0:T(8,128)(2,1)}, u32[]{:S(2)}, u32[]{:S(2)}) collective-permute-start(bf16[128,3072]{1,0:T(8,128)(2,1)S(1)} %get-tuple-element.53), channel_id=1, source_target_pairs={{0,2},{1,13},{2,0},{3,15},{4,6},{5,9},{6,4},{7,11},{8,10},{9,5},{1... | collective-permute-start | bytes 2359304 | tf_op jit(solution)/shard_map/ppermute | solution.py:349
  59.4 2.6 %collective-permute-start.16 = (bf16[128,3072]{1,0:T(8,128)(2,1)S(1)}, bf16[128,3072]{1,0:T(8,128)(2,1)}, u32[]{:S(2)}, u32[]{:S(2)}) collective-permute-start(bf16[128,3072]{1,0:T(8,128)(2,1)S(1)} %get-tuple-element.59), channel_id=1, source_target_pairs={{1,9},{3,11},{5,13},{7,15},{9,1},{11,3},{13,5},{15,7},{17,25},{19,... | collective-permute-start | bytes 2359304 | tf_op jit(solution)/shard_map/ppermute | solution.py:349
  62.1 19.7 %attend_foreign.1 = (bf16[512,512]{1,0:T(8,128)(2,1)S(1)}, bf16[256,512]{1,0:T(8,128)(2,1)}, bf16[256,512]{1,0:T(8,128)(2,1)}) custom-call(s32[13]{0:T(128)S(1)} %copy-done.3, bf16[2048,128]{1,0:T(8,128)(2,1)S(1)} %copy-done.2, bf16[16,32,512]{2,1,0:T(8,128)(2,1)S(1)} %collective-permute-done.11.refs_0_, ...), custom_call_target="tpu_custom_call" | custom-call | flops 4294967296 | bytes 4194304 | tf_op jit(solution)/shard_map/attend_foreign/pallas_call | solution.py:263
  81.8 0.5 collective-permute-start.13
  82.3 1.2 collective-permute-done.12.b0
  84.0 2.8 %copy-done = bf16[512,6144]{1,0:T(8,128)(2,1)S(1)} copy-done((bf16[512,6144]{1,0:T(8,128)(2,1)S(1)}, bf16[512,6144]{1,0:T(8,128)(2,1)}, u32[]{:S(2)}) %copy-start) | copy-done | bytes 6291480
  86.7 5.9 %project.3 = (bf16[128,3072]{1,0:T(8,128)(2,1)S(1)}, bf16[128,3072]{1,0:T(8,128)(2,1)S(1)}, bf16[128,3072]{1,0:T(8,128)(2,1)S(1)}, bf16[128,3072]{1,0:T(8,128)(2,1)S(1)}) custom-call(s32[13]{0:T(128)S(1)} %copy-done.3, bf16[512,512]{1,0:T(8,128)(2,1)S(1)} %get-tuple-element.47.a, bf16[256,512]{1,0:T(8,128)(2,1)S(1)} %collective-permute-done.12.b0, ...), custom_call_target="tpu_custom_call" | custom-call | tf_op jit(solution)/shard_map/project/pallas_call | solution.py:308
  92.6 1.6 %collective-permute-start.17 = (bf16[128,3072]{1,0:T(8,128)(2,1)S(1)}, bf16[128,3072]{1,0:T(8,128)(2,1)S(1)}, u32[]{:S(2)}, u32[]{:S(2)}) collective-permute-start(bf16[128,3072]{1,0:T(8,128)(2,1)S(1)} %get-tuple-element.55), channel_id=1, source_target_pairs={{0,4},{1,3},{2,6},{3,1},{4,0},{5,7},{6,2},{7,5},{8,12},{9,11},{10,... | collective-permute-start | bytes 2359304 | tf_op jit(solution)/shard_map/ppermute | solution.py:349
  94.3 0.7 collective-permute-start.19
  95.1 2.3 %fusion.2 = (bf16[128,3072]{1,0:T(8,128)(2,1)S(1)}, bf16[128,3072]{1,0:T(8,128)(2,1)S(1)}) fusion(bf16[128,3072]{1,0:T(8,128)(2,1)} %collective-permute-done.15, bf16[128,3072]{1,0:T(8,128)(2,1)} %collective-permute-done.16, bf16[128,3072]{1,0:T(8,128)(2,1)} %collective-permute-done.14, bf16[128,3072]{1,0:T(8,128)(2,1)S(1)} %get-tuple-element.51, ...), kind=kLoop, calls=%fused_computation.6 | loop fusion | flops 4718592 | bytes 5505025 | tf_op jit(solution)/shard_map/convert_element_type | solution.py:382
  97.4 1.4 collective-permute-start.20
  98.9 0.7 collective-permute-start.21
  99.6 4.3 %collective-permute-done.17 = bf16[128,3072]{1,0:T(8,128)(2,1)S(1)} collective-permute-done((bf16[128,3072]{1,0:T(8,128)(2,1)S(1)}, bf16[128,3072]{1,0:T(8,128)(2,1)S(1)}, u32[]{:S(2)}, u32[]{:S(2)}) %collective-permute-start.17) | collective-permute-done | bytes 786464 | tf_op jit(solution)/shard_map/ppermute | solution.py:349
  103.9 8.4 %collective-permute-done.18 = bf16[128,3072]{1,0:T(8,128)(2,1)S(1)} collective-permute-done((bf16[128,3072]{1,0:T(8,128)(2,1)S(1)}, bf16[128,3072]{1,0:T(8,128)(2,1)S(1)}, u32[]{:S(2)}, u32[]{:S(2)}) %collective-permute-start.18) | collective-permute-done | bytes 786464 | tf_op jit(solution)/shard_map/ppermute | solution.py:349
  112.3 0.7 fusion.7
  113.1 0.7 collective-permute-start.22
  113.8 4.0 %collective-permute-start.24 = (bf16[64,3072]{1,0:T(8,128)(2,1)S(1)}, bf16[64,3072]{1,0:T(8,128)(2,1)S(1)}, u32[]{:S(2)}, u32[]{:S(2)}) collective-permute-start(bf16[64,3072]{1,0:T(8,128)(2,1)S(1)} %get-tuple-element.65), channel_id=1, source_target_pairs={{1,13},{3,15},{5,9},{7,11},{9,5},{11,7},{13,1},{15,3},{17,29},{19,... | collective-permute-start | bytes 1179656 | tf_op jit(solution)/shard_map/ppermute | solution.py:349
  117.8 2.2 %collective-permute-start.25 = (bf16[64,3072]{1,0:T(8,128)(2,1)S(1)}, bf16[64,3072]{1,0:T(8,128)(2,1)S(1)}, u32[]{:S(2)}, u32[]{:S(2)}) collective-permute-start(bf16[64,3072]{1,0:T(8,128)(2,1)S(1)} %get-tuple-element.66), channel_id=1, source_target_pairs={{1,9},{3,11},{5,13},{7,15},{9,1},{11,3},{13,5},{15,7},{17,25},{19,... | collective-permute-start | bytes 1179656 | tf_op jit(solution)/shard_map/ppermute | solution.py:349
  120.1 0.9 collective-permute-start.23
  121.3 10.0 %collective-permute-start.27 = (bf16[32,3072]{1,0:T(8,128)(2,1)S(1)}, bf16[32,3072]{1,0:T(8,128)(2,1)S(1)}, u32[]{:S(2)}, u32[]{:S(2)}) collective-permute-start(bf16[32,3072]{1,0:T(8,128)(2,1)S(1)} %get-tuple-element.76), channel_id=1, source_target_pairs={{0,1},{1,0},{2,3},{3,2},{4,5},{5,4},{6,7},{7,6},{8,9},{9,8},{10,11... | collective-permute-start | bytes 589832 | tf_op jit(solution)/shard_map/ppermute | solution.py:349
  131.2 0.8 collective-permute-done.24
  132.0 2.5 %collective-permute-done.23 = bf16[64,3072]{1,0:T(8,128)(2,1)S(1)} collective-permute-done((bf16[64,3072]{1,0:T(8,128)(2,1)S(1)}, bf16[64,3072]{1,0:T(8,128)(2,1)S(1)}, u32[]{:S(2)}, u32[]{:S(2)}) %collective-permute-start.23) | collective-permute-done | bytes 393248 | tf_op jit(solution)/shard_map/ppermute | solution.py:349
  134.8 3.8 %collective-permute-start.26 = (bf16[32,3072]{1,0:T(8,128)(2,1)S(1)}, bf16[32,3072]{1,0:T(8,128)(2,1)S(1)}, u32[]{:S(2)}, u32[]{:S(2)}) collective-permute-start(bf16[32,3072]{1,0:T(8,128)(2,1)S(1)} %get-tuple-element.77), channel_id=1, source_target_pairs={{0,112},{1,113},{2,114},{3,115},{4,116},{5,117},{6,118},{7,119},{8... | collective-permute-start | bytes 589832 | tf_op jit(solution)/shard_map/ppermute | solution.py:349
  138.6 9.4 %collective-permute-done.28 = bf16[32,3072]{1,0:T(8,128)(2,1)S(1)} collective-permute-done((bf16[32,3072]{1,0:T(8,128)(2,1)S(1)}, bf16[32,3072]{1,0:T(8,128)(2,1)S(1)}, u32[]{:S(2)}, u32[]{:S(2)}) %collective-permute-start.28) | collective-permute-done | bytes 196640 | tf_op jit(solution)/shard_map/ppermute | solution.py:349
  148.2 0.9 pad_maximum_fusion
  (46 shorter events, 1.6 us)
Async XLA Ops:
  0.0 49.7 %collective-permute-start.10 = (bf16[512,6144]{1,0:T(8,128)(2,1)}, bf16[512,6144]{1,0:T(8,128)(2,1)}, u32[]{:S(2)}, u32[]{:S(2)}) collective-permute-start(bf16[512,6144]{1,0:T(8,128)(2,1)} %wa.3), channel_id=1, source_target_pairs={{0,1},{1,0},{2,3},{3,2},{4,5},{5,4},{6,7},{7,6},{8,9},{9,8},{10,11... | collective-permute-start | bytes 18874376 | tf_op jit(solution)/shard_map/ppermute | solution.py:349
  4.7 16.3 %collective-permute-start.3 = (bf16[2048,128]{1,0:T(8,128)(2,1)}, bf16[2048,128]{1,0:T(8,128)(2,1)S(1)}, u32[]{:S(2)}, u32[]{:S(2)}) collective-permute-start(bf16[2048,128]{1,0:T(8,128)(2,1)} %prep.1.kv_ref.own_ref), channel_id=1, source_target_pairs={{0,64},{2,66},{4,68},{6,70},{8,72},{10,74},{12,76},{14,78},{16,80}... | collective-permute-start | bytes 1572872 | tf_op jit(solution)/shard_map/ppermute | solution.py:349
  5.4 15.6 %collective-permute-start.2 = (bf16[2048,128]{1,0:T(8,128)(2,1)}, bf16[2048,128]{1,0:T(8,128)(2,1)S(1)}, u32[]{:S(2)}, u32[]{:S(2)}) collective-permute-start(bf16[2048,128]{1,0:T(8,128)(2,1)} %prep.1.kv_ref.own_ref), channel_id=1, source_target_pairs={{0,80},{1,17},{2,82},{3,19},{4,84},{5,21},{6,86},{7,23},{8,88},{9,... | collective-permute-start | bytes 1572872 | tf_op jit(solution)/shard_map/ppermute | solution.py:349
  11.0 16.1 %collective-permute-start.1 = (bf16[2048,128]{1,0:T(8,128)(2,1)}, bf16[2048,128]{1,0:T(8,128)(2,1)S(1)}, u32[]{:S(2)}, u32[]{:S(2)}) collective-permute-start(bf16[2048,128]{1,0:T(8,128)(2,1)} %prep.1.kv_ref.own_ref), channel_id=1, source_target_pairs={{0,96},{1,33},{2,98},{3,35},{4,100},{5,37},{6,102},{7,39},{8,104},... | collective-permute-start | bytes 1572872 | tf_op jit(solution)/shard_map/ppermute | solution.py:349
  14.1 26.9 %collective-permute-start = (bf16[2048,128]{1,0:T(8,128)(2,1)}, bf16[2048,128]{1,0:T(8,128)(2,1)S(1)}, u32[]{:S(2)}, u32[]{:S(2)}) collective-permute-start(bf16[2048,128]{1,0:T(8,128)(2,1)} %prep.1.kv_ref.own_ref), channel_id=1, source_target_pairs={{0,112},{1,49},{2,114},{3,51},{4,116},{5,53},{6,118},{7,55},{8,120... | collective-permute-start | bytes 1572872 | tf_op jit(solution)/shard_map/ppermute | solution.py:349
  16.1 1.1 copy-start.1
  17.1 1.2 copy-start.4
  18.3 27.8 %copy-start.2 = (bf16[2048,128]{1,0:T(8,128)(2,1)S(1)}, bf16[2048,128]{1,0:T(8,128)(2,1)}, u32[]{:S(2)}) copy-start(bf16[2048,128]{1,0:T(8,128)(2,1)} %prep.1.kv_ref.own_ref) | copy-start | bytes 1572868
  18.3 27.8 %copy-start.3 = (s32[13]{0:T(128)S(1)}, s32[13]{0:T(128)}, u32[]{:S(2)}) copy-start(s32[13]{0:T(128)} %stack.27.info) | copy-start | bytes 160
  41.0 2.8 %collective-permute-start.4 = (bf16[2048,128]{1,0:T(8,128)(2,1)S(1)}, bf16[2048,128]{1,0:T(8,128)(2,1)S(1)}, u32[]{:S(2)}, u32[]{:S(2)}) collective-permute-start(bf16[2048,128]{1,0:T(8,128)(2,1)S(1)} %collective-permute-done.refs_3_.refs_1_), channel_id=1, source_target_pairs={{0,1},{1,0},{2,3},{3,2},{4,5},{5,4},{6,7},{7,6},{8,9},{9,8},{10,11... | collective-permute-start | bytes 1572872 | tf_op jit(solution)/shard_map/ppermute | solution.py:349
  42.3 3.3 %collective-permute-start.5 = (bf16[2048,128]{1,0:T(8,128)(2,1)S(1)}, bf16[2048,128]{1,0:T(8,128)(2,1)S(1)}, u32[]{:S(2)}, u32[]{:S(2)}) collective-permute-start(bf16[2048,128]{1,0:T(8,128)(2,1)S(1)} %collective-permute-done.1.refs_4_.refs_2_), channel_id=1, source_target_pairs={{0,1},{1,0},{2,3},{3,2},{4,5},{5,4},{6,7},{7,6},{8,9},{9,8},{10,11... | collective-permute-start | bytes 1572872 | tf_op jit(solution)/shard_map/ppermute | solution.py:349
  42.3 3.3 %collective-permute-start.6 = (bf16[2048,128]{1,0:T(8,128)(2,1)S(1)}, bf16[2048,128]{1,0:T(8,128)(2,1)S(1)}, u32[]{:S(2)}, u32[]{:S(2)}) collective-permute-start(bf16[2048,128]{1,0:T(8,128)(2,1)S(1)} %collective-permute-done.2.refs_5_.refs_3_), channel_id=1, source_target_pairs={{0,1},{1,0},{2,3},{3,2},{4,5},{5,4},{6,7},{7,6},{8,9},{9,8},{10,11... | collective-permute-start | bytes 1572872 | tf_op jit(solution)/shard_map/ppermute | solution.py:349
  42.8 3.3 %collective-permute-start.7 = (bf16[2048,128]{1,0:T(8,128)(2,1)S(1)}, bf16[2048,128]{1,0:T(8,128)(2,1)S(1)}, u32[]{:S(2)}, u32[]{:S(2)}) collective-permute-start(bf16[2048,128]{1,0:T(8,128)(2,1)S(1)} %collective-permute-done.3.refs_6_.refs_4_), channel_id=1, source_target_pairs={{0,1},{1,0},{2,3},{3,2},{4,5},{5,4},{6,7},{7,6},{8,9},{9,8},{10,11... | collective-permute-start | bytes 1572872 | tf_op jit(solution)/shard_map/ppermute | solution.py:349
  43.8 18.2 %collective-permute-start.11 = (bf16[16,32,512]{2,1,0:T(8,128)(2,1)S(1)}, bf16[16,32,512]{2,1,0:T(8,128)(2,1)S(1)}, u32[]{:S(2)}, u32[]{:S(2)}) collective-permute-start(bf16[16,32,512]{2,1,0:T(8,128)(2,1)S(1)} %get-tuple-element.46), channel_id=1, source_target_pairs={{0,112},{1,113},{2,114},{3,115},{4,116},{5,117},{6,118},{7,119},{8... | collective-permute-start | bytes 1572872 | tf_op jit(solution)/shard_map/ppermute | solution.py:349
  46.1 3.6 %slice-start = ((s8[6291456]{0:T(1024)(128)(4,1)}), s8[4194304]{0:T(1024)(128)(4,1)S(1)}, s32[]{:S(2)}) async-start(s8[6291456]{0:T(1024)(128)(4,1)} %bitcast.7), calls=%async_computation | async-start | bytes 8388608
  46.1 3.6 %slice-start.1 = ((s8[6291456]{0:T(1024)(128)(4,1)}), s8[2097152]{0:T(1024)(128)(4,1)S(1)}, s32[]{:S(2)}) async-start(s8[6291456]{0:T(1024)(128)(4,1)} %bitcast.7), calls=%async_computation.1 | async-start | bytes 4194304
  47.7 1.6 %collective-permute-start.8 = (bf16[256,512]{1,0:T(8,128)(2,1)S(1)}, bf16[256,512]{1,0:T(8,128)(2,1)S(1)}, u32[]{:S(2)}, u32[]{:S(2)}) collective-permute-start(bf16[256,512]{1,0:T(8,128)(2,1)S(1)} %get-tuple-element.41), channel_id=1, source_target_pairs={{0,1},{1,0},{2,3},{3,2},{4,5},{5,4},{6,7},{7,6},{8,9},{9,8},{10,11... | collective-permute-start | bytes 786440 | tf_op jit(solution)/shard_map/ppermute | solution.py:349
  48.2 1.5 %collective-permute-start.9 = (bf16[256,512]{1,0:T(8,128)(2,1)S(1)}, bf16[256,512]{1,0:T(8,128)(2,1)S(1)}, u32[]{:S(2)}, u32[]{:S(2)}) collective-permute-start(bf16[256,512]{1,0:T(8,128)(2,1)S(1)} %get-tuple-element.42), channel_id=1, source_target_pairs={{0,1},{1,0},{2,3},{3,2},{4,5},{5,4},{6,7},{7,6},{8,9},{9,8},{10,11... | collective-permute-start | bytes 786440 | tf_op jit(solution)/shard_map/ppermute | solution.py:349
  56.2 38.1 %collective-permute-start.14 = (bf16[128,3072]{1,0:T(8,128)(2,1)}, bf16[128,3072]{1,0:T(8,128)(2,1)}, u32[]{:S(2)}, u32[]{:S(2)}) collective-permute-start(bf16[128,3072]{1,0:T(8,128)(2,1)} %get-tuple-element.52), channel_id=1, source_target_pairs={{0,2},{1,5},{2,0},{3,7},{4,6},{5,1},{6,4},{7,3},{8,10},{9,13},{10,... | collective-permute-start | bytes 2359304 | tf_op jit(solution)/shard_map/ppermute | solution.py:349
  57.5 37.5 %collective-permute-start.15 = (bf16[128,3072]{1,0:T(8,128)(2,1)S(1)}, bf16[128,3072]{1,0:T(8,128)(2,1)}, u32[]{:S(2)}, u32[]{:S(2)}) collective-permute-start(bf16[128,3072]{1,0:T(8,128)(2,1)S(1)} %get-tuple-element.53), channel_id=1, source_target_pairs={{0,2},{1,13},{2,0},{3,15},{4,6},{5,9},{6,4},{7,11},{8,10},{9,5},{1... | collective-permute-start | bytes 2359304 | tf_op jit(solution)/shard_map/ppermute | solution.py:349
  59.4 35.6 %collective-permute-start.16 = (bf16[128,3072]{1,0:T(8,128)(2,1)S(1)}, bf16[128,3072]{1,0:T(8,128)(2,1)}, u32[]{:S(2)}, u32[]{:S(2)}) collective-permute-start(bf16[128,3072]{1,0:T(8,128)(2,1)S(1)} %get-tuple-element.59), channel_id=1, source_target_pairs={{1,9},{3,11},{5,13},{7,15},{9,1},{11,3},{13,5},{15,7},{17,25},{19,... | collective-permute-start | bytes 2359304 | tf_op jit(solution)/shard_map/ppermute | solution.py:349
  81.8 1.8 %collective-permute-start.12 = (bf16[256,512]{1,0:T(8,128)(2,1)}, bf16[256,512]{1,0:T(8,128)(2,1)S(1)}, u32[]{:S(2)}, u32[]{:S(2)}) collective-permute-start(bf16[256,512]{1,0:T(8,128)(2,1)} %get-tuple-element.48), channel_id=1, source_target_pairs={{0,1},{1,0},{2,3},{3,2},{4,5},{5,4},{6,7},{7,6},{8,9},{9,8},{10,11... | collective-permute-start | bytes 786440 | tf_op jit(solution)/shard_map/ppermute | solution.py:349
  81.8 2.1 %collective-permute-start.13 = (bf16[256,512]{1,0:T(8,128)(2,1)}, bf16[256,512]{1,0:T(8,128)(2,1)S(1)}, u32[]{:S(2)}, u32[]{:S(2)}) collective-permute-start(bf16[256,512]{1,0:T(8,128)(2,1)} %get-tuple-element.49), channel_id=1, source_target_pairs={{0,1},{1,0},{2,3},{3,2},{4,5},{5,4},{6,7},{7,6},{8,9},{9,8},{10,11... | collective-permute-start | bytes 786440 | tf_op jit(solution)/shard_map/ppermute | solution.py:349
  84.0 2.8 %copy-start = (bf16[512,6144]{1,0:T(8,128)(2,1)S(1)}, bf16[512,6144]{1,0:T(8,128)(2,1)}, u32[]{:S(2)}) copy-start(bf16[512,6144]{1,0:T(8,128)(2,1)} %wa.3) | copy-start | bytes 18874372
  92.6 11.3 %collective-permute-start.17 = (bf16[128,3072]{1,0:T(8,128)(2,1)S(1)}, bf16[128,3072]{1,0:T(8,128)(2,1)S(1)}, u32[]{:S(2)}, u32[]{:S(2)}) collective-permute-start(bf16[128,3072]{1,0:T(8,128)(2,1)S(1)} %get-tuple-element.55), channel_id=1, source_target_pairs={{0,4},{1,3},{2,6},{3,1},{4,0},{5,7},{6,2},{7,5},{8,12},{9,11},{10,... | collective-permute-start | bytes 2359304 | tf_op jit(solution)/shard_map/ppermute | solution.py:349
  94.2 18.1 %collective-permute-start.18 = (bf16[128,3072]{1,0:T(8,128)(2,1)S(1)}, bf16[128,3072]{1,0:T(8,128)(2,1)S(1)}, u32[]{:S(2)}, u32[]{:S(2)}) collective-permute-start(bf16[128,3072]{1,0:T(8,128)(2,1)S(1)} %get-tuple-element.56), channel_id=1, source_target_pairs={{0,12},{1,3},{2,14},{3,1},{4,8},{5,7},{6,10},{7,5},{8,4},{9,11},{1... | collective-permute-start | bytes 2359304 | tf_op jit(solution)/shard_map/ppermute | solution.py:349
  94.3 18.0 %collective-permute-start.19 = (bf16[128,3072]{1,0:T(8,128)(2,1)S(1)}, bf16[128,3072]{1,0:T(8,128)(2,1)S(1)}, u32[]{:S(2)}, u32[]{:S(2)}) collective-permute-start(bf16[128,3072]{1,0:T(8,128)(2,1)S(1)} %get-tuple-element.57), channel_id=1, source_target_pairs={{0,8},{2,10},{4,12},{6,14},{8,0},{10,2},{12,4},{14,6},{16,24},{18,... | collective-permute-start | bytes 2359304 | tf_op jit(solution)/shard_map/ppermute | solution.py:349
  97.4 22.7 %collective-permute-start.20 = (bf16[64,3072]{1,0:T(8,128)(2,1)S(1)}, bf16[64,3072]{1,0:T(8,128)(2,1)S(1)}, u32[]{:S(2)}, u32[]{:S(2)}) collective-permute-start(bf16[64,3072]{1,0:T(8,128)(2,1)S(1)} %get-tuple-element.70), channel_id=1, source_target_pairs={{0,4},{1,3},{2,6},{3,1},{4,0},{5,7},{6,2},{7,5},{8,12},{9,11},{10,... | collective-permute-start | bytes 1179656 | tf_op jit(solution)/shard_map/ppermute | solution.py:349
  98.9 22.1 %collective-permute-start.21 = (bf16[64,3072]{1,0:T(8,128)(2,1)S(1)}, bf16[64,3072]{1,0:T(8,128)(2,1)S(1)}, u32[]{:S(2)}, u32[]{:S(2)}) collective-permute-start(bf16[64,3072]{1,0:T(8,128)(2,1)S(1)} %get-tuple-element.73), channel_id=1, source_target_pairs={{0,12},{2,14},{4,8},{6,10},{8,4},{10,6},{12,0},{14,2},{16,28},{18,... | collective-permute-start | bytes 1179656 | tf_op jit(solution)/shard_map/ppermute | solution.py:349
  113.1 7.9 %collective-permute-start.22 = (bf16[64,3072]{1,0:T(8,128)(2,1)S(1)}, bf16[64,3072]{1,0:T(8,128)(2,1)S(1)}, u32[]{:S(2)}, u32[]{:S(2)}) collective-permute-start(bf16[64,3072]{1,0:T(8,128)(2,1)S(1)} %get-tuple-element.60), channel_id=1, source_target_pairs={{0,8},{2,10},{4,12},{6,14},{8,0},{10,2},{12,4},{14,6},{16,24},{18,... | collective-permute-start | bytes 1179656 | tf_op jit(solution)/shard_map/ppermute | solution.py:349
  113.8 18.2 %collective-permute-start.24 = (bf16[64,3072]{1,0:T(8,128)(2,1)S(1)}, bf16[64,3072]{1,0:T(8,128)(2,1)S(1)}, u32[]{:S(2)}, u32[]{:S(2)}) collective-permute-start(bf16[64,3072]{1,0:T(8,128)(2,1)S(1)} %get-tuple-element.65), channel_id=1, source_target_pairs={{1,13},{3,15},{5,9},{7,11},{9,5},{11,7},{13,1},{15,3},{17,29},{19,... | collective-permute-start | bytes 1179656 | tf_op jit(solution)/shard_map/ppermute | solution.py:349
  117.8 14.2 %collective-permute-start.25 = (bf16[64,3072]{1,0:T(8,128)(2,1)S(1)}, bf16[64,3072]{1,0:T(8,128)(2,1)S(1)}, u32[]{:S(2)}, u32[]{:S(2)}) collective-permute-start(bf16[64,3072]{1,0:T(8,128)(2,1)S(1)} %get-tuple-element.66), channel_id=1, source_target_pairs={{1,9},{3,11},{5,13},{7,15},{9,1},{11,3},{13,5},{15,7},{17,25},{19,... | collective-permute-start | bytes 1179656 | tf_op jit(solution)/shard_map/ppermute | solution.py:349
  120.1 14.4 %collective-permute-start.23 = (bf16[64,3072]{1,0:T(8,128)(2,1)S(1)}, bf16[64,3072]{1,0:T(8,128)(2,1)S(1)}, u32[]{:S(2)}, u32[]{:S(2)}) collective-permute-start(bf16[64,3072]{1,0:T(8,128)(2,1)S(1)} %fusion.8), channel_id=1, source_target_pairs={{0,2},{1,5},{2,0},{3,7},{4,6},{5,1},{6,4},{7,3},{8,10},{9,13},{10,... | collective-permute-start | bytes 1179656 | tf_op jit(solution)/shard_map/ppermute | solution.py:349
  121.3 17.3 %collective-permute-start.27 = (bf16[32,3072]{1,0:T(8,128)(2,1)S(1)}, bf16[32,3072]{1,0:T(8,128)(2,1)S(1)}, u32[]{:S(2)}, u32[]{:S(2)}) collective-permute-start(bf16[32,3072]{1,0:T(8,128)(2,1)S(1)} %get-tuple-element.76), channel_id=1, source_target_pairs={{0,1},{1,0},{2,3},{3,2},{4,5},{5,4},{6,7},{7,6},{8,9},{9,8},{10,11... | collective-permute-start | bytes 589832 | tf_op jit(solution)/shard_map/ppermute | solution.py:349
  134.8 13.3 %collective-permute-start.26 = (bf16[32,3072]{1,0:T(8,128)(2,1)S(1)}, bf16[32,3072]{1,0:T(8,128)(2,1)S(1)}, u32[]{:S(2)}, u32[]{:S(2)}) collective-permute-start(bf16[32,3072]{1,0:T(8,128)(2,1)S(1)} %get-tuple-element.77), channel_id=1, source_target_pairs={{0,112},{1,113},{2,114},{3,115},{4,116},{5,117},{6,118},{7,119},{8... | collective-permute-start | bytes 589832 | tf_op jit(solution)/shard_map/ppermute | solution.py:349
  138.6 9.5 %collective-permute-start.28 = (bf16[32,3072]{1,0:T(8,128)(2,1)S(1)}, bf16[32,3072]{1,0:T(8,128)(2,1)S(1)}, u32[]{:S(2)}, u32[]{:S(2)}) collective-permute-start(bf16[32,3072]{1,0:T(8,128)(2,1)S(1)} %get-tuple-element.78), channel_id=1, source_target_pairs={{0,113},{1,112},{2,115},{3,114},{4,117},{5,116},{6,119},{7,118},{8... | collective-permute-start | bytes 589832 | tf_op jit(solution)/shard_map/ppermute | solution.py:349

commit v11 on v10

--- a/solution.py
+++ b/solution.py
@@ -148,7 +148,7 @@
     sub = qb // groups
     half = cols // 4
     limit = partner if foreign else place
-    y_first = core == (0 if foreign else 1)
+    y_first = core == 0
     n = len(SLOTS)
     if foreign:
         state = [pltpu.make_async_copy(refs[0], q_buf, sems.at[n + 1])]
@@ -293,11 +293,23 @@
     n = w.shape[1] // 2
     steps = n // tile
 
-    def body(info, a, b0, b1, wa, wb, *outs):
+    def body(info, a, b0, b1, w_hbm, wb, *refs):
+        *outs, w_buf, sems = refs
+        step = pl.program_id(0)
+
+        def copy(i):
+            first = pl.multiple_of((info[2] * steps + i) * tile, tile)
+            return pltpu.make_async_copy(w_hbm.at[:, pl.ds(first, tile)], w_buf.at[i], sems.at[i])
+
+        @pl.when(step == 0)
+        def _():
+            for i in range(steps):
+                copy(i).start()
+
         b = jnp.concatenate([b0[...], b1[...]], axis=0)
-        s = jnp.dot(a[...], wa[...], preferred_element_type=F32) + jnp.dot(
-            b, wb[...], preferred_element_type=F32
-        )
+        s = jnp.dot(b, wb[...], preferred_element_type=F32)
+        copy(step).wait()
+        s = s + jnp.dot(a[...], w_buf[step], preferred_element_type=F32)
         part = s.shape[0] // parts
         for i, o in enumerate(outs):
             o[...] = s[i * part : (i + 1) * part].astype(BF)
@@ -310,8 +322,9 @@
         grid_spec=pltpu.PrefetchScalarGridSpec(
             num_scalar_prefetch=1,
             grid=(steps,),
-            in_specs=[whole, half, half, weights, weights],
+            in_specs=[whole, half, half, pl.BlockSpec(memory_space=pltpu.HBM), weights],
             out_specs=[pl.BlockSpec((rows // parts, tile), lambda i, info: (0, i))] * parts,
+            scratch_shapes=[pltpu.VMEM((steps, width, tile), BF), pltpu.SemaphoreType.DMA((steps,))],
         ),
         out_shape=[jax.ShapeDtypeStruct((rows // parts, n), BF)] * parts,
         name="project",
@@ -369,27 +382,23 @@
     other = [swap_core(after(x, state[2])) for x in mine]
     q_far = over_all(after(q_away, state[2], *mine), lambda s, y, z, c: (n_seq - 1 - s, y, z, c))
 
-    def stage_one(parts, first):
-        return [
-            over_all(parts[1], lambda s, y, z, c: (s, y ^ 1, z, c) if c == first else (s, y, 1 - z, c)),
-            over_all(parts[3], lambda s, y, z, c: (s, y ^ 3, z, c) if c == first else (s, y, 1 - z, c)),
-            over_all(parts[2], lambda s, y, z, c: (s, y ^ 2, z, c) if c == first else None),
-        ]
-
-    def sum_one(parts, got, first):
+    def to_y_or_z(x, d):
+        return over_all(x, lambda s, y, z, c: (s, y, 1 - z, c) if c else (s, y ^ d, z, c))
+
+    def to_z_or_y(x):
+        return over_all(x, lambda s, y, z, c: (s, y ^ 1, z, c) if c else (s, y, 1 - z, c))
+
+    def to_y(x, *d):
+        d = (*d, None)
+        return over_all(x, lambda s, y, z, c: None if d[c] is None else (s, y ^ d[c], z, c))
+
+    def stage_sum(parts, got):
         along_y = parts[0].astype(F32) + got[0].astype(F32)
         extra = got[1].astype(F32) + got[2].astype(F32)
-        a = (along_y + jnp.where(core == first, extra, 0.0)).astype(BF)
+        a = (along_y + jnp.where(core == 0, extra, 0.0)).astype(BF)
         b = add(parts[2], got[1])
         n = a.shape[0] // 2
         return a[:n], a[n:], b[:n], b[n:]
-
-    def stage_two(total, first):
-        return [
-            over_all(total[1], lambda s, y, z, c: (s, y, 1 - z, c) if c == first else (s, y ^ 1, z, c)),
-            over_all(total[3], lambda s, y, z, c: None if c == first else (s, y ^ 3, z, c)),
-            over_all(total[2], lambda s, y, z, c: None if c == first else (s, y ^ 2, z, c)),
-        ]
 
     def by_core(x, same):
         return jnp.where((core == 0) == same, x[0], x[1])
@@ -398,18 +407,22 @@
     near, *near_peer = attend(info, kv, state, half, mine, other, n_y, n_seq)
     near_far = [swap_core(x) for x in near_peer]
     parts_n = project(info, near, near_far, w_out, w_other, n_y, cols // 4)
-    got_n = stage_one(parts_n, 1)
+    got_n = [to_y_or_z(parts_n[1], 1), to_y_or_z(parts_n[3], 3), to_y(parts_n[2], 2)]
     far, *far_peer = attend(after(info, parts_n[0]), kv, [q_far], half, mine, other, n_y, n_seq)
     far_far = [swap_core(x) for x in far_peer]
     parts_f = project(info, far, far_far, w_out, w_other, n_y, cols // 4)
-    got_f = stage_one(parts_f, 0)
-    total_n = sum_one([after(p, parts_f[0]) for p in parts_n], got_n, 1)
-    total_f = sum_one(parts_f, got_f, 0)
-    got2_n = stage_two((total_n[0], total_n[1], after(total_n[2], total_f[0]), total_n[3]), 1)
-    got2_f = stage_two(total_f, 0)
+    got_f = [to_y_or_z(parts_f[1], 1), to_y_or_z(parts_f[3], 3)]
+    total_n = stage_sum([after(p, parts_f[0]) for p in parts_n], got_n)
+    n = total_n[0].shape[0]
+    mixed_a = to_y(jnp.where(core == 0, parts_f[2][:n], total_n[2]), 2, 2)
+    mixed_b = to_y(jnp.where(core == 0, parts_f[2][n:], total_n[3]), 2, 3)
+    got_one = to_z_or_y(total_n[1])
+    total_f = stage_sum(parts_f, [*got_f, jnp.concatenate([mixed_a, mixed_b], axis=0)])
+    got2_f = [to_z_or_y(total_f[1]), to_y(total_f[3], None, 3), to_y(total_f[2], None, 2)]
+    rest = jnp.where(core == 0, 0.0, mixed_a.astype(F32) + mixed_b.astype(F32))
+    done_n = (total_n[0].astype(F32) + got_one.astype(F32) + rest).astype(BF).reshape(2, sub, cols // 2)
     done_f = add(total_f[0], *got2_f).reshape(2, sub, cols // 2)
-    done_n = add(after(total_n[0], total_f[0]), *got2_n).reshape(2, sub, cols // 2)
-    own_other = swap_core(after(by_core(done_n, False), done_f))
+    own_other = swap_core(by_core(done_n, False))
     home = over_all(by_core(done_f, True), lambda s, y, z, c: (n_seq - 1 - s, y, z, c))
     home_other = over_all(by_core(done_f, False), lambda s, y, z, c: (n_seq - 1 - s, y, z, 1 - c))
     here = jnp.concatenate([by_core(done_n, True), home], axis=0)

time: 150 us -> 161 us (1.073)
  waiting for transfers between devices: 50 us -> 60.7 us
  starting transfers between devices: 49.4 us -> 39.5 us
  other arithmetic: 4.53 us -> 7.99 us
  local copies, waits for them, and re-layouts: 5.95 us -> 9.35 us
  Pallas kernels: 39 us -> 41.1 us
    ppermute x29 -> x28, waiting for transfers between devices: 50 us -> 60.7 us  [over_all(): return lax.ppermute(x, ('seq', 'head'), pairs)]
    ppermute x29 -> x28, starting transfers between devices: 49.4 us -> 39.5 us  [over_all(): return lax.ppermute(x, ('seq', 'head'), pairs)]
    convert_element_type x1 -> x3, other arithmetic: 2.3 us -> 6.55 us  [the longest x2 5.33 us: stage_sum(): a = (along_y + jnp.where(core == 0, extra, 0.0)).astype(BF)]
    unnamed x15 -> x25, local copies, waits for them, and re-layouts: 5.08 us -> 8.59 us
    pallas_call x2, Pallas kernels: 12.4 us -> 14.6 us  [project(): pl.pallas_call(body, grid_spec=pltpu.PrefetchScalarGridSpec(num_scalar_pr...]
  transfers between devices with their start and end apart: 29 -> 28, of which waited for: 13 -> 14; matrix products, arithmetic and copies ran while one was open for 3% -> 5% of each run, Pallas kernels for 26% -> 26%
where the time goes in v11:
time: 161 us; the launch traced here: 159 us
  waiting for transfers between devices  60.7 us (38%)
  Pallas kernels  41.1 us (26%)
  starting transfers between devices  39.5 us (25%)
  local copies, waits for them, and re-layouts  9.35 us (6%)
  other arithmetic  7.99 us (5%)
    ppermute x28, waiting for transfers between devices, over_all(): return lax.ppermute(x, ('seq', 'head'), pairs)  60.7 us
    ppermute x28, starting transfers between devices, over_all(): return lax.ppermute(x, ('seq', 'head'), pairs)  39.5 us
    pallas_call x2, Pallas kernels, attend(): pl.pallas_call(functools.partial(attend_kernel, foreign, groups, n_y, n_s...  21.3 us
    pallas_call x2, Pallas kernels, project(): pl.pallas_call(body, grid_spec=pltpu.PrefetchScalarGridSpec(num_scalar_pr...  14.6 us
    unnamed x25, local copies, waits for them, and re-layouts  8.59 us
    convert_element_type x2, other arithmetic, stage_sum(): a = (along_y + jnp.where(core == 0, extra, 0.0)).astype(BF)  5.33 us
  transfers between devices with their start and end apart: 28, of which 14 were waited for; matrix products, arithmetic and copies ran while one was open for 5% of the time, Pallas kernels for 26%

profile of v11, /device:TPU:1, one launch (start us, length us, event | category | flops | bytes accessed | tf_op | source)
XLA Modules:
  0.0 159.0 jit_solution(836784222042682492)
XLA Ops:
  0.0 1.4 collective-permute-start.10
  1.4 0.6 stack.27.info
  2.1 2.6 %prep.1.kv_ref.own_ref = bf16[2048,128]{1,0:T(8,128)(2,1)} custom-call(s32[13]{0:T(128)} %stack.27.info, bf16[1024,1024]{1,0:T(8,128)(2,1)} %k_ref.1, bf16[1024,1024]{1,0:T(8,128)(2,1)} %v_ref.1), custom_call_target="tpu_custom_call" | custom-call | tf_op jit(solution)/shard_map/prep/pallas_call | solution.py:37
  4.7 0.7 collective-permute-start.3
  5.4 5.6 %collective-permute-start.2 = (bf16[2048,128]{1,0:T(8,128)(2,1)}, bf16[2048,128]{1,0:T(8,128)(2,1)S(1)}, u32[]{:S(2)}, u32[]{:S(2)}) collective-permute-start(bf16[2048,128]{1,0:T(8,128)(2,1)} %prep.1.kv_ref.own_ref), channel_id=1, source_target_pairs={{0,80},{1,17},{2,82},{3,19},{4,84},{5,21},{6,86},{7,23},{8,88},{9,... | collective-permute-start | bytes 1572872 | tf_op jit(solution)/shard_map/ppermute | solution.py:362
  11.0 3.1 %collective-permute-start.1 = (bf16[2048,128]{1,0:T(8,128)(2,1)}, bf16[2048,128]{1,0:T(8,128)(2,1)S(1)}, u32[]{:S(2)}, u32[]{:S(2)}) collective-permute-start(bf16[2048,128]{1,0:T(8,128)(2,1)} %prep.1.kv_ref.own_ref), channel_id=1, source_target_pairs={{0,96},{1,33},{2,98},{3,35},{4,100},{5,37},{6,102},{7,39},{8,104},... | collective-permute-start | bytes 1572872 | tf_op jit(solution)/shard_map/ppermute | solution.py:362
  14.1 1.9 %collective-permute-start = (bf16[2048,128]{1,0:T(8,128)(2,1)}, bf16[2048,128]{1,0:T(8,128)(2,1)S(1)}, u32[]{:S(2)}, u32[]{:S(2)}) collective-permute-start(bf16[2048,128]{1,0:T(8,128)(2,1)} %prep.1.kv_ref.own_ref), channel_id=1, source_target_pairs={{0,112},{1,49},{2,114},{3,51},{4,116},{5,53},{6,118},{7,55},{8,120... | collective-permute-start | bytes 1572872 | tf_op jit(solution)/shard_map/ppermute | solution.py:362
  16.0 1.0 copy-done.1
  17.1 1.2 copy-done.8
  18.3 2.6 %own.1 = (bf16[256,2048]{1,0:T(8,128)(2,1)S(1)}, f32[144,2048]{1,0:T(8,128)S(1)}, f32[8,2048]{1,0:T(8,128)S(1)}, bf16[16,32,512]{2,1,0:T(8,128)(2,1)S(1)}) custom-call(bf16[16,2,32,512]{3,2,1,0:T(8,128)(2,1)S(1)} %bitcast.9, bf16[16,2,32,512]{3,2,1,0:T(8,128)(2,1)S(1)} %bitcast.10, bf16[2048,128]{1,0:T(8,128)(2,1)S(1)} %copy-done.1), custom_call_target="tpu_custom_call" | custom-call | flops 2147483648 | bytes 8388608 | tf_op jit(solution)/shard_map/own/pallas_call | solution.py:108
  21.0 6.1 %collective-permute-done.1.refs_4_.refs_2_ = bf16[2048,128]{1,0:T(8,128)(2,1)S(1)} collective-permute-done((bf16[2048,128]{1,0:T(8,128)(2,1)}, bf16[2048,128]{1,0:T(8,128)(2,1)S(1)}, u32[]{:S(2)}, u32[]{:S(2)}) %collective-permute-start.1) | collective-permute-done | bytes 524320 | tf_op jit(solution)/shard_map/ppermute | solution.py:362
  27.1 13.9 %collective-permute-done.refs_3_.refs_1_ = bf16[2048,128]{1,0:T(8,128)(2,1)S(1)} collective-permute-done((bf16[2048,128]{1,0:T(8,128)(2,1)}, bf16[2048,128]{1,0:T(8,128)(2,1)S(1)}, u32[]{:S(2)}, u32[]{:S(2)}) %collective-permute-start) | collective-permute-done | bytes 524320 | tf_op jit(solution)/shard_map/ppermute | solution.py:362
  41.0 1.3 collective-permute-start.4
  42.3 0.5 collective-permute-start.6
  42.8 1.0 collective-permute-done.4.refs_7_.refs_5_
  43.8 1.7 %collective-permute-start.11 = (bf16[16,32,512]{2,1,0:T(8,128)(2,1)S(1)}, bf16[16,32,512]{2,1,0:T(8,128)(2,1)S(1)}, u32[]{:S(2)}, u32[]{:S(2)}) collective-permute-start(bf16[16,32,512]{2,1,0:T(8,128)(2,1)S(1)} %get-tuple-element.44), channel_id=1, source_target_pairs={{0,112},{1,113},{2,114},{3,115},{4,116},{5,117},{6,118},{7,119},{8... | collective-permute-start | bytes 1572872 | tf_op jit(solution)/shard_map/ppermute | solution.py:362
  45.5 0.5 collective-permute-done.7.refs_10_.refs_8_
  46.1 1.6 %attend_own.1 = (bf16[512,512]{1,0:T(8,128)(2,1)S(1)}, bf16[256,512]{1,0:T(8,128)(2,1)S(1)}, bf16[256,512]{1,0:T(8,128)(2,1)S(1)}) custom-call(s32[13]{0:T(128)S(1)} %copy-done.7, bf16[2048,128]{1,0:T(8,128)(2,1)S(1)} %copy-done.2, bf16[256,2048]{1,0:T(8,128)(2,1)S(1)} %get-tuple-element.31.refs_0_, f32[144,2048]{1,0:T(8,128)S(1)} %get-tuple-element.32.refs_1_, ...), custom_call_target="tpu_custom_call" | custom-call | flops 4294967296 | bytes 4194304 | tf_op jit(solution)/shard_map/attend_own/pallas_call | solution.py:263
  47.7 0.5 collective-permute-start.8
  48.3 1.0 collective-permute-done.8.b0
  49.3 0.4 collective-permute-done.9.b1
  49.7 7.3 %project.2 = (bf16[128,3072]{1,0:T(8,128)(2,1)S(1)}, bf16[128,3072]{1,0:T(8,128)(2,1)}, bf16[128,3072]{1,0:T(8,128)(2,1)S(1)}, bf16[128,3072]{1,0:T(8,128)(2,1)}) custom-call(s32[13]{0:T(128)S(1)} %copy-done.7, bf16[512,512]{1,0:T(8,128)(2,1)S(1)} %get-tuple-element.38.a, bf16[256,512]{1,0:T(8,128)(2,1)S(1)} %collective-permute-done.8.b0, ...), custom_call_target="tpu_custom_call" | custom-call | tf_op jit(solution)/shard_map/project/pallas_call | solution.py:320
  57.0 1.6 collective-permute-start.14
  58.7 1.6 %collective-permute-start.16 = (bf16[128,3072]{1,0:T(8,128)(2,1)S(1)}, bf16[128,3072]{1,0:T(8,128)(2,1)}, u32[]{:S(2)}, u32[]{:S(2)}) collective-permute-start(bf16[128,3072]{1,0:T(8,128)(2,1)S(1)} %get-tuple-element.54), channel_id=1, source_target_pairs={{0,8},{2,10},{4,12},{6,14},{8,0},{10,2},{12,4},{14,6},{16,24},{18,... | collective-permute-start | bytes 2359304 | tf_op jit(solution)/shard_map/ppermute | solution.py:362
  60.6 19.7 %attend_foreign.1 = (bf16[512,512]{1,0:T(8,128)(2,1)S(1)}, bf16[256,512]{1,0:T(8,128)(2,1)}, bf16[256,512]{1,0:T(8,128)(2,1)}) custom-call(s32[13]{0:T(128)S(1)} %copy-done.7, bf16[2048,128]{1,0:T(8,128)(2,1)S(1)} %copy-done.2, bf16[16,32,512]{2,1,0:T(8,128)(2,1)S(1)} %collective-permute-done.11.refs_0_, ...), custom_call_target="tpu_custom_call" | custom-call | flops 4294967296 | bytes 4194304 | tf_op jit(solution)/shard_map/attend_foreign/pallas_call | solution.py:263
  80.2 0.8 copy-done.3
  81.0 3.3 %collective-permute-start.12 = (bf16[256,512]{1,0:T(8,128)(2,1)}, bf16[256,512]{1,0:T(8,128)(2,1)S(1)}, u32[]{:S(2)}, u32[]{:S(2)}) collective-permute-start(bf16[256,512]{1,0:T(8,128)(2,1)} %get-tuple-element.46), channel_id=1, source_target_pairs={{0,1},{1,0},{2,3},{3,2},{4,5},{5,4},{6,7},{7,6},{8,9},{9,8},{10,11... | collective-permute-start | bytes 786440 | tf_op jit(solution)/shard_map/ppermute | solution.py:362
  84.3 1.4 collective-permute-done.12.b0
  86.1 0.7 copy-done.5
  86.8 2.8 %copy-done = bf16[512,6144]{1,0:T(8,128)(2,1)S(1)} copy-done((bf16[512,6144]{1,0:T(8,128)(2,1)S(1)}, bf16[512,6144]{1,0:T(8,128)(2,1)}, u32[]{:S(2)}) %copy-start) | copy-done | bytes 6291480
  89.6 1.0 copy-done.4
  90.6 0.9 copy-done.6
  91.6 7.3 %project.3 = (bf16[128,3072]{1,0:T(8,128)(2,1)S(1)}, bf16[128,3072]{1,0:T(8,128)(2,1)}, bf16[128,3072]{1,0:T(8,128)(2,1)S(1)}, bf16[128,3072]{1,0:T(8,128)(2,1)}) custom-call(s32[13]{0:T(128)S(1)} %copy-done.7, bf16[512,512]{1,0:T(8,128)(2,1)S(1)} %copy-done.4, bf16[256,512]{1,0:T(8,128)(2,1)S(1)} %collective-permute-done.12.b0, ...), custom_call_target="tpu_custom_call" | custom-call | tf_op jit(solution)/shard_map/project/pallas_call | solution.py:320
  98.9 1.6 collective-permute-start.20
  100.6 3.2 %fusion.2 = (bf16[128,3072]{1,0:T(8,128)(2,1)}, bf16[128,3072]{1,0:T(8,128)(2,1)S(1)}) fusion(bf16[128,3072]{1,0:T(8,128)(2,1)} %collective-permute-done.15, bf16[128,3072]{1,0:T(8,128)(2,1)} %collective-permute-done.16, bf16[128,3072]{1,0:T(8,128)(2,1)} %collective-permute-done.14, bf16[128,3072]{1,0:T(8,128)(2,1)S(1)} %get-tuple-element.49, pred[]{:T(512)S(6)} %eq.7, ...), kind=kLoop, calls=%fused_computation.6 | loop fusion | flops 4718592 | bytes 5505025 | tf_op jit(solution)/shard_map/convert_element_type | solution.py:398
  103.8 2.6 %collective-permute-start.18 = (bf16[64,3072]{1,0:T(8,128)(2,1)S(1)}, bf16[64,3072]{1,0:T(8,128)(2,1)S(1)}, u32[]{:S(2)}, u32[]{:S(2)}) collective-permute-start(bf16[64,3072]{1,0:T(8,128)(2,1)S(1)} %get-tuple-element.57), channel_id=1, source_target_pairs={{0,8},{1,9},{2,10},{3,11},{4,12},{5,13},{6,14},{7,15},{8,0},{9,1},... | collective-permute-start | bytes 1179656 | tf_op jit(solution)/shard_map/ppermute | solution.py:362
  106.5 0.8 collective-permute-start.19
  107.3 3.1 %collective-permute-done.20 = bf16[128,3072]{1,0:T(8,128)(2,1)} collective-permute-done((bf16[128,3072]{1,0:T(8,128)(2,1)}, bf16[128,3072]{1,0:T(8,128)(2,1)}, u32[]{:S(2)}, u32[]{:S(2)}) %collective-permute-start.20) | collective-permute-done | bytes 786464 | tf_op jit(solution)/shard_map/ppermute | solution.py:362
  110.5 12.6 %collective-permute-done.21 = bf16[128,3072]{1,0:T(8,128)(2,1)} collective-permute-done((bf16[128,3072]{1,0:T(8,128)(2,1)}, bf16[128,3072]{1,0:T(8,128)(2,1)}, u32[]{:S(2)}, u32[]{:S(2)}) %collective-permute-start.21) | collective-permute-done | bytes 786464 | tf_op jit(solution)/shard_map/ppermute | solution.py:362
  123.1 7.4 %collective-permute-done.19 = bf16[64,3072]{1,0:T(8,128)(2,1)} collective-permute-done((bf16[64,3072]{1,0:T(8,128)(2,1)S(1)}, bf16[64,3072]{1,0:T(8,128)(2,1)}, u32[]{:S(2)}, u32[]{:S(2)}) %collective-permute-start.19) | collective-permute-done | bytes 393248 | tf_op jit(solution)/shard_map/ppermute | solution.py:362
  130.5 2.2 %fusion.6 = (bf16[128,3072]{1,0:T(8,128)(2,1)S(1)}, bf16[128,3072]{1,0:T(8,128)(2,1)S(1)}) fusion(bf16[128,3072]{1,0:T(8,128)(2,1)} %collective-permute-done.21, bf16[128,3072]{1,0:T(8,128)(2,1)} %collective-permute-done.20, bf16[128,3072]{1,0:T(8,128)(2,1)S(1)} %get-tuple-element.48, bf16[64,3072]{1,0:T(8,128)(2,1)} %collective-permute-done.19, ...), kind=kLoop, calls=%fused_computation.10 | loop fusion | flops 5898240 | bytes 5505025 | tf_op jit(solution)/shard_map/convert_element_type | solution.py:398
  132.8 3.5 %collective-permute-start.23 = (bf16[64,3072]{1,0:T(8,128)(2,1)S(1)}, bf16[64,3072]{1,0:T(8,128)(2,1)S(1)}, u32[]{:S(2)}, u32[]{:S(2)}) collective-permute-start(bf16[64,3072]{1,0:T(8,128)(2,1)S(1)} %get-tuple-element.63), channel_id=1, source_target_pairs={{1,13},{3,15},{5,9},{7,11},{9,5},{11,7},{13,1},{15,3},{17,29},{19,... | collective-permute-start | bytes 1179656 | tf_op jit(solution)/shard_map/ppermute | solution.py:362
  136.3 3.5 %collective-permute-start.24 = (bf16[64,3072]{1,0:T(8,128)(2,1)S(1)}, bf16[64,3072]{1,0:T(8,128)(2,1)S(1)}, u32[]{:S(2)}, u32[]{:S(2)}) collective-permute-start(bf16[64,3072]{1,0:T(8,128)(2,1)S(1)} %get-tuple-element.64), channel_id=1, source_target_pairs={{1,9},{3,11},{5,13},{7,15},{9,1},{11,3},{13,5},{15,7},{17,25},{19,... | collective-permute-start | bytes 1179656 | tf_op jit(solution)/shard_map/ppermute | solution.py:362
  139.9 1.2 add_convert_fusion.1
  141.3 5.5 %collective-permute-done.23 = bf16[64,3072]{1,0:T(8,128)(2,1)S(1)} collective-permute-done((bf16[64,3072]{1,0:T(8,128)(2,1)S(1)}, bf16[64,3072]{1,0:T(8,128)(2,1)S(1)}, u32[]{:S(2)}, u32[]{:S(2)}) %collective-permute-start.23) | collective-permute-done | bytes 393248 | tf_op jit(solution)/shard_map/ppermute | solution.py:362
  147.1 3.6 %collective-permute-start.25 = (bf16[32,3072]{1,0:T(8,128)(2,1)S(1)}, bf16[32,3072]{1,0:T(8,128)(2,1)S(1)}, u32[]{:S(2)}, u32[]{:S(2)}) collective-permute-start(bf16[32,3072]{1,0:T(8,128)(2,1)S(1)} %get-tuple-element.69), channel_id=1, source_target_pairs={{0,112},{1,113},{2,114},{3,115},{4,116},{5,117},{6,118},{7,119},{8... | collective-permute-start | bytes 589832 | tf_op jit(solution)/shard_map/ppermute | solution.py:362
  150.7 7.1 %collective-permute-done.27 = bf16[32,3072]{1,0:T(8,128)(2,1)S(1)} collective-permute-done((bf16[32,3072]{1,0:T(8,128)(2,1)S(1)}, bf16[32,3072]{1,0:T(8,128)(2,1)S(1)}, u32[]{:S(2)}, u32[]{:S(2)}) %collective-permute-start.27) | collective-permute-done | bytes 196640 | tf_op jit(solution)/shard_map/ppermute | solution.py:362
  158.0 0.9 pad_maximum_fusion
  (54 shorter events, 2.0 us)
Async XLA Ops:
  0.0 49.7 %collective-permute-start.10 = (bf16[512,6144]{1,0:T(8,128)(2,1)}, bf16[512,6144]{1,0:T(8,128)(2,1)}, u32[]{:S(2)}, u32[]{:S(2)}) collective-permute-start(bf16[512,6144]{1,0:T(8,128)(2,1)} %w_hbm.3), channel_id=1, source_target_pairs={{0,1},{1,0},{2,3},{3,2},{4,5},{5,4},{6,7},{7,6},{8,9},{9,8},{10,11... | collective-permute-start | bytes 18874376 | tf_op jit(solution)/shard_map/ppermute | solution.py:362
  4.7 16.3 %collective-permute-start.3 = (bf16[2048,128]{1,0:T(8,128)(2,1)}, bf16[2048,128]{1,0:T(8,128)(2,1)S(1)}, u32[]{:S(2)}, u32[]{:S(2)}) collective-permute-start(bf16[2048,128]{1,0:T(8,128)(2,1)} %prep.1.kv_ref.own_ref), channel_id=1, source_target_pairs={{0,64},{2,66},{4,68},{6,70},{8,72},{10,74},{12,76},{14,78},{16,80}... | collective-permute-start | bytes 1572872 | tf_op jit(solution)/shard_map/ppermute | solution.py:362
  5.4 15.6 %collective-permute-start.2 = (bf16[2048,128]{1,0:T(8,128)(2,1)}, bf16[2048,128]{1,0:T(8,128)(2,1)S(1)}, u32[]{:S(2)}, u32[]{:S(2)}) collective-permute-start(bf16[2048,128]{1,0:T(8,128)(2,1)} %prep.1.kv_ref.own_ref), channel_id=1, source_target_pairs={{0,80},{1,17},{2,82},{3,19},{4,84},{5,21},{6,86},{7,23},{8,88},{9,... | collective-permute-start | bytes 1572872 | tf_op jit(solution)/shard_map/ppermute | solution.py:362
  11.0 16.1 %collective-permute-start.1 = (bf16[2048,128]{1,0:T(8,128)(2,1)}, bf16[2048,128]{1,0:T(8,128)(2,1)S(1)}, u32[]{:S(2)}, u32[]{:S(2)}) collective-permute-start(bf16[2048,128]{1,0:T(8,128)(2,1)} %prep.1.kv_ref.own_ref), channel_id=1, source_target_pairs={{0,96},{1,33},{2,98},{3,35},{4,100},{5,37},{6,102},{7,39},{8,104},... | collective-permute-start | bytes 1572872 | tf_op jit(solution)/shard_map/ppermute | solution.py:362
  14.1 26.9 %collective-permute-start = (bf16[2048,128]{1,0:T(8,128)(2,1)}, bf16[2048,128]{1,0:T(8,128)(2,1)S(1)}, u32[]{:S(2)}, u32[]{:S(2)}) collective-permute-start(bf16[2048,128]{1,0:T(8,128)(2,1)} %prep.1.kv_ref.own_ref), channel_id=1, source_target_pairs={{0,112},{1,49},{2,114},{3,51},{4,116},{5,53},{6,118},{7,55},{8,120... | collective-permute-start | bytes 1572872 | tf_op jit(solution)/shard_map/ppermute | solution.py:362
  16.0 1.1 copy-start.1
  17.1 1.2 copy-start.8
  18.3 27.8 %copy-start.2 = (bf16[2048,128]{1,0:T(8,128)(2,1)S(1)}, bf16[2048,128]{1,0:T(8,128)(2,1)}, u32[]{:S(2)}) copy-start(bf16[2048,128]{1,0:T(8,128)(2,1)} %prep.1.kv_ref.own_ref) | copy-start | bytes 1572868
  18.3 27.8 %copy-start.7 = (s32[13]{0:T(128)S(1)}, s32[13]{0:T(128)}, u32[]{:S(2)}) copy-start(s32[13]{0:T(128)} %stack.27.info) | copy-start | bytes 160
  41.0 2.8 %collective-permute-start.4 = (bf16[2048,128]{1,0:T(8,128)(2,1)S(1)}, bf16[2048,128]{1,0:T(8,128)(2,1)S(1)}, u32[]{:S(2)}, u32[]{:S(2)}) collective-permute-start(bf16[2048,128]{1,0:T(8,128)(2,1)S(1)} %collective-permute-done.refs_3_.refs_1_), channel_id=1, source_target_pairs={{0,1},{1,0},{2,3},{3,2},{4,5},{5,4},{6,7},{7,6},{8,9},{9,8},{10,11... | collective-permute-start | bytes 1572872 | tf_op jit(solution)/shard_map/ppermute | solution.py:362
  42.3 3.3 %collective-permute-start.5 = (bf16[2048,128]{1,0:T(8,128)(2,1)S(1)}, bf16[2048,128]{1,0:T(8,128)(2,1)S(1)}, u32[]{:S(2)}, u32[]{:S(2)}) collective-permute-start(bf16[2048,128]{1,0:T(8,128)(2,1)S(1)} %collective-permute-done.1.refs_4_.refs_2_), channel_id=1, source_target_pairs={{0,1},{1,0},{2,3},{3,2},{4,5},{5,4},{6,7},{7,6},{8,9},{9,8},{10,11... | collective-permute-start | bytes 1572872 | tf_op jit(solution)/shard_map/ppermute | solution.py:362
  42.3 3.3 %collective-permute-start.6 = (bf16[2048,128]{1,0:T(8,128)(2,1)S(1)}, bf16[2048,128]{1,0:T(8,128)(2,1)S(1)}, u32[]{:S(2)}, u32[]{:S(2)}) collective-permute-start(bf16[2048,128]{1,0:T(8,128)(2,1)S(1)} %collective-permute-done.2.refs_5_.refs_3_), channel_id=1, source_target_pairs={{0,1},{1,0},{2,3},{3,2},{4,5},{5,4},{6,7},{7,6},{8,9},{9,8},{10,11... | collective-permute-start | bytes 1572872 | tf_op jit(solution)/shard_map/ppermute | solution.py:362
  42.8 3.3 %collective-permute-start.7 = (bf16[2048,128]{1,0:T(8,128)(2,1)S(1)}, bf16[2048,128]{1,0:T(8,128)(2,1)S(1)}, u32[]{:S(2)}, u32[]{:S(2)}) collective-permute-start(bf16[2048,128]{1,0:T(8,128)(2,1)S(1)} %collective-permute-done.3.refs_6_.refs_4_), channel_id=1, source_target_pairs={{0,1},{1,0},{2,3},{3,2},{4,5},{5,4},{6,7},{7,6},{8,9},{9,8},{10,11... | collective-permute-start | bytes 1572872 | tf_op jit(solution)/shard_map/ppermute | solution.py:362
  43.8 16.8 %collective-permute-start.11 = (bf16[16,32,512]{2,1,0:T(8,128)(2,1)S(1)}, bf16[16,32,512]{2,1,0:T(8,128)(2,1)S(1)}, u32[]{:S(2)}, u32[]{:S(2)}) collective-permute-start(bf16[16,32,512]{2,1,0:T(8,128)(2,1)S(1)} %get-tuple-element.44), channel_id=1, source_target_pairs={{0,112},{1,113},{2,114},{3,115},{4,116},{5,117},{6,118},{7,119},{8... | collective-permute-start | bytes 1572872 | tf_op jit(solution)/shard_map/ppermute | solution.py:362
  46.0 3.6 %slice-start = ((s8[6291456]{0:T(1024)(128)(4,1)}), s8[4194304]{0:T(1024)(128)(4,1)S(1)}, s32[]{:S(2)}) async-start(s8[6291456]{0:T(1024)(128)(4,1)} %bitcast.7), calls=%async_computation | async-start | bytes 8388608
  46.1 3.6 %slice-start.1 = ((s8[6291456]{0:T(1024)(128)(4,1)}), s8[2097152]{0:T(1024)(128)(4,1)S(1)}, s32[]{:S(2)}) async-start(s8[6291456]{0:T(1024)(128)(4,1)} %bitcast.7), calls=%async_computation.1 | async-start | bytes 4194304
  47.7 1.6 %collective-permute-start.8 = (bf16[256,512]{1,0:T(8,128)(2,1)S(1)}, bf16[256,512]{1,0:T(8,128)(2,1)S(1)}, u32[]{:S(2)}, u32[]{:S(2)}) collective-permute-start(bf16[256,512]{1,0:T(8,128)(2,1)S(1)} %get-tuple-element.39), channel_id=1, source_target_pairs={{0,1},{1,0},{2,3},{3,2},{4,5},{5,4},{6,7},{7,6},{8,9},{9,8},{10,11... | collective-permute-start | bytes 786440 | tf_op jit(solution)/shard_map/ppermute | solution.py:362
  48.1 1.5 collective-permute-start.9
  57.0 43.6 %collective-permute-start.14 = (bf16[128,3072]{1,0:T(8,128)(2,1)}, bf16[128,3072]{1,0:T(8,128)(2,1)}, u32[]{:S(2)}, u32[]{:S(2)}) collective-permute-start(bf16[128,3072]{1,0:T(8,128)(2,1)} %get-tuple-element.50), channel_id=1, source_target_pairs={{0,4},{1,3},{2,6},{3,1},{4,0},{5,7},{6,2},{7,5},{8,12},{9,11},{10,... | collective-permute-start | bytes 2359304 | tf_op jit(solution)/shard_map/ppermute | solution.py:362
  58.6 42.0 %collective-permute-start.15 = (bf16[128,3072]{1,0:T(8,128)(2,1)}, bf16[128,3072]{1,0:T(8,128)(2,1)}, u32[]{:S(2)}, u32[]{:S(2)}) collective-permute-start(bf16[128,3072]{1,0:T(8,128)(2,1)} %get-tuple-element.51), channel_id=1, source_target_pairs={{0,12},{1,3},{2,14},{3,1},{4,8},{5,7},{6,10},{7,5},{8,4},{9,11},{1... | collective-permute-start | bytes 2359304 | tf_op jit(solution)/shard_map/ppermute | solution.py:362
  58.7 41.9 %collective-permute-start.16 = (bf16[128,3072]{1,0:T(8,128)(2,1)S(1)}, bf16[128,3072]{1,0:T(8,128)(2,1)}, u32[]{:S(2)}, u32[]{:S(2)}) collective-permute-start(bf16[128,3072]{1,0:T(8,128)(2,1)S(1)} %get-tuple-element.54), channel_id=1, source_target_pairs={{0,8},{2,10},{4,12},{6,14},{8,0},{10,2},{12,4},{14,6},{16,24},{18,... | collective-permute-start | bytes 2359304 | tf_op jit(solution)/shard_map/ppermute | solution.py:362
  80.2 0.8 copy-start.3
  81.0 4.7 %collective-permute-start.12 = (bf16[256,512]{1,0:T(8,128)(2,1)}, bf16[256,512]{1,0:T(8,128)(2,1)S(1)}, u32[]{:S(2)}, u32[]{:S(2)}) collective-permute-start(bf16[256,512]{1,0:T(8,128)(2,1)} %get-tuple-element.46), channel_id=1, source_target_pairs={{0,1},{1,0},{2,3},{3,2},{4,5},{5,4},{6,7},{7,6},{8,9},{9,8},{10,11... | collective-permute-start | bytes 786440 | tf_op jit(solution)/shard_map/ppermute | solution.py:362
  84.3 1.7 %collective-permute-start.13 = (bf16[256,512]{1,0:T(8,128)(2,1)}, bf16[256,512]{1,0:T(8,128)(2,1)S(1)}, u32[]{:S(2)}, u32[]{:S(2)}) collective-permute-start(bf16[256,512]{1,0:T(8,128)(2,1)} %get-tuple-element.47), channel_id=1, source_target_pairs={{0,1},{1,0},{2,3},{3,2},{4,5},{5,4},{6,7},{7,6},{8,9},{9,8},{10,11... | collective-permute-start | bytes 786440 | tf_op jit(solution)/shard_map/ppermute | solution.py:362
  86.1 0.7 copy-start.5
  86.8 2.8 %copy-start = (bf16[512,6144]{1,0:T(8,128)(2,1)S(1)}, bf16[512,6144]{1,0:T(8,128)(2,1)}, u32[]{:S(2)}) copy-start(bf16[512,6144]{1,0:T(8,128)(2,1)} %w_hbm.3) | copy-start | bytes 18874372
  89.6 1.0 copy-start.4
  90.6 0.9 copy-start.6
  98.9 11.6 %collective-permute-start.20 = (bf16[128,3072]{1,0:T(8,128)(2,1)}, bf16[128,3072]{1,0:T(8,128)(2,1)}, u32[]{:S(2)}, u32[]{:S(2)}) collective-permute-start(bf16[128,3072]{1,0:T(8,128)(2,1)} %get-tuple-element.55), channel_id=1, source_target_pairs={{0,4},{1,3},{2,6},{3,1},{4,0},{5,7},{6,2},{7,5},{8,12},{9,11},{10,... | collective-permute-start | bytes 2359304 | tf_op jit(solution)/shard_map/ppermute | solution.py:362
  100.5 22.6 %collective-permute-start.21 = (bf16[128,3072]{1,0:T(8,128)(2,1)}, bf16[128,3072]{1,0:T(8,128)(2,1)}, u32[]{:S(2)}, u32[]{:S(2)}) collective-permute-start(bf16[128,3072]{1,0:T(8,128)(2,1)} %get-tuple-element.56), channel_id=1, source_target_pairs={{0,12},{1,3},{2,14},{3,1},{4,8},{5,7},{6,10},{7,5},{8,4},{9,11},{1... | collective-permute-start | bytes 2359304 | tf_op jit(solution)/shard_map/ppermute | solution.py:362
  103.7 3.5 %copy-start.9 = (bf16[128,3072]{1,0:T(8,128)(2,1)S(1)}, bf16[128,3072]{1,0:T(8,128)(2,1)}, u32[]{:S(2)}) copy-start(bf16[128,3072]{1,0:T(8,128)(2,1)} %get-tuple-element.65) | copy-start | bytes 2359300
  103.8 19.2 %collective-permute-start.18 = (bf16[64,3072]{1,0:T(8,128)(2,1)S(1)}, bf16[64,3072]{1,0:T(8,128)(2,1)S(1)}, u32[]{:S(2)}, u32[]{:S(2)}) collective-permute-start(bf16[64,3072]{1,0:T(8,128)(2,1)S(1)} %get-tuple-element.57), channel_id=1, source_target_pairs={{0,8},{1,9},{2,10},{3,11},{4,12},{5,13},{6,14},{7,15},{8,0},{9,1},... | collective-permute-start | bytes 1179656 | tf_op jit(solution)/shard_map/ppermute | solution.py:362
  106.5 24.0 %collective-permute-start.19 = (bf16[64,3072]{1,0:T(8,128)(2,1)S(1)}, bf16[64,3072]{1,0:T(8,128)(2,1)}, u32[]{:S(2)}, u32[]{:S(2)}) collective-permute-start(bf16[64,3072]{1,0:T(8,128)(2,1)S(1)} %get-tuple-element.58), channel_id=1, source_target_pairs={{0,8},{1,13},{2,10},{3,15},{4,12},{5,9},{6,14},{7,11},{8,0},{9,5},... | collective-permute-start | bytes 1179656 | tf_op jit(solution)/shard_map/ppermute | solution.py:362
  107.3 32.6 %collective-permute-start.17 = (bf16[64,3072]{1,0:T(8,128)(2,1)S(1)}, bf16[64,3072]{1,0:T(8,128)(2,1)S(1)}, u32[]{:S(2)}, u32[]{:S(2)}) collective-permute-start(bf16[64,3072]{1,0:T(8,128)(2,1)S(1)} %slice.65), channel_id=1, source_target_pairs={{0,2},{1,5},{2,0},{3,7},{4,6},{5,1},{6,4},{7,3},{8,10},{9,13},{10,... | collective-permute-start | bytes 1179656 | tf_op jit(solution)/shard_map/ppermute | solution.py:362
  132.7 8.6 %collective-permute-start.22 = (bf16[64,3072]{1,0:T(8,128)(2,1)S(1)}, bf16[64,3072]{1,0:T(8,128)(2,1)S(1)}, u32[]{:S(2)}, u32[]{:S(2)}) collective-permute-start(bf16[64,3072]{1,0:T(8,128)(2,1)S(1)} %slice.71), channel_id=1, source_target_pairs={{0,2},{1,5},{2,0},{3,7},{4,6},{5,1},{6,4},{7,3},{8,10},{9,13},{10,... | collective-permute-start | bytes 1179656 | tf_op jit(solution)/shard_map/ppermute | solution.py:362
  132.8 13.9 %collective-permute-start.23 = (bf16[64,3072]{1,0:T(8,128)(2,1)S(1)}, bf16[64,3072]{1,0:T(8,128)(2,1)S(1)}, u32[]{:S(2)}, u32[]{:S(2)}) collective-permute-start(bf16[64,3072]{1,0:T(8,128)(2,1)S(1)} %get-tuple-element.63), channel_id=1, source_target_pairs={{1,13},{3,15},{5,9},{7,11},{9,5},{11,7},{13,1},{15,3},{17,29},{19,... | collective-permute-start | bytes 1179656 | tf_op jit(solution)/shard_map/ppermute | solution.py:362
  136.3 10.4 %collective-permute-start.24 = (bf16[64,3072]{1,0:T(8,128)(2,1)S(1)}, bf16[64,3072]{1,0:T(8,128)(2,1)S(1)}, u32[]{:S(2)}, u32[]{:S(2)}) collective-permute-start(bf16[64,3072]{1,0:T(8,128)(2,1)S(1)} %get-tuple-element.64), channel_id=1, source_target_pairs={{1,9},{3,11},{5,13},{7,15},{9,1},{11,3},{13,5},{15,7},{17,25},{19,... | collective-permute-start | bytes 1179656 | tf_op jit(solution)/shard_map/ppermute | solution.py:362
  141.2 5.9 %collective-permute-start.26 = (bf16[32,3072]{1,0:T(8,128)(2,1)S(1)}, bf16[32,3072]{1,0:T(8,128)(2,1)S(1)}, u32[]{:S(2)}, u32[]{:S(2)}) collective-permute-start(bf16[32,3072]{1,0:T(8,128)(2,1)S(1)} %get-tuple-element.68), channel_id=1, source_target_pairs={{0,1},{1,0},{2,3},{3,2},{4,5},{5,4},{6,7},{7,6},{8,9},{9,8},{10,11... | collective-permute-start | bytes 589832 | tf_op jit(solution)/shard_map/ppermute | solution.py:362
  147.0 10.9 %collective-permute-start.27 = (bf16[32,3072]{1,0:T(8,128)(2,1)S(1)}, bf16[32,3072]{1,0:T(8,128)(2,1)S(1)}, u32[]{:S(2)}, u32[]{:S(2)}) collective-permute-start(bf16[32,3072]{1,0:T(8,128)(2,1)S(1)} %get-tuple-element.70), channel_id=1, source_target_pairs={{0,113},{1,112},{2,115},{3,114},{4,117},{5,116},{6,119},{7,118},{8... | collective-permute-start | bytes 589832 | tf_op jit(solution)/shard_map/ppermute | solution.py:362
  147.1 10.8 %collective-permute-start.25 = (bf16[32,3072]{1,0:T(8,128)(2,1)S(1)}, bf16[32,3072]{1,0:T(8,128)(2,1)S(1)}, u32[]{:S(2)}, u32[]{:S(2)}) collective-permute-start(bf16[32,3072]{1,0:T(8,128)(2,1)S(1)} %get-tuple-element.69), channel_id=1, source_target_pairs={{0,112},{1,113},{2,114},{3,115},{4,116},{5,117},{6,118},{7,119},{8... | collective-permute-start | bytes 589832 | tf_op jit(solution)/shard_map/ppermute | solution.py:362

commit v12 on v10

--- a/solution.py
+++ b/solution.py
@@ -25,27 +25,27 @@
 
 
 def prep_kernel(info, k_ref, v_ref, kv_ref):
-    rows = k_ref.shape[0]
-    kv_ref[0:rows, :] = k_ref[...]
-    for t in range(rows // DH):
-        kv_ref[rows + t * DH : rows + (t + 1) * DH, :] = v_ref[t * DH : (t + 1) * DH, :].T
-
-
-def prep(info, keys, values):
+    kv_ref[0] = k_ref[...]
+    for t in range(v_ref.shape[0] // DH):
+        kv_ref[1, t * DH : (t + 1) * DH, :] = v_ref[t * DH : (t + 1) * DH, :].T
+
+
+def prep(info, keys, values, steps=4):
     rows = keys.shape[0]
-    col = pl.BlockSpec((rows, DH), lambda i, info: (0, info[1]))
+    part = rows // steps
+    col = pl.BlockSpec((part, DH), lambda i, info: (i, info[1]))
     return pl.pallas_call(
         prep_kernel,
         grid_spec=pltpu.PrefetchScalarGridSpec(
             num_scalar_prefetch=1,
-            grid=(1,),
+            grid=(steps,),
             in_specs=[col, col],
-            out_specs=pl.BlockSpec((2 * rows, DH), lambda i, info: (0, 0)),
+            out_specs=pl.BlockSpec((2, part, DH), lambda i, info: (0, i, 0)),
         ),
-        out_shape=jax.ShapeDtypeStruct((2 * rows, DH), BF),
+        out_shape=jax.ShapeDtypeStruct((2, rows, DH), BF),
         name="prep",
         compiler_params=pltpu.CompilerParams(vmem_limit_bytes=64 << 20),
-    )(info, keys, values)
+    )(info, keys, values).reshape(2 * rows, DH)
 
 
 def keys_of(kv):
@@ -135,7 +135,7 @@
 
 def attend_kernel(foreign, groups, n_y, n_seq, info, own_ref, *refs):
     ops = n_seq // 2
-    inputs = 1 if foreign else 3
+    inputs = 2 if foreign else 3
     mine, other = refs[inputs : inputs + ops], refs[inputs + ops : inputs + 2 * ops]
     o_ref, first_ref, second_ref, q_buf, kv_buf, qt_ref, acc_ref, m_ref, mx_ref, peer_buf, count, sems = refs[
         inputs + 2 * ops :
@@ -253,7 +253,7 @@
 
 
 def attend(info, kv, state, q_shape, mine, other, n_y, n_seq):
-    foreign = len(state) == 1
+    foreign = len(state) == 2
     groups, sub, width = q_shape
     qb = groups * sub
     cols = qb * width // DH
@@ -399,7 +399,7 @@
     near_far = [swap_core(x) for x in near_peer]
     parts_n = project(info, near, near_far, w_out, w_other, n_y, cols // 4)
     got_n = stage_one(parts_n, 1)
-    far, *far_peer = attend(after(info, parts_n[0]), kv, [q_far], half, mine, other, n_y, n_seq)
+    far, *far_peer = attend(after(info, parts_n[0]), kv, [q_far, w_out], half, mine, other, n_y, n_seq)
     far_far = [swap_core(x) for x in far_peer]
     parts_f = project(info, far, far_far, w_out, w_other, n_y, cols // 4)
     got_f = stage_one(parts_f, 0)

time: 150 us -> 151 us (level)
  transfers between devices with their start and end apart: 29 -> 29, of which waited for: 13 -> 13; matrix products, arithmetic and copies ran while one was open for 3% -> 3% of each run, Pallas kernels for 26% -> 27%
where the time goes in v12:
time: 151 us; the launch traced here: 150 us
  waiting for transfers between devices  49.7 us (33%)
  starting transfers between devices  48.9 us (32%)
  Pallas kernels  40.2 us (27%)
  local copies, waits for them, and re-layouts  5.95 us (4%)
  other arithmetic  4.53 us (3%)
    ppermute x29, waiting for transfers between devices, over_all(): return lax.ppermute(x, ('seq', 'head'), pairs)  49.7 us
    ppermute x29, starting transfers between devices, over_all(): return lax.ppermute(x, ('seq', 'head'), pairs)  48.9 us
    pallas_call x2, Pallas kernels, attend(): pl.pallas_call(functools.partial(attend_kernel, foreign, groups, n_y, n_s...  21.3 us
    pallas_call x2, Pallas kernels, project(): pl.pallas_call(body, grid_spec=pltpu.PrefetchScalarGridSpec(num_scalar_pr...  12.4 us
    unnamed x15, local copies, waits for them, and re-layouts  5.08 us
    pallas_call x1, Pallas kernels, prep(): pl.pallas_call(prep_kernel, grid_spec=pltpu.PrefetchScalarGridSpec(num_sc...  3.89 us
  transfers between devices with their start and end apart: 29, of which 13 were waited for; matrix products, arithmetic and copies ran while one was open for 3% of the time, Pallas kernels for 27%

profile of v12, /device:TPU:1, one launch (start us, length us, event | category | flops | bytes accessed | tf_op | source)
XLA Modules:
  0.0 149.6 jit_solution(1380728341086021612)
XLA Ops:
  0.0 1.4 collective-permute-start.10
  1.4 0.7 stack.27.info
  2.1 3.9 %prep.1 = bf16[2,1024,128]{2,1,0:T(8,128)(2,1)} custom-call(s32[13]{0:T(128)} %stack.27.info, bf16[1024,1024]{1,0:T(8,128)(2,1)} %k_ref.1, bf16[1024,1024]{1,0:T(8,128)(2,1)} %v_ref.1), custom_call_target="tpu_custom_call" | custom-call | tf_op jit(solution)/shard_map/prep/pallas_call | solution.py:37
  6.0 0.7 collective-permute-start.3
  6.7 5.6 %collective-permute-start.2 = (bf16[2048,128]{1,0:T(8,128)(2,1)}, bf16[2048,128]{1,0:T(8,128)(2,1)S(1)}, u32[]{:S(2)}, u32[]{:S(2)}) collective-permute-start(bf16[2048,128]{1,0:T(8,128)(2,1)} %bitcast.11), channel_id=1, source_target_pairs={{0,80},{1,17},{2,82},{3,19},{4,84},{5,21},{6,86},{7,23},{8,88},{9,... | collective-permute-start | bytes 1572872 | tf_op jit(solution)/shard_map/ppermute | solution.py:349
  12.3 3.1 %collective-permute-start.1 = (bf16[2048,128]{1,0:T(8,128)(2,1)}, bf16[2048,128]{1,0:T(8,128)(2,1)S(1)}, u32[]{:S(2)}, u32[]{:S(2)}) collective-permute-start(bf16[2048,128]{1,0:T(8,128)(2,1)} %bitcast.12), channel_id=1, source_target_pairs={{0,96},{1,33},{2,98},{3,35},{4,100},{5,37},{6,102},{7,39},{8,104},... | collective-permute-start | bytes 1572872 | tf_op jit(solution)/shard_map/ppermute | solution.py:349
  15.4 1.9 %collective-permute-start = (bf16[2048,128]{1,0:T(8,128)(2,1)}, bf16[2048,128]{1,0:T(8,128)(2,1)S(1)}, u32[]{:S(2)}, u32[]{:S(2)}) collective-permute-start(bf16[2048,128]{1,0:T(8,128)(2,1)} %bitcast.13), channel_id=1, source_target_pairs={{0,112},{1,49},{2,114},{3,51},{4,116},{5,53},{6,118},{7,55},{8,120... | collective-permute-start | bytes 1572872 | tf_op jit(solution)/shard_map/ppermute | solution.py:349
  17.3 1.0 copy-done.1
  18.4 1.2 copy-done.4
  19.6 2.6 %own.1 = (bf16[256,2048]{1,0:T(8,128)(2,1)S(1)}, f32[144,2048]{1,0:T(8,128)S(1)}, f32[8,2048]{1,0:T(8,128)S(1)}, bf16[16,32,512]{2,1,0:T(8,128)(2,1)S(1)}) custom-call(bf16[16,2,32,512]{3,2,1,0:T(8,128)(2,1)S(1)} %bitcast.17, bf16[16,2,32,512]{3,2,1,0:T(8,128)(2,1)S(1)} %bitcast.18, bf16[2048,128]{1,0:T(8,128)(2,1)S(1)} %bitcast.14), custom_call_target="tpu_custom_call" | custom-call | flops 2147483648 | bytes 8388608 | tf_op jit(solution)/shard_map/own/pallas_call | solution.py:108
  22.3 6.1 %collective-permute-done.1.refs_4_.refs_3_ = bf16[2048,128]{1,0:T(8,128)(2,1)S(1)} collective-permute-done((bf16[2048,128]{1,0:T(8,128)(2,1)}, bf16[2048,128]{1,0:T(8,128)(2,1)S(1)}, u32[]{:S(2)}, u32[]{:S(2)}) %collective-permute-start.1) | collective-permute-done | bytes 524320 | tf_op jit(solution)/shard_map/ppermute | solution.py:349
  28.4 13.9 %collective-permute-done.refs_3_.refs_2_ = bf16[2048,128]{1,0:T(8,128)(2,1)S(1)} collective-permute-done((bf16[2048,128]{1,0:T(8,128)(2,1)}, bf16[2048,128]{1,0:T(8,128)(2,1)S(1)}, u32[]{:S(2)}, u32[]{:S(2)}) %collective-permute-start) | collective-permute-done | bytes 524320 | tf_op jit(solution)/shard_map/ppermute | solution.py:349
  42.3 1.3 collective-permute-start.4
  43.6 0.5 collective-permute-start.6
  44.1 1.0 collective-permute-done.4.refs_7_.refs_6_
  45.1 1.7 %collective-permute-start.11 = (bf16[16,32,512]{2,1,0:T(8,128)(2,1)S(1)}, bf16[16,32,512]{2,1,0:T(8,128)(2,1)S(1)}, u32[]{:S(2)}, u32[]{:S(2)}) collective-permute-start(bf16[16,32,512]{2,1,0:T(8,128)(2,1)S(1)} %get-tuple-element.46), channel_id=1, source_target_pairs={{0,112},{1,113},{2,114},{3,115},{4,116},{5,117},{6,118},{7,119},{8... | collective-permute-start | bytes 1572872 | tf_op jit(solution)/shard_map/ppermute | solution.py:349
  46.9 0.5 collective-permute-done.7.refs_10_.refs_9_
  47.4 1.6 %attend_own.1 = (bf16[512,512]{1,0:T(8,128)(2,1)S(1)}, bf16[256,512]{1,0:T(8,128)(2,1)S(1)}, bf16[256,512]{1,0:T(8,128)(2,1)S(1)}) custom-call(s32[13]{0:T(128)S(1)} %copy-done.3, bf16[2048,128]{1,0:T(8,128)(2,1)S(1)} %bitcast.15, bf16[256,2048]{1,0:T(8,128)(2,1)S(1)} %get-tuple-element.33.refs_0_, f32[144,2048]{1,0:T(8,128)S(1)} %get-tuple-element.34.refs_1_, ...), custom_call_target="tpu_custom_call" | custom-call | flops 4294967296 | bytes 4194304 | tf_op jit(solution)/shard_map/attend_own/pallas_call | solution.py:263
  49.0 0.5 collective-permute-start.8
  49.6 1.0 collective-permute-done.8.b0
  51.0 6.5 %project.2 = (bf16[128,3072]{1,0:T(8,128)(2,1)S(1)}, bf16[128,3072]{1,0:T(8,128)(2,1)}, bf16[128,3072]{1,0:T(8,128)(2,1)S(1)}, bf16[128,3072]{1,0:T(8,128)(2,1)S(1)}) custom-call(s32[13]{0:T(128)S(1)} %copy-done.3, bf16[512,512]{1,0:T(8,128)(2,1)S(1)} %get-tuple-element.40.a, bf16[256,512]{1,0:T(8,128)(2,1)S(1)} %collective-permute-done.8.b0, ...), custom_call_target="tpu_custom_call" | custom-call | tf_op jit(solution)/shard_map/project/pallas_call | solution.py:308
  57.5 1.3 collective-permute-start.14
  58.8 1.9 %collective-permute-start.15 = (bf16[128,3072]{1,0:T(8,128)(2,1)S(1)}, bf16[128,3072]{1,0:T(8,128)(2,1)}, u32[]{:S(2)}, u32[]{:S(2)}) collective-permute-start(bf16[128,3072]{1,0:T(8,128)(2,1)S(1)} %get-tuple-element.53), channel_id=1, source_target_pairs={{0,2},{1,13},{2,0},{3,15},{4,6},{5,9},{6,4},{7,11},{8,10},{9,5},{1... | collective-permute-start | bytes 2359304 | tf_op jit(solution)/shard_map/ppermute | solution.py:349
  60.7 2.6 %collective-permute-start.16 = (bf16[128,3072]{1,0:T(8,128)(2,1)S(1)}, bf16[128,3072]{1,0:T(8,128)(2,1)}, u32[]{:S(2)}, u32[]{:S(2)}) collective-permute-start(bf16[128,3072]{1,0:T(8,128)(2,1)S(1)} %get-tuple-element.59), channel_id=1, source_target_pairs={{1,9},{3,11},{5,13},{7,15},{9,1},{11,3},{13,5},{15,7},{17,25},{19,... | collective-permute-start | bytes 2359304 | tf_op jit(solution)/shard_map/ppermute | solution.py:349
  63.4 19.7 %attend_foreign.1 = (bf16[512,512]{1,0:T(8,128)(2,1)S(1)}, bf16[256,512]{1,0:T(8,128)(2,1)}, bf16[256,512]{1,0:T(8,128)(2,1)}) custom-call(s32[13]{0:T(128)S(1)} %copy-done.3, bf16[2048,128]{1,0:T(8,128)(2,1)S(1)} %bitcast.16, bf16[16,32,512]{2,1,0:T(8,128)(2,1)S(1)} %collective-permute-done.11.refs_0_, bf16[512,6144]{1,0:T(8,128)(2,1)S(1)} %bitcast.9, ...), custom_call_target="tpu_custom_call" | custom-call | flops 4294967296 | bytes 4194304 | tf_op jit(solution)/shard_map/attend_foreign/pallas_call | solution.py:263
  83.1 0.5 collective-permute-start.13
  83.6 1.2 collective-permute-done.12.b0
  84.9 0.4 collective-permute-done.13.b1
  85.2 2.8 %copy-done = bf16[512,6144]{1,0:T(8,128)(2,1)S(1)} copy-done((bf16[512,6144]{1,0:T(8,128)(2,1)S(1)}, bf16[512,6144]{1,0:T(8,128)(2,1)}, u32[]{:S(2)}) %copy-start) | copy-done | bytes 6291480
  88.0 5.9 %project.3 = (bf16[128,3072]{1,0:T(8,128)(2,1)S(1)}, bf16[128,3072]{1,0:T(8,128)(2,1)S(1)}, bf16[128,3072]{1,0:T(8,128)(2,1)S(1)}, bf16[128,3072]{1,0:T(8,128)(2,1)S(1)}) custom-call(s32[13]{0:T(128)S(1)} %copy-done.3, bf16[512,512]{1,0:T(8,128)(2,1)S(1)} %get-tuple-element.47.a, bf16[256,512]{1,0:T(8,128)(2,1)S(1)} %collective-permute-done.12.b0, ...), custom_call_target="tpu_custom_call" | custom-call | tf_op jit(solution)/shard_map/project/pallas_call | solution.py:308
  93.9 1.6 %collective-permute-start.17 = (bf16[128,3072]{1,0:T(8,128)(2,1)S(1)}, bf16[128,3072]{1,0:T(8,128)(2,1)S(1)}, u32[]{:S(2)}, u32[]{:S(2)}) collective-permute-start(bf16[128,3072]{1,0:T(8,128)(2,1)S(1)} %get-tuple-element.55), channel_id=1, source_target_pairs={{0,4},{1,3},{2,6},{3,1},{4,0},{5,7},{6,2},{7,5},{8,12},{9,11},{10,... | collective-permute-start | bytes 2359304 | tf_op jit(solution)/shard_map/ppermute | solution.py:349
  95.6 0.7 collective-permute-start.19
  96.3 2.3 %fusion.2 = (bf16[128,3072]{1,0:T(8,128)(2,1)S(1)}, bf16[128,3072]{1,0:T(8,128)(2,1)S(1)}) fusion(bf16[128,3072]{1,0:T(8,128)(2,1)} %collective-permute-done.15, bf16[128,3072]{1,0:T(8,128)(2,1)} %collective-permute-done.16, bf16[128,3072]{1,0:T(8,128)(2,1)} %collective-permute-done.14, bf16[128,3072]{1,0:T(8,128)(2,1)S(1)} %get-tuple-element.51, ...), kind=kLoop, calls=%fused_computation.6 | loop fusion | flops 4718592 | bytes 5505025 | tf_op jit(solution)/shard_map/convert_element_type | solution.py:382
  98.7 1.4 collective-permute-start.20
  100.2 0.7 collective-permute-start.21
  100.9 4.3 %collective-permute-done.17 = bf16[128,3072]{1,0:T(8,128)(2,1)S(1)} collective-permute-done((bf16[128,3072]{1,0:T(8,128)(2,1)S(1)}, bf16[128,3072]{1,0:T(8,128)(2,1)S(1)}, u32[]{:S(2)}, u32[]{:S(2)}) %collective-permute-start.17) | collective-permute-done | bytes 786464 | tf_op jit(solution)/shard_map/ppermute | solution.py:349
  105.2 8.4 %collective-permute-done.18 = bf16[128,3072]{1,0:T(8,128)(2,1)S(1)} collective-permute-done((bf16[128,3072]{1,0:T(8,128)(2,1)S(1)}, bf16[128,3072]{1,0:T(8,128)(2,1)S(1)}, u32[]{:S(2)}, u32[]{:S(2)}) %collective-permute-start.18) | collective-permute-done | bytes 786464 | tf_op jit(solution)/shard_map/ppermute | solution.py:349
  113.6 0.7 fusion.7
  114.3 0.7 collective-permute-start.22
  115.1 4.0 %collective-permute-start.24 = (bf16[64,3072]{1,0:T(8,128)(2,1)S(1)}, bf16[64,3072]{1,0:T(8,128)(2,1)S(1)}, u32[]{:S(2)}, u32[]{:S(2)}) collective-permute-start(bf16[64,3072]{1,0:T(8,128)(2,1)S(1)} %get-tuple-element.65), channel_id=1, source_target_pairs={{1,13},{3,15},{5,9},{7,11},{9,5},{11,7},{13,1},{15,3},{17,29},{19,... | collective-permute-start | bytes 1179656 | tf_op jit(solution)/shard_map/ppermute | solution.py:349
  119.1 2.2 %collective-permute-start.25 = (bf16[64,3072]{1,0:T(8,128)(2,1)S(1)}, bf16[64,3072]{1,0:T(8,128)(2,1)S(1)}, u32[]{:S(2)}, u32[]{:S(2)}) collective-permute-start(bf16[64,3072]{1,0:T(8,128)(2,1)S(1)} %get-tuple-element.66), channel_id=1, source_target_pairs={{1,9},{3,11},{5,13},{7,15},{9,1},{11,3},{13,5},{15,7},{17,25},{19,... | collective-permute-start | bytes 1179656 | tf_op jit(solution)/shard_map/ppermute | solution.py:349
  121.4 0.9 collective-permute-start.23
  122.5 10.0 %collective-permute-start.27 = (bf16[32,3072]{1,0:T(8,128)(2,1)S(1)}, bf16[32,3072]{1,0:T(8,128)(2,1)S(1)}, u32[]{:S(2)}, u32[]{:S(2)}) collective-permute-start(bf16[32,3072]{1,0:T(8,128)(2,1)S(1)} %get-tuple-element.76), channel_id=1, source_target_pairs={{0,1},{1,0},{2,3},{3,2},{4,5},{5,4},{6,7},{7,6},{8,9},{9,8},{10,11... | collective-permute-start | bytes 589832 | tf_op jit(solution)/shard_map/ppermute | solution.py:349
  132.5 0.8 collective-permute-done.24
  133.3 2.5 %collective-permute-done.23 = bf16[64,3072]{1,0:T(8,128)(2,1)S(1)} collective-permute-done((bf16[64,3072]{1,0:T(8,128)(2,1)S(1)}, bf16[64,3072]{1,0:T(8,128)(2,1)S(1)}, u32[]{:S(2)}, u32[]{:S(2)}) %collective-permute-start.23) | collective-permute-done | bytes 393248 | tf_op jit(solution)/shard_map/ppermute | solution.py:349
  136.0 3.3 %collective-permute-start.26 = (bf16[32,3072]{1,0:T(8,128)(2,1)S(1)}, bf16[32,3072]{1,0:T(8,128)(2,1)S(1)}, u32[]{:S(2)}, u32[]{:S(2)}) collective-permute-start(bf16[32,3072]{1,0:T(8,128)(2,1)S(1)} %get-tuple-element.77), channel_id=1, source_target_pairs={{0,112},{1,113},{2,114},{3,115},{4,116},{5,117},{6,118},{7,119},{8... | collective-permute-start | bytes 589832 | tf_op jit(solution)/shard_map/ppermute | solution.py:349
  139.3 9.1 %collective-permute-done.28 = bf16[32,3072]{1,0:T(8,128)(2,1)S(1)} collective-permute-done((bf16[32,3072]{1,0:T(8,128)(2,1)S(1)}, bf16[32,3072]{1,0:T(8,128)(2,1)S(1)}, u32[]{:S(2)}, u32[]{:S(2)}) %collective-permute-start.28) | collective-permute-done | bytes 196640 | tf_op jit(solution)/shard_map/ppermute | solution.py:349
  148.7 0.9 pad_maximum_fusion
  (46 shorter events, 1.6 us)
Async XLA Ops:
  0.0 51.0 %collective-permute-start.10 = (bf16[512,6144]{1,0:T(8,128)(2,1)}, bf16[512,6144]{1,0:T(8,128)(2,1)}, u32[]{:S(2)}, u32[]{:S(2)}) collective-permute-start(bf16[512,6144]{1,0:T(8,128)(2,1)} %wa.3), channel_id=1, source_target_pairs={{0,1},{1,0},{2,3},{3,2},{4,5},{5,4},{6,7},{7,6},{8,9},{9,8},{10,11... | collective-permute-start | bytes 18874376 | tf_op jit(solution)/shard_map/ppermute | solution.py:349
  6.0 16.3 %collective-permute-start.3 = (bf16[2048,128]{1,0:T(8,128)(2,1)}, bf16[2048,128]{1,0:T(8,128)(2,1)S(1)}, u32[]{:S(2)}, u32[]{:S(2)}) collective-permute-start(bf16[2048,128]{1,0:T(8,128)(2,1)} %bitcast.10), channel_id=1, source_target_pairs={{0,64},{2,66},{4,68},{6,70},{8,72},{10,74},{12,76},{14,78},{16,80}... | collective-permute-start | bytes 1572872 | tf_op jit(solution)/shard_map/ppermute | solution.py:349
  6.7 15.6 %collective-permute-start.2 = (bf16[2048,128]{1,0:T(8,128)(2,1)}, bf16[2048,128]{1,0:T(8,128)(2,1)S(1)}, u32[]{:S(2)}, u32[]{:S(2)}) collective-permute-start(bf16[2048,128]{1,0:T(8,128)(2,1)} %bitcast.11), channel_id=1, source_target_pairs={{0,80},{1,17},{2,82},{3,19},{4,84},{5,21},{6,86},{7,23},{8,88},{9,... | collective-permute-start | bytes 1572872 | tf_op jit(solution)/shard_map/ppermute | solution.py:349
  12.3 16.1 %collective-permute-start.1 = (bf16[2048,128]{1,0:T(8,128)(2,1)}, bf16[2048,128]{1,0:T(8,128)(2,1)S(1)}, u32[]{:S(2)}, u32[]{:S(2)}) collective-permute-start(bf16[2048,128]{1,0:T(8,128)(2,1)} %bitcast.12), channel_id=1, source_target_pairs={{0,96},{1,33},{2,98},{3,35},{4,100},{5,37},{6,102},{7,39},{8,104},... | collective-permute-start | bytes 1572872 | tf_op jit(solution)/shard_map/ppermute | solution.py:349
  15.4 26.9 %collective-permute-start = (bf16[2048,128]{1,0:T(8,128)(2,1)}, bf16[2048,128]{1,0:T(8,128)(2,1)S(1)}, u32[]{:S(2)}, u32[]{:S(2)}) collective-permute-start(bf16[2048,128]{1,0:T(8,128)(2,1)} %bitcast.13), channel_id=1, source_target_pairs={{0,112},{1,49},{2,114},{3,51},{4,116},{5,53},{6,118},{7,55},{8,120... | collective-permute-start | bytes 1572872 | tf_op jit(solution)/shard_map/ppermute | solution.py:349
  17.3 1.1 copy-start.1
  18.4 1.2 copy-start.4
  19.6 27.8 %copy-start.2 = (bf16[2,1024,128]{2,1,0:T(8,128)(2,1)S(1)}, bf16[2,1024,128]{2,1,0:T(8,128)(2,1)}, u32[]{:S(2)}) copy-start(bf16[2,1024,128]{2,1,0:T(8,128)(2,1)} %prep.1) | copy-start | bytes 1572868
  19.6 27.8 %copy-start.3 = (s32[13]{0:T(128)S(1)}, s32[13]{0:T(128)}, u32[]{:S(2)}) copy-start(s32[13]{0:T(128)} %stack.27.info) | copy-start | bytes 160
  42.3 2.8 %collective-permute-start.4 = (bf16[2048,128]{1,0:T(8,128)(2,1)S(1)}, bf16[2048,128]{1,0:T(8,128)(2,1)S(1)}, u32[]{:S(2)}, u32[]{:S(2)}) collective-permute-start(bf16[2048,128]{1,0:T(8,128)(2,1)S(1)} %collective-permute-done.refs_3_.refs_2_), channel_id=1, source_target_pairs={{0,1},{1,0},{2,3},{3,2},{4,5},{5,4},{6,7},{7,6},{8,9},{9,8},{10,11... | collective-permute-start | bytes 1572872 | tf_op jit(solution)/shard_map/ppermute | solution.py:349
  43.6 3.3 %collective-permute-start.5 = (bf16[2048,128]{1,0:T(8,128)(2,1)S(1)}, bf16[2048,128]{1,0:T(8,128)(2,1)S(1)}, u32[]{:S(2)}, u32[]{:S(2)}) collective-permute-start(bf16[2048,128]{1,0:T(8,128)(2,1)S(1)} %collective-permute-done.1.refs_4_.refs_3_), channel_id=1, source_target_pairs={{0,1},{1,0},{2,3},{3,2},{4,5},{5,4},{6,7},{7,6},{8,9},{9,8},{10,11... | collective-permute-start | bytes 1572872 | tf_op jit(solution)/shard_map/ppermute | solution.py:349
  43.6 3.3 %collective-permute-start.6 = (bf16[2048,128]{1,0:T(8,128)(2,1)S(1)}, bf16[2048,128]{1,0:T(8,128)(2,1)S(1)}, u32[]{:S(2)}, u32[]{:S(2)}) collective-permute-start(bf16[2048,128]{1,0:T(8,128)(2,1)S(1)} %collective-permute-done.2.refs_5_.refs_4_), channel_id=1, source_target_pairs={{0,1},{1,0},{2,3},{3,2},{4,5},{5,4},{6,7},{7,6},{8,9},{9,8},{10,11... | collective-permute-start | bytes 1572872 | tf_op jit(solution)/shard_map/ppermute | solution.py:349
  44.1 3.3 %collective-permute-start.7 = (bf16[2048,128]{1,0:T(8,128)(2,1)S(1)}, bf16[2048,128]{1,0:T(8,128)(2,1)S(1)}, u32[]{:S(2)}, u32[]{:S(2)}) collective-permute-start(bf16[2048,128]{1,0:T(8,128)(2,1)S(1)} %collective-permute-done.3.refs_6_.refs_5_), channel_id=1, source_target_pairs={{0,1},{1,0},{2,3},{3,2},{4,5},{5,4},{6,7},{7,6},{8,9},{9,8},{10,11... | collective-permute-start | bytes 1572872 | tf_op jit(solution)/shard_map/ppermute | solution.py:349
  45.1 18.2 %collective-permute-start.11 = (bf16[16,32,512]{2,1,0:T(8,128)(2,1)S(1)}, bf16[16,32,512]{2,1,0:T(8,128)(2,1)S(1)}, u32[]{:S(2)}, u32[]{:S(2)}) collective-permute-start(bf16[16,32,512]{2,1,0:T(8,128)(2,1)S(1)} %get-tuple-element.46), channel_id=1, source_target_pairs={{0,112},{1,113},{2,114},{3,115},{4,116},{5,117},{6,118},{7,119},{8... | collective-permute-start | bytes 1572872 | tf_op jit(solution)/shard_map/ppermute | solution.py:349
  47.4 3.6 %slice-start = ((s8[6291456]{0:T(1024)(128)(4,1)}), s8[4194304]{0:T(1024)(128)(4,1)S(1)}, s32[]{:S(2)}) async-start(s8[6291456]{0:T(1024)(128)(4,1)} %bitcast.8), calls=%async_computation | async-start | bytes 8388608
  47.4 3.6 %slice-start.1 = ((s8[6291456]{0:T(1024)(128)(4,1)}), s8[2097152]{0:T(1024)(128)(4,1)S(1)}, s32[]{:S(2)}) async-start(s8[6291456]{0:T(1024)(128)(4,1)} %bitcast.8), calls=%async_computation.1 | async-start | bytes 4194304
  49.0 1.6 %collective-permute-start.8 = (bf16[256,512]{1,0:T(8,128)(2,1)S(1)}, bf16[256,512]{1,0:T(8,128)(2,1)S(1)}, u32[]{:S(2)}, u32[]{:S(2)}) collective-permute-start(bf16[256,512]{1,0:T(8,128)(2,1)S(1)} %get-tuple-element.41), channel_id=1, source_target_pairs={{0,1},{1,0},{2,3},{3,2},{4,5},{5,4},{6,7},{7,6},{8,9},{9,8},{10,11... | collective-permute-start | bytes 786440 | tf_op jit(solution)/shard_map/ppermute | solution.py:349
  49.4 1.5 %collective-permute-start.9 = (bf16[256,512]{1,0:T(8,128)(2,1)S(1)}, bf16[256,512]{1,0:T(8,128)(2,1)S(1)}, u32[]{:S(2)}, u32[]{:S(2)}) collective-permute-start(bf16[256,512]{1,0:T(8,128)(2,1)S(1)} %get-tuple-element.42), channel_id=1, source_target_pairs={{0,1},{1,0},{2,3},{3,2},{4,5},{5,4},{6,7},{7,6},{8,9},{9,8},{10,11... | collective-permute-start | bytes 786440 | tf_op jit(solution)/shard_map/ppermute | solution.py:349
  57.5 38.1 %collective-permute-start.14 = (bf16[128,3072]{1,0:T(8,128)(2,1)}, bf16[128,3072]{1,0:T(8,128)(2,1)}, u32[]{:S(2)}, u32[]{:S(2)}) collective-permute-start(bf16[128,3072]{1,0:T(8,128)(2,1)} %get-tuple-element.52), channel_id=1, source_target_pairs={{0,2},{1,5},{2,0},{3,7},{4,6},{5,1},{6,4},{7,3},{8,10},{9,13},{10,... | collective-permute-start | bytes 2359304 | tf_op jit(solution)/shard_map/ppermute | solution.py:349
  58.8 37.5 %collective-permute-start.15 = (bf16[128,3072]{1,0:T(8,128)(2,1)S(1)}, bf16[128,3072]{1,0:T(8,128)(2,1)}, u32[]{:S(2)}, u32[]{:S(2)}) collective-permute-start(bf16[128,3072]{1,0:T(8,128)(2,1)S(1)} %get-tuple-element.53), channel_id=1, source_target_pairs={{0,2},{1,13},{2,0},{3,15},{4,6},{5,9},{6,4},{7,11},{8,10},{9,5},{1... | collective-permute-start | bytes 2359304 | tf_op jit(solution)/shard_map/ppermute | solution.py:349
  60.7 35.6 %collective-permute-start.16 = (bf16[128,3072]{1,0:T(8,128)(2,1)S(1)}, bf16[128,3072]{1,0:T(8,128)(2,1)}, u32[]{:S(2)}, u32[]{:S(2)}) collective-permute-start(bf16[128,3072]{1,0:T(8,128)(2,1)S(1)} %get-tuple-element.59), channel_id=1, source_target_pairs={{1,9},{3,11},{5,13},{7,15},{9,1},{11,3},{13,5},{15,7},{17,25},{19,... | collective-permute-start | bytes 2359304 | tf_op jit(solution)/shard_map/ppermute | solution.py:349
  83.0 1.8 %collective-permute-start.12 = (bf16[256,512]{1,0:T(8,128)(2,1)}, bf16[256,512]{1,0:T(8,128)(2,1)S(1)}, u32[]{:S(2)}, u32[]{:S(2)}) collective-permute-start(bf16[256,512]{1,0:T(8,128)(2,1)} %get-tuple-element.48), channel_id=1, source_target_pairs={{0,1},{1,0},{2,3},{3,2},{4,5},{5,4},{6,7},{7,6},{8,9},{9,8},{10,11... | collective-permute-start | bytes 786440 | tf_op jit(solution)/shard_map/ppermute | solution.py:349
  83.1 2.1 %collective-permute-start.13 = (bf16[256,512]{1,0:T(8,128)(2,1)}, bf16[256,512]{1,0:T(8,128)(2,1)S(1)}, u32[]{:S(2)}, u32[]{:S(2)}) collective-permute-start(bf16[256,512]{1,0:T(8,128)(2,1)} %get-tuple-element.49), channel_id=1, source_target_pairs={{0,1},{1,0},{2,3},{3,2},{4,5},{5,4},{6,7},{7,6},{8,9},{9,8},{10,11... | collective-permute-start | bytes 786440 | tf_op jit(solution)/shard_map/ppermute | solution.py:349
  85.2 2.8 %copy-start = (bf16[512,6144]{1,0:T(8,128)(2,1)S(1)}, bf16[512,6144]{1,0:T(8,128)(2,1)}, u32[]{:S(2)}) copy-start(bf16[512,6144]{1,0:T(8,128)(2,1)} %wa.3) | copy-start | bytes 18874372
  93.9 11.3 %collective-permute-start.17 = (bf16[128,3072]{1,0:T(8,128)(2,1)S(1)}, bf16[128,3072]{1,0:T(8,128)(2,1)S(1)}, u32[]{:S(2)}, u32[]{:S(2)}) collective-permute-start(bf16[128,3072]{1,0:T(8,128)(2,1)S(1)} %get-tuple-element.55), channel_id=1, source_target_pairs={{0,4},{1,3},{2,6},{3,1},{4,0},{5,7},{6,2},{7,5},{8,12},{9,11},{10,... | collective-permute-start | bytes 2359304 | tf_op jit(solution)/shard_map/ppermute | solution.py:349
  95.5 18.1 %collective-permute-start.18 = (bf16[128,3072]{1,0:T(8,128)(2,1)S(1)}, bf16[128,3072]{1,0:T(8,128)(2,1)S(1)}, u32[]{:S(2)}, u32[]{:S(2)}) collective-permute-start(bf16[128,3072]{1,0:T(8,128)(2,1)S(1)} %get-tuple-element.56), channel_id=1, source_target_pairs={{0,12},{1,3},{2,14},{3,1},{4,8},{5,7},{6,10},{7,5},{8,4},{9,11},{1... | collective-permute-start | bytes 2359304 | tf_op jit(solution)/shard_map/ppermute | solution.py:349
  95.6 18.0 %collective-permute-start.19 = (bf16[128,3072]{1,0:T(8,128)(2,1)S(1)}, bf16[128,3072]{1,0:T(8,128)(2,1)S(1)}, u32[]{:S(2)}, u32[]{:S(2)}) collective-permute-start(bf16[128,3072]{1,0:T(8,128)(2,1)S(1)} %get-tuple-element.57), channel_id=1, source_target_pairs={{0,8},{2,10},{4,12},{6,14},{8,0},{10,2},{12,4},{14,6},{16,24},{18,... | collective-permute-start | bytes 2359304 | tf_op jit(solution)/shard_map/ppermute | solution.py:349
  98.7 22.7 %collective-permute-start.20 = (bf16[64,3072]{1,0:T(8,128)(2,1)S(1)}, bf16[64,3072]{1,0:T(8,128)(2,1)S(1)}, u32[]{:S(2)}, u32[]{:S(2)}) collective-permute-start(bf16[64,3072]{1,0:T(8,128)(2,1)S(1)} %get-tuple-element.70), channel_id=1, source_target_pairs={{0,4},{1,3},{2,6},{3,1},{4,0},{5,7},{6,2},{7,5},{8,12},{9,11},{10,... | collective-permute-start | bytes 1179656 | tf_op jit(solution)/shard_map/ppermute | solution.py:349
  100.2 22.1 %collective-permute-start.21 = (bf16[64,3072]{1,0:T(8,128)(2,1)S(1)}, bf16[64,3072]{1,0:T(8,128)(2,1)S(1)}, u32[]{:S(2)}, u32[]{:S(2)}) collective-permute-start(bf16[64,3072]{1,0:T(8,128)(2,1)S(1)} %get-tuple-element.73), channel_id=1, source_target_pairs={{0,12},{2,14},{4,8},{6,10},{8,4},{10,6},{12,0},{14,2},{16,28},{18,... | collective-permute-start | bytes 1179656 | tf_op jit(solution)/shard_map/ppermute | solution.py:349
  114.3 7.9 %collective-permute-start.22 = (bf16[64,3072]{1,0:T(8,128)(2,1)S(1)}, bf16[64,3072]{1,0:T(8,128)(2,1)S(1)}, u32[]{:S(2)}, u32[]{:S(2)}) collective-permute-start(bf16[64,3072]{1,0:T(8,128)(2,1)S(1)} %get-tuple-element.60), channel_id=1, source_target_pairs={{0,8},{2,10},{4,12},{6,14},{8,0},{10,2},{12,4},{14,6},{16,24},{18,... | collective-permute-start | bytes 1179656 | tf_op jit(solution)/shard_map/ppermute | solution.py:349
  115.1 18.2 %collective-permute-start.24 = (bf16[64,3072]{1,0:T(8,128)(2,1)S(1)}, bf16[64,3072]{1,0:T(8,128)(2,1)S(1)}, u32[]{:S(2)}, u32[]{:S(2)}) collective-permute-start(bf16[64,3072]{1,0:T(8,128)(2,1)S(1)} %get-tuple-element.65), channel_id=1, source_target_pairs={{1,13},{3,15},{5,9},{7,11},{9,5},{11,7},{13,1},{15,3},{17,29},{19,... | collective-permute-start | bytes 1179656 | tf_op jit(solution)/shard_map/ppermute | solution.py:349
  119.1 14.2 %collective-permute-start.25 = (bf16[64,3072]{1,0:T(8,128)(2,1)S(1)}, bf16[64,3072]{1,0:T(8,128)(2,1)S(1)}, u32[]{:S(2)}, u32[]{:S(2)}) collective-permute-start(bf16[64,3072]{1,0:T(8,128)(2,1)S(1)} %get-tuple-element.66), channel_id=1, source_target_pairs={{1,9},{3,11},{5,13},{7,15},{9,1},{11,3},{13,5},{15,7},{17,25},{19,... | collective-permute-start | bytes 1179656 | tf_op jit(solution)/shard_map/ppermute | solution.py:349
  121.4 14.4 %collective-permute-start.23 = (bf16[64,3072]{1,0:T(8,128)(2,1)S(1)}, bf16[64,3072]{1,0:T(8,128)(2,1)S(1)}, u32[]{:S(2)}, u32[]{:S(2)}) collective-permute-start(bf16[64,3072]{1,0:T(8,128)(2,1)S(1)} %fusion.8), channel_id=1, source_target_pairs={{0,2},{1,5},{2,0},{3,7},{4,6},{5,1},{6,4},{7,3},{8,10},{9,13},{10,... | collective-permute-start | bytes 1179656 | tf_op jit(solution)/shard_map/ppermute | solution.py:349
  122.5 16.8 %collective-permute-start.27 = (bf16[32,3072]{1,0:T(8,128)(2,1)S(1)}, bf16[32,3072]{1,0:T(8,128)(2,1)S(1)}, u32[]{:S(2)}, u32[]{:S(2)}) collective-permute-start(bf16[32,3072]{1,0:T(8,128)(2,1)S(1)} %get-tuple-element.76), channel_id=1, source_target_pairs={{0,1},{1,0},{2,3},{3,2},{4,5},{5,4},{6,7},{7,6},{8,9},{9,8},{10,11... | collective-permute-start | bytes 589832 | tf_op jit(solution)/shard_map/ppermute | solution.py:349
  136.0 12.4 %collective-permute-start.26 = (bf16[32,3072]{1,0:T(8,128)(2,1)S(1)}, bf16[32,3072]{1,0:T(8,128)(2,1)S(1)}, u32[]{:S(2)}, u32[]{:S(2)}) collective-permute-start(bf16[32,3072]{1,0:T(8,128)(2,1)S(1)} %get-tuple-element.77), channel_id=1, source_target_pairs={{0,112},{1,113},{2,114},{3,115},{4,116},{5,117},{6,118},{7,119},{8... | collective-permute-start | bytes 589832 | tf_op jit(solution)/shard_map/ppermute | solution.py:349
  139.3 9.1 %collective-permute-start.28 = (bf16[32,3072]{1,0:T(8,128)(2,1)S(1)}, bf16[32,3072]{1,0:T(8,128)(2,1)S(1)}, u32[]{:S(2)}, u32[]{:S(2)}) collective-permute-start(bf16[32,3072]{1,0:T(8,128)(2,1)S(1)} %get-tuple-element.78), channel_id=1, source_target_pairs={{0,113},{1,112},{2,115},{3,114},{4,117},{5,116},{6,119},{7,118},{8... | collective-permute-start | bytes 589832 | tf_op jit(solution)/shard_map/ppermute | solution.py:349

commit v13 on v10

--- a/solution.py
+++ b/solution.py
@@ -288,7 +288,7 @@
     )(info, kv, *state, *mine, *other)
 
 
-def project(info, mine, other, w, w_other, parts, tile):
+def project(info, mine, other, w, w_other, parts, tile, params=PARAMS):
     rows, width = mine.shape
     n = w.shape[1] // 2
     steps = n // tile
@@ -316,7 +316,7 @@
         out_shape=[jax.ShapeDtypeStruct((rows // parts, n), BF)] * parts,
         name="project",
         cost_estimate=pl.CostEstimate(flops=0, bytes_accessed=0, transcendentals=0),
-        compiler_params=PARAMS,
+        compiler_params=params,
     )(info, mine, *other, w, w_other)
 
 
@@ -401,7 +401,8 @@
     got_n = stage_one(parts_n, 1)
     far, *far_peer = attend(after(info, parts_n[0]), kv, [q_far], half, mine, other, n_y, n_seq)
     far_far = [swap_core(x) for x in far_peer]
-    parts_f = project(info, far, far_far, w_out, w_other, n_y, cols // 4)
+    wide = pltpu.CompilerParams(vmem_limit_bytes=50 << 20)
+    parts_f = project(info, far, far_far, w_out, w_other, n_y, cols // 4, wide)
     got_f = stage_one(parts_f, 0)
     total_n = sum_one([after(p, parts_f[0]) for p in parts_n], got_n, 1)
     total_f = sum_one(parts_f, got_f, 0)

time: 150 us -> 148 us (0.987)
  local copies, waits for them, and re-layouts: 5.95 us -> 3.13 us
    unnamed x15 -> x13, local copies, waits for them, and re-layouts: 5.08 us -> 2.3 us
  transfers between devices with their start and end apart: 29 -> 29, of which waited for: 13 -> 13; matrix products, arithmetic and copies ran while one was open for 3% -> 3% of each run, Pallas kernels for 26% -> 27%
where the time goes in v13:
time: 148 us; the launch traced here: 147 us
  starting transfers between devices  50.6 us (34%)
  waiting for transfers between devices  48.8 us (33%)
  Pallas kernels  40 us (27%)
  other arithmetic  4.53 us (3%)
  local copies, waits for them, and re-layouts  3.13 us (2%)
    ppermute x29, starting transfers between devices, over_all(): return lax.ppermute(x, ('seq', 'head'), pairs)  50.6 us
    ppermute x29, waiting for transfers between devices, over_all(): return lax.ppermute(x, ('seq', 'head'), pairs)  48.8 us
    pallas_call x2, Pallas kernels, attend(): pl.pallas_call(functools.partial(attend_kernel, foreign, groups, n_y, n_s...  21.3 us
    pallas_call x2, Pallas kernels, project(): pl.pallas_call(body, grid_spec=pltpu.PrefetchScalarGridSpec(num_scalar_pr...  13.5 us
  transfers between devices with their start and end apart: 29, of which 13 were waited for; matrix products, arithmetic and copies ran while one was open for 3% of the time, Pallas kernels for 27%

profile of v13, /device:TPU:1, one launch (start us, length us, event | category | flops | bytes accessed | tf_op | source)
XLA Modules:
  0.0 147.4 jit_solution(7150577796272900425)
XLA Ops:
  0.0 1.4 collective-permute-start.10
  1.4 0.6 stack.27.info
  2.1 2.6 %prep.1.kv_ref.own_ref = bf16[2048,128]{1,0:T(8,128)(2,1)} custom-call(s32[13]{0:T(128)} %stack.27.info, bf16[1024,1024]{1,0:T(8,128)(2,1)} %k_ref.1, bf16[1024,1024]{1,0:T(8,128)(2,1)} %v_ref.1), custom_call_target="tpu_custom_call" | custom-call | tf_op jit(solution)/shard_map/prep/pallas_call | solution.py:37
  4.7 0.7 collective-permute-start.3
  5.4 5.6 %collective-permute-start.2 = (bf16[2048,128]{1,0:T(8,128)(2,1)}, bf16[2048,128]{1,0:T(8,128)(2,1)S(1)}, u32[]{:S(2)}, u32[]{:S(2)}) collective-permute-start(bf16[2048,128]{1,0:T(8,128)(2,1)} %prep.1.kv_ref.own_ref), channel_id=1, source_target_pairs={{0,80},{1,17},{2,82},{3,19},{4,84},{5,21},{6,86},{7,23},{8,88},{9,... | collective-permute-start | bytes 1572872 | tf_op jit(solution)/shard_map/ppermute | solution.py:349
  11.0 3.1 %collective-permute-start.1 = (bf16[2048,128]{1,0:T(8,128)(2,1)}, bf16[2048,128]{1,0:T(8,128)(2,1)S(1)}, u32[]{:S(2)}, u32[]{:S(2)}) collective-permute-start(bf16[2048,128]{1,0:T(8,128)(2,1)} %prep.1.kv_ref.own_ref), channel_id=1, source_target_pairs={{0,96},{1,33},{2,98},{3,35},{4,100},{5,37},{6,102},{7,39},{8,104},... | collective-permute-start | bytes 1572872 | tf_op jit(solution)/shard_map/ppermute | solution.py:349
  14.1 1.9 %collective-permute-start = (bf16[2048,128]{1,0:T(8,128)(2,1)}, bf16[2048,128]{1,0:T(8,128)(2,1)S(1)}, u32[]{:S(2)}, u32[]{:S(2)}) collective-permute-start(bf16[2048,128]{1,0:T(8,128)(2,1)} %prep.1.kv_ref.own_ref), channel_id=1, source_target_pairs={{0,112},{1,49},{2,114},{3,51},{4,116},{5,53},{6,118},{7,55},{8,120... | collective-permute-start | bytes 1572872 | tf_op jit(solution)/shard_map/ppermute | solution.py:349
  16.0 1.0 copy-done
  17.1 1.2 copy-done.3
  18.3 2.6 %own.1 = (bf16[256,2048]{1,0:T(8,128)(2,1)S(1)}, f32[144,2048]{1,0:T(8,128)S(1)}, f32[8,2048]{1,0:T(8,128)S(1)}, bf16[16,32,512]{2,1,0:T(8,128)(2,1)S(1)}) custom-call(bf16[16,2,32,512]{3,2,1,0:T(8,128)(2,1)S(1)} %bitcast.9, bf16[16,2,32,512]{3,2,1,0:T(8,128)(2,1)S(1)} %bitcast.10, bf16[2048,128]{1,0:T(8,128)(2,1)S(1)} %copy-done), custom_call_target="tpu_custom_call" | custom-call | flops 2147483648 | bytes 8388608 | tf_op jit(solution)/shard_map/own/pallas_call | solution.py:108
  21.0 6.1 %collective-permute-done.1.refs_4_.refs_2_ = bf16[2048,128]{1,0:T(8,128)(2,1)S(1)} collective-permute-done((bf16[2048,128]{1,0:T(8,128)(2,1)}, bf16[2048,128]{1,0:T(8,128)(2,1)S(1)}, u32[]{:S(2)}, u32[]{:S(2)}) %collective-permute-start.1) | collective-permute-done | bytes 524320 | tf_op jit(solution)/shard_map/ppermute | solution.py:349
  27.1 13.9 %collective-permute-done.refs_3_.refs_1_ = bf16[2048,128]{1,0:T(8,128)(2,1)S(1)} collective-permute-done((bf16[2048,128]{1,0:T(8,128)(2,1)}, bf16[2048,128]{1,0:T(8,128)(2,1)S(1)}, u32[]{:S(2)}, u32[]{:S(2)}) %collective-permute-start) | collective-permute-done | bytes 524320 | tf_op jit(solution)/shard_map/ppermute | solution.py:349
  41.0 1.3 collective-permute-start.4
  42.3 0.5 collective-permute-start.6
  42.8 1.0 collective-permute-done.4.refs_7_.refs_5_
  43.8 1.7 %collective-permute-start.11 = (bf16[16,32,512]{2,1,0:T(8,128)(2,1)S(1)}, bf16[16,32,512]{2,1,0:T(8,128)(2,1)S(1)}, u32[]{:S(2)}, u32[]{:S(2)}) collective-permute-start(bf16[16,32,512]{2,1,0:T(8,128)(2,1)S(1)} %get-tuple-element.46), channel_id=1, source_target_pairs={{0,112},{1,113},{2,114},{3,115},{4,116},{5,117},{6,118},{7,119},{8... | collective-permute-start | bytes 1572872 | tf_op jit(solution)/shard_map/ppermute | solution.py:349
  45.5 0.5 collective-permute-done.7.refs_10_.refs_8_
  46.1 1.6 %attend_own.1 = (bf16[512,512]{1,0:T(8,128)(2,1)S(1)}, bf16[256,512]{1,0:T(8,128)(2,1)S(1)}, bf16[256,512]{1,0:T(8,128)(2,1)S(1)}) custom-call(s32[13]{0:T(128)S(1)} %copy-done.2, bf16[2048,128]{1,0:T(8,128)(2,1)S(1)} %copy-done.1, bf16[256,2048]{1,0:T(8,128)(2,1)S(1)} %get-tuple-element.33.refs_0_, f32[144,2048]{1,0:T(8,128)S(1)} %get-tuple-element.34.refs_1_, ...), custom_call_target="tpu_custom_call" | custom-call | flops 4294967296 | bytes 4194304 | tf_op jit(solution)/shard_map/attend_own/pallas_call | solution.py:263
  47.7 0.5 collective-permute-start.8
  48.3 1.0 collective-permute-done.8.b0
  49.3 0.4 collective-permute-done.9.b1
  49.7 6.5 %project.2 = (bf16[128,3072]{1,0:T(8,128)(2,1)S(1)}, bf16[128,3072]{1,0:T(8,128)(2,1)}, bf16[128,3072]{1,0:T(8,128)(2,1)S(1)}, bf16[128,3072]{1,0:T(8,128)(2,1)S(1)}) custom-call(s32[13]{0:T(128)S(1)} %copy-done.2, bf16[512,512]{1,0:T(8,128)(2,1)S(1)} %get-tuple-element.40.a, bf16[256,512]{1,0:T(8,128)(2,1)S(1)} %collective-permute-done.8.b0, ...), custom_call_target="tpu_custom_call" | custom-call | tf_op jit(solution)/shard_map/project/pallas_call | solution.py:308
  56.2 1.3 collective-permute-start.14
  57.5 1.9 %collective-permute-start.15 = (bf16[128,3072]{1,0:T(8,128)(2,1)S(1)}, bf16[128,3072]{1,0:T(8,128)(2,1)}, u32[]{:S(2)}, u32[]{:S(2)}) collective-permute-start(bf16[128,3072]{1,0:T(8,128)(2,1)S(1)} %get-tuple-element.53), channel_id=1, source_target_pairs={{0,2},{1,13},{2,0},{3,15},{4,6},{5,9},{6,4},{7,11},{8,10},{9,5},{1... | collective-permute-start | bytes 2359304 | tf_op jit(solution)/shard_map/ppermute | solution.py:349
  59.4 2.6 %collective-permute-start.16 = (bf16[128,3072]{1,0:T(8,128)(2,1)S(1)}, bf16[128,3072]{1,0:T(8,128)(2,1)}, u32[]{:S(2)}, u32[]{:S(2)}) collective-permute-start(bf16[128,3072]{1,0:T(8,128)(2,1)S(1)} %get-tuple-element.59), channel_id=1, source_target_pairs={{1,9},{3,11},{5,13},{7,15},{9,1},{11,3},{13,5},{15,7},{17,25},{19,... | collective-permute-start | bytes 2359304 | tf_op jit(solution)/shard_map/ppermute | solution.py:349
  62.1 19.7 %attend_foreign.1 = (bf16[512,512]{1,0:T(8,128)(2,1)S(1)}, bf16[256,512]{1,0:T(8,128)(2,1)}, bf16[256,512]{1,0:T(8,128)(2,1)}) custom-call(s32[13]{0:T(128)S(1)} %copy-done.2, bf16[2048,128]{1,0:T(8,128)(2,1)S(1)} %copy-done.1, bf16[16,32,512]{2,1,0:T(8,128)(2,1)S(1)} %collective-permute-done.11.refs_0_, ...), custom_call_target="tpu_custom_call" | custom-call | flops 4294967296 | bytes 4194304 | tf_op jit(solution)/shard_map/attend_foreign/pallas_call | solution.py:263
  81.8 0.5 collective-permute-start.13
  82.3 1.2 collective-permute-done.12.b0
  83.5 0.4 collective-permute-done.13.b1
  83.9 7.0 %project.3 = (bf16[128,3072]{1,0:T(8,128)(2,1)S(1)}, bf16[128,3072]{1,0:T(8,128)(2,1)S(1)}, bf16[128,3072]{1,0:T(8,128)(2,1)S(1)}, bf16[128,3072]{1,0:T(8,128)(2,1)}) custom-call(s32[13]{0:T(128)S(1)} %copy-done.2, bf16[512,512]{1,0:T(8,128)(2,1)S(1)} %get-tuple-element.47.a, bf16[256,512]{1,0:T(8,128)(2,1)S(1)} %collective-permute-done.12.b0, ...), custom_call_target="tpu_custom_call" | custom-call | tf_op jit(solution)/shard_map/project/pallas_call | solution.py:308
  90.9 1.5 %collective-permute-start.17 = (bf16[128,3072]{1,0:T(8,128)(2,1)S(1)}, bf16[128,3072]{1,0:T(8,128)(2,1)S(1)}, u32[]{:S(2)}, u32[]{:S(2)}) collective-permute-start(bf16[128,3072]{1,0:T(8,128)(2,1)S(1)} %get-tuple-element.55), channel_id=1, source_target_pairs={{0,4},{1,3},{2,6},{3,1},{4,0},{5,7},{6,2},{7,5},{8,12},{9,11},{10,... | collective-permute-start | bytes 2359304 | tf_op jit(solution)/shard_map/ppermute | solution.py:349
  92.5 0.7 collective-permute-start.19
  93.2 2.3 %fusion.2 = (bf16[128,3072]{1,0:T(8,128)(2,1)S(1)}, bf16[128,3072]{1,0:T(8,128)(2,1)S(1)}) fusion(bf16[128,3072]{1,0:T(8,128)(2,1)} %collective-permute-done.15, bf16[128,3072]{1,0:T(8,128)(2,1)} %collective-permute-done.16, bf16[128,3072]{1,0:T(8,128)(2,1)} %collective-permute-done.14, bf16[128,3072]{1,0:T(8,128)(2,1)S(1)} %get-tuple-element.51, ...), kind=kLoop, calls=%fused_computation.6 | loop fusion | flops 4718592 | bytes 5505025 | tf_op jit(solution)/shard_map/convert_element_type | solution.py:382
  95.6 1.5 %collective-permute-start.20 = (bf16[64,3072]{1,0:T(8,128)(2,1)S(1)}, bf16[64,3072]{1,0:T(8,128)(2,1)S(1)}, u32[]{:S(2)}, u32[]{:S(2)}) collective-permute-start(bf16[64,3072]{1,0:T(8,128)(2,1)S(1)} %get-tuple-element.70), channel_id=1, source_target_pairs={{0,4},{1,3},{2,6},{3,1},{4,0},{5,7},{6,2},{7,5},{8,12},{9,11},{10,... | collective-permute-start | bytes 1179656 | tf_op jit(solution)/shard_map/ppermute | solution.py:349
  97.1 0.7 collective-permute-start.21
  97.8 4.3 %collective-permute-done.17 = bf16[128,3072]{1,0:T(8,128)(2,1)S(1)} collective-permute-done((bf16[128,3072]{1,0:T(8,128)(2,1)S(1)}, bf16[128,3072]{1,0:T(8,128)(2,1)S(1)}, u32[]{:S(2)}, u32[]{:S(2)}) %collective-permute-start.17) | collective-permute-done | bytes 786464 | tf_op jit(solution)/shard_map/ppermute | solution.py:349
  102.1 8.4 %collective-permute-done.18 = bf16[128,3072]{1,0:T(8,128)(2,1)S(1)} collective-permute-done((bf16[128,3072]{1,0:T(8,128)(2,1)}, bf16[128,3072]{1,0:T(8,128)(2,1)S(1)}, u32[]{:S(2)}, u32[]{:S(2)}) %collective-permute-start.18) | collective-permute-done | bytes 786464 | tf_op jit(solution)/shard_map/ppermute | solution.py:349
  110.5 0.7 fusion.7
  111.2 0.7 collective-permute-start.22
  112.0 4.0 %collective-permute-start.24 = (bf16[64,3072]{1,0:T(8,128)(2,1)S(1)}, bf16[64,3072]{1,0:T(8,128)(2,1)S(1)}, u32[]{:S(2)}, u32[]{:S(2)}) collective-permute-start(bf16[64,3072]{1,0:T(8,128)(2,1)S(1)} %get-tuple-element.65), channel_id=1, source_target_pairs={{1,13},{3,15},{5,9},{7,11},{9,5},{11,7},{13,1},{15,3},{17,29},{19,... | collective-permute-start | bytes 1179656 | tf_op jit(solution)/shard_map/ppermute | solution.py:349
  116.0 2.3 %collective-permute-start.25 = (bf16[64,3072]{1,0:T(8,128)(2,1)S(1)}, bf16[64,3072]{1,0:T(8,128)(2,1)S(1)}, u32[]{:S(2)}, u32[]{:S(2)}) collective-permute-start(bf16[64,3072]{1,0:T(8,128)(2,1)S(1)} %get-tuple-element.66), channel_id=1, source_target_pairs={{1,9},{3,11},{5,13},{7,15},{9,1},{11,3},{13,5},{15,7},{17,25},{19,... | collective-permute-start | bytes 1179656 | tf_op jit(solution)/shard_map/ppermute | solution.py:349
  118.3 0.9 collective-permute-start.23
  119.4 10.4 %collective-permute-start.27 = (bf16[32,3072]{1,0:T(8,128)(2,1)S(1)}, bf16[32,3072]{1,0:T(8,128)(2,1)S(1)}, u32[]{:S(2)}, u32[]{:S(2)}) collective-permute-start(bf16[32,3072]{1,0:T(8,128)(2,1)S(1)} %get-tuple-element.76), channel_id=1, source_target_pairs={{0,1},{1,0},{2,3},{3,2},{4,5},{5,4},{6,7},{7,6},{8,9},{9,8},{10,11... | collective-permute-start | bytes 589832 | tf_op jit(solution)/shard_map/ppermute | solution.py:349
  129.8 0.4 collective-permute-done.24
  130.2 2.5 %collective-permute-done.23 = bf16[64,3072]{1,0:T(8,128)(2,1)S(1)} collective-permute-done((bf16[64,3072]{1,0:T(8,128)(2,1)S(1)}, bf16[64,3072]{1,0:T(8,128)(2,1)S(1)}, u32[]{:S(2)}, u32[]{:S(2)}) %collective-permute-start.23) | collective-permute-done | bytes 393248 | tf_op jit(solution)/shard_map/ppermute | solution.py:349
  132.9 4.7 %collective-permute-start.26 = (bf16[32,3072]{1,0:T(8,128)(2,1)S(1)}, bf16[32,3072]{1,0:T(8,128)(2,1)S(1)}, u32[]{:S(2)}, u32[]{:S(2)}) collective-permute-start(bf16[32,3072]{1,0:T(8,128)(2,1)S(1)} %get-tuple-element.77), channel_id=1, source_target_pairs={{0,112},{1,113},{2,114},{3,115},{4,116},{5,117},{6,118},{7,119},{8... | collective-permute-start | bytes 589832 | tf_op jit(solution)/shard_map/ppermute | solution.py:349
  137.6 8.7 %collective-permute-done.28 = bf16[32,3072]{1,0:T(8,128)(2,1)S(1)} collective-permute-done((bf16[32,3072]{1,0:T(8,128)(2,1)S(1)}, bf16[32,3072]{1,0:T(8,128)(2,1)S(1)}, u32[]{:S(2)}, u32[]{:S(2)}) %collective-permute-start.28) | collective-permute-done | bytes 196640 | tf_op jit(solution)/shard_map/ppermute | solution.py:349
  146.5 0.9 pad_maximum_fusion
  (44 shorter events, 1.1 us)
Async XLA Ops:
  0.0 49.7 %collective-permute-start.10 = (bf16[512,6144]{1,0:T(8,128)(2,1)}, bf16[512,6144]{1,0:T(8,128)(2,1)}, u32[]{:S(2)}, u32[]{:S(2)}) collective-permute-start(bf16[512,6144]{1,0:T(8,128)(2,1)} %wa.3), channel_id=1, source_target_pairs={{0,1},{1,0},{2,3},{3,2},{4,5},{5,4},{6,7},{7,6},{8,9},{9,8},{10,11... | collective-permute-start | bytes 18874376 | tf_op jit(solution)/shard_map/ppermute | solution.py:349
  4.7 16.3 %collective-permute-start.3 = (bf16[2048,128]{1,0:T(8,128)(2,1)}, bf16[2048,128]{1,0:T(8,128)(2,1)S(1)}, u32[]{:S(2)}, u32[]{:S(2)}) collective-permute-start(bf16[2048,128]{1,0:T(8,128)(2,1)} %prep.1.kv_ref.own_ref), channel_id=1, source_target_pairs={{0,64},{2,66},{4,68},{6,70},{8,72},{10,74},{12,76},{14,78},{16,80}... | collective-permute-start | bytes 1572872 | tf_op jit(solution)/shard_map/ppermute | solution.py:349
  5.4 15.6 %collective-permute-start.2 = (bf16[2048,128]{1,0:T(8,128)(2,1)}, bf16[2048,128]{1,0:T(8,128)(2,1)S(1)}, u32[]{:S(2)}, u32[]{:S(2)}) collective-permute-start(bf16[2048,128]{1,0:T(8,128)(2,1)} %prep.1.kv_ref.own_ref), channel_id=1, source_target_pairs={{0,80},{1,17},{2,82},{3,19},{4,84},{5,21},{6,86},{7,23},{8,88},{9,... | collective-permute-start | bytes 1572872 | tf_op jit(solution)/shard_map/ppermute | solution.py:349
  11.0 16.1 %collective-permute-start.1 = (bf16[2048,128]{1,0:T(8,128)(2,1)}, bf16[2048,128]{1,0:T(8,128)(2,1)S(1)}, u32[]{:S(2)}, u32[]{:S(2)}) collective-permute-start(bf16[2048,128]{1,0:T(8,128)(2,1)} %prep.1.kv_ref.own_ref), channel_id=1, source_target_pairs={{0,96},{1,33},{2,98},{3,35},{4,100},{5,37},{6,102},{7,39},{8,104},... | collective-permute-start | bytes 1572872 | tf_op jit(solution)/shard_map/ppermute | solution.py:349
  14.1 26.9 %collective-permute-start = (bf16[2048,128]{1,0:T(8,128)(2,1)}, bf16[2048,128]{1,0:T(8,128)(2,1)S(1)}, u32[]{:S(2)}, u32[]{:S(2)}) collective-permute-start(bf16[2048,128]{1,0:T(8,128)(2,1)} %prep.1.kv_ref.own_ref), channel_id=1, source_target_pairs={{0,112},{1,49},{2,114},{3,51},{4,116},{5,53},{6,118},{7,55},{8,120... | collective-permute-start | bytes 1572872 | tf_op jit(solution)/shard_map/ppermute | solution.py:349
  16.0 1.1 copy-start
  17.1 1.2 copy-start.3
  18.3 27.8 %copy-start.1 = (bf16[2048,128]{1,0:T(8,128)(2,1)S(1)}, bf16[2048,128]{1,0:T(8,128)(2,1)}, u32[]{:S(2)}) copy-start(bf16[2048,128]{1,0:T(8,128)(2,1)} %prep.1.kv_ref.own_ref) | copy-start | bytes 1572868
  18.3 27.8 %copy-start.2 = (s32[13]{0:T(128)S(1)}, s32[13]{0:T(128)}, u32[]{:S(2)}) copy-start(s32[13]{0:T(128)} %stack.27.info) | copy-start | bytes 160
  41.0 2.8 %collective-permute-start.4 = (bf16[2048,128]{1,0:T(8,128)(2,1)S(1)}, bf16[2048,128]{1,0:T(8,128)(2,1)S(1)}, u32[]{:S(2)}, u32[]{:S(2)}) collective-permute-start(bf16[2048,128]{1,0:T(8,128)(2,1)S(1)} %collective-permute-done.refs_3_.refs_1_), channel_id=1, source_target_pairs={{0,1},{1,0},{2,3},{3,2},{4,5},{5,4},{6,7},{7,6},{8,9},{9,8},{10,11... | collective-permute-start | bytes 1572872 | tf_op jit(solution)/shard_map/ppermute | solution.py:349
  42.3 3.3 %collective-permute-start.5 = (bf16[2048,128]{1,0:T(8,128)(2,1)S(1)}, bf16[2048,128]{1,0:T(8,128)(2,1)S(1)}, u32[]{:S(2)}, u32[]{:S(2)}) collective-permute-start(bf16[2048,128]{1,0:T(8,128)(2,1)S(1)} %collective-permute-done.1.refs_4_.refs_2_), channel_id=1, source_target_pairs={{0,1},{1,0},{2,3},{3,2},{4,5},{5,4},{6,7},{7,6},{8,9},{9,8},{10,11... | collective-permute-start | bytes 1572872 | tf_op jit(solution)/shard_map/ppermute | solution.py:349
  42.3 3.3 %collective-permute-start.6 = (bf16[2048,128]{1,0:T(8,128)(2,1)S(1)}, bf16[2048,128]{1,0:T(8,128)(2,1)S(1)}, u32[]{:S(2)}, u32[]{:S(2)}) collective-permute-start(bf16[2048,128]{1,0:T(8,128)(2,1)S(1)} %collective-permute-done.2.refs_5_.refs_3_), channel_id=1, source_target_pairs={{0,1},{1,0},{2,3},{3,2},{4,5},{5,4},{6,7},{7,6},{8,9},{9,8},{10,11... | collective-permute-start | bytes 1572872 | tf_op jit(solution)/shard_map/ppermute | solution.py:349
  42.8 3.3 %collective-permute-start.7 = (bf16[2048,128]{1,0:T(8,128)(2,1)S(1)}, bf16[2048,128]{1,0:T(8,128)(2,1)S(1)}, u32[]{:S(2)}, u32[]{:S(2)}) collective-permute-start(bf16[2048,128]{1,0:T(8,128)(2,1)S(1)} %collective-permute-done.3.refs_6_.refs_4_), channel_id=1, source_target_pairs={{0,1},{1,0},{2,3},{3,2},{4,5},{5,4},{6,7},{7,6},{8,9},{9,8},{10,11... | collective-permute-start | bytes 1572872 | tf_op jit(solution)/shard_map/ppermute | solution.py:349
  43.8 18.2 %collective-permute-start.11 = (bf16[16,32,512]{2,1,0:T(8,128)(2,1)S(1)}, bf16[16,32,512]{2,1,0:T(8,128)(2,1)S(1)}, u32[]{:S(2)}, u32[]{:S(2)}) collective-permute-start(bf16[16,32,512]{2,1,0:T(8,128)(2,1)S(1)} %get-tuple-element.46), channel_id=1, source_target_pairs={{0,112},{1,113},{2,114},{3,115},{4,116},{5,117},{6,118},{7,119},{8... | collective-permute-start | bytes 1572872 | tf_op jit(solution)/shard_map/ppermute | solution.py:349
  46.0 3.6 %slice-start = ((s8[6291456]{0:T(1024)(128)(4,1)}), s8[4194304]{0:T(1024)(128)(4,1)S(1)}, s32[]{:S(2)}) async-start(s8[6291456]{0:T(1024)(128)(4,1)} %bitcast.7), calls=%async_computation | async-start | bytes 8388608
  46.1 3.6 %slice-start.1 = ((s8[6291456]{0:T(1024)(128)(4,1)}), s8[2097152]{0:T(1024)(128)(4,1)S(1)}, s32[]{:S(2)}) async-start(s8[6291456]{0:T(1024)(128)(4,1)} %bitcast.7), calls=%async_computation.1 | async-start | bytes 4194304
  47.7 1.6 %collective-permute-start.8 = (bf16[256,512]{1,0:T(8,128)(2,1)S(1)}, bf16[256,512]{1,0:T(8,128)(2,1)S(1)}, u32[]{:S(2)}, u32[]{:S(2)}) collective-permute-start(bf16[256,512]{1,0:T(8,128)(2,1)S(1)} %get-tuple-element.41), channel_id=1, source_target_pairs={{0,1},{1,0},{2,3},{3,2},{4,5},{5,4},{6,7},{7,6},{8,9},{9,8},{10,11... | collective-permute-start | bytes 786440 | tf_op jit(solution)/shard_map/ppermute | solution.py:349
  48.1 1.5 %collective-permute-start.9 = (bf16[256,512]{1,0:T(8,128)(2,1)S(1)}, bf16[256,512]{1,0:T(8,128)(2,1)S(1)}, u32[]{:S(2)}, u32[]{:S(2)}) collective-permute-start(bf16[256,512]{1,0:T(8,128)(2,1)S(1)} %get-tuple-element.42), channel_id=1, source_target_pairs={{0,1},{1,0},{2,3},{3,2},{4,5},{5,4},{6,7},{7,6},{8,9},{9,8},{10,11... | collective-permute-start | bytes 786440 | tf_op jit(solution)/shard_map/ppermute | solution.py:349
  56.2 36.2 %collective-permute-start.14 = (bf16[128,3072]{1,0:T(8,128)(2,1)}, bf16[128,3072]{1,0:T(8,128)(2,1)}, u32[]{:S(2)}, u32[]{:S(2)}) collective-permute-start(bf16[128,3072]{1,0:T(8,128)(2,1)} %get-tuple-element.52), channel_id=1, source_target_pairs={{0,2},{1,5},{2,0},{3,7},{4,6},{5,1},{6,4},{7,3},{8,10},{9,13},{10,... | collective-permute-start | bytes 2359304 | tf_op jit(solution)/shard_map/ppermute | solution.py:349
  57.5 35.7 %collective-permute-start.15 = (bf16[128,3072]{1,0:T(8,128)(2,1)S(1)}, bf16[128,3072]{1,0:T(8,128)(2,1)}, u32[]{:S(2)}, u32[]{:S(2)}) collective-permute-start(bf16[128,3072]{1,0:T(8,128)(2,1)S(1)} %get-tuple-element.53), channel_id=1, source_target_pairs={{0,2},{1,13},{2,0},{3,15},{4,6},{5,9},{6,4},{7,11},{8,10},{9,5},{1... | collective-permute-start | bytes 2359304 | tf_op jit(solution)/shard_map/ppermute | solution.py:349
  59.4 33.8 %collective-permute-start.16 = (bf16[128,3072]{1,0:T(8,128)(2,1)S(1)}, bf16[128,3072]{1,0:T(8,128)(2,1)}, u32[]{:S(2)}, u32[]{:S(2)}) collective-permute-start(bf16[128,3072]{1,0:T(8,128)(2,1)S(1)} %get-tuple-element.59), channel_id=1, source_target_pairs={{1,9},{3,11},{5,13},{7,15},{9,1},{11,3},{13,5},{15,7},{17,25},{19,... | collective-permute-start | bytes 2359304 | tf_op jit(solution)/shard_map/ppermute | solution.py:349
  81.7 1.8 %collective-permute-start.12 = (bf16[256,512]{1,0:T(8,128)(2,1)}, bf16[256,512]{1,0:T(8,128)(2,1)S(1)}, u32[]{:S(2)}, u32[]{:S(2)}) collective-permute-start(bf16[256,512]{1,0:T(8,128)(2,1)} %get-tuple-element.48), channel_id=1, source_target_pairs={{0,1},{1,0},{2,3},{3,2},{4,5},{5,4},{6,7},{7,6},{8,9},{9,8},{10,11... | collective-permute-start | bytes 786440 | tf_op jit(solution)/shard_map/ppermute | solution.py:349
  81.8 2.1 %collective-permute-start.13 = (bf16[256,512]{1,0:T(8,128)(2,1)}, bf16[256,512]{1,0:T(8,128)(2,1)S(1)}, u32[]{:S(2)}, u32[]{:S(2)}) collective-permute-start(bf16[256,512]{1,0:T(8,128)(2,1)} %get-tuple-element.49), channel_id=1, source_target_pairs={{0,1},{1,0},{2,3},{3,2},{4,5},{5,4},{6,7},{7,6},{8,9},{9,8},{10,11... | collective-permute-start | bytes 786440 | tf_op jit(solution)/shard_map/ppermute | solution.py:349
  90.9 11.2 %collective-permute-start.17 = (bf16[128,3072]{1,0:T(8,128)(2,1)S(1)}, bf16[128,3072]{1,0:T(8,128)(2,1)S(1)}, u32[]{:S(2)}, u32[]{:S(2)}) collective-permute-start(bf16[128,3072]{1,0:T(8,128)(2,1)S(1)} %get-tuple-element.55), channel_id=1, source_target_pairs={{0,4},{1,3},{2,6},{3,1},{4,0},{5,7},{6,2},{7,5},{8,12},{9,11},{10,... | collective-permute-start | bytes 2359304 | tf_op jit(solution)/shard_map/ppermute | solution.py:349
  92.4 18.1 %collective-permute-start.18 = (bf16[128,3072]{1,0:T(8,128)(2,1)}, bf16[128,3072]{1,0:T(8,128)(2,1)S(1)}, u32[]{:S(2)}, u32[]{:S(2)}) collective-permute-start(bf16[128,3072]{1,0:T(8,128)(2,1)} %get-tuple-element.56), channel_id=1, source_target_pairs={{0,12},{1,3},{2,14},{3,1},{4,8},{5,7},{6,10},{7,5},{8,4},{9,11},{1... | collective-permute-start | bytes 2359304 | tf_op jit(solution)/shard_map/ppermute | solution.py:349
  92.5 18.1 %collective-permute-start.19 = (bf16[128,3072]{1,0:T(8,128)(2,1)S(1)}, bf16[128,3072]{1,0:T(8,128)(2,1)S(1)}, u32[]{:S(2)}, u32[]{:S(2)}) collective-permute-start(bf16[128,3072]{1,0:T(8,128)(2,1)S(1)} %get-tuple-element.57), channel_id=1, source_target_pairs={{0,8},{2,10},{4,12},{6,14},{8,0},{10,2},{12,4},{14,6},{16,24},{18,... | collective-permute-start | bytes 2359304 | tf_op jit(solution)/shard_map/ppermute | solution.py:349
  95.6 22.7 %collective-permute-start.20 = (bf16[64,3072]{1,0:T(8,128)(2,1)S(1)}, bf16[64,3072]{1,0:T(8,128)(2,1)S(1)}, u32[]{:S(2)}, u32[]{:S(2)}) collective-permute-start(bf16[64,3072]{1,0:T(8,128)(2,1)S(1)} %get-tuple-element.70), channel_id=1, source_target_pairs={{0,4},{1,3},{2,6},{3,1},{4,0},{5,7},{6,2},{7,5},{8,12},{9,11},{10,... | collective-permute-start | bytes 1179656 | tf_op jit(solution)/shard_map/ppermute | solution.py:349
  97.1 22.1 %collective-permute-start.21 = (bf16[64,3072]{1,0:T(8,128)(2,1)S(1)}, bf16[64,3072]{1,0:T(8,128)(2,1)S(1)}, u32[]{:S(2)}, u32[]{:S(2)}) collective-permute-start(bf16[64,3072]{1,0:T(8,128)(2,1)S(1)} %get-tuple-element.73), channel_id=1, source_target_pairs={{0,12},{2,14},{4,8},{6,10},{8,4},{10,6},{12,0},{14,2},{16,28},{18,... | collective-permute-start | bytes 1179656 | tf_op jit(solution)/shard_map/ppermute | solution.py:349
  111.2 7.9 %collective-permute-start.22 = (bf16[64,3072]{1,0:T(8,128)(2,1)S(1)}, bf16[64,3072]{1,0:T(8,128)(2,1)S(1)}, u32[]{:S(2)}, u32[]{:S(2)}) collective-permute-start(bf16[64,3072]{1,0:T(8,128)(2,1)S(1)} %get-tuple-element.60), channel_id=1, source_target_pairs={{0,8},{2,10},{4,12},{6,14},{8,0},{10,2},{12,4},{14,6},{16,24},{18,... | collective-permute-start | bytes 1179656 | tf_op jit(solution)/shard_map/ppermute | solution.py:349
  112.0 18.2 %collective-permute-start.24 = (bf16[64,3072]{1,0:T(8,128)(2,1)S(1)}, bf16[64,3072]{1,0:T(8,128)(2,1)S(1)}, u32[]{:S(2)}, u32[]{:S(2)}) collective-permute-start(bf16[64,3072]{1,0:T(8,128)(2,1)S(1)} %get-tuple-element.65), channel_id=1, source_target_pairs={{1,13},{3,15},{5,9},{7,11},{9,5},{11,7},{13,1},{15,3},{17,29},{19,... | collective-permute-start | bytes 1179656 | tf_op jit(solution)/shard_map/ppermute | solution.py:349
  116.0 14.2 %collective-permute-start.25 = (bf16[64,3072]{1,0:T(8,128)(2,1)S(1)}, bf16[64,3072]{1,0:T(8,128)(2,1)S(1)}, u32[]{:S(2)}, u32[]{:S(2)}) collective-permute-start(bf16[64,3072]{1,0:T(8,128)(2,1)S(1)} %get-tuple-element.66), channel_id=1, source_target_pairs={{1,9},{3,11},{5,13},{7,15},{9,1},{11,3},{13,5},{15,7},{17,25},{19,... | collective-permute-start | bytes 1179656 | tf_op jit(solution)/shard_map/ppermute | solution.py:349
  118.3 14.4 %collective-permute-start.23 = (bf16[64,3072]{1,0:T(8,128)(2,1)S(1)}, bf16[64,3072]{1,0:T(8,128)(2,1)S(1)}, u32[]{:S(2)}, u32[]{:S(2)}) collective-permute-start(bf16[64,3072]{1,0:T(8,128)(2,1)S(1)} %fusion.8), channel_id=1, source_target_pairs={{0,2},{1,5},{2,0},{3,7},{4,6},{5,1},{6,4},{7,3},{8,10},{9,13},{10,... | collective-permute-start | bytes 1179656 | tf_op jit(solution)/shard_map/ppermute | solution.py:349
  119.4 18.2 %collective-permute-start.27 = (bf16[32,3072]{1,0:T(8,128)(2,1)S(1)}, bf16[32,3072]{1,0:T(8,128)(2,1)S(1)}, u32[]{:S(2)}, u32[]{:S(2)}) collective-permute-start(bf16[32,3072]{1,0:T(8,128)(2,1)S(1)} %get-tuple-element.76), channel_id=1, source_target_pairs={{0,1},{1,0},{2,3},{3,2},{4,5},{5,4},{6,7},{7,6},{8,9},{9,8},{10,11... | collective-permute-start | bytes 589832 | tf_op jit(solution)/shard_map/ppermute | solution.py:349
  132.9 13.4 %collective-permute-start.26 = (bf16[32,3072]{1,0:T(8,128)(2,1)S(1)}, bf16[32,3072]{1,0:T(8,128)(2,1)S(1)}, u32[]{:S(2)}, u32[]{:S(2)}) collective-permute-start(bf16[32,3072]{1,0:T(8,128)(2,1)S(1)} %get-tuple-element.77), channel_id=1, source_target_pairs={{0,112},{1,113},{2,114},{3,115},{4,116},{5,117},{6,118},{7,119},{8... | collective-permute-start | bytes 589832 | tf_op jit(solution)/shard_map/ppermute | solution.py:349
  137.6 8.7 %collective-permute-start.28 = (bf16[32,3072]{1,0:T(8,128)(2,1)S(1)}, bf16[32,3072]{1,0:T(8,128)(2,1)S(1)}, u32[]{:S(2)}, u32[]{:S(2)}) collective-permute-start(bf16[32,3072]{1,0:T(8,128)(2,1)S(1)} %get-tuple-element.78), channel_id=1, source_target_pairs={{0,113},{1,112},{2,115},{3,114},{4,117},{5,116},{6,119},{7,118},{8... | collective-permute-start | bytes 589832 | tf_op jit(solution)/shard_map/ppermute | solution.py:349

commit v14 on v13

--- a/solution.py
+++ b/solution.py
@@ -137,9 +137,7 @@
     ops = n_seq // 2
     inputs = 1 if foreign else 3
     mine, other = refs[inputs : inputs + ops], refs[inputs + ops : inputs + 2 * ops]
-    o_ref, first_ref, second_ref, q_buf, kv_buf, qt_ref, acc_ref, m_ref, mx_ref, peer_buf, count, sems = refs[
-        inputs + 2 * ops :
-    ]
+    o_ref, *peer_refs, q_buf, kv_buf, qt_ref, acc_ref, m_ref, mx_ref, peer_buf, count, sems = refs[inputs + 2 * ops :]
     place, core, partner = info[0], info[2], info[5]
     rows = own_ref.shape[0] // 2
     cols = qt_ref.shape[1]
@@ -248,8 +246,8 @@
                 there = pl.multiple_of(jnp.where(y_first, by_z, by_y), sub)
                 o_ref[pl.ds(here, sub), h * DH : (h + 1) * DH] = piece
                 peer_buf[pl.ds(there, sub), h * DH : (h + 1) * DH] = piece
-    first_ref[...] = peer_buf[: qb // 2, :]
-    second_ref[...] = peer_buf[qb // 2 :, :]
+    for i, ref in enumerate(peer_refs):
+        ref[...] = peer_buf[i * ref.shape[0] : (i + 1) * ref.shape[0], :]
 
 
 def attend(info, kv, state, q_shape, mine, other, n_y, n_seq):
@@ -259,14 +257,15 @@
     cols = qb * width // DH
     any_space = pl.BlockSpec(memory_space=pl.ANY)
     out = pl.BlockSpec((qb, width), lambda i, info: (0, 0))
-    part = pl.BlockSpec((qb // 2, width), lambda i, info: (0, 0))
+    pieces = 1 if foreign else 2
+    part = pl.BlockSpec((qb // pieces, width), lambda i, info: (0, 0))
     return pl.pallas_call(
         functools.partial(attend_kernel, foreign, groups, n_y, n_seq),
         grid_spec=pltpu.PrefetchScalarGridSpec(
             num_scalar_prefetch=1,
             grid=(1,),
             in_specs=[any_space] * (1 + len(state) + 2 * len(mine)),
-            out_specs=[out, part, part],
+            out_specs=[out] + [part] * pieces,
             scratch_shapes=[
                 pltpu.VMEM(q_shape, BF),
                 pltpu.VMEM((len(SLOTS) + 1, *kv.shape), BF),
@@ -279,7 +278,7 @@
                 pltpu.SemaphoreType.DMA((len(SLOTS) + 4,)),
             ],
         ),
-        out_shape=[jax.ShapeDtypeStruct((rows, width), BF) for rows in (qb, qb // 2, qb // 2)],
+        out_shape=[jax.ShapeDtypeStruct((rows, width), BF) for rows in [qb] + [qb // pieces] * pieces],
         name="attend_foreign" if foreign else "attend_own",
         cost_estimate=pl.CostEstimate(
             flops=2 * cols * kv.shape[0] * 4 * DH, bytes_accessed=4 << 20, transcendentals=0
@@ -293,8 +292,9 @@
     n = w.shape[1] // 2
     steps = n // tile
 
-    def body(info, a, b0, b1, wa, wb, *outs):
-        b = jnp.concatenate([b0[...], b1[...]], axis=0)
+    def body(info, a, *refs):
+        pieces, (wa, wb), outs = refs[: len(other)], refs[len(other) : len(other) + 2], refs[len(other) + 2 :]
+        b = jnp.concatenate([ref[...] for ref in pieces], axis=0)
         s = jnp.dot(a[...], wa[...], preferred_element_type=F32) + jnp.dot(
             b, wb[...], preferred_element_type=F32
         )
@@ -303,14 +303,14 @@
             o[...] = s[i * part : (i + 1) * part].astype(BF)
 
     whole = pl.BlockSpec((rows, width), lambda i, info: (0, 0))
-    half = pl.BlockSpec((rows // 2, width), lambda i, info: (0, 0))
+    piece = pl.BlockSpec((rows // len(other), width), lambda i, info: (0, 0))
     weights = pl.BlockSpec((width, tile), lambda i, info: (0, info[2] * steps + i))
     return pl.pallas_call(
         body,
         grid_spec=pltpu.PrefetchScalarGridSpec(
             num_scalar_prefetch=1,
             grid=(steps,),
-            in_specs=[whole, half, half, weights, weights],
+            in_specs=[whole] + [piece] * len(other) + [weights, weights],
             out_specs=[pl.BlockSpec((rows // parts, tile), lambda i, info: (0, i))] * parts,
         ),
         out_shape=[jax.ShapeDtypeStruct((rows // parts, n), BF)] * parts,

time: 148 us -> 149 us (level)
  starting transfers between devices: 50.6 us -> 53.5 us
  waiting for transfers between devices: 48.8 us -> 47.1 us
    ppermute x29 -> x28, starting transfers between devices: 50.6 us -> 53.5 us  [over_all(): return lax.ppermute(x, ('seq', 'head'), pairs)]
    ppermute x29 -> x28, waiting for transfers between devices: 48.8 us -> 47.1 us  [over_all(): return lax.ppermute(x, ('seq', 'head'), pairs)]
  transfers between devices with their start and end apart: 29 -> 28, of which waited for: 13 -> 11; matrix products, arithmetic and copies ran while one was open for 3% -> 3% of each run, Pallas kernels for 27% -> 27%
where the time goes in v14:
time: 149 us
  starting transfers between devices  53.5 us (36%)
  waiting for transfers between devices  47.1 us (32%)
  Pallas kernels  40.1 us (27%)
  other arithmetic  4.54 us (3%)
  local copies, waits for them, and re-layouts  3.18 us (2%)
    ppermute x28, starting transfers between devices, over_all(): return lax.ppermute(x, ('seq', 'head'), pairs)  53.5 us
    ppermute x28, waiting for transfers between devices, over_all(): return lax.ppermute(x, ('seq', 'head'), pairs)  47.1 us
    pallas_call x2, Pallas kernels, attend(): pl.pallas_call(functools.partial(attend_kernel, foreign, groups, n_y, n_s...  21.3 us
    pallas_call x2, Pallas kernels, project(): pl.pallas_call(body, grid_spec=pltpu.PrefetchScalarGridSpec(num_scalar_pr...  13.5 us
  transfers between devices with their start and end apart: 28, of which 11 were waited for; matrix products, arithmetic and copies ran while one was open for 3% of the time, Pallas kernels for 27%

profile of v14, /device:TPU:1, one launch (start us, length us, event | category | flops | bytes accessed | tf_op | source)
XLA Modules:
  0.0 148.6 jit_solution(6653272569009937487)
XLA Ops:
  0.0 1.4 collective-permute-start.10
  1.4 0.7 stack.27.info
  2.1 2.6 %prep.1.kv_ref.own_ref = bf16[2048,128]{1,0:T(8,128)(2,1)} custom-call(s32[13]{0:T(128)} %stack.27.info, bf16[1024,1024]{1,0:T(8,128)(2,1)} %k_ref.1, bf16[1024,1024]{1,0:T(8,128)(2,1)} %v_ref.1), custom_call_target="tpu_custom_call" | custom-call | tf_op jit(solution)/shard_map/prep/pallas_call | solution.py:37
  4.7 0.7 collective-permute-start.3
  5.4 5.6 %collective-permute-start.2 = (bf16[2048,128]{1,0:T(8,128)(2,1)}, bf16[2048,128]{1,0:T(8,128)(2,1)S(1)}, u32[]{:S(2)}, u32[]{:S(2)}) collective-permute-start(bf16[2048,128]{1,0:T(8,128)(2,1)} %prep.1.kv_ref.own_ref), channel_id=1, source_target_pairs={{0,80},{1,17},{2,82},{3,19},{4,84},{5,21},{6,86},{7,23},{8,88},{9,... | collective-permute-start | bytes 1572872 | tf_op jit(solution)/shard_map/ppermute | solution.py:349
  11.0 3.1 %collective-permute-start.1 = (bf16[2048,128]{1,0:T(8,128)(2,1)}, bf16[2048,128]{1,0:T(8,128)(2,1)S(1)}, u32[]{:S(2)}, u32[]{:S(2)}) collective-permute-start(bf16[2048,128]{1,0:T(8,128)(2,1)} %prep.1.kv_ref.own_ref), channel_id=1, source_target_pairs={{0,96},{1,33},{2,98},{3,35},{4,100},{5,37},{6,102},{7,39},{8,104},... | collective-permute-start | bytes 1572872 | tf_op jit(solution)/shard_map/ppermute | solution.py:349
  14.1 1.9 %collective-permute-start = (bf16[2048,128]{1,0:T(8,128)(2,1)}, bf16[2048,128]{1,0:T(8,128)(2,1)S(1)}, u32[]{:S(2)}, u32[]{:S(2)}) collective-permute-start(bf16[2048,128]{1,0:T(8,128)(2,1)} %prep.1.kv_ref.own_ref), channel_id=1, source_target_pairs={{0,112},{1,49},{2,114},{3,51},{4,116},{5,53},{6,118},{7,55},{8,120... | collective-permute-start | bytes 1572872 | tf_op jit(solution)/shard_map/ppermute | solution.py:349
  16.1 1.0 copy-done
  17.1 1.2 copy-done.3
  18.3 2.6 %own.1 = (bf16[256,2048]{1,0:T(8,128)(2,1)S(1)}, f32[144,2048]{1,0:T(8,128)S(1)}, f32[8,2048]{1,0:T(8,128)S(1)}, bf16[16,32,512]{2,1,0:T(8,128)(2,1)S(1)}) custom-call(bf16[16,2,32,512]{3,2,1,0:T(8,128)(2,1)S(1)} %bitcast.9, bf16[16,2,32,512]{3,2,1,0:T(8,128)(2,1)S(1)} %bitcast.10, bf16[2048,128]{1,0:T(8,128)(2,1)S(1)} %copy-done), custom_call_target="tpu_custom_call" | custom-call | flops 2147483648 | bytes 8388608 | tf_op jit(solution)/shard_map/own/pallas_call | solution.py:108
  21.0 6.1 %collective-permute-done.1.refs_4_.refs_2_ = bf16[2048,128]{1,0:T(8,128)(2,1)S(1)} collective-permute-done((bf16[2048,128]{1,0:T(8,128)(2,1)}, bf16[2048,128]{1,0:T(8,128)(2,1)S(1)}, u32[]{:S(2)}, u32[]{:S(2)}) %collective-permute-start.1) | collective-permute-done | bytes 524320 | tf_op jit(solution)/shard_map/ppermute | solution.py:349
  27.1 13.9 %collective-permute-done.refs_3_.refs_1_ = bf16[2048,128]{1,0:T(8,128)(2,1)S(1)} collective-permute-done((bf16[2048,128]{1,0:T(8,128)(2,1)}, bf16[2048,128]{1,0:T(8,128)(2,1)S(1)}, u32[]{:S(2)}, u32[]{:S(2)}) %collective-permute-start) | collective-permute-done | bytes 524320 | tf_op jit(solution)/shard_map/ppermute | solution.py:349
  41.0 1.3 collective-permute-start.4
  42.3 0.5 collective-permute-start.6
  42.8 1.0 collective-permute-done.4.refs_7_.refs_5_
  43.8 1.7 %collective-permute-start.11 = (bf16[16,32,512]{2,1,0:T(8,128)(2,1)S(1)}, bf16[16,32,512]{2,1,0:T(8,128)(2,1)S(1)}, u32[]{:S(2)}, u32[]{:S(2)}) collective-permute-start(bf16[16,32,512]{2,1,0:T(8,128)(2,1)S(1)} %get-tuple-element.45), channel_id=1, source_target_pairs={{0,112},{1,113},{2,114},{3,115},{4,116},{5,117},{6,118},{7,119},{8... | collective-permute-start | bytes 1572872 | tf_op jit(solution)/shard_map/ppermute | solution.py:349
  45.6 0.5 collective-permute-done.7.refs_10_.refs_8_
  46.1 1.6 %attend_own.1 = (bf16[512,512]{1,0:T(8,128)(2,1)S(1)}, bf16[256,512]{1,0:T(8,128)(2,1)S(1)}, bf16[256,512]{1,0:T(8,128)(2,1)S(1)}) custom-call(s32[13]{0:T(128)S(1)} %copy-done.2, bf16[2048,128]{1,0:T(8,128)(2,1)S(1)} %copy-done.1, bf16[256,2048]{1,0:T(8,128)(2,1)S(1)} %get-tuple-element.32.refs_0_, f32[144,2048]{1,0:T(8,128)S(1)} %get-tuple-element.33.refs_1_, ...), custom_call_target="tpu_custom_call" | custom-call | flops 4294967296 | bytes 4194304 | tf_op jit(solution)/shard_map/attend_own/pallas_call | solution.py:262
  47.7 0.5 collective-permute-start.8
  48.2 0.1 collective-permute-start.9
  48.3 1.0 collective-permute-done.8.refs_0_
  49.3 0.4 collective-permute-done.9.refs_1_
  49.7 6.5 %project.2 = (bf16[128,3072]{1,0:T(8,128)(2,1)S(1)}, bf16[128,3072]{1,0:T(8,128)(2,1)}, bf16[128,3072]{1,0:T(8,128)(2,1)S(1)}, bf16[128,3072]{1,0:T(8,128)(2,1)S(1)}) custom-call(s32[13]{0:T(128)S(1)} %copy-done.2, bf16[512,512]{1,0:T(8,128)(2,1)S(1)} %get-tuple-element.39.a, bf16[256,512]{1,0:T(8,128)(2,1)S(1)} %collective-permute-done.8.refs_0_, ...), custom_call_target="tpu_custom_call" | custom-call | tf_op jit(solution)/shard_map/project/pallas_call | solution.py:308
  56.3 1.3 collective-permute-start.13
  57.6 1.9 %collective-permute-start.14 = (bf16[128,3072]{1,0:T(8,128)(2,1)S(1)}, bf16[128,3072]{1,0:T(8,128)(2,1)}, u32[]{:S(2)}, u32[]{:S(2)}) collective-permute-start(bf16[128,3072]{1,0:T(8,128)(2,1)S(1)} %get-tuple-element.51), channel_id=1, source_target_pairs={{0,2},{1,13},{2,0},{3,15},{4,6},{5,9},{6,4},{7,11},{8,10},{9,5},{1... | collective-permute-start | bytes 2359304 | tf_op jit(solution)/shard_map/ppermute | solution.py:349
  59.5 2.6 %collective-permute-start.15 = (bf16[128,3072]{1,0:T(8,128)(2,1)S(1)}, bf16[128,3072]{1,0:T(8,128)(2,1)}, u32[]{:S(2)}, u32[]{:S(2)}) collective-permute-start(bf16[128,3072]{1,0:T(8,128)(2,1)S(1)} %get-tuple-element.57), channel_id=1, source_target_pairs={{1,9},{3,11},{5,13},{7,15},{9,1},{11,3},{13,5},{15,7},{17,25},{19,... | collective-permute-start | bytes 2359304 | tf_op jit(solution)/shard_map/ppermute | solution.py:349
  62.1 19.7 %attend_foreign.1 = (bf16[512,512]{1,0:T(8,128)(2,1)S(1)}, bf16[512,512]{1,0:T(8,128)(2,1)}) custom-call(s32[13]{0:T(128)S(1)} %copy-done.2, bf16[2048,128]{1,0:T(8,128)(2,1)S(1)} %copy-done.1, bf16[16,32,512]{2,1,0:T(8,128)(2,1)S(1)} %collective-permute-done.11.refs_0_, bf16[2048,128]{1,0:T(8,128)(2,1)S(1)} %collective-permute-done.refs_3_.refs_1_, ...), custom_call_target="tpu_custom_call" | custom-call | flops 4294967296 | bytes 4194304 | tf_op jit(solution)/shard_map/attend_foreign/pallas_call | solution.py:262
  81.9 2.1 %collective-permute-done.12.refs_0_ = bf16[512,512]{1,0:T(8,128)(2,1)S(1)} collective-permute-done((bf16[512,512]{1,0:T(8,128)(2,1)}, bf16[512,512]{1,0:T(8,128)(2,1)S(1)}, u32[]{:S(2)}, u32[]{:S(2)}) %collective-permute-start.12) | collective-permute-done | bytes 524320 | tf_op jit(solution)/shard_map/ppermute | solution.py:349
  84.0 7.0 %project.3 = (bf16[128,3072]{1,0:T(8,128)(2,1)S(1)}, bf16[128,3072]{1,0:T(8,128)(2,1)S(1)}, bf16[128,3072]{1,0:T(8,128)(2,1)S(1)}, bf16[128,3072]{1,0:T(8,128)(2,1)}) custom-call(s32[13]{0:T(128)S(1)} %copy-done.2, bf16[512,512]{1,0:T(8,128)(2,1)S(1)} %get-tuple-element.46.a, bf16[512,512]{1,0:T(8,128)(2,1)S(1)} %collective-permute-done.12.refs_0_, ...), custom_call_target="tpu_custom_call" | custom-call | tf_op jit(solution)/shard_map/project/pallas_call | solution.py:308
  91.0 1.5 %collective-permute-start.16 = (bf16[128,3072]{1,0:T(8,128)(2,1)S(1)}, bf16[128,3072]{1,0:T(8,128)(2,1)S(1)}, u32[]{:S(2)}, u32[]{:S(2)}) collective-permute-start(bf16[128,3072]{1,0:T(8,128)(2,1)S(1)} %get-tuple-element.53), channel_id=1, source_target_pairs={{0,4},{1,3},{2,6},{3,1},{4,0},{5,7},{6,2},{7,5},{8,12},{9,11},{10,... | collective-permute-start | bytes 2359304 | tf_op jit(solution)/shard_map/ppermute | solution.py:349
  92.5 0.7 collective-permute-start.18
  93.2 2.3 %fusion.2 = (bf16[128,3072]{1,0:T(8,128)(2,1)S(1)}, bf16[128,3072]{1,0:T(8,128)(2,1)S(1)}) fusion(bf16[128,3072]{1,0:T(8,128)(2,1)} %collective-permute-done.14, bf16[128,3072]{1,0:T(8,128)(2,1)} %collective-permute-done.15, bf16[128,3072]{1,0:T(8,128)(2,1)} %collective-permute-done.13, bf16[128,3072]{1,0:T(8,128)(2,1)S(1)} %get-tuple-element.49, ...), kind=kLoop, calls=%fused_computation.6 | loop fusion | flops 4718592 | bytes 5505025 | tf_op jit(solution)/shard_map/convert_element_type | solution.py:382
  95.6 1.5 %collective-permute-start.19 = (bf16[64,3072]{1,0:T(8,128)(2,1)S(1)}, bf16[64,3072]{1,0:T(8,128)(2,1)S(1)}, u32[]{:S(2)}, u32[]{:S(2)}) collective-permute-start(bf16[64,3072]{1,0:T(8,128)(2,1)S(1)} %get-tuple-element.68), channel_id=1, source_target_pairs={{0,4},{1,3},{2,6},{3,1},{4,0},{5,7},{6,2},{7,5},{8,12},{9,11},{10,... | collective-permute-start | bytes 1179656 | tf_op jit(solution)/shard_map/ppermute | solution.py:349
  97.2 0.7 collective-permute-start.20
  97.9 4.3 %collective-permute-done.16 = bf16[128,3072]{1,0:T(8,128)(2,1)S(1)} collective-permute-done((bf16[128,3072]{1,0:T(8,128)(2,1)S(1)}, bf16[128,3072]{1,0:T(8,128)(2,1)S(1)}, u32[]{:S(2)}, u32[]{:S(2)}) %collective-permute-start.16) | collective-permute-done | bytes 786464 | tf_op jit(solution)/shard_map/ppermute | solution.py:349
  102.1 8.4 %collective-permute-done.17 = bf16[128,3072]{1,0:T(8,128)(2,1)S(1)} collective-permute-done((bf16[128,3072]{1,0:T(8,128)(2,1)}, bf16[128,3072]{1,0:T(8,128)(2,1)S(1)}, u32[]{:S(2)}, u32[]{:S(2)}) %collective-permute-start.17) | collective-permute-done | bytes 786464 | tf_op jit(solution)/shard_map/ppermute | solution.py:349
  110.6 0.7 fusion.7
  111.3 0.7 collective-permute-start.21
  112.0 4.0 %collective-permute-start.23 = (bf16[64,3072]{1,0:T(8,128)(2,1)S(1)}, bf16[64,3072]{1,0:T(8,128)(2,1)S(1)}, u32[]{:S(2)}, u32[]{:S(2)}) collective-permute-start(bf16[64,3072]{1,0:T(8,128)(2,1)S(1)} %get-tuple-element.63), channel_id=1, source_target_pairs={{1,13},{3,15},{5,9},{7,11},{9,5},{11,7},{13,1},{15,3},{17,29},{19,... | collective-permute-start | bytes 1179656 | tf_op jit(solution)/shard_map/ppermute | solution.py:349
  116.0 4.3 %collective-permute-start.24 = (bf16[64,3072]{1,0:T(8,128)(2,1)S(1)}, bf16[64,3072]{1,0:T(8,128)(2,1)S(1)}, u32[]{:S(2)}, u32[]{:S(2)}) collective-permute-start(bf16[64,3072]{1,0:T(8,128)(2,1)S(1)} %get-tuple-element.64), channel_id=1, source_target_pairs={{1,9},{3,11},{5,13},{7,15},{9,1},{11,3},{13,5},{15,7},{17,25},{19,... | collective-permute-start | bytes 1179656 | tf_op jit(solution)/shard_map/ppermute | solution.py:349
  120.5 0.2 add_convert_fusion.1
  120.7 11.9 %collective-permute-start.26 = (bf16[32,3072]{1,0:T(8,128)(2,1)S(1)}, bf16[32,3072]{1,0:T(8,128)(2,1)S(1)}, u32[]{:S(2)}, u32[]{:S(2)}) collective-permute-start(bf16[32,3072]{1,0:T(8,128)(2,1)S(1)} %get-tuple-element.74), channel_id=1, source_target_pairs={{0,1},{1,0},{2,3},{3,2},{4,5},{5,4},{6,7},{7,6},{8,9},{9,8},{10,11... | collective-permute-start | bytes 589832 | tf_op jit(solution)/shard_map/ppermute | solution.py:349
  132.8 0.2 add_convert_fusion
  133.0 3.3 %collective-permute-start.25 = (bf16[32,3072]{1,0:T(8,128)(2,1)S(1)}, bf16[32,3072]{1,0:T(8,128)(2,1)S(1)}, u32[]{:S(2)}, u32[]{:S(2)}) collective-permute-start(bf16[32,3072]{1,0:T(8,128)(2,1)S(1)} %get-tuple-element.75), channel_id=1, source_target_pairs={{0,112},{1,113},{2,114},{3,115},{4,116},{5,117},{6,118},{7,119},{8... | collective-permute-start | bytes 589832 | tf_op jit(solution)/shard_map/ppermute | solution.py:349
  136.3 2.0 %collective-permute-start.27 = (bf16[32,3072]{1,0:T(8,128)(2,1)S(1)}, bf16[32,3072]{1,0:T(8,128)(2,1)S(1)}, u32[]{:S(2)}, u32[]{:S(2)}) collective-permute-start(bf16[32,3072]{1,0:T(8,128)(2,1)S(1)} %get-tuple-element.76), channel_id=1, source_target_pairs={{0,113},{1,112},{2,115},{3,114},{4,117},{5,116},{6,119},{7,118},{8... | collective-permute-start | bytes 589832 | tf_op jit(solution)/shard_map/ppermute | solution.py:349
  138.3 9.2 %collective-permute-done.27 = bf16[32,3072]{1,0:T(8,128)(2,1)S(1)} collective-permute-done((bf16[32,3072]{1,0:T(8,128)(2,1)S(1)}, bf16[32,3072]{1,0:T(8,128)(2,1)S(1)}, u32[]{:S(2)}, u32[]{:S(2)}) %collective-permute-start.27) | collective-permute-done | bytes 196640 | tf_op jit(solution)/shard_map/ppermute | solution.py:349
  147.6 0.1 broadcast_select_fusion.1
  147.7 0.9 pad_maximum_fusion
  (42 shorter events, 0.6 us)
Async XLA Ops:
  0.0 49.7 %collective-permute-start.10 = (bf16[512,6144]{1,0:T(8,128)(2,1)}, bf16[512,6144]{1,0:T(8,128)(2,1)}, u32[]{:S(2)}, u32[]{:S(2)}) collective-permute-start(bf16[512,6144]{1,0:T(8,128)(2,1)} %refs_1_.1), channel_id=1, source_target_pairs={{0,1},{1,0},{2,3},{3,2},{4,5},{5,4},{6,7},{7,6},{8,9},{9,8},{10,11... | collective-permute-start | bytes 18874376 | tf_op jit(solution)/shard_map/ppermute | solution.py:349
  4.7 16.3 %collective-permute-start.3 = (bf16[2048,128]{1,0:T(8,128)(2,1)}, bf16[2048,128]{1,0:T(8,128)(2,1)S(1)}, u32[]{:S(2)}, u32[]{:S(2)}) collective-permute-start(bf16[2048,128]{1,0:T(8,128)(2,1)} %prep.1.kv_ref.own_ref), channel_id=1, source_target_pairs={{0,64},{2,66},{4,68},{6,70},{8,72},{10,74},{12,76},{14,78},{16,80}... | collective-permute-start | bytes 1572872 | tf_op jit(solution)/shard_map/ppermute | solution.py:349
  5.4 15.6 %collective-permute-start.2 = (bf16[2048,128]{1,0:T(8,128)(2,1)}, bf16[2048,128]{1,0:T(8,128)(2,1)S(1)}, u32[]{:S(2)}, u32[]{:S(2)}) collective-permute-start(bf16[2048,128]{1,0:T(8,128)(2,1)} %prep.1.kv_ref.own_ref), channel_id=1, source_target_pairs={{0,80},{1,17},{2,82},{3,19},{4,84},{5,21},{6,86},{7,23},{8,88},{9,... | collective-permute-start | bytes 1572872 | tf_op jit(solution)/shard_map/ppermute | solution.py:349
  11.0 16.1 %collective-permute-start.1 = (bf16[2048,128]{1,0:T(8,128)(2,1)}, bf16[2048,128]{1,0:T(8,128)(2,1)S(1)}, u32[]{:S(2)}, u32[]{:S(2)}) collective-permute-start(bf16[2048,128]{1,0:T(8,128)(2,1)} %prep.1.kv_ref.own_ref), channel_id=1, source_target_pairs={{0,96},{1,33},{2,98},{3,35},{4,100},{5,37},{6,102},{7,39},{8,104},... | collective-permute-start | bytes 1572872 | tf_op jit(solution)/shard_map/ppermute | solution.py:349
  14.1 26.9 %collective-permute-start = (bf16[2048,128]{1,0:T(8,128)(2,1)}, bf16[2048,128]{1,0:T(8,128)(2,1)S(1)}, u32[]{:S(2)}, u32[]{:S(2)}) collective-permute-start(bf16[2048,128]{1,0:T(8,128)(2,1)} %prep.1.kv_ref.own_ref), channel_id=1, source_target_pairs={{0,112},{1,49},{2,114},{3,51},{4,116},{5,53},{6,118},{7,55},{8,120... | collective-permute-start | bytes 1572872 | tf_op jit(solution)/shard_map/ppermute | solution.py:349
  16.1 1.1 copy-start
  17.1 1.2 copy-start.3
  18.3 27.8 %copy-start.1 = (bf16[2048,128]{1,0:T(8,128)(2,1)S(1)}, bf16[2048,128]{1,0:T(8,128)(2,1)}, u32[]{:S(2)}) copy-start(bf16[2048,128]{1,0:T(8,128)(2,1)} %prep.1.kv_ref.own_ref) | copy-start | bytes 1572868
  18.3 27.8 %copy-start.2 = (s32[13]{0:T(128)S(1)}, s32[13]{0:T(128)}, u32[]{:S(2)}) copy-start(s32[13]{0:T(128)} %stack.27.info) | copy-start | bytes 160
  41.0 2.8 %collective-permute-start.4 = (bf16[2048,128]{1,0:T(8,128)(2,1)S(1)}, bf16[2048,128]{1,0:T(8,128)(2,1)S(1)}, u32[]{:S(2)}, u32[]{:S(2)}) collective-permute-start(bf16[2048,128]{1,0:T(8,128)(2,1)S(1)} %collective-permute-done.refs_3_.refs_1_), channel_id=1, source_target_pairs={{0,1},{1,0},{2,3},{3,2},{4,5},{5,4},{6,7},{7,6},{8,9},{9,8},{10,11... | collective-permute-start | bytes 1572872 | tf_op jit(solution)/shard_map/ppermute | solution.py:349
  42.3 3.3 %collective-permute-start.5 = (bf16[2048,128]{1,0:T(8,128)(2,1)S(1)}, bf16[2048,128]{1,0:T(8,128)(2,1)S(1)}, u32[]{:S(2)}, u32[]{:S(2)}) collective-permute-start(bf16[2048,128]{1,0:T(8,128)(2,1)S(1)} %collective-permute-done.1.refs_4_.refs_2_), channel_id=1, source_target_pairs={{0,1},{1,0},{2,3},{3,2},{4,5},{5,4},{6,7},{7,6},{8,9},{9,8},{10,11... | collective-permute-start | bytes 1572872 | tf_op jit(solution)/shard_map/ppermute | solution.py:349
  42.3 3.3 %collective-permute-start.6 = (bf16[2048,128]{1,0:T(8,128)(2,1)S(1)}, bf16[2048,128]{1,0:T(8,128)(2,1)S(1)}, u32[]{:S(2)}, u32[]{:S(2)}) collective-permute-start(bf16[2048,128]{1,0:T(8,128)(2,1)S(1)} %collective-permute-done.2.refs_5_.refs_3_), channel_id=1, source_target_pairs={{0,1},{1,0},{2,3},{3,2},{4,5},{5,4},{6,7},{7,6},{8,9},{9,8},{10,11... | collective-permute-start | bytes 1572872 | tf_op jit(solution)/shard_map/ppermute | solution.py:349
  42.8 3.3 %collective-permute-start.7 = (bf16[2048,128]{1,0:T(8,128)(2,1)S(1)}, bf16[2048,128]{1,0:T(8,128)(2,1)S(1)}, u32[]{:S(2)}, u32[]{:S(2)}) collective-permute-start(bf16[2048,128]{1,0:T(8,128)(2,1)S(1)} %collective-permute-done.3.refs_6_.refs_4_), channel_id=1, source_target_pairs={{0,1},{1,0},{2,3},{3,2},{4,5},{5,4},{6,7},{7,6},{8,9},{9,8},{10,11... | collective-permute-start | bytes 1572872 | tf_op jit(solution)/shard_map/ppermute | solution.py:349
  43.8 18.2 %collective-permute-start.11 = (bf16[16,32,512]{2,1,0:T(8,128)(2,1)S(1)}, bf16[16,32,512]{2,1,0:T(8,128)(2,1)S(1)}, u32[]{:S(2)}, u32[]{:S(2)}) collective-permute-start(bf16[16,32,512]{2,1,0:T(8,128)(2,1)S(1)} %get-tuple-element.45), channel_id=1, source_target_pairs={{0,112},{1,113},{2,114},{3,115},{4,116},{5,117},{6,118},{7,119},{8... | collective-permute-start | bytes 1572872 | tf_op jit(solution)/shard_map/ppermute | solution.py:349
  46.1 3.6 %slice-start = ((s8[6291456]{0:T(1024)(128)(4,1)}), s8[4194304]{0:T(1024)(128)(4,1)S(1)}, s32[]{:S(2)}) async-start(s8[6291456]{0:T(1024)(128)(4,1)} %bitcast.7), calls=%async_computation | async-start | bytes 8388608
  46.1 3.6 %slice-start.1 = ((s8[6291456]{0:T(1024)(128)(4,1)}), s8[2097152]{0:T(1024)(128)(4,1)S(1)}, s32[]{:S(2)}) async-start(s8[6291456]{0:T(1024)(128)(4,1)} %bitcast.7), calls=%async_computation.1 | async-start | bytes 4194304
  47.7 1.6 %collective-permute-start.8 = (bf16[256,512]{1,0:T(8,128)(2,1)S(1)}, bf16[256,512]{1,0:T(8,128)(2,1)S(1)}, u32[]{:S(2)}, u32[]{:S(2)}) collective-permute-start(bf16[256,512]{1,0:T(8,128)(2,1)S(1)} %get-tuple-element.40), channel_id=1, source_target_pairs={{0,1},{1,0},{2,3},{3,2},{4,5},{5,4},{6,7},{7,6},{8,9},{9,8},{10,11... | collective-permute-start | bytes 786440 | tf_op jit(solution)/shard_map/ppermute | solution.py:349
  48.2 1.5 %collective-permute-start.9 = (bf16[256,512]{1,0:T(8,128)(2,1)S(1)}, bf16[256,512]{1,0:T(8,128)(2,1)S(1)}, u32[]{:S(2)}, u32[]{:S(2)}) collective-permute-start(bf16[256,512]{1,0:T(8,128)(2,1)S(1)} %get-tuple-element.41), channel_id=1, source_target_pairs={{0,1},{1,0},{2,3},{3,2},{4,5},{5,4},{6,7},{7,6},{8,9},{9,8},{10,11... | collective-permute-start | bytes 786440 | tf_op jit(solution)/shard_map/ppermute | solution.py:349
  56.3 36.2 %collective-permute-start.13 = (bf16[128,3072]{1,0:T(8,128)(2,1)}, bf16[128,3072]{1,0:T(8,128)(2,1)}, u32[]{:S(2)}, u32[]{:S(2)}) collective-permute-start(bf16[128,3072]{1,0:T(8,128)(2,1)} %get-tuple-element.50), channel_id=1, source_target_pairs={{0,2},{1,5},{2,0},{3,7},{4,6},{5,1},{6,4},{7,3},{8,10},{9,13},{10,... | collective-permute-start | bytes 2359304 | tf_op jit(solution)/shard_map/ppermute | solution.py:349
  57.6 35.7 %collective-permute-start.14 = (bf16[128,3072]{1,0:T(8,128)(2,1)S(1)}, bf16[128,3072]{1,0:T(8,128)(2,1)}, u32[]{:S(2)}, u32[]{:S(2)}) collective-permute-start(bf16[128,3072]{1,0:T(8,128)(2,1)S(1)} %get-tuple-element.51), channel_id=1, source_target_pairs={{0,2},{1,13},{2,0},{3,15},{4,6},{5,9},{6,4},{7,11},{8,10},{9,5},{1... | collective-permute-start | bytes 2359304 | tf_op jit(solution)/shard_map/ppermute | solution.py:349
  59.5 33.8 %collective-permute-start.15 = (bf16[128,3072]{1,0:T(8,128)(2,1)S(1)}, bf16[128,3072]{1,0:T(8,128)(2,1)}, u32[]{:S(2)}, u32[]{:S(2)}) collective-permute-start(bf16[128,3072]{1,0:T(8,128)(2,1)S(1)} %get-tuple-element.57), channel_id=1, source_target_pairs={{1,9},{3,11},{5,13},{7,15},{9,1},{11,3},{13,5},{15,7},{17,25},{19,... | collective-permute-start | bytes 2359304 | tf_op jit(solution)/shard_map/ppermute | solution.py:349
  81.8 2.2 %collective-permute-start.12 = (bf16[512,512]{1,0:T(8,128)(2,1)}, bf16[512,512]{1,0:T(8,128)(2,1)S(1)}, u32[]{:S(2)}, u32[]{:S(2)}) collective-permute-start(bf16[512,512]{1,0:T(8,128)(2,1)} %get-tuple-element.47), channel_id=1, source_target_pairs={{0,1},{1,0},{2,3},{3,2},{4,5},{5,4},{6,7},{7,6},{8,9},{9,8},{10,11... | collective-permute-start | bytes 1572872 | tf_op jit(solution)/shard_map/ppermute | solution.py:349
  91.0 11.2 %collective-permute-start.16 = (bf16[128,3072]{1,0:T(8,128)(2,1)S(1)}, bf16[128,3072]{1,0:T(8,128)(2,1)S(1)}, u32[]{:S(2)}, u32[]{:S(2)}) collective-permute-start(bf16[128,3072]{1,0:T(8,128)(2,1)S(1)} %get-tuple-element.53), channel_id=1, source_target_pairs={{0,4},{1,3},{2,6},{3,1},{4,0},{5,7},{6,2},{7,5},{8,12},{9,11},{10,... | collective-permute-start | bytes 2359304 | tf_op jit(solution)/shard_map/ppermute | solution.py:349
  92.5 18.1 %collective-permute-start.17 = (bf16[128,3072]{1,0:T(8,128)(2,1)}, bf16[128,3072]{1,0:T(8,128)(2,1)S(1)}, u32[]{:S(2)}, u32[]{:S(2)}) collective-permute-start(bf16[128,3072]{1,0:T(8,128)(2,1)} %get-tuple-element.54), channel_id=1, source_target_pairs={{0,12},{1,3},{2,14},{3,1},{4,8},{5,7},{6,10},{7,5},{8,4},{9,11},{1... | collective-permute-start | bytes 2359304 | tf_op jit(solution)/shard_map/ppermute | solution.py:349
  92.5 18.1 %collective-permute-start.18 = (bf16[128,3072]{1,0:T(8,128)(2,1)S(1)}, bf16[128,3072]{1,0:T(8,128)(2,1)S(1)}, u32[]{:S(2)}, u32[]{:S(2)}) collective-permute-start(bf16[128,3072]{1,0:T(8,128)(2,1)S(1)} %get-tuple-element.55), channel_id=1, source_target_pairs={{0,8},{2,10},{4,12},{6,14},{8,0},{10,2},{12,4},{14,6},{16,24},{18,... | collective-permute-start | bytes 2359304 | tf_op jit(solution)/shard_map/ppermute | solution.py:349
  95.6 24.7 %collective-permute-start.19 = (bf16[64,3072]{1,0:T(8,128)(2,1)S(1)}, bf16[64,3072]{1,0:T(8,128)(2,1)S(1)}, u32[]{:S(2)}, u32[]{:S(2)}) collective-permute-start(bf16[64,3072]{1,0:T(8,128)(2,1)S(1)} %get-tuple-element.68), channel_id=1, source_target_pairs={{0,4},{1,3},{2,6},{3,1},{4,0},{5,7},{6,2},{7,5},{8,12},{9,11},{10,... | collective-permute-start | bytes 1179656 | tf_op jit(solution)/shard_map/ppermute | solution.py:349
  97.2 23.3 %collective-permute-start.20 = (bf16[64,3072]{1,0:T(8,128)(2,1)S(1)}, bf16[64,3072]{1,0:T(8,128)(2,1)S(1)}, u32[]{:S(2)}, u32[]{:S(2)}) collective-permute-start(bf16[64,3072]{1,0:T(8,128)(2,1)S(1)} %get-tuple-element.71), channel_id=1, source_target_pairs={{0,12},{2,14},{4,8},{6,10},{8,4},{10,6},{12,0},{14,2},{16,28},{18,... | collective-permute-start | bytes 1179656 | tf_op jit(solution)/shard_map/ppermute | solution.py:349
  111.3 9.2 %collective-permute-start.21 = (bf16[64,3072]{1,0:T(8,128)(2,1)S(1)}, bf16[64,3072]{1,0:T(8,128)(2,1)S(1)}, u32[]{:S(2)}, u32[]{:S(2)}) collective-permute-start(bf16[64,3072]{1,0:T(8,128)(2,1)S(1)} %get-tuple-element.58), channel_id=1, source_target_pairs={{0,8},{2,10},{4,12},{6,14},{8,0},{10,2},{12,4},{14,6},{16,24},{18,... | collective-permute-start | bytes 1179656 | tf_op jit(solution)/shard_map/ppermute | solution.py:349
  112.0 20.6 %collective-permute-start.23 = (bf16[64,3072]{1,0:T(8,128)(2,1)S(1)}, bf16[64,3072]{1,0:T(8,128)(2,1)S(1)}, u32[]{:S(2)}, u32[]{:S(2)}) collective-permute-start(bf16[64,3072]{1,0:T(8,128)(2,1)S(1)} %get-tuple-element.63), channel_id=1, source_target_pairs={{1,13},{3,15},{5,9},{7,11},{9,5},{11,7},{13,1},{15,3},{17,29},{19,... | collective-permute-start | bytes 1179656 | tf_op jit(solution)/shard_map/ppermute | solution.py:349
  116.0 16.6 %collective-permute-start.24 = (bf16[64,3072]{1,0:T(8,128)(2,1)S(1)}, bf16[64,3072]{1,0:T(8,128)(2,1)S(1)}, u32[]{:S(2)}, u32[]{:S(2)}) collective-permute-start(bf16[64,3072]{1,0:T(8,128)(2,1)S(1)} %get-tuple-element.64), channel_id=1, source_target_pairs={{1,9},{3,11},{5,13},{7,15},{9,1},{11,3},{13,5},{15,7},{17,25},{19,... | collective-permute-start | bytes 1179656 | tf_op jit(solution)/shard_map/ppermute | solution.py:349
  120.4 12.4 %collective-permute-start.22 = (bf16[64,3072]{1,0:T(8,128)(2,1)S(1)}, bf16[64,3072]{1,0:T(8,128)(2,1)S(1)}, u32[]{:S(2)}, u32[]{:S(2)}) collective-permute-start(bf16[64,3072]{1,0:T(8,128)(2,1)S(1)} %fusion.8), channel_id=1, source_target_pairs={{0,2},{1,5},{2,0},{3,7},{4,6},{5,1},{6,4},{7,3},{8,10},{9,13},{10,... | collective-permute-start | bytes 1179656 | tf_op jit(solution)/shard_map/ppermute | solution.py:349
  120.7 17.6 %collective-permute-start.26 = (bf16[32,3072]{1,0:T(8,128)(2,1)S(1)}, bf16[32,3072]{1,0:T(8,128)(2,1)S(1)}, u32[]{:S(2)}, u32[]{:S(2)}) collective-permute-start(bf16[32,3072]{1,0:T(8,128)(2,1)S(1)} %get-tuple-element.74), channel_id=1, source_target_pairs={{0,1},{1,0},{2,3},{3,2},{4,5},{5,4},{6,7},{7,6},{8,9},{9,8},{10,11... | collective-permute-start | bytes 589832 | tf_op jit(solution)/shard_map/ppermute | solution.py:349
  133.0 14.6 %collective-permute-start.25 = (bf16[32,3072]{1,0:T(8,128)(2,1)S(1)}, bf16[32,3072]{1,0:T(8,128)(2,1)S(1)}, u32[]{:S(2)}, u32[]{:S(2)}) collective-permute-start(bf16[32,3072]{1,0:T(8,128)(2,1)S(1)} %get-tuple-element.75), channel_id=1, source_target_pairs={{0,112},{1,113},{2,114},{3,115},{4,116},{5,117},{6,118},{7,119},{8... | collective-permute-start | bytes 589832 | tf_op jit(solution)/shard_map/ppermute | solution.py:349
  136.3 11.3 %collective-permute-start.27 = (bf16[32,3072]{1,0:T(8,128)(2,1)S(1)}, bf16[32,3072]{1,0:T(8,128)(2,1)S(1)}, u32[]{:S(2)}, u32[]{:S(2)}) collective-permute-start(bf16[32,3072]{1,0:T(8,128)(2,1)S(1)} %get-tuple-element.76), channel_id=1, source_target_pairs={{0,113},{1,112},{2,115},{3,114},{4,117},{5,116},{6,119},{7,118},{8... | collective-permute-start | bytes 589832 | tf_op jit(solution)/shard_map/ppermute | solution.py:349
